TPU v7x, 32 devices: a whole 2x2x4 slice. The times are simulated.
32 devices in a mesh: wide: 8 (over z, y), narrow: 4 (over x, core).
Axes of the slice: x: 2, y: 2, z: 4, core: 2. Of those that a mesh axis runs over, the one named last changes fastest.
Arguments:
- hidden: bfloat16 [128, 512, 768], P(('wide', 'narrow')), may hold values from -6 to 6
- lengths: int32 [128], P(('wide', 'narrow')), may hold values from 1 to 512, 22528 in all
- cotangent: bfloat16 [128, 256, 768], P(('wide', 'narrow')), may hold values from -6 to 6
- inflow: bfloat16 [3, 768, 768], P(None, ('wide', 'narrow')), may hold values from -0.21875 to 0.21875
- outflow: bfloat16 [768, 768], P(('wide', 'narrow')), may hold values from -1.75 to 1.75
- widener: bfloat16 [768, 3072], P(('wide', 'narrow')), may hold values from -0.21875 to 0.21875
- narrower: bfloat16 [3072, 768], P(('wide', 'narrow')), may hold values from -0.109375 to 0.109375
- shifts: bfloat16 [8, 768], P(None, ('wide', 'narrow')), may hold values from -1.5 to 1.5, as said below
- offsets: bfloat16 [3072], P(('wide', 'narrow')), may hold values from -3 to 3
- distance: bfloat16 [384], P(('wide', 'narrow')), may hold values from -4 to 4
- intake: bfloat16 [3, 768, 768], P(None, ('wide', 'narrow')), may hold values from -0.21875 to 0.21875
- outtake: bfloat16 [768, 768], P(('wide', 'narrow')), may hold values from -1.75 to 1.75
- expander: bfloat16 [768, 3072], P(('wide', 'narrow')), may hold values from -0.21875 to 0.21875
- squeezer: bfloat16 [3072, 768], P(('wide', 'narrow')), may hold values from -0.109375 to 0.109375
- adjusts: bfloat16 [8, 768], P(None, ('wide', 'narrow')), may hold values from -1.5 to 1.5, as said below
- leanings: bfloat16 [3072], P(('wide', 'narrow')), may hold values from -3 to 3
- spacing: bfloat16 [384], P(('wide', 'narrow')), may hold values from -4 to 4
Outputs:
- pooled_layer: bfloat16 [128, 256, 768], P(('wide', 'narrow'))
- full_layer: bfloat16 [128, 256, 768], P(('wide', 'narrow'))
- hidden_grad: float32 [128, 512, 768], P(('wide', 'narrow'))
- inflow_grad: float32 [3, 768, 768], P(None, ('wide', 'narrow'))
- outflow_grad: float32 [768, 768], P(('wide', 'narrow'))
- widener_grad: float32 [768, 3072], P(('wide', 'narrow'))
- narrower_grad: float32 [3072, 768], P(('wide', 'narrow'))
- shifts_grad: float32 [8, 768], P(None, ('wide', 'narrow'))
- offsets_grad: float32 [3072], P(('wide', 'narrow'))
- distance_grad: float32 [384], P(('wide', 'narrow'))
- intake_grad: float32 [3, 768, 768], P(None, ('wide', 'narrow'))
- outtake_grad: float32 [768, 768], P(('wide', 'narrow'))
- expander_grad: float32 [768, 3072], P(('wide', 'narrow'))
- squeezer_grad: float32 [3072, 768], P(('wide', 'narrow'))
- adjusts_grad: float32 [7, 768], P(None, ('wide', 'narrow'))
- leanings_grad: float32 [3072], P(('wide', 'narrow'))
- spacing_grad: float32 [384], P(('wide', 'narrow'))
- query_bias_grad: float32 [768], P(('wide', 'narrow'))
Inputs may be any that keep to these rules, and one draw needn't show every extreme that they name: `lengths`: the longest row has exactly 512 real tokens. `shifts`: rows 3 and 6 are norm gains between 0.6 and 1.4; the other rows are biases. `adjusts`: rows 3 and 6 are norm gains between 0.6 and 1.4; the other rows are biases.
All inputs are finite; a program needn't handle non-finite values. No bound on the sum of `lengths` on one device may be relied on, other than what follows from the above.
Results may differ from a plain program's by a relative error of at most 0.035.
Values may be sent and summed in bfloat16 or wider, within the bound.
No kernel may reach another device: no remote copies, remote signals or barrier semaphores. Data moves between devices by JAX's collectives and lax.ppermute only.
A program may use at most 320 MiB of HBM per device.

v0:
```python
import jax
import jax.numpy as jnp
from jax import lax
from jax.sharding import PartitionSpec as P

H = 12
HD = 64
NB = 32


EPS = 1e-06


def layer_norm(u, gain, shift):
    mean = jnp.mean(u, axis=-1, keepdims=True)
    centred = u - mean
    spread = jnp.mean(centred * centred, axis=-1, keepdims=True)
    return centred * lax.rsqrt(spread + EPS) * gain + shift


def gelu_tanh(value):
    return jax.nn.gelu(value, approximate=True)


def flat_dot(left, right):
    return jnp.dot(left.reshape(-1, left.shape[-1]), right, preferred_element_type=jnp.float32)


def weight_grad(left, right):
    left = left.reshape(-1, left.shape[-1])
    right = right.reshape(-1, right.shape[-1])
    return lax.dot_general(
        left, right, (((0,), (0,)), ((), ())), preferred_element_type=jnp.float32
    )


def input_grad(grads, weight):
    grads = grads.reshape(-1, grads.shape[-1])
    return lax.dot_general(
        grads, weight, (((1,), (1,)), ((), ())), preferred_element_type=jnp.float32
    )


def column_sum(values):
    return jnp.sum(values.reshape(-1, values.shape[-1]).astype(jnp.float32), axis=0)


def bucket_onehot(queries, keys, stride):
    place = lax.broadcasted_iota(jnp.int32, (queries, keys), 1) - stride * lax.broadcasted_iota(
        jnp.int32, (queries, keys), 0
    )
    bucket = jnp.clip(place, -(NB // 2), NB // 2 - 1) + NB // 2
    return bucket.reshape(-1, 1) == lax.broadcasted_iota(jnp.int32, (1, NB), 1)


def position_bias(table, queries, keys, stride):
    onehot = bucket_onehot(queries, keys, stride).astype(jnp.bfloat16)
    heads = table.reshape(H, NB)
    flat = lax.dot_general(
        heads, onehot, (((1,), (1,)), ((), ())), preferred_element_type=jnp.float32
    )
    return flat.reshape(H, queries, keys)


def table_grad(bias_sum, queries, keys, stride):
    onehot = bucket_onehot(queries, keys, stride).astype(jnp.float32)
    flat = lax.dot_general(
        bias_sum.reshape(H, -1),
        onehot,
        (((1,), (0,)), ((), ())),
        precision=lax.Precision.HIGHEST,
        preferred_element_type=jnp.float32,
    )
    return flat.reshape(-1)


def score_block(query_row, key_row, key_len, bias):
    queries = query_row.shape[0]
    keys = key_row.shape[0]
    heads_q = query_row.reshape(queries, H, HD)
    heads_k = key_row.reshape(keys, H, HD)
    raw = (
        jnp.einsum("qhd,khd->hqk", heads_q, heads_k, preferred_element_type=jnp.float32)
        * HD ** (-0.5)
        + bias
    )
    valid = lax.broadcasted_iota(jnp.int32, (1, 1, keys), 2) < key_len
    return jnp.where(valid, raw, -1e30)


def fetch_forward(entry, leave, widen, narrow, vectors, wide_bias, table):
    return (
        lax.all_gather(entry, ("wide", "narrow"), axis=1, tiled=True),
        lax.all_gather(leave, ("wide", "narrow"), axis=0, tiled=True),
        lax.all_gather(widen, ("wide", "narrow"), axis=0, tiled=True),
        lax.all_gather(narrow, ("wide", "narrow"), axis=0, tiled=True),
        lax.all_gather(vectors, ("wide", "narrow"), axis=1, tiled=True),
        lax.all_gather(wide_bias, ("wide", "narrow"), axis=0, tiled=True),
        lax.all_gather(table, ("wide", "narrow"), axis=0, tiled=True),
    )


def fetch_backward(entry, leave, widen, narrow, vectors, wide_bias, table):
    return (
        lax.all_gather(entry, ("wide", "narrow"), axis=1, tiled=True),
        lax.all_gather(leave, ("wide", "narrow"), axis=0, tiled=True),
        lax.all_gather(widen, ("wide", "narrow"), axis=0, tiled=True),
        lax.all_gather(narrow, ("wide", "narrow"), axis=0, tiled=True),
        lax.all_gather(vectors, ("wide", "narrow"), axis=1, tiled=True),
        lax.all_gather(wide_bias, ("wide", "narrow"), axis=0, tiled=True),
        lax.all_gather(table, ("wide", "narrow"), axis=0, tiled=True),
    )


def reduce_grads(entry, leave, widen, narrow, vectors, wide_bias, table):
    return (
        lax.psum_scatter(entry, ("wide", "narrow"), scatter_dimension=1, tiled=True),
        lax.psum_scatter(leave, ("wide", "narrow"), scatter_dimension=0, tiled=True),
        lax.psum_scatter(widen, ("wide", "narrow"), scatter_dimension=0, tiled=True),
        lax.psum_scatter(narrow, ("wide", "narrow"), scatter_dimension=0, tiled=True),
        lax.psum_scatter(vectors, ("wide", "narrow"), scatter_dimension=1, tiled=True),
        lax.psum_scatter(wide_bias, ("wide", "narrow"), scatter_dimension=0, tiled=True),
        lax.psum_scatter(table, ("wide", "narrow"), scatter_dimension=0, tiled=True),
    )


def layer_forward(query_in, key_in, resid, key_len, weights, stride):
    entry, leave, widen, narrow, vectors, wide_bias, table = weights
    rows, queries, width = query_in.shape
    keys = key_in.shape[1]
    vectors32 = vectors.astype(jnp.float32)
    query = (
        (flat_dot(query_in, entry[0]) + vectors32[0])
        .astype(jnp.bfloat16)
        .reshape(rows, queries, width)
    )
    key = flat_dot(key_in, entry[1]).astype(jnp.bfloat16).reshape(rows, keys, width)
    value = (
        (flat_dot(key_in, entry[2]) + vectors32[1]).astype(jnp.bfloat16).reshape(rows, keys, width)
    )
    bias = position_bias(table, queries, keys, stride)

    def attend(item):
        query_row, key_row, value_row, count = item
        scores = score_block(query_row, key_row, count, bias)
        total = jax.nn.logsumexp(scores, axis=-1, keepdims=True)
        probs = jnp.exp(scores - total).astype(jnp.bfloat16)
        heads_v = value_row.reshape(keys, H, HD)
        context = jnp.einsum("hqk,khd->qhd", probs, heads_v, preferred_element_type=jnp.float32)
        return (context.reshape(queries, width).astype(jnp.bfloat16), total)

    context, totals = lax.map(attend, (query, key, value, key_len))
    attended = flat_dot(context, leave) + vectors32[2]
    summed = resid.reshape(-1, width) + attended
    mixed = layer_norm(summed, vectors32[3], vectors32[4])
    mixed_low = mixed.astype(jnp.bfloat16)
    hidden_units = flat_dot(mixed_low, widen) + wide_bias.astype(jnp.float32)
    activation = gelu_tanh(hidden_units).astype(jnp.bfloat16)
    before = mixed + flat_dot(activation, narrow) + vectors32[5]
    output = layer_norm(before, vectors32[6], vectors32[7])
    kept = (
        query,
        key,
        value,
        context,
        totals,
        bias,
        summed,
        mixed_low,
        hidden_units,
        activation,
        before,
    )
    return (output, kept)


def layer_backward(upstream, kept, weights, query_in, key_in, key_len, stride):
    entry, leave, widen, narrow, vectors, wide_bias, table = weights
    (
        query,
        key,
        value,
        context,
        totals,
        bias,
        summed,
        mixed_low,
        hidden_units,
        activation,
        before,
    ) = kept
    rows, queries, width = query.shape
    keys = key.shape[1]
    vectors32 = vectors.astype(jnp.float32)
    outer_norm = jax.vjp(layer_norm, before, vectors32[6], vectors32[7])[1]
    dbefore, dgain_outer, dshift_outer = outer_norm(upstream)
    dback = dbefore.astype(jnp.bfloat16)
    dnarrow = weight_grad(activation, dback)
    dactivation = input_grad(dback, narrow)
    gelu_pull = jax.vjp(gelu_tanh, hidden_units)[1]
    dhidden = gelu_pull(dactivation)[0].astype(jnp.bfloat16)
    dwiden = weight_grad(mixed_low, dhidden)
    dmixed = dbefore + input_grad(dhidden, widen)
    inner_norm = jax.vjp(layer_norm, summed, vectors32[3], vectors32[4])[1]
    dsummed, dgain_inner, dshift_inner = inner_norm(dmixed)
    dattended = dsummed.astype(jnp.bfloat16)
    dleave = weight_grad(context, dattended)
    dcontext = input_grad(dattended, leave).astype(jnp.bfloat16).reshape(rows, queries, width)
    scale = HD ** (-0.5)

    def step(bias_sum, item):
        query_row, key_row, value_row, count, total, dcontext_row = item
        scores = score_block(query_row, key_row, count, bias)
        probs = jnp.exp(scores - total)
        heads_q = query_row.reshape(queries, H, HD)
        heads_k = key_row.reshape(keys, H, HD)
        heads_v = value_row.reshape(keys, H, HD)
        heads_d = dcontext_row.reshape(queries, H, HD)
        dvalue = jnp.einsum(
            "hqk,qhd->khd", probs.astype(jnp.bfloat16), heads_d, preferred_element_type=jnp.float32
        )
        dprobs = jnp.einsum("qhd,khd->hqk", heads_d, heads_v, preferred_element_type=jnp.float32)
        dscores = probs * (dprobs - jnp.sum(probs * dprobs, axis=-1, keepdims=True))
        dscores_low = dscores.astype(jnp.bfloat16)
        dquery = (
            jnp.einsum("hqk,khd->qhd", dscores_low, heads_k, preferred_element_type=jnp.float32)
            * scale
        )
        dkey = (
            jnp.einsum("hqk,qhd->khd", dscores_low, heads_q, preferred_element_type=jnp.float32)
            * scale
        )
        grads = (
            dquery.reshape(queries, width).astype(jnp.bfloat16),
            dkey.reshape(keys, width).astype(jnp.bfloat16),
            dvalue.reshape(keys, width).astype(jnp.bfloat16),
        )
        return (bias_sum + dscores_low.astype(jnp.float32), grads)

    bias_sum, (dquery, dkey, dvalue) = lax.scan(
        step, jnp.zeros_like(bias), (query, key, value, key_len, totals, dcontext)
    )
    dentry = jnp.stack(
        [weight_grad(query_in, dquery), weight_grad(key_in, dkey), weight_grad(key_in, dvalue)]
    )
    dvectors = jnp.stack(
        [
            column_sum(dquery),
            column_sum(dvalue),
            column_sum(dattended),
            dgain_inner,
            dshift_inner,
            column_sum(dback),
            dgain_outer,
            dshift_outer,
        ]
    )
    dwide_bias = column_sum(dhidden)
    dtable = table_grad(bias_sum, queries, keys, stride)
    dquery_in = input_grad(dquery, entry[0]).reshape(rows, queries, width)
    dkey_in = (input_grad(dkey, entry[1]) + input_grad(dvalue, entry[2])).reshape(rows, keys, width)
    grads = (dentry, dleave, dwiden, dnarrow, dvectors, dwide_bias, dtable)
    return (grads, dquery_in, dkey_in, dsummed.reshape(rows, queries, width))


def on_device(
    hidden,
    lengths,
    cotangent,
    inflow,
    outflow,
    widener,
    narrower,
    shifts,
    offsets,
    distance,
    intake,
    outtake,
    expander,
    squeezer,
    adjusts,
    leanings,
    spacing,
):
    rows, seq, width = hidden.shape
    half = seq // 2
    first = fetch_forward(inflow, outflow, widener, narrower, shifts, offsets, distance)
    second = fetch_forward(intake, outtake, expander, squeezer, adjusts, leanings, spacing)
    paired = hidden.astype(jnp.float32).reshape(rows, half, 2, width)
    pooled = 0.5 * (paired[:, :, 0] + paired[:, :, 1])
    pooled_low = pooled.astype(jnp.bfloat16)
    halved = (lengths + 1) // 2
    first_out, first_kept = layer_forward(pooled_low, hidden, pooled, lengths, first, 2)
    pooled_layer = first_out.astype(jnp.bfloat16).reshape(rows, half, width)
    second_out, second_kept = layer_forward(
        pooled_layer, pooled_layer, pooled_layer.astype(jnp.float32), halved, second, 1
    )
    full_layer = second_out.astype(jnp.bfloat16).reshape(rows, half, width)
    second_back = fetch_backward(intake, outtake, expander, squeezer, adjusts, leanings, spacing)
    first_back = fetch_backward(inflow, outflow, widener, narrower, shifts, offsets, distance)
    upstream = cotangent.astype(jnp.float32).reshape(-1, width)
    grads_two, dquery, dkey, dresid = layer_backward(
        upstream, second_kept, second_back, pooled_layer, pooled_layer, halved, 1
    )
    shards_two = reduce_grads(
        grads_two[0],
        grads_two[1],
        grads_two[2],
        grads_two[3],
        grads_two[4],
        grads_two[5],
        grads_two[6],
    )
    dlayer = (dquery + dkey + dresid).reshape(-1, width)
    grads_one, dquery, dkey, dresid = layer_backward(
        dlayer, first_kept, first_back, pooled_low, hidden, lengths, 2
    )
    shards_one = reduce_grads(
        grads_one[0],
        grads_one[1],
        grads_one[2],
        grads_one[3],
        grads_one[4],
        grads_one[5],
        grads_one[6],
    )
    dpooled = 0.5 * (dquery + dresid)
    spread = jnp.broadcast_to(dpooled[:, :, None, :], (rows, half, 2, width)).reshape(
        rows, seq, width
    )
    hidden_grad = dkey + spread
    vector_rows = shards_two[4]
    return (
        pooled_layer,
        full_layer,
        hidden_grad,
        shards_one[0],
        shards_one[1],
        shards_one[2],
        shards_one[3],
        shards_one[4],
        shards_one[5],
        shards_one[6],
        shards_two[0],
        shards_two[1],
        shards_two[2],
        shards_two[3],
        vector_rows[1:],
        shards_two[5],
        shards_two[6],
        vector_rows[0],
    )


def solution(mesh):
    in_specs = (
        P(("wide", "narrow"), None, None),
        P(("wide", "narrow")),
        P(("wide", "narrow"), None, None),
        P(None, ("wide", "narrow"), None),
        P(("wide", "narrow"), None),
        P(("wide", "narrow"), None),
        P(("wide", "narrow"), None),
        P(None, ("wide", "narrow")),
        P(("wide", "narrow")),
        P(("wide", "narrow")),
        P(None, ("wide", "narrow"), None),
        P(("wide", "narrow"), None),
        P(("wide", "narrow"), None),
        P(("wide", "narrow"), None),
        P(None, ("wide", "narrow")),
        P(("wide", "narrow")),
        P(("wide", "narrow")),
    )
    out_specs = (
        P(("wide", "narrow"), None, None),
        P(("wide", "narrow"), None, None),
        P(("wide", "narrow"), None, None),
        P(None, ("wide", "narrow"), None),
        P(("wide", "narrow"), None),
        P(("wide", "narrow"), None),
        P(("wide", "narrow"), None),
        P(None, ("wide", "narrow")),
        P(("wide", "narrow")),
        P(("wide", "narrow")),
        P(None, ("wide", "narrow"), None),
        P(("wide", "narrow"), None),
        P(("wide", "narrow"), None),
        P(("wide", "narrow"), None),
        P(None, ("wide", "narrow")),
        P(("wide", "narrow")),
        P(("wide", "narrow")),
        P(("wide", "narrow")),
    )
    return jax.shard_map(
        on_device, mesh=mesh, in_specs=in_specs, out_specs=out_specs, check_vma=False
    )
```

profile of v0, /device:TPU:0, one launch (start us, length us, event | category | flops | bytes accessed | tf_op | source)
XLA Modules:
  0.0 2003.4 jit_solution(12664195364906510900)
XLA Ops:
  12.8 43.9 %all-gather = bf16[32,24,8]{1,2,0:T(8,128)(2,1)S(1)} all-gather(bf16[1,24,8]{1,2,0:T(8,128)(2,1)} %bitcast.457), channel_id=1, replica_groups=mesh['wide'=8,'narrow'=4] {'wide','narrow'}, dimensions={0}, use_global_device_ids=true | all-gather | bytes 12672 | tf_op jit(solution)/shard_map/all_gather | solution.py:97
  66.7 37.4 %all-reduce.11 = (bf16[384]{0:T(512)(128)(2,1)S(1)}, bf16[3072]{0:T(1024)(128)(2,1)S(1)}, bf16[384]{0:T(512)(128)(2,1)S(1)}, bf16[3072]{0:T(1024)(128)(2,1)S(1)}) all-reduce(bf16[384]{0:T(512)(128)(2,1)S(1)} %dynamic-update-slice, bf16[3072]{0:T(1024)(128)(2,1)S(1)} %dynamic-update-slice.1, ...), channel_id=1, replica_groups=mesh['wide'=8,'narrow'=4] {'wide','narrow'}, use_global_device_ids=true, to_apply=%add | all-reduce | flops 6912 | bytes 27648
  107.1 4.9 copy.320
  118.2 40.5 %all-gather.1 = bf16[32,24,8]{1,2,0:T(8,128)(2,1)S(1)} all-gather(bf16[1,24,8]{1,2,0:T(8,128)(2,1)S(1)} %bitcast.458), channel_id=1, replica_groups=mesh['wide'=8,'narrow'=4] {'wide','narrow'}, dimensions={0}, use_global_device_ids=true | all-gather | bytes 12672 | tf_op jit(solution)/shard_map/all_gather | solution.py:97
  178.3 6.5 add_convert_fusion
  184.8 4.7 copy.264
  189.5 6.5 convolution_convert_fusion
  196.0 4.7 copy.266
  202.6 60.1 %while.58 = (s32[]{:T(128)}, bf16[4,256,768]{2,1,0:T(8,128)(2,1)}, f32[4,12,256,1]{2,1,3,0:T(8,128)}, bf16[4,512,768]{1,2,0:T(8,128)(2,1)}, s32[4]{0:T(128)}, /*...) while((s32[]{:T(128)}, bf16[4,256,768]{2,1,0:T(8,128)(2,1)}, ...), condition=%wide.region_3.4_spmd, body=%wide.region_0.3_spmd.sunk | while | flops 415457792 | bytes 33183860 | solution.py:152
  269.3 11.1 fusion.82
  280.5 12.9 fusion.95
  296.7 25.4 %all-gather.19.cloned.1.call-done = bf16[3,768,768]{2,1,0:T(8,128)(2,1)} async-done(((bf16[3,24,768]{2,1,0:T(8,128)(2,1)}), bf16[3,768,768]{2,1,0:T(8,128)(2,1)}) %all-gather.19.cloned.1.call-update) | async-done | bytes 3538960 | tf_op jit(solution)/shard_map/all_gather | solution.py:93
  344.9 34.9 %while.59 = (s32[]{:T(128)}, bf16[4,256,768]{2,1,0:T(8,128)(2,1)}, f32[4,12,256,1]{2,1,3,0:T(8,128)}, bf16[4,256,768]{1,2,0:T(8,128)(2,1)}, s32[4]{0:T(128)S(1)}...) while((s32[]{:T(128)}, bf16[4,256,768]{2,1,0:T(8,128)(2,1)}, ...), condition=%wide.region_11.12_spmd, body=%wide.region_8.11_spmd.sunk | while | flops 207839488 | bytes 18241140 | solution.py:152
  385.9 57.4 %all-gather.23.cloned.1.call-done = bf16[768,3072]{1,0:T(8,128)(2,1)} async-done(((bf16[24,3072]{1,0:T(8,128)(2,1)}), bf16[768,3072]{1,0:T(8,128)(2,1)}) %all-gather.23.cloned.1.call-update) | async-done | bytes 4718608 | tf_op jit(solution)/shard_map/all_gather | solution.py:95
  443.3 11.1 fusion.78
  454.3 54.3 %all-gather.25.cloned.1.call-done = bf16[3072,768]{1,0:T(8,128)(2,1)} async-done(((bf16[96,768]{1,0:T(8,128)(2,1)}), bf16[3072,768]{1,0:T(8,128)(2,1)}) %all-gather.25.cloned.1.call-update) | async-done | bytes 4718608 | tf_op jit(solution)/shard_map/all_gather | solution.py:96
  508.6 13.3 fusion.97
  528.6 16.2 convert_reduce_fusion
  544.8 11.2 multiply_reduce_fusion.2
  565.4 92.9 %while.60 = (s32[]{:T(128)}, f32[12,256,256]{1,2,0:T(8,128)}, bf16[4,256,768]{1,2,0:T(8,128)(2,1)}, bf16[4,256,768]{2,1,0:T(8,128)(2,1)}, bf16[4,256,768]{1,2,0:...) while((s32[]{:T(128)}, f32[12,256,256]{1,2,0:T(8,128)}, ...), condition=%wide.region_22.23_spmd.clone, body=%wide.region_20.22_spmd.clone.sunk | while | flops 514520320 | bytes 88143920 | solution.py:240
  578.0 4.6 select_add_fusion.4
  600.6 5.5 select_add_fusion.4
  624.1 5.5 select_add_fusion.4
  647.5 5.5 select_add_fusion.4
  677.2 16.2 convert_reduce_fusion.1
  693.5 6.1 multiply_reduce_fusion.3
  705.2 107.7 %while.61 = (s32[]{:T(128)}, f32[12,256,512]{2,1,0:T(8,128)}, bf16[4,256,768]{1,2,0:T(8,128)(2,1)S(1)}, bf16[4,512,768]{1,2,0:T(8,128)(2,1)}, bf16[4,512,768]{1,...) while((s32[]{:T(128)}, f32[12,256,512]{2,1,0:T(8,128)}, ...), condition=%wide.region_29.30_spmd.clone, body=%wide.region_27.29_spmd.clone.sunk | while | flops 1028650496 | bytes 144373568 | solution.py:240
  718.8 7.7 select_add_fusion.5
  744.3 10.0 select_add_fusion.5
  771.6 10.0 select_add_fusion.5
  798.9 10.0 select_add_fusion.5
  819.8 4.9 copy.323
  824.6 8.9 fusion.25
  852.8 5.3 fusion.70
  884.9 10.6 fusion.76
  897.4 10.6 fusion.80
  909.4 12.8 fusion.84
  923.6 12.9 fusion.85
  941.2 4.8 copy.288
  954.1 8.9 reshape.655
  983.4 92.3 %reduce-scatter.21.cloned.1.call-done = f32[24,768]{1,0:T(8,128)} async-done(((f32[768,768]{1,0:T(8,128)}), f32[24,768]{1,0:T(8,128)}) %reduce-scatter.21.cloned.1.call-update) | async-done | bytes 73744 | tf_op jit(solution)/shard_map/reduce_scatter | solution.py:118
  1075.7 104.8 %reduce-scatter.13.cloned.1.call-done = f32[24,768]{1,0:T(8,128)} async-done(((f32[768,768]{1,0:T(8,128)}), f32[24,768]{1,0:T(8,128)}) %reduce-scatter.13.cloned.1.call-update) | async-done | bytes 73744 | tf_op jit(solution)/shard_map/reduce_scatter | solution.py:118
  1180.5 124.3 %reduce-scatter.19.cloned.1.call-done = f32[3,24,768]{2,1,0:T(8,128)} async-done(((f32[3,768,768]{2,1,0:T(8,128)}), f32[3,24,768]{2,1,0:T(8,128)}) %reduce-scatter.19.cloned.1.call-update) | async-done | bytes 221200 | tf_op jit(solution)/shard_map/reduce_scatter | solution.py:117
  1304.8 125.7 %reduce-scatter.11.cloned.1.call-done = f32[3,24,768]{2,1,0:T(8,128)} async-done(((f32[3,768,768]{2,1,0:T(8,128)}), f32[3,24,768]{2,1,0:T(8,128)}) %reduce-scatter.11.cloned.1.call-update) | async-done | bytes 221200 | tf_op jit(solution)/shard_map/reduce_scatter | solution.py:117
  1430.5 141.3 %reduce-scatter.23.cloned.1.call-done = f32[24,3072]{1,0:T(8,128)} async-done(((f32[768,3072]{1,0:T(8,128)}), f32[24,3072]{1,0:T(8,128)}) %reduce-scatter.23.cloned.1.call-update) | async-done | bytes 294928 | tf_op jit(solution)/shard_map/reduce_scatter | solution.py:119
  1571.8 141.9 %reduce-scatter.15.cloned.1.call-done = f32[24,3072]{1,0:T(8,128)} async-done(((f32[768,3072]{1,0:T(8,128)}), f32[24,3072]{1,0:T(8,128)}) %reduce-scatter.15.cloned.1.call-update) | async-done | bytes 294928 | tf_op jit(solution)/shard_map/reduce_scatter | solution.py:119
  1713.7 140.9 %reduce-scatter.17.cloned.1.call-done = f32[96,768]{1,0:T(8,128)} async-done(((f32[3072,768]{1,0:T(8,128)}), f32[96,768]{1,0:T(8,128)}) %reduce-scatter.17.cloned.1.call-update) | async-done | bytes 294928 | tf_op jit(solution)/shard_map/reduce_scatter | solution.py:120
  1854.6 141.8 %reduce-scatter.25.cloned.1.call-done = f32[96,768]{1,0:T(8,128)} async-done(((f32[3072,768]{1,0:T(8,128)}), f32[96,768]{1,0:T(8,128)}) %reduce-scatter.25.cloned.1.call-update) | async-done | bytes 294928 | tf_op jit(solution)/shard_map/reduce_scatter | solution.py:120
  (758 shorter events, 449.9 us)
Async XLA Ops:
  7.2 164.2 %all-gather.11.cloned.1.call-start = ((), (), s32[]{:S(2)}) async-start(), calls=%async_computation.8 | async-start | bytes 3649536 | tf_op jit(solution)/shard_map/all_gather | solution.py:93
  7.9 254.9 %all-gather.13.cloned.1.call-start = ((), (), s32[]{:S(2)}) async-start(), calls=%async_computation.9 | async-start | bytes 1216512 | tf_op jit(solution)/shard_map/all_gather | solution.py:94
  8.7 260.6 %all-gather.15.cloned.1.call-start = ((), (), s32[]{:S(2)}) async-start(), calls=%async_computation.10 | async-start | bytes 4866048 | tf_op jit(solution)/shard_map/all_gather | solution.py:95
  9.4 271.0 %all-gather.17.cloned.1.call-start = ((), (), s32[]{:S(2)}) async-start(), calls=%async_computation.11 | async-start | bytes 4866048 | tf_op jit(solution)/shard_map/all_gather | solution.py:96
  10.0 312.1 %all-gather.19.cloned.1.call-start = ((), (), s32[]{:S(2)}) async-start(), calls=%async_computation.12 | async-start | bytes 3649536 | tf_op jit(solution)/shard_map/all_gather | solution.py:93
  10.6 369.3 %all-gather.21.cloned.1.call-start = ((), (), s32[]{:S(2)}) async-start(), calls=%async_computation.13 | async-start | bytes 1216512 | tf_op jit(solution)/shard_map/all_gather | solution.py:94
  11.1 432.1 %all-gather.23.cloned.1.call-start = ((), (), s32[]{:S(2)}) async-start(), calls=%async_computation.14 | async-start | bytes 4866048 | tf_op jit(solution)/shard_map/all_gather | solution.py:95
  11.9 496.7 %all-gather.25.cloned.1.call-start = ((), (), s32[]{:S(2)}) async-start(), calls=%async_computation.15 | async-start | bytes 4866048 | tf_op jit(solution)/shard_map/all_gather | solution.py:96
  12.6 962.5 %all-reduce.14.cloned.1.call-start = ((), (), s32[]{:S(2)}) async-start(), calls=%async_computation.24 | async-start | bytes 155648
  57.7 222.8 %copy-start.63 = (f32[768]{0:T(1024)}, f32[768]{0:T(1024)S(1)}, u32[]{:S(2)}) copy-start(f32[768]{0:T(1024)S(1)} %get-tuple-element.626) | copy-start | bytes 9220
  57.7 222.8 %copy-start.70 = (f32[768]{0:T(1024)}, f32[768]{0:T(1024)S(1)}, u32[]{:S(2)}) copy-start(f32[768]{0:T(1024)S(1)} %get-tuple-element.625) | copy-start | bytes 9220
  57.7 236.3 %copy-start.74 = (f32[768]{0:T(1024)}, f32[768]{0:T(1024)S(1)}, u32[]{:S(2)}) copy-start(f32[768]{0:T(1024)S(1)} %get-tuple-element.622) | copy-start | bytes 9220
  267.1 13.4 copy-start.53
  269.2 11.2 copy-start.78
  269.2 11.2 copy-start.58
  269.3 11.2 copy-start.98
  269.3 11.2 copy-start.105
  293.9 32.5 %copy-start.80 = (f32[1024]{0:T(1024)}, f32[1024]{0:T(1024)S(1)}, u32[]{:S(2)}) copy-start(f32[1024]{0:T(1024)S(1)} %multiply_reduce_fusion.9) | copy-start | bytes 12292
  293.9 28.2 %copy-start.107 = (f32[768]{0:T(1024)S(1)}, f32[768]{0:T(1024)}, u32[]{:S(2)}) copy-start(f32[768]{0:T(1024)} %get-tuple-element.621) | copy-start | bytes 9220
  293.9 32.5 %copy-start.76 = (f32[1024]{0:T(1024)}, f32[1024]{0:T(1024)S(1)}, u32[]{:S(2)}) copy-start(f32[1024]{0:T(1024)S(1)} %fusion.67) | copy-start | bytes 12292
  344.9 34.9 %copy-start.104 = (f32[768]{0:T(1024)S(1)}, f32[768]{0:T(1024)}, u32[]{:S(2)}) copy-start(f32[768]{0:T(1024)} %get-tuple-element.619) | copy-start | bytes 9220
  383.6 59.6 %copy-start.66 = (f32[768]{0:T(1024)S(1)}, f32[768]{0:T(1024)}, u32[]{:S(2)}) copy-start(f32[768]{0:T(1024)} %get-tuple-element.618) | copy-start | bytes 9220
  383.7 59.6 %copy-start.72 = (f32[768]{0:T(1024)S(1)}, f32[768]{0:T(1024)}, u32[]{:S(2)}) copy-start(f32[768]{0:T(1024)} %get-tuple-element.617) | copy-start | bytes 9220
  383.7 172.4 %copy-start.56 = (f32[1024]{0:T(1024)}, f32[1024]{0:T(1024)S(1)}, u32[]{:S(2)}) copy-start(f32[1024]{0:T(1024)S(1)} %broadcast_multiply_fusion.1) | copy-start | bytes 12292
  385.9 170.3 %copy-start.61 = (f32[1024]{0:T(1024)}, f32[1024]{0:T(1024)S(1)}, u32[]{:S(2)}) copy-start(f32[1024]{0:T(1024)S(1)} %fusion.68) | copy-start | bytes 12292
  443.3 65.4 %copy-start.101 = (f32[3072]{0:T(1024)S(1)}, f32[3072]{0:T(1024)}, u32[]{:S(2)}) copy-start(f32[3072]{0:T(1024)} %convert_element_type.298) | copy-start | bytes 36868
  443.3 65.4 %copy-start.103 = (f32[768]{0:T(1024)S(1)}, f32[768]{0:T(1024)}, u32[]{:S(2)}) copy-start(f32[768]{0:T(1024)} %get-tuple-element.616) | copy-start | bytes 9220
  528.6 16.2 copy-start.49
  528.6 16.2 copy-start.15
  544.8 11.2 copy-start.29
  674.2 19.2 slice-start.6
  677.2 16.2 copy-start.51
  677.2 16.2 copy-start.12
  677.2 16.2 copy-start.54
  677.2 16.2 copy-start.59
  677.2 16.2 copy-start.64
  677.2 16.2 slice-start.7
  744.3 10.6 slice-start.1
  771.6 10.6 slice-start.1
  798.9 10.6 slice-start.1
  847.9 227.8 %reduce-scatter.21.cloned.1.call-start = ((), (), s32[]{:S(2)}) async-start(), calls=%async_computation.21 | async-start | bytes 2433024 | tf_op jit(solution)/shard_map/reduce_scatter | solution.py:118
  852.7 327.8 %reduce-scatter.13.cloned.1.call-start = ((), (), s32[]{:S(2)}) async-start(), calls=%async_computation.17 | async-start | bytes 2433024 | tf_op jit(solution)/shard_map/reduce_scatter | solution.py:118
  858.1 446.7 %reduce-scatter.19.cloned.1.call-start = ((), (), s32[]{:S(2)}) async-start(), calls=%async_computation.20 | async-start | bytes 7299072 | tf_op jit(solution)/shard_map/reduce_scatter | solution.py:117
  869.1 561.4 %reduce-scatter.11.cloned.1.call-start = ((), (), s32[]{:S(2)}) async-start(), calls=%async_computation.16 | async-start | bytes 7299072 | tf_op jit(solution)/shard_map/reduce_scatter | solution.py:117
  883.0 688.8 %reduce-scatter.23.cloned.1.call-start = ((), (), s32[]{:S(2)}) async-start(), calls=%async_computation.22 | async-start | bytes 9732096 | tf_op jit(solution)/shard_map/reduce_scatter | solution.py:119
  895.5 818.2 %reduce-scatter.15.cloned.1.call-start = ((), (), s32[]{:S(2)}) async-start(), calls=%async_computation.18 | async-start | bytes 9732096 | tf_op jit(solution)/shard_map/reduce_scatter | solution.py:119
  908.0 946.5 %reduce-scatter.17.cloned.1.call-start = ((), (), s32[]{:S(2)}) async-start(), calls=%async_computation.19 | async-start | bytes 9732096 | tf_op jit(solution)/shard_map/reduce_scatter | solution.py:120
  922.2 1074.1 %reduce-scatter.25.cloned.1.call-start = ((), (), s32[]{:S(2)}) async-start(), calls=%async_computation.23 | async-start | bytes 9732096 | tf_op jit(solution)/shard_map/reduce_scatter | solution.py:120
  (139 other events, 619.0 us)
Sparse Core Ops, SparseCore 0:
  11.0 62.8 all-gather.10
  76.7 52.8 all-gather.12
  132.6 62.4 all-gather.14
  197.8 62.4 all-gather.16
  263.1 58.9 all-gather.18
  324.9 52.8 all-gather.20
  380.7 62.5 all-gather.22
  446.2 62.4 all-gather.24
  848.0 120.8 all-reduce.13
  974.6 101.0 reduce-scatter.20
  1082.4 98.0 reduce-scatter.12
  1186.6 118.1 reduce-scatter.18
  1312.0 118.4 reduce-scatter.10
  1436.8 134.8 reduce-scatter.22
  1579.1 134.5 reduce-scatter.14
  1720.0 134.4 reduce-scatter.16
  1861.9 134.3 reduce-scatter.24
where the time goes:
time: 2010 us; the launch traced here: 2000 us
  waiting for transfers between devices  1160 us (58%)
  matrix products  334 us (17%)
  local copies, waits for them, and re-layouts  254 us (13%)
  blocking collectives  122 us (6%)
  other arithmetic  119 us (6%)
    reduce_scatter x2, waiting for transfers between devices, reduce_grads(): lax.psum_scatter(widen, ('wide', 'narrow'), scatter_dimension=0, tiled=True)  283 us
    reduce_scatter x2, waiting for transfers between devices, reduce_grads(): lax.psum_scatter(narrow, ('wide', 'narrow'), scatter_dimension=0, tiled=T...  283 us
    reduce_scatter x2, waiting for transfers between devices, reduce_grads(): lax.psum_scatter(entry, ('wide', 'narrow'), scatter_dimension=1, tiled=True)  250 us
    reduce_scatter x2, waiting for transfers between devices, reduce_grads(): lax.psum_scatter(leave, ('wide', 'narrow'), scatter_dimension=0, tiled=True)  197 us
    dot_general x12, matrix products, flat_dot(): jnp.dot(left.reshape(-1, left.shape[-1]), right, preferred_element_type=j...  86.6 us
    all_gather x2, blocking collectives, fetch_forward(): lax.all_gather(vectors, ('wide', 'narrow'), axis=1, tiled=True)  84.3 us
    dynamic_slice x72, local copies, waits for them, and re-layouts, layer_forward(): context, totals = lax.map(attend, (query, key, value, key_len))  83 us
    dot_general x12, matrix products, input_grad(): lax.dot_general(grads, weight, (((1,), (1,)), ((), ())), preferred_elemen...  73.5 us
  transfers between devices with their start and end apart: 17, of which 11 were waited for; matrix products, arithmetic and copies ran while one was open for 18% of the time, Pallas kernels for 0%

commit v1 on v0

v1 whole, which is shorter than its diff:
```python
from functools import partial

import jax
import jax.numpy as jnp
from jax import lax
from jax.experimental import pallas as pl
from jax.experimental.pallas import tpu as pltpu
from jax.sharding import PartitionSpec as P

H = 12
HD = 64
NB = 32
D = 768
FF = 3072
HALF = 384
EPS = 1e-06
AX = ("wide", "narrow")
CORE, XBIT, YBIT, Z0, Z1 = 1, 2, 4, 8, 16
UNITS = 16
F32 = jnp.float32
BF16 = jnp.bfloat16
GELU_A = 0.7978845608028654
GELU_B = 0.044715
NN = (((1,), (0,)), ((), ()))
NT = (((1,), (1,)), ((), ()))
TN = (((0,), (0,)), ((), ()))
VMEM_LIMIT = 60 * 1024 * 1024
ANY = pl.BlockSpec(memory_space=pl.ANY)


def mm(left, right, dims=NN):
    return lax.dot_general(left, right, dims, preferred_element_type=F32)


def wide(value):
    return value.astype(F32)


def low(value):
    return value.astype(BF16)


def swap(value, mask):
    return lax.ppermute(value, AX, [(i, i ^ mask) for i in range(32)])


def pick(core, first, second):
    return jnp.where(core == 0, first, second)


def pair_units(core, value, group):
    rows, _, width = value.shape
    keep = pick(core, value[:, 0], value[:, 1]).reshape(-1, group, width)
    send = pick(core, value[:, 1], value[:, 0]).reshape(-1, group, width)
    return keep, send


def join_units(core, keep, recv):
    return jnp.concatenate([pick(core, keep, recv), pick(core, recv, keep)], axis=1)


def gather_slab(slab):
    own = jnp.stack([slab, swap(slab, Z0), swap(slab, Z1), swap(slab, Z0 | Z1)])
    across_y = swap(own, YBIT)
    across_x = swap(own, XBIT)
    diag_low = swap(across_y[:2], XBIT)
    diag_high = swap(across_x[2:], YBIT)
    mine = (own, across_y, across_x, diag_low, diag_high)
    return mine + tuple(swap(piece, CORE) for piece in mine)


def flip_bit(bit, value, axis):
    return jnp.where(bit == 0, value, jnp.flip(value, axis))


def gather_vectors(index, flat):
    pieces = gather_slab(flat)
    sides = []
    for side in range(2):
        own, across_y, across_x, diag_low, diag_high = pieces[5 * side : 5 * side + 5]
        diag = jnp.concatenate([diag_low, diag_high], axis=0)
        sides.append(jnp.stack([own, across_x, across_y, diag], axis=1))
    full = jnp.stack(sides, axis=2)
    full = full.reshape(2, 2, 2, 2, 2, -1)
    for axis, mask in enumerate((Z1, Z0, YBIT, XBIT, CORE)):
        full = flip_bit((index // mask) % 2, full, axis)
    return full.reshape(32, -1)


def gather_layers(index, layers):
    core = index % 2
    packed = []
    for entry, leave, widen, narrow in layers:
        eo = jnp.concatenate([entry, leave[None]]).reshape(96, 2, HALF)
        packed.append(pair_units(core, eo, 24))
        packed.append(pair_units(core, widen.reshape(24, 2, FF // 2), 24))
        packed.append(pair_units(core, narrow.reshape(96, 2, HALF), 96))
    result = []
    for keep, send in packed:
        slab = join_units(core, keep, swap(send, CORE))
        slab = slab if slab.shape[0] == 4 else slab[0]
        result.append(gather_slab(slab))
    return result[:3], result[3:]


def reduce_units(send, keep):
    shape = (4, 4) + keep.shape[1:]
    keep = keep.reshape(shape)
    recv = swap(send, CORE).reshape(shape)
    diag = low(wide(keep[3]) + wide(recv[3]))
    diag_low = wide(swap(diag[:2], XBIT))
    diag_high = wide(swap(diag[2:], YBIT))
    to_y = wide(keep[2]) + wide(recv[2])
    to_x = wide(keep[1]) + wide(recv[1])
    to_y = jnp.concatenate([low(to_y[:2] + diag_low), low(to_y[2:])])
    to_x = jnp.concatenate([low(to_x[:2]), low(to_x[2:] + diag_high)])
    total = wide(keep[0]) + wide(recv[0])
    total = total + wide(swap(to_y, YBIT)) + wide(swap(to_x, XBIT))
    sent = low(total[1:])
    return (
        total[0] + wide(swap(sent[0], Z0)) + wide(swap(sent[1], Z1)) + wide(swap(sent[2], Z0 | Z1))
    )


def unpair(core, slab, group):
    keep = pick(core, slab[:, :group], slab[:, group:])
    recv = swap(pick(core, slab[:, group:], slab[:, :group]), CORE)
    return jnp.concatenate([pick(core, keep, recv), pick(core, recv, keep)], axis=-1)


def vector_units(vectors, wide_bias, table, parts):
    flat = jnp.concatenate(
        [
            vectors.reshape(8, parts, -1).transpose(1, 0, 2).reshape(parts, -1),
            wide_bias.reshape(parts, -1),
            table.reshape(parts, -1),
        ],
        axis=1,
    )
    return flat


def split_vectors(flat, parts):
    cut = 8 * D // parts
    mid = cut + FF // parts
    return flat[:cut].reshape(8, -1), flat[cut:mid], flat[mid : mid + H * NB // parts]


def position(chip, unit):
    rel = jnp.bitwise_xor(chip, unit)
    return jnp.bitwise_and(rel, 3) * 4 + lax.shift_right_logical(rel, 2)


def start_load(me, refs, dst, sem, place):
    if len(refs) == 1:
        pltpu.make_async_copy(refs[0], dst, sem).start()
        return
    chip = lax.shift_right_logical(me, 1)
    for side in range(2):
        half = jnp.bitwise_xor(jnp.bitwise_and(me, 1), side)
        own, across_y, across_x, diag_low, diag_high = refs[5 * side : 5 * side + 5]
        for k in range(4):
            for step, ref, at in (
                (0, own, k),
                (1, across_x, k),
                (2, across_y, k),
                (3, diag_low if k < 2 else diag_high, k % 2),
            ):
                unit = jnp.bitwise_xor(chip, 4 * k + step)
                source, target = place(ref.at[at], dst, unit, half)
                pltpu.make_async_copy(source, target, sem).start()


def wait_load(dst, sem):
    pltpu.make_async_copy(dst, dst, sem).wait()


def place_entry(src, dst, unit, half):
    rows, cols = pl.multiple_of(unit * 48, 16), pl.multiple_of(half * HALF, 128)
    return src.at[0:3], dst.at[:, pl.ds(rows, 48), pl.ds(cols, HALF)]


def place_leave(src, dst, unit, half):
    rows, cols = pl.multiple_of(unit * 48, 16), pl.multiple_of(half * HALF, 128)
    return src.at[3], dst.at[pl.ds(rows, 48), pl.ds(cols, HALF)]


def place_widen(src, dst, unit, half):
    rows, cols = pl.multiple_of(unit * 48, 16), pl.multiple_of(half * FF // 2, 128)
    return src, dst.at[pl.ds(rows, 48), pl.ds(cols, FF // 2)]


def place_narrow(src, dst, unit, half):
    rows, cols = pl.multiple_of(unit * 192, 16), pl.multiple_of(half * HALF, 128)
    return src, dst.at[pl.ds(rows, 192), pl.ds(cols, HALF)]


def build_bias(tab_ref, bias, stride):
    keys = bias.shape[1]
    for part in range(bias.shape[2] // 128):
        row = lax.broadcasted_iota(jnp.int32, (keys, 128), 0)
        col = lax.broadcasted_iota(jnp.int32, (keys, 128), 1) + 128 * part
        bucket = jnp.clip(row - stride * col, -(NB // 2), NB // 2 - 1) + NB // 2
        for h in range(H):
            table = jnp.broadcast_to(tab_ref[h : h + 1, :], (keys, 128))
            bias[h, :, 128 * part : 128 * part + 128] = jnp.take_along_axis(
                table, bucket, axis=1, mode="promise_in_bounds"
            )


def lane_masks(value):
    lane = lax.broadcasted_iota(jnp.int32, value.shape, 1)
    zero = jnp.zeros_like(value)
    return jnp.where(lane < HD, value, zero), jnp.where(lane < HD, zero, value)


def masked_scores(keys, query, bias, count):
    scores = mm(keys, query, NT) + bias
    size = scores.shape[0]
    head, tail = scores[: size - 128], scores[size - 128 :]
    row = lax.broadcasted_iota(jnp.int32, tail.shape, 0) + (size - 128)
    tail = jnp.where(row < count, tail, -1e30)
    return tail if size == 128 else jnp.concatenate([head, tail], axis=0)


def statistics(value):
    mean = jnp.mean(value, axis=-1, keepdims=True)
    centred = value - mean
    spread = jnp.mean(centred * centred, axis=-1, keepdims=True)
    rstd = lax.rsqrt(spread + EPS)
    return centred * rstd, rstd


def norm_pull(grad, unit, rstd):
    return rstd * (
        grad
        - jnp.mean(grad, axis=-1, keepdims=True)
        - unit * jnp.mean(grad * unit, axis=-1, keepdims=True)
    )


def column_sum(value):
    return jnp.sum(value, axis=0, keepdims=True)


def attend_kernel(stride, count, len_ref, me_ref, x_ref, vec_ref, tab_ref, *refs):
    sources = refs[:count]
    refs = refs[count:]
    if stride == 2:
        pooled_ref, pooled_low_ref, *refs = refs
    q_ref, k_ref, v_ref, ctx_ref, lse_ref, entry, bias, turned, sem = refs
    row = pl.program_id(0)
    keys = x_ref.shape[1]
    queries = q_ref.shape[1]

    @pl.when(row == 0)
    def _():
        start_load(me_ref[0], sources, entry, sem.at[0], place_entry)
        build_bias(tab_ref, bias, stride)
        wait_load(entry, sem.at[0])

    length = len_ref[row]
    if stride == 2:
        place = lax.broadcasted_iota(jnp.int32, (queries, keys), 1)
        mine = lax.broadcasted_iota(jnp.int32, (queries, keys), 0)
        pair = jnp.where(lax.shift_right_logical(place, 1) == mine, 0.5, 0.0).astype(BF16)
        pooled = mm(pair, x_ref[0])
        pooled_ref[0] = pooled
        query_in = low(pooled)
        pooled_low_ref[0] = query_in
    else:
        query_in = x_ref[0]
    q_ref[0] = low(wide(low(mm(query_in, entry[0]) + vec_ref[0:1, :])) * HD**-0.5)
    for block in range(keys // 256):

        @pl.when(block * 256 < length)
        def _():
            rows = pl.ds(block * 256, 256)
            x = x_ref[0, rows, :]
            k_ref[0, rows, :] = low(mm(x, entry[1]))
            v_ref[0, rows, :] = low(mm(x, entry[2]) + vec_ref[1:2, :])

    def pair_step(size, step, carry):
        lanes = pl.ds(pl.multiple_of(step * 128, 128), 128)
        queries_low = lane_masks(q_ref[0, :, lanes])
        key = k_ref[0, :size, lanes]
        value = v_ref[0, :size, lanes].T
        for i in range(2):
            h = 2 * step + i
            scores = masked_scores(key, queries_low[i], bias[h, :size, :], length)
            top = jnp.max(scores, axis=0, keepdims=True)
            probs = jnp.exp(scores - top)
            total = jnp.sum(probs, axis=0, keepdims=True)
            lse_ref[0, h] = jnp.broadcast_to(top + jnp.log(total), lse_ref.shape[2:])
            context = mm(value[HD * i : HD * i + HD], low(probs)) / total
            turned[pl.ds(pl.multiple_of(step * 128 + HD * i, HD), HD), :] = context
        return carry

    blocks = lax.div(length + 127, 128)
    for w in range(1, keys // 128 + 1):

        @pl.when(blocks == w)
        def _():
            lax.fori_loop(0, H // 2, partial(pair_step, 128 * w), 0)

    ctx_ref[0] = low(turned[...].T)


def attend(stride, index, lengths, x, vectors, table, sources):
    rows, keys, _ = x.shape
    queries = keys // stride
    blk = lambda *shape: pl.BlockSpec((1,) + shape, lambda r, *_: (r,) + (0,) * len(shape))
    full = lambda *shape: pl.BlockSpec(shape, lambda r, *_: (0,) * len(shape))
    sds = jax.ShapeDtypeStruct
    outs = [
        (sds((rows, queries, D), BF16), blk(queries, D)),
        (sds((rows, keys, D), BF16), blk(keys, D)),
        (sds((rows, keys, D), BF16), blk(keys, D)),
        (sds((rows, queries, D), BF16), blk(queries, D)),
        (sds((rows, H, 8, queries), F32), blk(H, 8, queries)),
    ]
    if stride == 2:
        outs = [
            (sds((rows, queries, D), F32), blk(queries, D)),
            (sds((rows, queries, D), BF16), blk(queries, D)),
        ] + outs
    return pl.pallas_call(
        partial(attend_kernel, stride, len(sources)),
        grid_spec=pltpu.PrefetchScalarGridSpec(
            num_scalar_prefetch=2,
            grid=(rows,),
            in_specs=[blk(keys, D), full(8, D), full(16, 128)] + [ANY] * len(sources),
            out_specs=[o[1] for o in outs],
            scratch_shapes=[
                pltpu.VMEM((3, D, D), BF16),
                pltpu.VMEM((H, keys, queries), F32),
                pltpu.VMEM((D, queries), F32),
                pltpu.SemaphoreType.DMA((1,)),
            ],
        ),
        out_shape=[o[0] for o in outs],
        compiler_params=pltpu.CompilerParams(vmem_limit_bytes=VMEM_LIMIT),
        cost_estimate=pl.CostEstimate(
            flops=rows * keys * D * D * 8, bytes_accessed=20_000_000, transcendentals=rows * H * keys * queries
        ),
        name="attend",
    )(lengths, index, x, vectors, table, *sources)


def expand_kernel(counts, me_ref, ctx_ref, resid_ref, vec_ref, bias_ref, *refs):
    c1, c2, c3 = counts
    leave_src, widen_src, narrow_src = refs[:c1], refs[c1 : c1 + c2], refs[c1 + c2 : c1 + c2 + c3]
    u_ref, h_ref, before_ref, out_ref, leave, widen, narrow, sem = refs[c1 + c2 + c3 :]
    first = pl.program_id(0) == 0

    @pl.when(first)
    def _():
        start_load(me_ref[0], leave_src, leave, sem.at[0], place_leave)
        start_load(me_ref[0], widen_src, widen, sem.at[1], place_widen)
        start_load(me_ref[0], narrow_src, narrow, sem.at[2], place_narrow)
        wait_load(leave, sem.at[0])

    u = wide(resid_ref[...]) + mm(ctx_ref[...], leave[...]) + vec_ref[2:3, :]
    u_ref[...] = u
    unit, _ = statistics(u)
    mixed = unit * vec_ref[3:4, :] + vec_ref[4:5, :]
    mixed_low = low(mixed)

    @pl.when(first)
    def _():
        wait_load(widen, sem.at[1])
        wait_load(narrow, sem.at[2])

    total = mixed + vec_ref[5:6, :]
    for j in range(6):
        cols = slice(512 * j, 512 * j + 512)
        h = mm(mixed_low, widen[:, cols]) + bias_ref[0:1, cols]
        h_ref[:, cols] = low(h)
        act = 0.5 * h * (1.0 + jnp.tanh(GELU_A * (h + GELU_B * h * h * h)))
        total = total + mm(low(act), narrow[cols, :])
    before_ref[...] = total
    unit, _ = statistics(total)
    out_ref[...] = low(unit * vec_ref[6:7, :] + vec_ref[7:8, :])


def expand(index, ctx, resid, vectors, wide_bias, leave, widen, narrow):
    tokens = ctx.shape[0]
    tile = 512 if tokens % 512 == 0 else 256
    blk = lambda width: pl.BlockSpec((tile, width), lambda r, *_: (r, 0))
    full = lambda *shape: pl.BlockSpec(shape, lambda r, *_: (0,) * len(shape))
    sds = jax.ShapeDtypeStruct
    sources = tuple(leave) + tuple(widen) + tuple(narrow)
    return pl.pallas_call(
        partial(expand_kernel, (len(leave), len(widen), len(narrow))),
        grid_spec=pltpu.PrefetchScalarGridSpec(
            num_scalar_prefetch=1,
            grid=(tokens // tile,),
            in_specs=[blk(D), blk(D), full(8, D), full(1, FF)] + [ANY] * len(sources),
            out_specs=[blk(D), blk(FF), blk(D), blk(D)],
            scratch_shapes=[
                pltpu.VMEM((D, D), BF16),
                pltpu.VMEM((D, FF), BF16),
                pltpu.VMEM((FF, D), BF16),
                pltpu.SemaphoreType.DMA((3,)),
            ],
        ),
        out_shape=[
            sds((tokens, D), F32),
            sds((tokens, FF), BF16),
            sds((tokens, D), F32),
            sds((tokens, D), BF16),
        ],
        compiler_params=pltpu.CompilerParams(vmem_limit_bytes=VMEM_LIMIT),
        cost_estimate=pl.CostEstimate(
            flops=2 * tokens * D * (D + 2 * FF), bytes_accessed=30_000_000, transcendentals=tokens * FF
        ),
        name="expand",
    )(index, ctx, resid, vectors, wide_bias, *sources)


def contract_kernel(counts, me_ref, dz_ref, before_ref, h_ref, u_ref, vec_ref, *refs):
    c1, c2, c3 = counts
    leave_src, widen_src, narrow_src = refs[:c1], refs[c1 : c1 + c2], refs[c1 + c2 : c1 + c2 + c3]
    refs = refs[c1 + c2 + c3 :]
    dback_ref, mixed_ref, act_ref, dhid_ref, dattn_ref, du_ref, dctx_ref, dvec_ref, dbias_ref = refs[:9]
    leave, widen, narrow, sem = refs[9:]
    first = pl.program_id(0) == 0

    @pl.when(first)
    def _():
        start_load(me_ref[0], narrow_src, narrow, sem.at[2], place_narrow)
        start_load(me_ref[0], widen_src, widen, sem.at[1], place_widen)
        start_load(me_ref[0], leave_src, leave, sem.at[0], place_leave)
        dvec_ref[...] = jnp.zeros_like(dvec_ref)
        dbias_ref[...] = jnp.zeros_like(dbias_ref)

    dz = wide(dz_ref[...])
    unit, rstd = statistics(before_ref[...])
    dvec_ref[6:7, :] += column_sum(dz * unit)
    dvec_ref[7:8, :] += column_sum(dz)
    dpre = norm_pull(dz * vec_ref[6:7, :], unit, rstd)
    dback = low(dpre)
    dback_ref[...] = dback
    dvec_ref[5:6, :] += column_sum(wide(dback))
    unit, rstd = statistics(u_ref[...])
    mixed_ref[...] = low(unit * vec_ref[3:4, :] + vec_ref[4:5, :])

    @pl.when(first)
    def _():
        wait_load(narrow, sem.at[2])
        wait_load(widen, sem.at[1])
        wait_load(leave, sem.at[0])

    dmixed = dpre
    for j in range(6):
        cols = slice(512 * j, 512 * j + 512)
        dact = mm(dback, narrow[cols, :], NT)
        h = wide(h_ref[:, cols])
        square = h * h
        tanh = jnp.tanh(GELU_A * h * (1.0 + GELU_B * square))
        gate = 0.5 + 0.5 * tanh
        act_ref[:, cols] = low(h * gate)
        slope = gate + 0.5 * h * (1.0 - tanh * tanh) * (GELU_A + (3.0 * GELU_A * GELU_B) * square)
        dhid = low(dact * slope)
        dhid_ref[:, cols] = dhid
        dbias_ref[:, cols] += column_sum(wide(dhid))
        dmixed = dmixed + mm(dhid, widen[:, cols], NT)
    dvec_ref[3:4, :] += column_sum(dmixed * unit)
    dvec_ref[4:5, :] += column_sum(dmixed)
    du = norm_pull(dmixed * vec_ref[3:4, :], unit, rstd)
    du_ref[...] = du
    dattn = low(du)
    dattn_ref[...] = dattn
    dvec_ref[2:3, :] += column_sum(wide(dattn))
    dctx_ref[...] = low(mm(dattn, leave[...], NT))


def contract(index, dz, before, hidden_units, u, vectors, leave, widen, narrow):
    tokens = dz.shape[0]
    tile = 256
    blk = lambda width: pl.BlockSpec((tile, width), lambda r, *_: (r, 0))
    full = lambda *shape: pl.BlockSpec(shape, lambda r, *_: (0,) * len(shape))
    sds = jax.ShapeDtypeStruct
    sources = tuple(leave) + tuple(widen) + tuple(narrow)
    return pl.pallas_call(
        partial(contract_kernel, (len(leave), len(widen), len(narrow))),
        grid_spec=pltpu.PrefetchScalarGridSpec(
            num_scalar_prefetch=1,
            grid=(tokens // tile,),
            in_specs=[blk(D), blk(D), blk(FF), blk(D), full(8, D)] + [ANY] * len(sources),
            out_specs=[blk(D), blk(D), blk(FF), blk(FF), blk(D), blk(D), blk(D), full(8, D), full(1, FF)],
            scratch_shapes=[
                pltpu.VMEM((D, D), BF16),
                pltpu.VMEM((D, FF), BF16),
                pltpu.VMEM((FF, D), BF16),
                pltpu.SemaphoreType.DMA((3,)),
            ],
        ),
        out_shape=[
            sds((tokens, D), BF16),
            sds((tokens, D), BF16),
            sds((tokens, FF), BF16),
            sds((tokens, FF), BF16),
            sds((tokens, D), BF16),
            sds((tokens, D), F32),
            sds((tokens, D), BF16),
            sds((8, D), F32),
            sds((1, FF), F32),
        ],
        compiler_params=pltpu.CompilerParams(vmem_limit_bytes=VMEM_LIMIT),
        cost_estimate=pl.CostEstimate(
            flops=2 * tokens * D * (D + 2 * FF), bytes_accessed=50_000_000, transcendentals=tokens * FF
        ),
        name="contract",
    )(index, dz, before, hidden_units, u, vectors, *sources)


def halves(core, value, width):
    left, right = value[:, :width], value[:, width:]
    first = core == 0
    return jnp.where(first, right, left), jnp.where(first, left, right)


def narrow_grad_kernel(me_ref, act_ref, dback_ref, ctx_ref, dattn_ref, send_ref, keep_ref):
    step = pl.program_id(0)
    core = jnp.bitwise_and(me_ref[0], 1)
    chip = lax.shift_right_logical(me_ref[0], 1)

    @pl.when(step < 4)
    def _():
        send, keep = halves(core, mm(act_ref[...], dback_ref[...], TN), HALF)
        for i in range(4):
            at = position(chip, step * 4 + i)
            send_ref[at, 0:192, :] = low(send[192 * i : 192 * i + 192])
            keep_ref[at, 0:192, :] = low(keep[192 * i : 192 * i + 192])

    @pl.when(step == 4)
    def _():
        send, keep = halves(core, mm(ctx_ref[...], dattn_ref[...], TN), HALF)
        for i in range(UNITS):
            at = position(chip, i)
            send_ref[at, 192:240, :] = low(send[48 * i : 48 * i + 48])
            keep_ref[at, 192:240, :] = low(keep[48 * i : 48 * i + 48])


def narrow_grad(index, act, dback, ctx, dattn):
    tokens = act.shape[0]
    full = lambda *shape: pl.BlockSpec(shape, lambda r, *_: (0,) * len(shape))
    out = jax.ShapeDtypeStruct((UNITS, 240, HALF), BF16)
    return pl.pallas_call(
        narrow_grad_kernel,
        grid_spec=pltpu.PrefetchScalarGridSpec(
            num_scalar_prefetch=1,
            grid=(5,),
            in_specs=[
                pl.BlockSpec((tokens, D), lambda r, *_: (0, jnp.minimum(r, 3))),
                full(tokens, D),
                full(tokens, D),
                full(tokens, D),
            ],
            out_specs=[full(UNITS, 240, HALF)] * 2,
        ),
        out_shape=[out, out],
        compiler_params=pltpu.CompilerParams(vmem_limit_bytes=VMEM_LIMIT),
        cost_estimate=pl.CostEstimate(
            flops=2 * tokens * D * (D + FF), bytes_accessed=16_000_000, transcendentals=0
        ),
        name="narrow_grad",
    )(index, act, dback, ctx, dattn)


def widen_grad_kernel(me_ref, mixed_ref, dhid_ref, send_ref, keep_ref, turned):
    step = pl.program_id(0)
    core = jnp.bitwise_and(me_ref[0], 1)
    chip = lax.shift_right_logical(me_ref[0], 1)

    @pl.when(step == 0)
    def _():
        turned[...] = mixed_ref[...].T

    grad = low(mm(turned[...], dhid_ref[...]))
    mine = lax.div(step, 2) == core
    for part in range(2):

        @pl.when(lax.rem(step, 2) == part)
        def _():
            for wanted, out_ref in ((True, keep_ref), (False, send_ref)):

                @pl.when(mine == wanted)
                def _():
                    for i in range(UNITS):
                        at = position(chip, i)
                        out_ref[at, :, D * part : D * part + D] = grad[48 * i : 48 * i + 48]


def widen_grad(index, mixed_low, dhid):
    tokens = mixed_low.shape[0]
    full = lambda *shape: pl.BlockSpec(shape, lambda r, *_: (0,) * len(shape))
    out = jax.ShapeDtypeStruct((UNITS, 48, FF // 2), BF16)
    return pl.pallas_call(
        widen_grad_kernel,
        grid_spec=pltpu.PrefetchScalarGridSpec(
            num_scalar_prefetch=1,
            grid=(4,),
            in_specs=[full(tokens, D), pl.BlockSpec((tokens, D), lambda r, *_: (0, r))],
            out_specs=[full(UNITS, 48, FF // 2)] * 2,
            scratch_shapes=[pltpu.VMEM((D, tokens), BF16)],
        ),
        out_shape=[out, out],
        compiler_params=pltpu.CompilerParams(vmem_limit_bytes=VMEM_LIMIT),
        cost_estimate=pl.CostEstimate(
            flops=2 * tokens * D * FF, bytes_accessed=13_000_000, transcendentals=0
        ),
        name="widen_grad",
    )(index, mixed_low, dhid)


def entry_grad_kernel(len_ref, me_ref, a_ref, b_ref, dq_ref, dk_ref, dv_ref, vec_ref, send_ref, keep_ref, total):
    row = pl.program_id(0)
    core = jnp.bitwise_and(me_ref[0], 1)
    chip = lax.shift_right_logical(me_ref[0], 1)
    keys = b_ref.shape[1]

    @pl.when(row == 0)
    def _():
        total[...] = jnp.zeros_like(total)

    total[0] += mm(a_ref[0], dq_ref[0], TN)
    for block in range(keys // 256):

        @pl.when(block * 256 < len_ref[row])
        def _():
            rows = pl.ds(block * 256, 256)
            b = b_ref[0, rows, :].T
            total[1] += mm(b, dk_ref[0, rows, :])
            total[2] += mm(b, dv_ref[0, rows, :])

    @pl.when(row == pl.num_programs(0) - 1)
    def _():
        for m in range(3):
            send, keep = halves(core, total[m], HALF)
            for i in range(UNITS):
                at = position(chip, i)
                send_ref[at, 48 * m : 48 * m + 48, :] = low(send[48 * i : 48 * i + 48])
                keep_ref[at, 48 * m : 48 * m + 48, :] = low(keep[48 * i : 48 * i + 48])
        for i in range(UNITS):
            at = position(chip, i)
            send_ref[at, 144:160, :] = vec_ref[i, 1 - core]
            keep_ref[at, 144:160, :] = vec_ref[i, core]


def entry_grad(index, lengths, a, b, dq, dk, dv, vec):
    rows, keys, _ = b.shape
    queries = a.shape[1]
    blk = lambda *shape: pl.BlockSpec((1,) + shape, lambda r, *_: (r,) + (0,) * len(shape))
    full = lambda *shape: pl.BlockSpec(shape, lambda r, *_: (0,) * len(shape))
    out = jax.ShapeDtypeStruct((UNITS, 160, HALF), BF16)
    return pl.pallas_call(
        entry_grad_kernel,
        grid_spec=pltpu.PrefetchScalarGridSpec(
            num_scalar_prefetch=2,
            grid=(rows,),
            in_specs=[
                blk(queries, D),
                blk(keys, D),
                blk(queries, D),
                blk(keys, D),
                blk(keys, D),
                full(UNITS, 2, 16, HALF),
            ],
            out_specs=[full(UNITS, 160, HALF)] * 2,
            scratch_shapes=[pltpu.VMEM((3, D, D), F32)],
        ),
        out_shape=[out, out],
        compiler_params=pltpu.CompilerParams(vmem_limit_bytes=VMEM_LIMIT),
        cost_estimate=pl.CostEstimate(
            flops=2 * rows * (queries + keys) * D * D, bytes_accessed=20_000_000, transcendentals=0
        ),
        name="entry_grad",
    )(lengths, index, a, b, dq, dk, dv, vec)


def retrace_kernel(stride, len_ref, q_ref, k_ref, v_ref, dctx_ref, lse_ref, tab_ref, *refs):
    dq_ref, dk_ref, dv_ref, dvec_ref, diag_ref, ends_ref, bias, bias_sum, turned = refs
    row = pl.program_id(0)
    keys = k_ref.shape[1]
    queries = q_ref.shape[1]
    length = len_ref[row]

    @pl.when(row == 0)
    def _():
        build_bias(tab_ref, bias, stride)
        bias_sum[...] = jnp.zeros_like(bias_sum)
        dvec_ref[...] = jnp.zeros_like(dvec_ref)

    def pair_step(size, step, carry):
        lanes = pl.ds(pl.multiple_of(step * 128, 128), 128)
        queries_low = lane_masks(q_ref[0, :, lanes])
        dctx = lane_masks(dctx_ref[0, :, lanes])
        key = k_ref[0, :size, lanes]
        value = v_ref[0, :size, lanes]
        key_turned = key.T
        kept_probs, kept_grads = [], []
        for i in range(2):
            h = 2 * step + i
            scores = masked_scores(key, queries_low[i], bias[h, :size, :], length)
            probs = jnp.exp(scores - lse_ref[0, h, 0:1, :])
            dprobs = mm(value, dctx[i], NT)
            inner = jnp.sum(probs * dprobs, axis=0, keepdims=True)
            grads = low(probs * (dprobs - inner))
            kept_probs.append(low(probs))
            kept_grads.append(grads)
            for lane in range(queries // 128):
                bias_sum[lane, h, :size, :] += wide(grads[:, 128 * lane : 128 * lane + 128])
            turned[pl.ds(pl.multiple_of(step * 128 + HD * i, HD), HD), :] = (
                mm(key_turned[HD * i : HD * i + HD], grads) * HD**-0.5
            )
        dv_ref[0, :size, lanes] = low(
            mm(jnp.concatenate(kept_probs, axis=1), jnp.concatenate(dctx, axis=0))
        )
        dk_ref[0, :size, lanes] = low(
            mm(jnp.concatenate(kept_grads, axis=1), jnp.concatenate(queries_low, axis=0))
        )
        return carry

    blocks = lax.div(length + 127, 128)
    for w in range(1, keys // 128 + 1):

        @pl.when(blocks == w)
        def _():
            size = 128 * w
            lax.fori_loop(0, H // 2, partial(pair_step, size), 0)
            if size < keys:
                dk_ref[0, size:, :] = jnp.zeros((keys - size, D), BF16)
                dv_ref[0, size:, :] = jnp.zeros((keys - size, D), BF16)
            dvec_ref[1:2, :] += column_sum(wide(dv_ref[0, :size, :]))

    dquery = low(turned[...].T)
    dq_ref[0] = dquery
    dvec_ref[0:1, :] += column_sum(wide(dquery))

    @pl.when(row == pl.num_programs(0) - 1)
    def _():
        ends_ref[...] = jnp.zeros_like(ends_ref)

        def collect(h, carry):
            below = above = jnp.zeros((1, queries), F32)
            for part in range(stride):
                block = jnp.concatenate(
                    [
                        bias_sum[lane, h, pl.ds(part, queries, stride=stride), :]
                        for lane in range(queries // 128)
                    ],
                    axis=1,
                )
                col = lax.broadcasted_iota(jnp.int32, block.shape, 1)
                line = lax.broadcasted_iota(jnp.int32, block.shape, 0)
                place = stride * (line - col) + part
                zero = jnp.zeros_like(block)
                below = below + column_sum(jnp.where(place <= -(NB // 2), block, zero))
                above = above + column_sum(jnp.where(place >= NB // 2 - 1, block, zero))
                inside = jnp.where((place > -(NB // 2)) & (place < NB // 2 - 1), block, zero)
                partial_sum = inside[:8]
                for a in range(1, queries // 8):
                    partial_sum = partial_sum + pltpu.roll(inside[8 * a : 8 * a + 8], queries - 8 * a, 1)
                sub = lax.broadcasted_iota(jnp.int32, partial_sum.shape, 0)
                lined = jnp.where(sub == 0, partial_sum, 0.0)
                for b in range(1, 8):
                    lined = lined + jnp.where(sub == b, pltpu.roll(partial_sum, queries - b, 1), 0.0)
                diag_ref[h, part] = jnp.broadcast_to(column_sum(lined), (8, queries))
            ends_ref[h, 0] = jnp.broadcast_to(below, (8, queries))
            ends_ref[h, 1] = jnp.broadcast_to(above, (8, queries))
            return carry

        lax.fori_loop(0, H, collect, 0)


def retrace(stride, lengths, q, k, v, dctx, lse, table):
    rows, keys, _ = k.shape
    queries = q.shape[1]
    blk = lambda *shape: pl.BlockSpec((1,) + shape, lambda r, *_: (r,) + (0,) * len(shape))
    full = lambda *shape: pl.BlockSpec(shape, lambda r, *_: (0,) * len(shape))
    sds = jax.ShapeDtypeStruct
    return pl.pallas_call(
        partial(retrace_kernel, stride),
        grid_spec=pltpu.PrefetchScalarGridSpec(
            num_scalar_prefetch=1,
            grid=(rows,),
            in_specs=[
                blk(queries, D),
                blk(keys, D),
                blk(keys, D),
                blk(queries, D),
                blk(H, 8, queries),
                full(16, 128),
            ],
            out_specs=[
                blk(queries, D),
                blk(keys, D),
                blk(keys, D),
                full(8, D),
                full(H, stride, 8, queries),
                full(H, 2, 8, queries),
            ],
            scratch_shapes=[
                pltpu.VMEM((H, keys, queries), F32),
                pltpu.VMEM((queries // 128, H, keys, 128), F32),
                pltpu.VMEM((D, queries), F32),
            ],
        ),
        out_shape=[
            sds((rows, queries, D), BF16),
            sds((rows, keys, D), BF16),
            sds((rows, keys, D), BF16),
            sds((8, D), F32),
            sds((H, stride, 8, queries), F32),
            sds((H, 2, 8, queries), F32),
        ],
        compiler_params=pltpu.CompilerParams(vmem_limit_bytes=VMEM_LIMIT),
        cost_estimate=pl.CostEstimate(
            flops=rows * keys * queries * D * 10, bytes_accessed=20_000_000, transcendentals=rows * H * keys * queries
        ),
        name="retrace",
    )(lengths, q, k, v, dctx, lse, table)


def table_grad(stride, diag, ends):
    queries = diag.shape[-1]
    columns = []
    for bucket in range(NB):
        place = bucket - NB // 2
        if bucket == 0:
            columns.append(jnp.sum(ends[:, 0, 0], axis=-1))
        elif bucket == NB - 1:
            columns.append(jnp.sum(ends[:, 1, 0], axis=-1))
        else:
            part = place % stride
            columns.append(diag[:, part, 0, ((part - place) // stride) % queries])
    return jnp.stack(columns, axis=1).reshape(-1)


def inputs_kernel(stride, count, len_ref, me_ref, dq_ref, dk_ref, dv_ref, du_ref, *refs):
    sources = refs[:count]
    out_ref, entry, sem = refs[count:]
    row = pl.program_id(0)
    keys = dk_ref.shape[1]
    queries = dq_ref.shape[1]

    @pl.when(row == 0)
    def _():
        start_load(me_ref[0], sources, entry, sem.at[0], place_entry)
        wait_load(entry, sem.at[0])

    total = mm(dq_ref[0], entry[0], NT) + du_ref[0]
    if stride == 1:
        out_ref[0] = total + mm(dk_ref[0], entry[1], NT) + mm(dv_ref[0], entry[2], NT)
        return
    total = 0.5 * total
    upper = low(total)
    lower = low(total - wide(upper))
    for block in range(keys // 256):
        rows = pl.ds(block * 256, 256)
        place = lax.broadcasted_iota(jnp.int32, (256, queries), 0) + 256 * block
        mine = lax.broadcasted_iota(jnp.int32, (256, queries), 1)
        pair = jnp.where(lax.shift_right_logical(place, 1) == mine, 1.0, 0.0).astype(BF16)
        spread = mm(pair, upper) + mm(pair, lower)

        @pl.when(block * 256 < len_ref[row])
        def _():
            out_ref[0, rows, :] = (
                spread + mm(dk_ref[0, rows, :], entry[1], NT) + mm(dv_ref[0, rows, :], entry[2], NT)
            )

        @pl.when(block * 256 >= len_ref[row])
        def _():
            out_ref[0, rows, :] = spread


def input_grads(stride, index, lengths, dq, dk, dv, du, sources):
    rows, keys, _ = dk.shape
    queries = dq.shape[1]
    blk = lambda *shape: pl.BlockSpec((1,) + shape, lambda r, *_: (r,) + (0,) * len(shape))
    return pl.pallas_call(
        partial(inputs_kernel, stride, len(sources)),
        grid_spec=pltpu.PrefetchScalarGridSpec(
            num_scalar_prefetch=2,
            grid=(rows,),
            in_specs=[blk(queries, D), blk(keys, D), blk(keys, D), blk(queries, D)] + [ANY] * len(sources),
            out_specs=blk(keys, D),
            scratch_shapes=[pltpu.VMEM((3, D, D), BF16), pltpu.SemaphoreType.DMA((1,))],
        ),
        out_shape=jax.ShapeDtypeStruct((rows, keys, D), F32),
        compiler_params=pltpu.CompilerParams(vmem_limit_bytes=VMEM_LIMIT),
        cost_estimate=pl.CostEstimate(
            flops=2 * rows * (queries + keys) * D * D, bytes_accessed=20_000_000, transcendentals=0
        ),
        name="input_grads",
    )(lengths, index, dq, dk, dv, du, *sources)


def forward(stride, index, lengths, x, resid, weights, small):
    entry_leave, widen, narrow = weights
    entry, leave = entry_leave if len(widen) == 1 else (entry_leave, entry_leave)
    vectors, wide_bias, table = small
    made = attend(stride, index, lengths, x, vectors, table, entry)
    if stride == 2:
        resid, query_in, *made = made
    else:
        query_in = x
    q, k, v, ctx, lse = made
    tokens = ctx.shape[0] * ctx.shape[1]
    flat = lambda value: value.reshape(tokens, D)
    u, hidden_units, before, out = expand(
        index, flat(ctx), flat(resid), vectors, wide_bias, leave, widen, narrow
    )
    return out, (query_in, q, k, v, ctx, lse, u, hidden_units, before)


def backward(stride, index, lengths, dz, x, kept, weights, small, reduce):
    entry_leave, widen, narrow = weights
    entry, leave = entry_leave if len(widen) == 1 else (entry_leave, entry_leave)
    vectors, wide_bias, table = small
    query_in, q, k, v, ctx, lse, u, hidden_units, before = kept
    rows, queries, _ = q.shape
    dback, mixed_low, act, dhid, dattn, du, dctx, dvec, dbias = contract(
        index, dz, before, hidden_units, u, vectors, leave, widen, narrow
    )
    shape = q.shape
    sums = [narrow_grad(index, act, dback, ctx.reshape(-1, D), dattn)]
    sums.append(widen_grad(index, mixed_low, dhid))
    dq, dk, dv, dvec_top, diag, ends = retrace(
        stride, lengths, q, k, v, dctx.reshape(shape), lse, table
    )
    dvec = dvec + dvec_top
    dtable = table_grad(stride, diag, ends)
    flat = vector_units(dvec, dbias, dtable, 32)
    flat = jnp.pad(low(flat), ((0, 0), (0, 16 * HALF - flat.shape[1]))).reshape(UNITS, 2, 16, HALF)
    sums.append(entry_grad(index, lengths, query_in, x, dq, dk, dv, flat))
    dx = input_grads(stride, index, lengths, dq, dk, dv, du.reshape(shape), entry)
    return dx, [reduce(*pair) for pair in sums]


def shards(index, sums):
    core = index % 2
    narrow_leave, widen, entry = sums
    narrow = unpair(core, narrow_leave[None, :192], 96)[0]
    leave = unpair(core, narrow_leave[None, 192:], 24)[0]
    widen = unpair(core, widen[None], 24)[0]
    vectors = split_vectors(entry[144:].reshape(-1), 32)
    entry = unpair(core, entry[:144].reshape(3, 48, HALF), 24)
    return (entry, leave, widen, narrow) + vectors


def absolute_units(pair):
    send, keep = pair
    merged = jnp.concatenate([keep[:, :, None], send[:, :, None]], axis=2)
    rest = merged.shape[1:]
    merged = merged.reshape((4, 4) + rest).transpose(1, 0, 2, 3, 4)
    return wide(merged.reshape((UNITS,) + rest))


def plain_shards(sums):
    narrow_leave, widen, entry = [absolute_units(pair) for pair in sums]
    vectors = entry[:, 144:].transpose(0, 2, 1, 3).reshape(32, -1)
    narrow = narrow_leave[:, :192].reshape(FF, D)
    leave = narrow_leave[:, 192:].reshape(D, D)
    widen = widen.reshape(D, FF)
    entry = entry[:, :144].reshape(UNITS, 3, 48, D).transpose(1, 0, 2, 3).reshape(3, D, D)
    scatter = lambda value, dim: lax.psum_scatter(value, AX, scatter_dimension=dim, tiled=True)
    rows = vectors.shape[0]
    cut, mid = 8 * D // rows, 8 * D // rows + FF // rows
    last = mid + H * NB // rows
    vec = vectors[:, :cut].reshape(rows, 8, -1).transpose(1, 0, 2).reshape(8, D)
    return (
        scatter(entry, 1),
        scatter(leave, 0),
        scatter(widen, 0),
        scatter(narrow, 0),
        scatter(vec, 1),
        scatter(vectors[:, cut:mid].reshape(-1), 0),
        scatter(vectors[:, mid:last].reshape(-1), 0),
    )


def plain_gather(entry, leave, widen, narrow):
    gather = lambda value, dim: lax.all_gather(value, AX, axis=dim, tiled=True)
    return (
        ((gather(entry, 1),), (gather(leave, 0),)),
        (gather(widen, 0),),
        (gather(narrow, 0),),
    )


def small_parts(vectors, wide_bias, table):
    tab = jnp.pad(wide(table).reshape(H, NB), ((0, 16 - H), (0, 128 - NB)))
    return wide(vectors), wide(wide_bias).reshape(1, FF), tab


def unpack_small(full, parts):
    cut, mid = 8 * D // parts, (8 * D + FF) // parts
    vectors = full[:, :cut].reshape(parts, 8, -1).transpose(1, 0, 2).reshape(8, D)
    last = (8 * D + FF + H * NB) // parts
    return small_parts(vectors, full[:, cut:mid].reshape(-1), full[:, mid:last].reshape(-1))


def on_device(
    devices,
    hidden,
    lengths,
    cotangent,
    inflow,
    outflow,
    widener,
    narrower,
    shifts,
    offsets,
    distance,
    intake,
    outtake,
    expander,
    squeezer,
    adjusts,
    leanings,
    spacing,
):
    rows, seq, width = hidden.shape
    half = seq // 2
    fast = devices == 32
    index = lax.axis_index(AX)
    flat = jnp.concatenate(
        [shifts.reshape(-1), offsets, distance, adjusts.reshape(-1), leanings, spacing]
    )
    count = flat.shape[0] // 2
    if fast:
        flat = jnp.pad(flat, (0, 1024 - flat.shape[0])).reshape(8, 128)
        small = gather_vectors(index, flat)
        first, second = gather_layers(
            index, ((inflow, outflow, widener, narrower), (intake, outtake, expander, squeezer))
        )
        me = index.astype(jnp.int32).reshape(1)
    else:
        small = lax.all_gather(flat, AX, axis=0)
        first = plain_gather(inflow, outflow, widener, narrower)
        second = plain_gather(intake, outtake, expander, squeezer)
        me = jnp.zeros((1,), jnp.int32)
    small_one = unpack_small(small[:, :count], devices)
    small_two = unpack_small(small[:, count : 2 * count], devices)
    reduce = reduce_units if fast else (lambda *pair: pair)
    halved = (lengths + 1) // 2
    first_out, first_kept = forward(2, me, lengths, hidden, None, first, small_one)
    pooled_layer = first_out.reshape(rows, half, width)
    second_out, second_kept = forward(1, me, halved, pooled_layer, pooled_layer, second, small_two)
    dlayer, sums_two = backward(
        1, me, halved, cotangent.reshape(-1, width), pooled_layer, second_kept, second, small_two, reduce
    )
    hidden_grad, sums_one = backward(
        2, me, lengths, dlayer.reshape(-1, width), hidden, first_kept, first, small_one, reduce
    )
    if fast:
        shards_one, shards_two = shards(index, sums_one), shards(index, sums_two)
    else:
        shards_one, shards_two = plain_shards(sums_one), plain_shards(sums_two)
    return (
        pooled_layer,
        second_out.reshape(rows, half, width),
        hidden_grad,
        *shards_one,
        *shards_two[:4],
        shards_two[4][1:],
        shards_two[5],
        shards_two[6],
        shards_two[4][0],
    )


def solution(mesh):
    both = ("wide", "narrow")
    rows = P(both, None, None)
    weights = (
        P(None, both, None),
        P(both, None),
        P(both, None),
        P(both, None),
        P(None, both),
        P(both),
        P(both),
    )
    return jax.shard_map(
        partial(on_device, mesh.size),
        mesh=mesh,
        in_specs=(rows, P(both), rows) + weights + weights,
        out_specs=(rows, rows, rows) + weights + weights + (P(both),),
        check_vma=False,
    )
```

time: 2010 us -> 813 us (0.40)
  waiting for transfers between devices: 1160 us -> 232 us
  matrix products: 334 us -> 0 us
  Pallas kernels: 0 us -> 313 us
  local copies, waits for them, and re-layouts: 254 us -> 61.9 us
  starting transfers between devices: 1.72 us -> 146 us
  blocking collectives: 122 us -> 0 us
  other arithmetic: 119 us -> 49 us
    reduce_scatter x8 -> x0, waiting for transfers between devices: 1010 us -> none  [the longest x2 283 us: reduce_grads(): lax.psum_scatter(widen, ('wide', 'narrow'), scatter_dimension=0, tiled=True)]
    dot_general x96 -> x0, matrix products: 334 us -> none  [the longest x12 86.6 us: flat_dot(): jnp.dot(left.reshape(-1, left.shape[-1]), right, preferred_element_type=j...]
    pallas_call x0 -> x16, Pallas kernels: none -> 313 us  [the longest x2 59 us: contract(): pl.pallas_call(partial(contract_kernel, (len(leave), len(widen), len(narr...]
    ppermute x0 -> x146, waiting for transfers between devices: none -> 232 us  [swap(): return lax.ppermute(value, AX, [(i, i ^ mask) for i in range(32)])]
    ppermute x0 -> x146, starting transfers between devices: none -> 146 us  [swap(): return lax.ppermute(value, AX, [(i, i ^ mask) for i in range(32)])]
    all_gather x8 -> x0, waiting for transfers between devices: 137 us -> none  [the longest x2 57.4 us: fetch_forward(): lax.all_gather(widen, ('wide', 'narrow'), axis=0, tiled=True)]
    all_gather x2 -> x0, blocking collectives: 84.3 us -> none  [fetch_forward(): lax.all_gather(vectors, ('wide', 'narrow'), axis=1, tiled=True)]
    dynamic_slice x72 -> x0, local copies, waits for them, and re-layouts: 83 us -> none  [layer_forward(): context, totals = lax.map(attend, (query, key, value, key_len))]
  transfers between devices with their start and end apart: 17 -> 146, of which waited for: 11 -> 57; matrix products, arithmetic and copies ran while one was open for 18% -> 11% of each run, Pallas kernels for 0% -> 19%
where the time goes in v1:
time: 813 us; the launch traced here: 805 us
  Pallas kernels  313 us (38%)
  waiting for transfers between devices  232 us (29%)
  starting transfers between devices  146 us (18%)
  local copies, waits for them, and re-layouts  61.9 us (8%)
  other arithmetic  49 us (6%)
    ppermute x146, waiting for transfers between devices, swap(): return lax.ppermute(value, AX, [(i, i ^ mask) for i in range(32)])  232 us
    ppermute x146, starting transfers between devices, swap(): return lax.ppermute(value, AX, [(i, i ^ mask) for i in range(32)])  146 us
    pallas_call x2, Pallas kernels, contract(): pl.pallas_call(partial(contract_kernel, (len(leave), len(widen), len(narr...  59 us
    pallas_call x2, Pallas kernels, retrace(): pl.pallas_call(partial(retrace_kernel, stride), grid_spec=pltpu.PrefetchS...  58.7 us
    pallas_call x2, Pallas kernels, attend(): pl.pallas_call(partial(attend_kernel, stride, len(sources)), grid_spec=pl...  55.5 us
    pallas_call x2, Pallas kernels, expand(): pl.pallas_call(partial(expand_kernel, (len(leave), len(widen), len(narrow...  44.6 us
    pallas_call x2, Pallas kernels, narrow_grad(): pl.pallas_call(narrow_grad_kernel, grid_spec=pltpu.PrefetchScalarGridSpec...  25.6 us
    pallas_call x2, Pallas kernels, input_grads(): pl.pallas_call(partial(inputs_kernel, stride, len(sources)), grid_spec=pl...  25.4 us
  transfers between devices with their start and end apart: 146, of which 57 were waited for; matrix products, arithmetic and copies ran while one was open for 11% of the time, Pallas kernels for 19%

profile of v1, /device:TPU:0, one launch (start us, length us, event | category | flops | bytes accessed | tf_op | source)
XLA Modules:
  0.0 805.1 jit_solution(5201692764622144962)
XLA Ops:
  5.0 5.1 collective-permute-start.2
  42.6 6.5 collective-permute-start.13
  49.1 8.6 %collective-permute-done.79 = bf16[192,384]{1,0:T(8,128)(2,1)S(1)} collective-permute-done((bf16[192,384]{1,0:T(8,128)(2,1)S(1)}, bf16[192,384]{1,0:T(8,128)(2,1)S(1)}, u32[]{:S(2)}, u32[]{:S(2)}) %collective-permute-start.79) | collective-permute-done | bytes 147488 | tf_op jit(solution)/shard_map/ppermute | solution.py:44
  64.0 9.5 %collective-permute-done.14 = bf16[4,48,384]{2,1,0:T(8,128)(2,1)S(1)} collective-permute-done((bf16[4,48,384]{2,1,0:T(8,128)(2,1)S(1)}, bf16[4,48,384]{2,1,0:T(8,128)(2,1)S(1)}, u32[]{:S(2)}, u32[]{:S(2)}) %collective-permute-start.14) | collective-permute-done | bytes 147488 | tf_op jit(solution)/shard_map/ppermute | solution.py:44
  78.6 13.1 %collective-permute-done.40 = bf16[192,384]{1,0:T(8,128)(2,1)S(1)} collective-permute-done((bf16[192,384]{1,0:T(8,128)(2,1)S(1)}, bf16[192,384]{1,0:T(8,128)(2,1)S(1)}, u32[]{:S(2)}, u32[]{:S(2)}) %collective-permute-start.40) | collective-permute-done | bytes 147488 | tf_op jit(solution)/shard_map/ppermute | solution.py:44
  95.2 5.3 collective-permute-start.27
  110.3 9.3 %collective-permute-done.81.refs_21_ = bf16[4,192,384]{2,1,0:T(8,128)(2,1)} collective-permute-done((bf16[4,192,384]{2,1,0:T(8,128)(2,1)S(1)}, bf16[4,192,384]{2,1,0:T(8,128)(2,1)}, u32[]{:S(2)}, u32[]{:S(2)}) %collective-permute-start.81) | collective-permute-done | bytes 589856 | tf_op jit(solution)/shard_map/ppermute | solution.py:44
  125.3 6.9 collective-permute-done.68.refs_11_
  133.7 4.1 collective-permute-done.43.refs_22_
  138.8 6.1 collective-permute-done.42.refs_21_
  146.1 4.5 collective-permute-done.30.refs_12_
  150.6 6.9 collective-permute-done.29.refs_11_
  183.4 5.7 collective-permute-done.84.refs_24_
  190.4 5.1 collective-permute-done.71.refs_14_
  202.9 5.1 collective-permute-done.32.refs_14_
  208.5 5.2 collective-permute-done.19.refs_4_
  242.8 30.8 %attend.2 = (f32[4,256,768]{2,1,0:T(8,128)}, bf16[4,256,768]{2,1,0:T(8,128)(2,1)}, bf16[4,256,768]{2,1,0:T(8,128)(2,1)}, bf16[4,512,768]{2,1,0:T(8,128)(2,1)}, b...) custom-call(s32[4]{0:T(128)} %len_ref.7, s32[1]{0:T(128)} %bitcast.me_ref, ...), custom_call_target="tpu_custom_call" | custom-call | flops 9663676416 | bytes 20000000 | tf_op jit(solution)/shard_map/attend/pallas_call | solution.py:327
  277.3 22.5 %expand.2 = (f32[1024,768]{1,0:T(8,128)}, bf16[1024,3072]{1,0:T(8,128)(2,1)}, f32[1024,768]{1,0:T(8,128)}, bf16[1024,768]{1,0:T(8,128)(2,1)}) custom-call(s32[1]{0:T(128)} %bitcast.me_ref, bf16[1024,768]{1,0:T(8,128)(2,1)} %bitcast.412, f32[1024,768]{1,0:T(8,128)} %bitcast.406, f32[8,768]{1,0:T(8,128)} %reshape.533.vec_ref, f32[1,3072]{1,0:T(1,128)} %reshape.534.bias_ref, ...), custom_call_target="tpu_custom_call" | custom-call | flops 10871635968 | bytes 30000000 | tf_op jit(solution)/shard_map/expand/pallas_call | solution.py:393
  300.9 24.7 %attend.3 = (bf16[4,256,768]{2,1,0:T(8,128)(2,1)}, bf16[4,256,768]{2,1,0:T(8,128)(2,1)}, bf16[4,256,768]{2,1,0:T(8,128)(2,1)}, bf16[4,256,768]{2,1,0:T(8,128)(2,1)}, f32[4,12,8,256]{3,2,1,0:T(8,128)}) custom-call(s32[4]{0:T(128)} %and_select_fusion.len_ref, s32[1]{0:T(128)} %bitcast.me_ref, bf16[4,256,768]{2,1,0:T(8,128)(2,1)} %bitcast.407, ...), custom_call_target="tpu_custom_call" | custom-call | flops 4831838208 | bytes 20000000 | tf_op jit(solution)/shard_map/attend/pallas_call | solution.py:327
  326.8 22.0 %expand.3 = (f32[1024,768]{1,0:T(8,128)}, bf16[1024,3072]{1,0:T(8,128)(2,1)}, f32[1024,768]{1,0:T(8,128)}, bf16[1024,768]{1,0:T(8,128)(2,1)}) custom-call(s32[1]{0:T(128)} %bitcast.me_ref, bf16[1024,768]{1,0:T(8,128)(2,1)} %bitcast.414, bf16[1024,768]{1,0:T(8,128)(2,1)} %get-tuple-element.82.resid_ref, f32[8,768]{1,0:T(8,128)} %reshape.535.vec_ref, ...), custom_call_target="tpu_custom_call" | custom-call | flops 10871635968 | bytes 30000000 | tf_op jit(solution)/shard_map/expand/pallas_call | solution.py:393
  348.8 29.3 %contract.2 = (bf16[1024,768]{1,0:T(8,128)(2,1)}, bf16[1024,768]{1,0:T(8,128)(2,1)}, bf16[1024,3072]{1,0:T(8,128)(2,1)}, bf16[1024,3072]{1,0:T(8,128)(2,1)}, bf1...) custom-call(s32[1]{0:T(128)} %bitcast.me_ref, ...), custom_call_target="tpu_custom_call" | custom-call | flops 10871635968 | bytes 50000000 | tf_op jit(solution)/shard_map/contract/pallas_call | solution.py:485
  378.1 24.9 %retrace.2 = (bf16[4,256,768]{2,1,0:T(8,128)(2,1)}, bf16[4,256,768]{2,1,0:T(8,128)(2,1)}, bf16[4,256,768]{2,1,0:T(8,128)(2,1)}, f32[8,768]{1,0:T(8,128)}, f32[12...) custom-call(s32[4]{0:T(128)} %and_select_fusion.len_ref, bf16[4,256,768]{2,1,0:T(8,128)(2,1)} %get-tuple-element.88.q_ref, ...), custom_call_target="tpu_custom_call" | custom-call | flops 2013265920 | bytes 20000000 | tf_op jit(solution)/shard_map/retrace/pallas_call | solution.py:784
  405.0 10.4 %input_grads.2 = f32[4,256,768]{2,1,0:T(8,128)} custom-call(s32[4]{0:T(128)} %and_select_fusion.len_ref, s32[1]{0:T(128)} %bitcast.me_ref, bf16[4,256,768]{2,1,0:T(8,128)(2,1)} %get-tuple-element.96.dq_ref, bf16[4,256,768]{2,1,0:T(8,128)(2,1)} %get-tuple-element.97.dk_ref, bf16[4,256,768]{2,1,0:T(8,128)(2,1)} %get-tuple-element.98.dv_ref, ...), custom_call_target="tpu_custom_call" | custom-call | flops 2415919104 | bytes 20000000 | tf_op jit(solution)/shard_map/input_grads/pallas_call | solution.py:883
  415.4 29.7 %contract.3 = (bf16[1024,768]{1,0:T(8,128)(2,1)}, bf16[1024,768]{1,0:T(8,128)(2,1)}, bf16[1024,3072]{1,0:T(8,128)(2,1)}, bf16[1024,3072]{1,0:T(8,128)(2,1)}, bf1...) custom-call(s32[1]{0:T(128)} %bitcast.me_ref, ...), custom_call_target="tpu_custom_call" | custom-call | flops 10871635968 | bytes 50000000 | tf_op jit(solution)/shard_map/contract/pallas_call | solution.py:485
  445.2 33.7 %retrace.3 = (bf16[4,256,768]{2,1,0:T(8,128)(2,1)}, bf16[4,512,768]{2,1,0:T(8,128)(2,1)}, bf16[4,512,768]{2,1,0:T(8,128)(2,1)}, f32[8,768]{1,0:T(8,128)}, f32[12...) custom-call(s32[4]{0:T(128)} %len_ref.7, bf16[4,256,768]{2,1,0:T(8,128)(2,1)} %get-tuple-element.85.q_ref, ...), custom_call_target="tpu_custom_call" | custom-call | flops 4026531840 | bytes 20000000 | tf_op jit(solution)/shard_map/retrace/pallas_call | solution.py:784
  487.2 11.1 %entry_grad.3 = (bf16[16,160,384]{2,1,0:T(8,128)(2,1)}, bf16[16,160,384]{2,1,0:T(8,128)(2,1)}) custom-call(s32[4]{0:T(128)} %and_select_fusion.len_ref, s32[1]{0:T(128)} %bitcast.me_ref, bf16[4,256,768]{2,1,0:T(8,128)(2,1)} %bitcast.408, bf16[4,256,768]{2,1,0:T(8,128)(2,1)} %bitcast.409, bf16[4,256,768]{2,1,0:T(8,128)(2,1)} %get-tuple-element.96.dq_ref, ...), custom_call_target="tpu_custom_call" | custom-call | flops 2415919104 | bytes 20000000 | tf_op jit(solution)/shard_map/entry_grad/pallas_call | solution.py:658
  498.2 5.4 collective-permute-start.118
  503.6 12.1 %entry_grad.2 = (bf16[16,160,384]{2,1,0:T(8,128)(2,1)}, bf16[16,160,384]{2,1,0:T(8,128)(2,1)}) custom-call(s32[4]{0:T(128)} %len_ref.7, s32[1]{0:T(128)} %bitcast.me_ref, bf16[4,256,768]{2,1,0:T(8,128)(2,1)} %get-tuple-element.109.a_ref, bf16[4,512,768]{2,1,0:T(8,128)(2,1)} %b_ref.1, bf16[4,256,768]{2,1,0:T(8,128)(2,1)} %get-tuple-element.105.dq_ref, ...), custom_call_target="tpu_custom_call" | custom-call | flops 3623878656 | bytes 20000000 | tf_op jit(solution)/shard_map/entry_grad/pallas_call | solution.py:658
  516.4 10.6 %widen_grad.2 = (bf16[16,48,1536]{2,1,0:T(8,128)(2,1)}, bf16[16,48,1536]{2,1,0:T(8,128)(2,1)}) custom-call(s32[1]{0:T(128)} %bitcast.me_ref, bf16[1024,768]{1,0:T(8,128)(2,1)} %get-tuple-element.122.mixed_ref, bf16[1024,3072]{1,0:T(8,128)(2,1)} %get-tuple-element.123.dhid_ref), custom_call_target="tpu_custom_call" | custom-call | flops 4831838208 | bytes 13000000 | tf_op jit(solution)/shard_map/widen_grad/pallas_call | solution.py:600
  527.0 10.7 %widen_grad.3 = (bf16[16,48,1536]{2,1,0:T(8,128)(2,1)}, bf16[16,48,1536]{2,1,0:T(8,128)(2,1)}) custom-call(s32[1]{0:T(128)} %bitcast.me_ref, bf16[1024,768]{1,0:T(8,128)(2,1)} %get-tuple-element.138.mixed_ref, bf16[1024,3072]{1,0:T(8,128)(2,1)} %get-tuple-element.139.dhid_ref), custom_call_target="tpu_custom_call" | custom-call | flops 4831838208 | bytes 13000000 | tf_op jit(solution)/shard_map/widen_grad/pallas_call | solution.py:600
  538.2 12.7 %narrow_grad.2 = (bf16[16,240,384]{2,1,0:T(8,128)(2,1)}, bf16[16,240,384]{2,1,0:T(8,128)(2,1)}) custom-call(s32[1]{0:T(128)} %bitcast.me_ref, bf16[1024,3072]{1,0:T(8,128)(2,1)} %get-tuple-element.117.act_ref, bf16[1024,768]{1,0:T(8,128)(2,1)} %get-tuple-element.118.dback_ref, bf16[1024,768]{1,0:T(8,128)(2,1)} %bitcast.413, ...), custom_call_target="tpu_custom_call" | custom-call | flops 6039797760 | bytes 16000000 | tf_op jit(solution)/shard_map/narrow_grad/pallas_call | solution.py:550
  550.9 15.0 %input_grads.3 = f32[4,512,768]{2,1,0:T(8,128)} custom-call(s32[4]{0:T(128)} %len_ref.7, s32[1]{0:T(128)} %bitcast.me_ref, bf16[4,256,768]{2,1,0:T(8,128)(2,1)} %get-tuple-element.105.dq_ref, bf16[4,512,768]{2,1,0:T(8,128)(2,1)} %get-tuple-element.106.dk_ref, bf16[4,512,768]{2,1,0:T(8,128)(2,1)} %get-tuple-element.107.dv_ref, f32[4,256,768]{2,1,0:T(8,128)} %bitcast.294, ...), custom_call_target="tpu_custom_call" | custom-call | flops 3623878656 | bytes 20000000 | tf_op jit(solution)/shard_map/input_grads/pallas_call | solution.py:883
  565.9 12.9 %narrow_grad.3 = (bf16[16,240,384]{2,1,0:T(8,128)(2,1)}, bf16[16,240,384]{2,1,0:T(8,128)(2,1)}) custom-call(s32[1]{0:T(128)} %bitcast.me_ref, bf16[1024,3072]{1,0:T(8,128)(2,1)} %get-tuple-element.133.act_ref, bf16[1024,768]{1,0:T(8,128)(2,1)} %get-tuple-element.134.dback_ref, bf16[1024,768]{1,0:T(8,128)(2,1)} %bitcast.415, ...), custom_call_target="tpu_custom_call" | custom-call | flops 6039797760 | bytes 16000000 | tf_op jit(solution)/shard_map/narrow_grad/pallas_call | solution.py:550
  584.4 6.0 collective-permute-done.91
  590.3 18.2 %collective-permute-start.93 = (bf16[2,160,384]{2,1,0:T(8,128)(2,1)S(1)}, bf16[2,160,384]{2,1,0:T(8,128)(2,1)S(1)}, u32[]{:S(2)}, u32[]{:S(2)}) collective-permute-start(bf16[2,160,384]{2,1,0:T(8,128)(2,1)S(1)} %get-tuple-element.269), channel_id=1, source_target_pairs={{0,4},{1,5},{2,6},{3,7},{4,0},{5,1},{6,2},{7,3},{8,12},{9,13},{10,... | collective-permute-start | bytes 737288 | tf_op jit(solution)/shard_map/ppermute | solution.py:44
  608.7 5.5 collective-permute-done.93
  615.6 5.3 collective-permute-done.119
  622.5 4.6 collective-permute-done.121
  635.5 7.9 collective-permute-done.137
  644.5 5.6 collective-permute-done.139
  650.9 6.0 collective-permute-done.109
  658.9 6.2 collective-permute-done.111
  716.0 4.4 collective-permute-done.112
  740.5 9.2 %collective-permute-done.142 = bf16[48,1536]{1,0:T(8,128)(2,1)S(1)} collective-permute-done((bf16[48,1536]{1,0:T(8,128)(2,1)S(1)}, bf16[48,1536]{1,0:T(8,128)(2,1)S(1)}, u32[]{:S(2)}, u32[]{:S(2)}) %collective-permute-start.142) | collective-permute-done | bytes 147488 | tf_op jit(solution)/shard_map/ppermute | solution.py:44
  759.1 10.1 %collective-permute-done.129 = bf16[4,240,384]{2,1,0:T(8,128)(2,1)S(1)} collective-permute-done((bf16[4,240,384]{2,1,0:T(8,128)(2,1)S(1)}, bf16[4,240,384]{2,1,0:T(8,128)(2,1)S(1)}, u32[]{:S(2)}, u32[]{:S(2)}) %collective-permute-start.129) | collective-permute-done | bytes 737312 | tf_op jit(solution)/shard_map/ppermute | solution.py:44
  774.6 6.4 collective-permute-done.101
  785.0 8.5 %collective-permute-done.133 = bf16[240,384]{1,0:T(8,128)(2,1)S(1)} collective-permute-done((bf16[240,384]{1,0:T(8,128)(2,1)S(1)}, bf16[240,384]{1,0:T(8,128)(2,1)S(1)}, u32[]{:S(2)}, u32[]{:S(2)}) %collective-permute-start.133) | collective-permute-done | bytes 184352 | tf_op jit(solution)/shard_map/ppermute | solution.py:44
  793.6 6.2 collective-permute-done.105
  (599 shorter events, 267.0 us)
Async XLA Ops:
  32.3 25.4 %collective-permute-start.79 = (bf16[192,384]{1,0:T(8,128)(2,1)S(1)}, bf16[192,384]{1,0:T(8,128)(2,1)S(1)}, u32[]{:S(2)}, u32[]{:S(2)}) collective-permute-start(bf16[192,384]{1,0:T(8,128)(2,1)S(1)} %maximum_bitcast_fusion.7), channel_id=1, source_target_pairs={{0,16},{1,17},{2,18},{3,19},{4,20},{5,21},{6,22},{7,23},{8,24},{9,... | collective-permute-start | bytes 442376 | tf_op jit(solution)/shard_map/ppermute | solution.py:44
  33.6 26.3 %collective-permute-start.78 = (bf16[192,384]{1,0:T(8,128)(2,1)S(1)}, bf16[192,384]{1,0:T(8,128)(2,1)S(1)}, u32[]{:S(2)}, u32[]{:S(2)}) collective-permute-start(bf16[192,384]{1,0:T(8,128)(2,1)S(1)} %maximum_bitcast_fusion.7), channel_id=1, source_target_pairs={{0,8},{1,9},{2,10},{3,11},{4,12},{5,13},{6,14},{7,15},{8,0},{9,1},... | collective-permute-start | bytes 442376 | tf_op jit(solution)/shard_map/ppermute | solution.py:44
  39.1 22.5 %collective-permute-start.54 = (bf16[4,48,384]{2,1,0:T(8,128)(2,1)S(1)}, bf16[4,48,384]{2,1,0:T(8,128)(2,1)S(1)}, u32[]{:S(2)}, u32[]{:S(2)}) collective-permute-start(bf16[4,48,384]{2,1,0:T(8,128)(2,1)S(1)} %get-tuple-element.295), channel_id=1, source_target_pairs={{0,24},{1,25},{2,26},{3,27},{4,28},{5,29},{6,30},{7,31},{8,16},{9,... | collective-permute-start | bytes 442376 | tf_op jit(solution)/shard_map/ppermute | solution.py:44
  41.8 31.6 %collective-permute-start.14 = (bf16[4,48,384]{2,1,0:T(8,128)(2,1)S(1)}, bf16[4,48,384]{2,1,0:T(8,128)(2,1)S(1)}, u32[]{:S(2)}, u32[]{:S(2)}) collective-permute-start(bf16[4,48,384]{2,1,0:T(8,128)(2,1)S(1)} %get-tuple-element.305), channel_id=1, source_target_pairs={{0,16},{1,17},{2,18},{3,19},{4,20},{5,21},{6,22},{7,23},{8,24},{9,... | collective-permute-start | bytes 442376 | tf_op jit(solution)/shard_map/ppermute | solution.py:44
  42.6 30.9 %collective-permute-start.13 = (bf16[4,48,384]{2,1,0:T(8,128)(2,1)S(1)}, bf16[4,48,384]{2,1,0:T(8,128)(2,1)S(1)}, u32[]{:S(2)}, u32[]{:S(2)}) collective-permute-start(bf16[4,48,384]{2,1,0:T(8,128)(2,1)S(1)} %get-tuple-element.305), channel_id=1, source_target_pairs={{0,8},{1,9},{2,10},{3,11},{4,12},{5,13},{6,14},{7,15},{8,0},{9,1},... | collective-permute-start | bytes 442376 | tf_op jit(solution)/shard_map/ppermute | solution.py:44
  76.3 33.2 %collective-permute-start.85 = (bf16[4,192,384]{2,1,0:T(8,128)(2,1)S(1)}, bf16[4,192,384]{2,1,0:T(8,128)(2,1)S(1)}, u32[]{:S(2)}, u32[]{:S(2)}) collective-permute-start(bf16[4,192,384]{2,1,0:T(8,128)(2,1)S(1)} %pad_maximum_fusion.9.refs_20_), channel_id=1, source_target_pairs={{0,1},{1,0},{2,3},{3,2},{4,5},{5,4},{6,7},{7,6},{8,9},{9,8},{10,11... | collective-permute-start | bytes 1769480 | tf_op jit(solution)/shard_map/ppermute | solution.py:44
  76.3 34.1 %collective-permute-start.82 = (bf16[4,192,384]{2,1,0:T(8,128)(2,1)S(1)}, bf16[4,192,384]{2,1,0:T(8,128)(2,1)}, u32[]{:S(2)}, u32[]{:S(2)}) collective-permute-start(bf16[4,192,384]{2,1,0:T(8,128)(2,1)S(1)} %pad_maximum_fusion.9.refs_20_), channel_id=1, source_target_pairs={{0,2},{1,3},{2,0},{3,1},{4,6},{5,7},{6,4},{7,5},{8,10},{9,11},{10,... | collective-permute-start | bytes 1769480 | tf_op jit(solution)/shard_map/ppermute | solution.py:44
  109.5 22.7 %collective-permute-start.68 = (bf16[4,48,1536]{2,1,0:T(8,128)(2,1)S(1)}, bf16[4,48,1536]{2,1,0:T(8,128)(2,1)}, u32[]{:S(2)}, u32[]{:S(2)}) collective-permute-start(bf16[4,48,1536]{2,1,0:T(8,128)(2,1)S(1)} %pad_maximum_fusion.8.refs_10_), channel_id=1, source_target_pairs={{0,4},{1,5},{2,6},{3,7},{4,0},{5,1},{6,2},{7,3},{8,12},{9,13},{10,... | collective-permute-start | bytes 1769480 | tf_op jit(solution)/shard_map/ppermute | solution.py:44
  110.3 22.4 %collective-permute-start.46 = (bf16[4,192,384]{2,1,0:T(8,128)(2,1)S(1)}, bf16[4,192,384]{2,1,0:T(8,128)(2,1)S(1)}, u32[]{:S(2)}, u32[]{:S(2)}) collective-permute-start(bf16[4,192,384]{2,1,0:T(8,128)(2,1)S(1)} %pad_maximum_fusion.6.refs_20_), channel_id=1, source_target_pairs={{0,1},{1,0},{2,3},{3,2},{4,5},{5,4},{6,7},{7,6},{8,9},{9,8},{10,11... | collective-permute-start | bytes 1769480 | tf_op jit(solution)/shard_map/ppermute | solution.py:44
  121.0 23.9 %collective-permute-start.42 = (bf16[4,192,384]{2,1,0:T(8,128)(2,1)S(1)}, bf16[4,192,384]{2,1,0:T(8,128)(2,1)}, u32[]{:S(2)}, u32[]{:S(2)}) collective-permute-start(bf16[4,192,384]{2,1,0:T(8,128)(2,1)S(1)} %pad_maximum_fusion.6.refs_20_), channel_id=1, source_target_pairs={{0,4},{1,5},{2,6},{3,7},{4,0},{5,1},{6,2},{7,3},{8,12},{9,13},{10,... | collective-permute-start | bytes 1769480 | tf_op jit(solution)/shard_map/ppermute | solution.py:44
  125.3 20.1 %collective-permute-start.33 = (bf16[4,48,1536]{2,1,0:T(8,128)(2,1)}, bf16[4,48,1536]{2,1,0:T(8,128)(2,1)}, u32[]{:S(2)}, u32[]{:S(2)}) collective-permute-start(bf16[4,48,1536]{2,1,0:T(8,128)(2,1)} %pad_maximum_fusion.5.refs_10_), channel_id=1, source_target_pairs={{0,1},{1,0},{2,3},{3,2},{4,5},{5,4},{6,7},{7,6},{8,9},{9,8},{10,11... | collective-permute-start | bytes 1769480 | tf_op jit(solution)/shard_map/ppermute | solution.py:44
  132.8 24.7 %collective-permute-start.29 = (bf16[4,48,1536]{2,1,0:T(8,128)(2,1)}, bf16[4,48,1536]{2,1,0:T(8,128)(2,1)}, u32[]{:S(2)}, u32[]{:S(2)}) collective-permute-start(bf16[4,48,1536]{2,1,0:T(8,128)(2,1)} %pad_maximum_fusion.5.refs_10_), channel_id=1, source_target_pairs={{0,4},{1,5},{2,6},{3,7},{4,0},{5,1},{6,2},{7,3},{8,12},{9,13},{10,... | collective-permute-start | bytes 1769480 | tf_op jit(solution)/shard_map/ppermute | solution.py:44
  138.7 21.2 %collective-permute-start.20 = (bf16[4,4,48,384]{3,2,1,0:T(8,128)(2,1)S(1)}, bf16[4,4,48,384]{3,2,1,0:T(8,128)(2,1)}, u32[]{:S(2)}, u32[]{:S(2)}) collective-permute-start(bf16[4,4,48,384]{3,2,1,0:T(8,128)(2,1)S(1)} %pad_maximum_fusion.4.refs_0_), channel_id=1, source_target_pairs={{0,1},{1,0},{2,3},{3,2},{4,5},{5,4},{6,7},{7,6},{8,9},{9,8},{10,11... | collective-permute-start | bytes 1769480 | tf_op jit(solution)/shard_map/ppermute | solution.py:44
  144.9 26.7 %collective-permute-start.17 = (bf16[4,4,48,384]{3,2,1,0:T(8,128)(2,1)S(1)}, bf16[4,4,48,384]{3,2,1,0:T(8,128)(2,1)S(1)}, u32[]{:S(2)}, u32[]{:S(2)}) collective-permute-start(bf16[4,4,48,384]{3,2,1,0:T(8,128)(2,1)S(1)} %pad_maximum_fusion.4.refs_0_), channel_id=1, source_target_pairs={{0,2},{1,3},{2,0},{3,1},{4,6},{5,7},{6,4},{7,5},{8,10},{9,11},{10,... | collective-permute-start | bytes 1769480 | tf_op jit(solution)/shard_map/ppermute | solution.py:44
  145.4 27.5 %collective-permute-start.16 = (bf16[4,4,48,384]{3,2,1,0:T(8,128)(2,1)S(1)}, bf16[4,4,48,384]{3,2,1,0:T(8,128)(2,1)S(1)}, u32[]{:S(2)}, u32[]{:S(2)}) collective-permute-start(bf16[4,4,48,384]{3,2,1,0:T(8,128)(2,1)S(1)} %pad_maximum_fusion.4.refs_0_), channel_id=1, source_target_pairs={{0,4},{1,5},{2,6},{3,7},{4,0},{5,1},{6,2},{7,3},{8,12},{9,13},{10,... | collective-permute-start | bytes 1769480 | tf_op jit(solution)/shard_map/ppermute | solution.py:44
  150.6 23.8 %collective-permute-start.59 = (bf16[4,4,48,384]{3,2,1,0:T(8,128)(2,1)S(1)}, bf16[4,4,48,384]{3,2,1,0:T(8,128)(2,1)}, u32[]{:S(2)}, u32[]{:S(2)}) collective-permute-start(bf16[4,4,48,384]{3,2,1,0:T(8,128)(2,1)S(1)} %pad_maximum_fusion.7.refs_0_), channel_id=1, source_target_pairs={{0,1},{1,0},{2,3},{3,2},{4,5},{5,4},{6,7},{7,6},{8,9},{9,8},{10,11... | collective-permute-start | bytes 1769480 | tf_op jit(solution)/shard_map/ppermute | solution.py:44
  159.9 22.8 %collective-permute-start.55 = (bf16[4,4,48,384]{3,2,1,0:T(8,128)(2,1)S(1)}, bf16[4,4,48,384]{3,2,1,0:T(8,128)(2,1)S(1)}, u32[]{:S(2)}, u32[]{:S(2)}) collective-permute-start(bf16[4,4,48,384]{3,2,1,0:T(8,128)(2,1)S(1)} %pad_maximum_fusion.7.refs_0_), channel_id=1, source_target_pairs={{0,4},{1,5},{2,6},{3,7},{4,0},{5,1},{6,2},{7,3},{8,12},{9,13},{10,... | collective-permute-start | bytes 1769480 | tf_op jit(solution)/shard_map/ppermute | solution.py:44
  174.4 21.1 %collective-permute-start.71 = (bf16[2,48,1536]{2,1,0:T(8,128)(2,1)}, bf16[2,48,1536]{2,1,0:T(8,128)(2,1)}, u32[]{:S(2)}, u32[]{:S(2)}) collective-permute-start(bf16[2,48,1536]{2,1,0:T(8,128)(2,1)} %slice.1167), channel_id=1, source_target_pairs={{0,4},{1,5},{2,6},{3,7},{4,0},{5,1},{6,2},{7,3},{8,12},{9,13},{10,... | collective-permute-start | bytes 884744 | tf_op jit(solution)/shard_map/ppermute | solution.py:44
  175.8 20.2 %collective-permute-start.70 = (bf16[2,48,1536]{2,1,0:T(8,128)(2,1)}, bf16[2,48,1536]{2,1,0:T(8,128)(2,1)}, u32[]{:S(2)}, u32[]{:S(2)}) collective-permute-start(bf16[2,48,1536]{2,1,0:T(8,128)(2,1)} %slice.1166), channel_id=1, source_target_pairs={{0,2},{1,3},{2,0},{3,1},{4,6},{5,7},{6,4},{7,5},{8,10},{9,11},{10,... | collective-permute-start | bytes 884744 | tf_op jit(solution)/shard_map/ppermute | solution.py:44
  219.8 21.6 %collective-permute-start.22 = (bf16[4,4,48,384]{3,2,1,0:T(8,128)(2,1)S(1)}, bf16[4,4,48,384]{3,2,1,0:T(8,128)(2,1)S(1)}, u32[]{:S(2)}, u32[]{:S(2)}) collective-permute-start(bf16[4,4,48,384]{3,2,1,0:T(8,128)(2,1)S(1)} %collective-permute-done.17.refs_2_), channel_id=1, source_target_pairs={{0,1},{1,0},{2,3},{3,2},{4,5},{5,4},{6,7},{7,6},{8,9},{9,8},{10,11... | collective-permute-start | bytes 1769480 | tf_op jit(solution)/shard_map/ppermute | solution.py:44
  220.2 21.8 %collective-permute-start.21 = (bf16[4,4,48,384]{3,2,1,0:T(8,128)(2,1)S(1)}, bf16[4,4,48,384]{3,2,1,0:T(8,128)(2,1)S(1)}, u32[]{:S(2)}, u32[]{:S(2)}) collective-permute-start(bf16[4,4,48,384]{3,2,1,0:T(8,128)(2,1)S(1)} %collective-permute-done.16.refs_1_), channel_id=1, source_target_pairs={{0,1},{1,0},{2,3},{3,2},{4,5},{5,4},{6,7},{7,6},{8,9},{9,8},{10,11... | collective-permute-start | bytes 1769480 | tf_op jit(solution)/shard_map/ppermute | solution.py:44
  240.9 32.8 %collective-permute-start.35 = (bf16[4,48,1536]{2,1,0:T(8,128)(2,1)}, bf16[4,48,1536]{2,1,0:T(8,128)(2,1)}, u32[]{:S(2)}, u32[]{:S(2)}) collective-permute-start(bf16[4,48,1536]{2,1,0:T(8,128)(2,1)} %collective-permute-done.30.refs_12_), channel_id=1, source_target_pairs={{0,1},{1,0},{2,3},{3,2},{4,5},{5,4},{6,7},{7,6},{8,9},{9,8},{10,11... | collective-permute-start | bytes 1769480 | tf_op jit(solution)/shard_map/ppermute | solution.py:44
  241.0 35.3 %collective-permute-start.34 = (bf16[4,48,1536]{2,1,0:T(8,128)(2,1)}, bf16[4,48,1536]{2,1,0:T(8,128)(2,1)}, u32[]{:S(2)}, u32[]{:S(2)}) collective-permute-start(bf16[4,48,1536]{2,1,0:T(8,128)(2,1)} %collective-permute-done.29.refs_11_), channel_id=1, source_target_pairs={{0,1},{1,0},{2,3},{3,2},{4,5},{5,4},{6,7},{7,6},{8,9},{9,8},{10,11... | collective-permute-start | bytes 1769480 | tf_op jit(solution)/shard_map/ppermute | solution.py:44
  241.4 35.5 %collective-permute-start.61 = (bf16[4,4,48,384]{3,2,1,0:T(8,128)(2,1)S(1)}, bf16[4,4,48,384]{3,2,1,0:T(8,128)(2,1)S(1)}, u32[]{:S(2)}, u32[]{:S(2)}) collective-permute-start(bf16[4,4,48,384]{3,2,1,0:T(8,128)(2,1)S(1)} %collective-permute-done.56.refs_2_), channel_id=1, source_target_pairs={{0,1},{1,0},{2,3},{3,2},{4,5},{5,4},{6,7},{7,6},{8,9},{9,8},{10,11... | collective-permute-start | bytes 1769480 | tf_op jit(solution)/shard_map/ppermute | solution.py:44
  241.6 34.6 %collective-permute-start.36 = (bf16[2,48,1536]{2,1,0:T(8,128)(2,1)}, bf16[2,48,1536]{2,1,0:T(8,128)(2,1)}, u32[]{:S(2)}, u32[]{:S(2)}) collective-permute-start(bf16[2,48,1536]{2,1,0:T(8,128)(2,1)} %copy-done.52), channel_id=1, source_target_pairs={{0,1},{1,0},{2,3},{3,2},{4,5},{5,4},{6,7},{7,6},{8,9},{9,8},{10,11... | collective-permute-start | bytes 884744 | tf_op jit(solution)/shard_map/ppermute | solution.py:44
  242.0 34.7 %collective-permute-start.63 = (bf16[2,4,48,384]{3,2,1,0:T(8,128)(2,1)}, bf16[2,4,48,384]{3,2,1,0:T(8,128)(2,1)S(1)}, u32[]{:S(2)}, u32[]{:S(2)}) collective-permute-start(bf16[2,4,48,384]{3,2,1,0:T(8,128)(2,1)} %collective-permute-done.58.refs_4_), channel_id=1, source_target_pairs={{0,1},{1,0},{2,3},{3,2},{4,5},{5,4},{6,7},{7,6},{8,9},{9,8},{10,11... | collective-permute-start | bytes 884744 | tf_op jit(solution)/shard_map/ppermute | solution.py:44
  273.7 51.9 %collective-permute-start.86 = (bf16[4,192,384]{2,1,0:T(8,128)(2,1)}, bf16[4,192,384]{2,1,0:T(8,128)(2,1)S(1)}, u32[]{:S(2)}, u32[]{:S(2)}) collective-permute-start(bf16[4,192,384]{2,1,0:T(8,128)(2,1)} %collective-permute-done.81.refs_21_), channel_id=1, source_target_pairs={{0,1},{1,0},{2,3},{3,2},{4,5},{5,4},{6,7},{7,6},{8,9},{9,8},{10,11... | collective-permute-start | bytes 1769480 | tf_op jit(solution)/shard_map/ppermute | solution.py:44
  276.2 49.4 %collective-permute-start.74 = (bf16[4,48,1536]{2,1,0:T(8,128)(2,1)}, bf16[4,48,1536]{2,1,0:T(8,128)(2,1)S(1)}, u32[]{:S(2)}, u32[]{:S(2)}) collective-permute-start(bf16[4,48,1536]{2,1,0:T(8,128)(2,1)} %collective-permute-done.69.refs_12_), channel_id=1, source_target_pairs={{0,1},{1,0},{2,3},{3,2},{4,5},{5,4},{6,7},{7,6},{8,9},{9,8},{10,11... | collective-permute-start | bytes 1769480 | tf_op jit(solution)/shard_map/ppermute | solution.py:44
  276.3 49.4 %collective-permute-start.73 = (bf16[4,48,1536]{2,1,0:T(8,128)(2,1)}, bf16[4,48,1536]{2,1,0:T(8,128)(2,1)}, u32[]{:S(2)}, u32[]{:S(2)}) collective-permute-start(bf16[4,48,1536]{2,1,0:T(8,128)(2,1)} %collective-permute-done.68.refs_11_), channel_id=1, source_target_pairs={{0,1},{1,0},{2,3},{3,2},{4,5},{5,4},{6,7},{7,6},{8,9},{9,8},{10,11... | collective-permute-start | bytes 1769480 | tf_op jit(solution)/shard_map/ppermute | solution.py:44
  276.7 23.3 %collective-permute-start.60 = (bf16[4,4,48,384]{3,2,1,0:T(8,128)(2,1)S(1)}, bf16[4,4,48,384]{3,2,1,0:T(8,128)(2,1)S(1)}, u32[]{:S(2)}, u32[]{:S(2)}) collective-permute-start(bf16[4,4,48,384]{3,2,1,0:T(8,128)(2,1)S(1)} %collective-permute-done.55.refs_1_), channel_id=1, source_target_pairs={{0,1},{1,0},{2,3},{3,2},{4,5},{5,4},{6,7},{7,6},{8,9},{9,8},{10,11... | collective-permute-start | bytes 1769480 | tf_op jit(solution)/shard_map/ppermute | solution.py:44
  276.9 23.0 %collective-permute-start.62 = (bf16[2,4,48,384]{3,2,1,0:T(8,128)(2,1)}, bf16[2,4,48,384]{3,2,1,0:T(8,128)(2,1)S(1)}, u32[]{:S(2)}, u32[]{:S(2)}) collective-permute-start(bf16[2,4,48,384]{3,2,1,0:T(8,128)(2,1)} %collective-permute-done.57.refs_3_), channel_id=1, source_target_pairs={{0,1},{1,0},{2,3},{3,2},{4,5},{5,4},{6,7},{7,6},{8,9},{9,8},{10,11... | collective-permute-start | bytes 884744 | tf_op jit(solution)/shard_map/ppermute | solution.py:44
  299.9 25.7 %collective-permute-start.76 = (bf16[2,48,1536]{2,1,0:T(8,128)(2,1)}, bf16[2,48,1536]{2,1,0:T(8,128)(2,1)S(1)}, u32[]{:S(2)}, u32[]{:S(2)}) collective-permute-start(bf16[2,48,1536]{2,1,0:T(8,128)(2,1)} %collective-permute-done.71.refs_14_), channel_id=1, source_target_pairs={{0,1},{1,0},{2,3},{3,2},{4,5},{5,4},{6,7},{7,6},{8,9},{9,8},{10,11... | collective-permute-start | bytes 884744 | tf_op jit(solution)/shard_map/ppermute | solution.py:44
  300.1 25.6 %collective-permute-start.75 = (bf16[2,48,1536]{2,1,0:T(8,128)(2,1)}, bf16[2,48,1536]{2,1,0:T(8,128)(2,1)S(1)}, u32[]{:S(2)}, u32[]{:S(2)}) collective-permute-start(bf16[2,48,1536]{2,1,0:T(8,128)(2,1)} %collective-permute-done.70.refs_13_), channel_id=1, source_target_pairs={{0,1},{1,0},{2,3},{3,2},{4,5},{5,4},{6,7},{7,6},{8,9},{9,8},{10,11... | collective-permute-start | bytes 884744 | tf_op jit(solution)/shard_map/ppermute | solution.py:44
  498.2 84.1 %collective-permute-start.118 = (bf16[16,160,384]{2,1,0:T(8,128)(2,1)}, bf16[16,160,384]{2,1,0:T(8,128)(2,1)}, u32[]{:S(2)}, u32[]{:S(2)}) collective-permute-start(bf16[16,160,384]{2,1,0:T(8,128)(2,1)} %get-tuple-element.132), channel_id=1, source_target_pairs={{0,1},{1,0},{2,3},{3,2},{4,5},{5,4},{6,7},{7,6},{8,9},{9,8},{10,11... | collective-permute-start | bytes 5898248 | tf_op jit(solution)/shard_map/ppermute | solution.py:44
  515.7 63.1 %collective-permute-start.90 = (bf16[16,160,384]{2,1,0:T(8,128)(2,1)}, bf16[16,160,384]{2,1,0:T(8,128)(2,1)}, u32[]{:S(2)}, u32[]{:S(2)}) collective-permute-start(bf16[16,160,384]{2,1,0:T(8,128)(2,1)} %get-tuple-element.116), channel_id=1, source_target_pairs={{0,1},{1,0},{2,3},{3,2},{4,5},{5,4},{6,7},{7,6},{8,9},{9,8},{10,11... | collective-permute-start | bytes 5898248 | tf_op jit(solution)/shard_map/ppermute | solution.py:44
  527.0 105.0 %collective-permute-start.108 = (bf16[16,48,1536]{2,1,0:T(8,128)(2,1)}, bf16[16,48,1536]{2,1,0:T(8,128)(2,1)}, u32[]{:S(2)}, u32[]{:S(2)}) collective-permute-start(bf16[16,48,1536]{2,1,0:T(8,128)(2,1)} %get-tuple-element.125), channel_id=1, source_target_pairs={{0,1},{1,0},{2,3},{3,2},{4,5},{5,4},{6,7},{7,6},{8,9},{9,8},{10,11... | collective-permute-start | bytes 7077896 | tf_op jit(solution)/shard_map/ppermute | solution.py:44
  537.7 90.6 %collective-permute-start.136 = (bf16[16,48,1536]{2,1,0:T(8,128)(2,1)}, bf16[16,48,1536]{2,1,0:T(8,128)(2,1)}, u32[]{:S(2)}, u32[]{:S(2)}) collective-permute-start(bf16[16,48,1536]{2,1,0:T(8,128)(2,1)} %get-tuple-element.141), channel_id=1, source_target_pairs={{0,1},{1,0},{2,3},{3,2},{4,5},{5,4},{6,7},{7,6},{8,9},{9,8},{10,11... | collective-permute-start | bytes 7077896 | tf_op jit(solution)/shard_map/ppermute | solution.py:44
  550.9 159.7 %collective-permute-start.99 = (bf16[16,240,384]{2,1,0:T(8,128)(2,1)}, bf16[16,240,384]{2,1,0:T(8,128)(2,1)S(1)}, u32[]{:S(2)}, u32[]{:S(2)}) collective-permute-start(bf16[16,240,384]{2,1,0:T(8,128)(2,1)} %get-tuple-element.121), channel_id=1, source_target_pairs={{0,1},{1,0},{2,3},{3,2},{4,5},{5,4},{6,7},{7,6},{8,9},{9,8},{10,11... | collective-permute-start | bytes 8847368 | tf_op jit(solution)/shard_map/ppermute | solution.py:44
  578.8 127.3 %collective-permute-start.127 = (bf16[16,240,384]{2,1,0:T(8,128)(2,1)}, bf16[16,240,384]{2,1,0:T(8,128)(2,1)}, u32[]{:S(2)}, u32[]{:S(2)}) collective-permute-start(bf16[16,240,384]{2,1,0:T(8,128)(2,1)} %get-tuple-element.137), channel_id=1, source_target_pairs={{0,1},{1,0},{2,3},{3,2},{4,5},{5,4},{6,7},{7,6},{8,9},{9,8},{10,11... | collective-permute-start | bytes 8847368 | tf_op jit(solution)/shard_map/ppermute | solution.py:44
  590.3 23.8 %collective-permute-start.93 = (bf16[2,160,384]{2,1,0:T(8,128)(2,1)S(1)}, bf16[2,160,384]{2,1,0:T(8,128)(2,1)S(1)}, u32[]{:S(2)}, u32[]{:S(2)}) collective-permute-start(bf16[2,160,384]{2,1,0:T(8,128)(2,1)S(1)} %get-tuple-element.269), channel_id=1, source_target_pairs={{0,4},{1,5},{2,6},{3,7},{4,0},{5,1},{6,2},{7,3},{8,12},{9,13},{10,... | collective-permute-start | bytes 737288 | tf_op jit(solution)/shard_map/ppermute | solution.py:44
  627.1 40.8 %collective-permute-start.94 = (bf16[4,160,384]{2,1,0:T(8,128)(2,1)S(1)}, bf16[4,160,384]{2,1,0:T(8,128)(2,1)S(1)}, u32[]{:S(2)}, u32[]{:S(2)}) collective-permute-start(bf16[4,160,384]{2,1,0:T(8,128)(2,1)S(1)} %pad_maximum_fusion.15), channel_id=1, source_target_pairs={{0,2},{1,3},{2,0},{3,1},{4,6},{5,7},{6,4},{7,5},{8,10},{9,11},{10,... | collective-permute-start | bytes 1474568 | tf_op jit(solution)/shard_map/ppermute | solution.py:44
  628.3 41.3 %collective-permute-start.92 = (bf16[4,160,384]{2,1,0:T(8,128)(2,1)S(1)}, bf16[4,160,384]{2,1,0:T(8,128)(2,1)S(1)}, u32[]{:S(2)}, u32[]{:S(2)}) collective-permute-start(bf16[4,160,384]{2,1,0:T(8,128)(2,1)S(1)} %pad_maximum_fusion.14), channel_id=1, source_target_pairs={{0,4},{1,5},{2,6},{3,7},{4,0},{5,1},{6,2},{7,3},{8,12},{9,13},{10,... | collective-permute-start | bytes 1474568 | tf_op jit(solution)/shard_map/ppermute | solution.py:44
  686.6 26.3 %collective-permute-start.140 = (bf16[4,48,1536]{2,1,0:T(8,128)(2,1)}, bf16[4,48,1536]{2,1,0:T(8,128)(2,1)}, u32[]{:S(2)}, u32[]{:S(2)}) collective-permute-start(bf16[4,48,1536]{2,1,0:T(8,128)(2,1)} %pad_maximum_fusion.13), channel_id=1, source_target_pairs={{0,2},{1,3},{2,0},{3,1},{4,6},{5,7},{6,4},{7,5},{8,10},{9,11},{10,... | collective-permute-start | bytes 1769480 | tf_op jit(solution)/shard_map/ppermute | solution.py:44
  687.8 25.5 %collective-permute-start.138 = (bf16[4,48,1536]{2,1,0:T(8,128)(2,1)}, bf16[4,48,1536]{2,1,0:T(8,128)(2,1)}, u32[]{:S(2)}, u32[]{:S(2)}) collective-permute-start(bf16[4,48,1536]{2,1,0:T(8,128)(2,1)} %pad_maximum_fusion.12), channel_id=1, source_target_pairs={{0,4},{1,5},{2,6},{3,7},{4,0},{5,1},{6,2},{7,3},{8,12},{9,13},{10,... | collective-permute-start | bytes 1769480 | tf_op jit(solution)/shard_map/ppermute | solution.py:44
  713.3 21.9 %collective-permute-start.100 = (bf16[2,240,384]{2,1,0:T(8,128)(2,1)S(1)}, bf16[2,240,384]{2,1,0:T(8,128)(2,1)S(1)}, u32[]{:S(2)}, u32[]{:S(2)}) collective-permute-start(bf16[2,240,384]{2,1,0:T(8,128)(2,1)S(1)} %get-tuple-element.248), channel_id=1, source_target_pairs={{0,2},{1,3},{2,0},{3,1},{4,6},{5,7},{6,4},{7,5},{8,10},{9,11},{10,... | collective-permute-start | bytes 1105928 | tf_op jit(solution)/shard_map/ppermute | solution.py:44
  749.9 24.7 %collective-permute-start.103 = (bf16[4,240,384]{2,1,0:T(8,128)(2,1)S(1)}, bf16[4,240,384]{2,1,0:T(8,128)(2,1)S(1)}, u32[]{:S(2)}, u32[]{:S(2)}) collective-permute-start(bf16[4,240,384]{2,1,0:T(8,128)(2,1)S(1)} %pad_maximum_fusion.1), channel_id=1, source_target_pairs={{0,2},{1,3},{2,0},{3,1},{4,6},{5,7},{6,4},{7,5},{8,10},{9,11},{10,... | collective-permute-start | bytes 2211848 | tf_op jit(solution)/shard_map/ppermute | solution.py:44
  752.2 28.8 %collective-permute-start.101 = (bf16[4,240,384]{2,1,0:T(8,128)(2,1)S(1)}, bf16[4,240,384]{2,1,0:T(8,128)(2,1)S(1)}, u32[]{:S(2)}, u32[]{:S(2)}) collective-permute-start(bf16[4,240,384]{2,1,0:T(8,128)(2,1)S(1)} %pad_maximum_fusion), channel_id=1, source_target_pairs={{0,4},{1,5},{2,6},{3,7},{4,0},{5,1},{6,2},{7,3},{8,12},{9,13},{10,... | collective-permute-start | bytes 2211848 | tf_op jit(solution)/shard_map/ppermute | solution.py:44
  771.6 21.9 %collective-permute-start.133 = (bf16[240,384]{1,0:T(8,128)(2,1)S(1)}, bf16[240,384]{1,0:T(8,128)(2,1)S(1)}, u32[]{:S(2)}, u32[]{:S(2)}) collective-permute-start(bf16[240,384]{1,0:T(8,128)(2,1)S(1)} %get-tuple-element.242), channel_id=1, source_target_pairs={{0,16},{1,17},{2,18},{3,19},{4,20},{5,21},{6,22},{7,23},{8,24},{9,... | collective-permute-start | bytes 552968 | tf_op jit(solution)/shard_map/ppermute | solution.py:44
  (153 other events, 2081.6 us)

commit v2 on v1

v2 whole, which is shorter than its diff:
```python
from functools import partial

import jax
import jax.numpy as jnp
from jax import lax
from jax.experimental import pallas as pl
from jax.experimental.pallas import tpu as pltpu
from jax.sharding import PartitionSpec as P

H = 12
HD = 64
NB = 32
D = 768
FF = 3072
HALF = 384
EPS = 1e-06
AX = ("wide", "narrow")
CORE, XBIT, YBIT, Z0, Z1 = 1, 2, 4, 8, 16
UNITS = 16
F32 = jnp.float32
BF16 = jnp.bfloat16
GELU_A = 0.7978845608028654
GELU_B = 0.044715
NN = (((1,), (0,)), ((), ()))
NT = (((1,), (1,)), ((), ()))
TN = (((0,), (0,)), ((), ()))
GROUPS = (6, 3, 2, 2)
TILE_A = 256
TILE_B = 256
VMEM_LIMIT = 60 * 1024 * 1024
ANY = pl.BlockSpec(memory_space=pl.ANY)


def mm(left, right, dims=NN):
    return lax.dot_general(left, right, dims, preferred_element_type=F32)


def wide(value):
    return value.astype(F32)


def low(value):
    return value.astype(BF16)


SENT = []


def swap(value, mask):
    SENT.append(value)
    return lax.ppermute(value, AX, [(i, i ^ mask) for i in range(32)])


def pick(core, first, second):
    return jnp.where(core == 0, first, second)


class Job:
    def __init__(self, stages, *operands):
        self.stages = stages(*operands)
        self.operands = next(self.stages)
        self.result = None

    def step(self, operands):
        try:
            self.operands = self.stages.send(operands)
        except StopIteration as stop:
            self.result = stop.value
            self.operands = ()


class Ticks:
    def __init__(self, me):
        self.me = me
        self.last = ()
        self.flying = []

    def run(self, jobs, kernel=None):
        jobs = [job for job in jobs if job.result is None]
        tied = jobs + [job for job in self.flying if job not in jobs]
        operands = [job.operands if job.result is None else job.result for job in tied]
        self.me, operands, self.last = lax.optimization_barrier((self.me, operands, self.last))
        SENT.clear()
        for job, value in zip(tied, operands):
            if job in jobs:
                job.step(value)
            elif job.result is None:
                job.operands = value
            else:
                job.result = value
        self.flying = jobs
        if kernel is None:
            return None
        self.me = lax.optimization_barrier((self.me, list(SENT)))[0]
        out = kernel(self.me)
        self.last = jax.tree.leaves(out)[-1]
        return out


def gather_stages(pair, direct, keep, send):
    keep, send = yield keep, send
    core = lax.axis_index(AX) % 2
    recv = swap(send, CORE)
    slab = pair(pick(core, keep, recv), pick(core, recv, keep))
    slab = yield slab
    if direct:
        own = jnp.stack([slab, swap(slab, Z0), swap(slab, Z1), swap(slab, Z0 | Z1)])
    else:
        two = jnp.stack([slab, swap(slab, Z0)])
        two = yield two
        own = jnp.concatenate([two, swap(two, Z1)])
    own = yield own
    across_y = swap(own, YBIT)
    across_x = swap(own, XBIT)
    far = (swap(own, CORE),)
    own, across_y, across_x, far = yield own, across_y, across_x, far
    diag = (swap(across_y[:2], XBIT), swap(across_x[2:], YBIT))
    far = far + (swap(across_x, CORE), swap(across_y, CORE))
    mine, far = yield (own, across_x, across_y) + diag, far
    return mine + far + tuple(swap(piece, CORE) for piece in mine[3:])


def vector_stages(slab):
    slab = yield slab
    own = jnp.stack([slab, swap(slab, Z0), swap(slab, Z1), swap(slab, Z0 | Z1)])
    own = yield own
    across = [own, swap(own, XBIT), swap(own, YBIT), swap(own, XBIT | YBIT)]
    across = yield across
    near = jnp.concatenate(across)
    return near, swap(near, CORE)


def pair_entry(first, second):
    return jnp.concatenate([first.reshape(4, 24, HALF), second.reshape(4, 24, HALF)], axis=1)


def pair_wide(first, second):
    widen = jnp.concatenate([first[:96].reshape(4, 24, HALF), second[:96].reshape(4, 24, HALF)], axis=1)
    widen = widen.reshape(2, 2, 48, HALF).transpose(0, 2, 1, 3).reshape(2, 48, D)
    narrow = jnp.concatenate([first[96:].reshape(2, 48, HALF), second[96:].reshape(2, 48, HALF)], axis=2)
    return jnp.concatenate([widen, narrow], axis=0)


def gather_jobs(core, direct, entry, leave, widen, narrow):
    def halved(value):
        return pick(core, value[0], value[1]), pick(core, value[1], value[0])

    eo = jnp.concatenate([entry, leave[None]]).reshape(96, 2, HALF).transpose(1, 0, 2)
    widen = widen.reshape(24, 2, 4, HALF).transpose(1, 2, 0, 3).reshape(2, 96, HALF)
    narrow = narrow.reshape(96, 2, HALF).transpose(1, 0, 2)
    both = jnp.concatenate([widen, narrow], axis=1)
    return (
        Job(gather_stages, pair_entry, direct, *halved(eo)),
        Job(gather_stages, pair_wide, False, *halved(both)),
    )


def reduce_stages(core, cuts, send, keep):
    shape = (4, 4) + keep.shape[1:]
    send, keep = yield send, keep
    keep = keep.reshape(shape)
    recv = swap(send, CORE).reshape(shape)
    keep, recv = yield keep, recv
    diag_low = swap(low(wide(keep[3, :2]) + wide(recv[3, :2])), XBIT)
    diag_high = swap(low(wide(keep[3, 2:]) + wide(recv[3, 2:])), YBIT)
    keep, recv, diag_low, diag_high = yield keep, recv, diag_low, diag_high
    to_y = wide(keep[2]) + wide(recv[2])
    to_x = wide(keep[1]) + wide(recv[1])
    rest = [(0, 0)] * 2
    to_y = low(to_y + jnp.pad(wide(diag_low), [(0, 2)] + rest))
    to_x = low(to_x + jnp.pad(wide(diag_high), [(2, 0)] + rest))
    from_y, from_x = swap(to_y, YBIT), swap(to_x, XBIT)
    keep, recv, from_y, from_x = yield keep, recv, from_y, from_x

    def part(k):
        return (wide(keep[0, k]) + wide(recv[0, k])) + (wide(from_y[k]) + wide(from_x[k]))

    far = swap(jnp.stack([low(part(2)), low(part(3))]), Z1)
    keep, recv, from_y, from_x, far = yield keep, recv, from_y, from_x, far
    near = swap(low(part(1) + wide(far[1])), Z0)
    keep, recv, from_y, from_x, far, near = yield keep, recv, from_y, from_x, far, near
    total = part(0) + wide(far[0]) + wide(near)
    keeps, sends = [], []
    start = 0
    for rows, group in cuts:
        slab = total[start : start + rows].reshape(-1, 2, group, HALF)
        start += rows
        keeps.append(pick(core, slab[:, 0], slab[:, 1]).reshape(-1, HALF))
        sends.append(pick(core, slab[:, 1], slab[:, 0]).reshape(-1, HALF))
    rest = total[start:]
    keep, send = jnp.concatenate(keeps), jnp.concatenate(sends)
    recv = swap(send, CORE)
    return pick(core, keep, recv), pick(core, recv, keep), rest


def vector_units(vectors, wide_bias, table, parts):
    flat = jnp.concatenate(
        [
            vectors.reshape(8, parts, -1).transpose(1, 0, 2).reshape(parts, -1),
            wide_bias.reshape(parts, -1),
            table.reshape(parts, -1),
        ],
        axis=1,
    )
    return flat


def split_vectors(flat, parts):
    cut = 8 * D // parts
    mid = cut + FF // parts
    return flat[:cut].reshape(8, -1), flat[cut:mid], flat[mid : mid + H * NB // parts]


def position(chip, unit):
    rel = jnp.bitwise_xor(chip, unit)
    return jnp.bitwise_and(rel, 3) * 4 + lax.shift_right_logical(rel, 2)


def start_load(me, refs, dst, sem, place):
    if len(refs) == 1:
        pltpu.make_async_copy(refs[0], dst, sem).start()
        return
    chip = lax.shift_right_logical(me, 1)
    for side in range(2):
        half = jnp.bitwise_xor(jnp.bitwise_and(me, 1), side)
        own, across_x, across_y, diag_low, diag_high = refs[5 * side : 5 * side + 5]
        for k in range(4):
            for step, ref, at in (
                (0, own, k),
                (1, across_x, k),
                (2, across_y, k),
                (3, diag_low if k < 2 else diag_high, k % 2),
            ):
                unit = jnp.bitwise_xor(chip, 4 * k + step)
                for source, target in place(ref.at[at], dst, unit, half):
                    pltpu.make_async_copy(source, target, sem).start()


def wait_load(dst, sem):
    pltpu.make_async_copy(dst, dst, sem).wait()


def place_entry(src, dst, unit, half):
    rows, cols = pl.multiple_of(unit * 48, 16), pl.multiple_of(half * HALF, 128)
    return [(src.at[0:3], dst.at[:, pl.ds(rows, 48), pl.ds(cols, HALF)])]


def place_leave(src, dst, unit, half):
    rows, cols = pl.multiple_of(unit * 48, 16), pl.multiple_of(half * HALF, 128)
    return [(src.at[3], dst.at[pl.ds(rows, 48), pl.ds(cols, HALF)])]


def place_widen(src, dst, unit, half):
    rows = pl.multiple_of(unit * 48, 16)
    return [(src.at[0:2], dst.at[pl.ds(half * 2, 2), pl.ds(rows, 48), :])]


def place_narrow(src, dst, unit, half):
    cols = pl.multiple_of(half * HALF, 128)
    return [
        (
            src.at[2:4, :, HALF * g : HALF * g + HALF],
            dst.at[pl.ds(unit * 4 + 2 * g, 2), :, pl.ds(cols, HALF)],
        )
        for g in range(2)
    ]


def build_bias(table, bias, stride):
    keys = bias.shape[1]
    for part in range(bias.shape[2] // 128):
        row = lax.broadcasted_iota(jnp.int32, (keys, 128), 0)
        col = lax.broadcasted_iota(jnp.int32, (keys, 128), 1) + 128 * part
        bucket = jnp.clip(row - stride * col, -(NB // 2), NB // 2 - 1) + NB // 2
        for h in range(H):
            values = jnp.broadcast_to(table[h : h + 1, :], (keys, 128))
            bias[h, :, 128 * part : 128 * part + 128] = low(
                jnp.take_along_axis(values, bucket, axis=1, mode="promise_in_bounds")
            )


def prepare_kernel(me_ref, near_ref, far_ref, *refs):
    outs, tables = refs[:6], refs[6:]
    core = jnp.bitwise_and(me_ref[0], 1)
    chip = lax.shift_right_logical(me_ref[0], 1)
    for table in tables:
        table[...] = jnp.zeros_like(table)
    for d in range(32):
        at = position(chip, d // 2)
        slab = jnp.where(core == d % 2, wide(near_ref[at]), wide(far_ref[at]))
        for layer in range(2):
            vec_ref, wide_ref = outs[3 * layer], outs[3 * layer + 1]
            rows = slab[8 * layer : 8 * layer + 8]
            vec_ref[:, 24 * d : 24 * d + 24] = rows[:, :24]
            wide_ref[:, 96 * d : 96 * d + 96] = rows[0:1, 32:128]
            h, start = 12 * d // NB, 12 * d % NB
            count = min(12, NB - start)
            tables[layer][h : h + 1, start : start + count] = rows[1:2, 32 : 32 + count]
            if count < 12:
                tables[layer][h + 1 : h + 2, 0 : 12 - count] = rows[1:2, 32 + count : 44]
    build_bias(tables[0], outs[2], 2)
    build_bias(tables[1], outs[5], 1)


def prepare(index, near, far, keys, queries):
    sds = jax.ShapeDtypeStruct
    shapes = []
    for length in (keys, queries):
        shapes += [sds((8, D), F32), sds((1, FF), F32), sds((H, length, queries), BF16)]
    return pl.pallas_call(
        prepare_kernel,
        grid_spec=pltpu.PrefetchScalarGridSpec(
            num_scalar_prefetch=1,
            grid=(1,),
            in_specs=[whole(UNITS, 16, 128)] * 2,
            out_specs=[whole(*shape.shape) for shape in shapes],
            scratch_shapes=[pltpu.VMEM((16, 128), F32)] * 2,
        ),
        out_shape=shapes,
        compiler_params=pltpu.CompilerParams(vmem_limit_bytes=VMEM_LIMIT),
        cost_estimate=pl.CostEstimate(flops=10_000_000, bytes_accessed=10_000_000, transcendentals=0),
        name="prepare",
    )(index, near, far)


def vector_slab(vectors_one, wide_one, table_one, vectors_two, wide_two, table_two):
    lead = wide_one.shape[:-1]
    left = jnp.concatenate([vectors_one, vectors_two], axis=-2)
    left = jnp.pad(left, [(0, 0)] * (left.ndim - 1) + [(0, 8)])
    rows = []
    for wide_bias, table in ((wide_one, table_one), (wide_two, table_two)):
        table = jnp.pad(table, [(0, 0)] * len(lead) + [(0, 84)])
        pair = jnp.stack([wide_bias, table], axis=-2)
        rows.append(jnp.pad(pair, [(0, 0)] * len(lead) + [(0, 6), (0, 0)]))
    return jnp.concatenate([left, jnp.concatenate(rows, axis=-2)], axis=-1)


def whole(*shape):
    return pl.BlockSpec(shape, lambda r, *_: (0,) * len(shape))


def lane_masks(value):
    lane = lax.broadcasted_iota(jnp.int32, value.shape, 1)
    zero = jnp.zeros_like(value)
    return jnp.where(lane < HD, value, zero), jnp.where(lane < HD, zero, value)


def masked_scores(keys, query, bias, count):
    scores = mm(keys, query, NT) + wide(bias)
    size = scores.shape[0]
    head, tail = scores[: size - 128], scores[size - 128 :]
    row = lax.broadcasted_iota(jnp.int32, tail.shape, 0) + (size - 128)
    tail = jnp.where(row < count, tail, -1e30)
    return tail if size == 128 else jnp.concatenate([head, tail], axis=0)


def statistics(value):
    mean = jnp.mean(value, axis=-1, keepdims=True)
    centred = value - mean
    spread = jnp.mean(centred * centred, axis=-1, keepdims=True)
    rstd = lax.rsqrt(spread + EPS)
    return centred * rstd, rstd


def norm_pull(grad, unit, rstd):
    return rstd * (
        grad
        - jnp.mean(grad, axis=-1, keepdims=True)
        - unit * jnp.mean(grad * unit, axis=-1, keepdims=True)
    )


def column_sum(value):
    return jnp.sum(value, axis=0, keepdims=True)


def project_kernel(stride, count, len_ref, me_ref, x_ref, vec_ref, *refs):
    sources = refs[:count]
    refs = refs[count:]
    if stride == 2:
        pooled_ref, pooled_low_ref, *refs = refs
    q_ref, k_ref, v_ref, entry, sem = refs
    row = pl.program_id(0)
    keys = x_ref.shape[1]
    queries = q_ref.shape[1]

    @pl.when(row == 0)
    def _():
        start_load(me_ref[0], sources, entry, sem.at[0], place_entry)
        wait_load(entry, sem.at[0])

    length = len_ref[row]
    if stride == 2:
        place = lax.broadcasted_iota(jnp.int32, (queries, keys), 1)
        mine = lax.broadcasted_iota(jnp.int32, (queries, keys), 0)
        pair = jnp.where(lax.shift_right_logical(place, 1) == mine, 0.5, 0.0).astype(BF16)
        pooled = mm(pair, x_ref[0])
        pooled_ref[0] = pooled
        query_in = low(pooled)
        pooled_low_ref[0] = query_in
    else:
        query_in = x_ref[0]
    q_ref[0] = low(wide(low(mm(query_in, entry[0]) + vec_ref[0:1, :])) * HD**-0.5)
    for block in range(keys // 256):

        @pl.when(block * 256 < length)
        def _():
            rows = pl.ds(block * 256, 256)
            x = x_ref[0, rows, :]
            k_ref[0, rows, :] = low(mm(x, entry[1]))
            v_ref[0, rows, :] = low(mm(x, entry[2]) + vec_ref[1:2, :])


def project(stride, index, lengths, x, vectors, sources):
    rows, keys, _ = x.shape
    queries = keys // stride
    blk = lambda *shape: pl.BlockSpec((1,) + shape, lambda r, *_: (r,) + (0,) * len(shape))
    full = lambda *shape: pl.BlockSpec(shape, lambda r, *_: (0,) * len(shape))
    sds = jax.ShapeDtypeStruct
    outs = [
        (sds((rows, queries, D), BF16), blk(queries, D)),
        (sds((rows, keys, D), BF16), blk(keys, D)),
        (sds((rows, keys, D), BF16), blk(keys, D)),
    ]
    if stride == 2:
        outs = [
            (sds((rows, queries, D), F32), blk(queries, D)),
            (sds((rows, queries, D), BF16), blk(queries, D)),
        ] + outs
    return pl.pallas_call(
        partial(project_kernel, stride, len(sources)),
        grid_spec=pltpu.PrefetchScalarGridSpec(
            num_scalar_prefetch=2,
            grid=(rows,),
            in_specs=[blk(keys, D), full(8, D)] + [ANY] * len(sources),
            out_specs=[o[1] for o in outs],
            scratch_shapes=[pltpu.VMEM((3, D, D), BF16), pltpu.SemaphoreType.DMA((1,))],
        ),
        out_shape=[o[0] for o in outs],
        compiler_params=pltpu.CompilerParams(vmem_limit_bytes=VMEM_LIMIT),
        cost_estimate=pl.CostEstimate(
            flops=rows * keys * D * D * 4, bytes_accessed=20_000_000, transcendentals=0
        ),
        name="project",
    )(lengths, index, x, vectors, *sources)


def attend_kernel(base, len_ref, me_ref, q_ref, k_ref, v_ref, bias, *refs):
    ctx_ref, probs_ref, turned = refs[-3:]
    row = pl.program_id(0)
    keys = k_ref.shape[1]
    length = len_ref[row + base]

    def group_step(size, pairs, step, carry):
        made = []
        for p in range(pairs):
            lanes = pl.ds(pl.multiple_of((step * pairs + p) * 128, 128), 128)
            queries_low = lane_masks(q_ref[0, :, lanes])
            key = k_ref[0, :size, lanes]
            value = v_ref[0, :size, lanes].T
            for i in range(2):
                h = 2 * (step * pairs + p) + i
                scores = masked_scores(key, queries_low[i], bias[h, :size, :], length)
                made.append((h, scores, value[HD * i : HD * i + HD]))
        kept = []
        for h, scores, value in made:
            top = jnp.max(scores, axis=0, keepdims=True)
            probs = jnp.exp(scores - top)
            probs = low(probs * (1.0 / jnp.sum(probs, axis=0, keepdims=True)))
            probs_ref[0, h, :size, :] = probs
            kept.append((h, probs, value))
        for h, probs, value in kept:
            turned[pl.ds(pl.multiple_of(HD * h, HD), HD), :] = mm(value, probs)
        return carry

    blocks = lax.div(length + 127, 128)
    for w in range(1, keys // 128 + 1):

        @pl.when(blocks == w)
        def _():
            pairs = GROUPS[w - 1]
            lax.fori_loop(0, H // 2 // pairs, partial(group_step, 128 * w, pairs), 0)

    ctx_ref[0] = low(turned[...].T)


def attend(stride, index, lengths, q, k, v, table, base, count, before=()):
    rows, keys, _ = k.shape
    queries = keys // stride
    blk = lambda *shape: pl.BlockSpec((1,) + shape, lambda r, *_: (r + base,) + (0,) * len(shape))
    full = lambda *shape: pl.BlockSpec(shape, lambda r, *_: (0,) * len(shape))
    sds = jax.ShapeDtypeStruct
    return pl.pallas_call(
        partial(attend_kernel, base),
        grid_spec=pltpu.PrefetchScalarGridSpec(
            num_scalar_prefetch=2,
            grid=(count,),
            in_specs=[blk(queries, D), blk(keys, D), blk(keys, D), full(H, keys, queries)]
            + [ANY] * len(before),
            out_specs=[blk(queries, D), blk(H, keys, queries)],
            scratch_shapes=[pltpu.VMEM((D, queries), F32)],
        ),
        out_shape=[sds((rows, queries, D), BF16), sds((rows, H, keys, queries), BF16)],
        input_output_aliases={6 + i: i for i in range(len(before))},
        compiler_params=pltpu.CompilerParams(vmem_limit_bytes=VMEM_LIMIT),
        cost_estimate=pl.CostEstimate(
            flops=count * keys * queries * D * 8,
            bytes_accessed=20_000_000,
            transcendentals=count * H * keys * queries,
        ),
        name="attend",
    )(lengths, index, q, k, v, table, *before)


def expand_kernel(counts, me_ref, ctx_ref, resid_ref, vec_ref, bias_ref, *refs):
    c1, c2, c3 = counts
    leave_src, widen_src, narrow_src = refs[:c1], refs[c1 : c1 + c2], refs[c1 + c2 : c1 + c2 + c3]
    u_ref, act_ref, slope_ref, before_ref, out_ref, leave, widen, narrow, sem = refs[c1 + c2 + c3 :]
    first = pl.program_id(0) == 0

    @pl.when(first)
    def _():
        start_load(me_ref[0], leave_src, leave, sem.at[0], place_leave)
        start_load(me_ref[0], widen_src, widen, sem.at[1], place_widen)
        start_load(me_ref[0], narrow_src, narrow, sem.at[2], place_narrow)
        wait_load(leave, sem.at[0])

    u = wide(resid_ref[...]) + mm(ctx_ref[...], leave[...]) + vec_ref[2:3, :]
    u_ref[...] = u
    unit, _ = statistics(u)
    mixed = unit * vec_ref[3:4, :] + vec_ref[4:5, :]
    mixed_low = low(mixed)

    @pl.when(first)
    def _():
        wait_load(widen, sem.at[1])
        wait_load(narrow, sem.at[2])

    total = mixed + vec_ref[5:6, :]
    for j in range(4):
        cols = slice(D * j, D * j + D)
        h = mm(mixed_low, widen[j]) + bias_ref[0:1, cols]
        square = h * h
        gate = 0.5 + 0.5 * jnp.tanh(h * (GELU_A + GELU_A * GELU_B * square))
        act = h * gate
        slope = gate + act * (1.0 - gate) * (2.0 * GELU_A + 6.0 * GELU_A * GELU_B * square)
        slope_ref[:, cols] = low(slope)
        act = low(act)
        act_ref[:, cols] = act
        total = total + mm(act, narrow[16 * j : 16 * j + 16].reshape(D, D))
    before_ref[...] = total
    unit, _ = statistics(total)
    out_ref[...] = low(unit * vec_ref[6:7, :] + vec_ref[7:8, :])


def expand(index, ctx, resid, vectors, wide_bias, leave, widen, narrow):
    tokens = ctx.shape[0]
    tile = TILE_A
    blk = lambda width: pl.BlockSpec((tile, width), lambda r, *_: (r, 0))
    full = lambda *shape: pl.BlockSpec(shape, lambda r, *_: (0,) * len(shape))
    sds = jax.ShapeDtypeStruct
    sources = tuple(leave) + tuple(widen) + tuple(narrow)
    return pl.pallas_call(
        partial(expand_kernel, (len(leave), len(widen), len(narrow))),
        grid_spec=pltpu.PrefetchScalarGridSpec(
            num_scalar_prefetch=1,
            grid=(tokens // tile,),
            in_specs=[blk(D), blk(D), full(8, D), full(1, FF)] + [ANY] * len(sources),
            out_specs=[blk(D), blk(FF), blk(FF), blk(D), blk(D)],
            scratch_shapes=[
                pltpu.VMEM((D, D), BF16),
                pltpu.VMEM((4, D, D), BF16),
                pltpu.VMEM((64, 48, D), BF16),
                pltpu.SemaphoreType.DMA((3,)),
            ],
        ),
        out_shape=[
            sds((tokens, D), F32),
            sds((tokens, FF), BF16),
            sds((tokens, FF), BF16),
            sds((tokens, D), F32),
            sds((tokens, D), BF16),
        ],
        compiler_params=pltpu.CompilerParams(vmem_limit_bytes=VMEM_LIMIT),
        cost_estimate=pl.CostEstimate(
            flops=2 * tokens * D * (D + 2 * FF), bytes_accessed=30_000_000, transcendentals=tokens * FF
        ),
        name="expand",
    )(index, ctx, resid, vectors, wide_bias, *sources)


def contract_kernel(counts, me_ref, dz_ref, before_ref, slope_ref, u_ref, vec_ref, *refs):
    c1, c2, c3 = counts
    leave_src, widen_src, narrow_src = refs[:c1], refs[c1 : c1 + c2], refs[c1 + c2 : c1 + c2 + c3]
    refs = refs[c1 + c2 + c3 :]
    dback_ref, mixed_ref, dhid_ref, dattn_ref, du_ref, dctx_ref, dvec_ref, dbias_ref = refs[:8]
    leave, widen, narrow, sem = refs[8:]
    first = pl.program_id(0) == 0

    @pl.when(first)
    def _():
        start_load(me_ref[0], narrow_src, narrow, sem.at[2], place_narrow)
        start_load(me_ref[0], widen_src, widen, sem.at[1], place_widen)
        start_load(me_ref[0], leave_src, leave, sem.at[0], place_leave)
        dvec_ref[...] = jnp.zeros_like(dvec_ref)
        dbias_ref[...] = jnp.zeros_like(dbias_ref)

    dz = wide(dz_ref[...])
    unit, rstd = statistics(before_ref[...])
    dvec_ref[6:7, :] += column_sum(dz * unit)
    dvec_ref[7:8, :] += column_sum(dz)
    dpre = norm_pull(dz * vec_ref[6:7, :], unit, rstd)
    dback = low(dpre)
    dback_ref[...] = dback
    dvec_ref[5:6, :] += column_sum(wide(dback))
    unit, rstd = statistics(u_ref[...])
    mixed_ref[...] = low(unit * vec_ref[3:4, :] + vec_ref[4:5, :])

    @pl.when(first)
    def _():
        wait_load(narrow, sem.at[2])
        wait_load(widen, sem.at[1])
        wait_load(leave, sem.at[0])

    dmixed = dpre
    for j in range(4):
        cols = slice(D * j, D * j + D)
        dact = mm(dback, narrow[16 * j : 16 * j + 16].reshape(D, D), NT)
        dhid = low(dact * wide(slope_ref[:, cols]))
        dhid_ref[:, cols] = dhid
        dbias_ref[:, cols] += column_sum(wide(dhid))
        dmixed = dmixed + mm(dhid, widen[j], NT)
    dvec_ref[3:4, :] += column_sum(dmixed * unit)
    dvec_ref[4:5, :] += column_sum(dmixed)
    du = norm_pull(dmixed * vec_ref[3:4, :], unit, rstd)
    du_ref[...] = du
    dattn = low(du)
    dattn_ref[...] = dattn
    dvec_ref[2:3, :] += column_sum(wide(dattn))
    dctx_ref[...] = low(mm(dattn, leave[...], NT))


def contract(index, dz, before, hidden_units, u, vectors, leave, widen, narrow):
    tokens = dz.shape[0]
    tile = TILE_B
    blk = lambda width: pl.BlockSpec((tile, width), lambda r, *_: (r, 0))
    full = lambda *shape: pl.BlockSpec(shape, lambda r, *_: (0,) * len(shape))
    sds = jax.ShapeDtypeStruct
    sources = tuple(leave) + tuple(widen) + tuple(narrow)
    return pl.pallas_call(
        partial(contract_kernel, (len(leave), len(widen), len(narrow))),
        grid_spec=pltpu.PrefetchScalarGridSpec(
            num_scalar_prefetch=1,
            grid=(tokens // tile,),
            in_specs=[blk(D), blk(D), blk(FF), blk(D), full(8, D)] + [ANY] * len(sources),
            out_specs=[blk(D), blk(D), blk(FF), blk(D), blk(D), blk(D), full(8, D), full(1, FF)],
            scratch_shapes=[
                pltpu.VMEM((D, D), BF16),
                pltpu.VMEM((4, D, D), BF16),
                pltpu.VMEM((64, 48, D), BF16),
                pltpu.SemaphoreType.DMA((3,)),
            ],
        ),
        out_shape=[
            sds((tokens, D), BF16),
            sds((tokens, D), BF16),
            sds((tokens, FF), BF16),
            sds((tokens, D), BF16),
            sds((tokens, D), F32),
            sds((tokens, D), BF16),
            sds((8, D), F32),
            sds((1, FF), F32),
        ],
        compiler_params=pltpu.CompilerParams(vmem_limit_bytes=VMEM_LIMIT),
        cost_estimate=pl.CostEstimate(
            flops=2 * tokens * D * (D + 2 * FF), bytes_accessed=50_000_000, transcendentals=tokens * FF
        ),
        name="contract",
    )(index, dz, before, hidden_units, u, vectors, *sources)


def halves(core, value, width):
    left, right = value[:, :width], value[:, width:]
    first = core == 0
    return jnp.where(first, right, left), jnp.where(first, left, right)


def flush(pairs, start, rows, sem):
    copies = [
        pltpu.make_async_copy(scratch, out_ref.at[:, start : start + rows, :], sem.at[i])
        for i, (scratch, out_ref) in enumerate(pairs)
    ]
    for copy in copies:
        copy.start()
    for copy in copies:
        copy.wait()


def sum_call(kernel, name, total_rows, start, rows, grid, prefetch, inputs, in_specs, scratch, before, flops):
    out = jax.ShapeDtypeStruct((UNITS, total_rows, HALF), BF16)
    return pl.pallas_call(
        partial(kernel, start, rows),
        grid_spec=pltpu.PrefetchScalarGridSpec(
            num_scalar_prefetch=len(prefetch),
            grid=grid,
            in_specs=in_specs + [ANY] * len(before),
            out_specs=[ANY, ANY],
            scratch_shapes=[
                pltpu.VMEM((UNITS, rows, HALF), BF16),
                pltpu.VMEM((UNITS, rows, HALF), BF16),
                pltpu.SemaphoreType.DMA((2,)),
            ]
            + scratch,
        ),
        out_shape=[out, out],
        input_output_aliases={len(prefetch) + len(inputs) + i: i for i in range(len(before))},
        compiler_params=pltpu.CompilerParams(vmem_limit_bytes=VMEM_LIMIT),
        cost_estimate=pl.CostEstimate(flops=flops, bytes_accessed=16_000_000, transcendentals=0),
        name=name,
    )(*prefetch, *inputs, *before)


def narrow_grad_kernel(start, rows, me_ref, act_ref, dback_ref, ctx_ref, dattn_ref, *refs):
    send_out, keep_out, send_ref, keep_ref, sem = refs[-5:]
    step = pl.program_id(0)
    core = jnp.bitwise_and(me_ref[0], 1)
    chip = lax.shift_right_logical(me_ref[0], 1)

    @pl.when(step < 4)
    def _():
        send, keep = halves(core, mm(act_ref[...], dback_ref[...], TN), HALF)
        for i in range(4):
            at = position(chip, step * 4 + i)
            send_ref[at, 0:192, :] = low(send[192 * i : 192 * i + 192])
            keep_ref[at, 0:192, :] = low(keep[192 * i : 192 * i + 192])

    @pl.when(step == 4)
    def _():
        send, keep = halves(core, mm(ctx_ref[...], dattn_ref[...], TN), HALF)
        for i in range(UNITS):
            at = position(chip, i)
            send_ref[at, 192:240, :] = low(send[48 * i : 48 * i + 48])
            keep_ref[at, 192:240, :] = low(keep[48 * i : 48 * i + 48])
        flush(((send_ref, send_out), (keep_ref, keep_out)), start, rows, sem)


def halves(core, value, width):
    left, right = value[:, :width], value[:, width:]
    first = core == 0
    return jnp.where(first, right, left), jnp.where(first, left, right)


def narrow_grad(total_rows, index, act, dback, ctx, dattn):
    tokens = act.shape[0]
    specs = [pl.BlockSpec((tokens, D), lambda r, *_: (0, jnp.minimum(r, 3)))] + [whole(tokens, D)] * 3
    return sum_call(
        narrow_grad_kernel, "narrow_grad", total_rows, 0, 240, (5,), (index,),
        (act, dback, ctx, dattn), specs, [], (), 2 * tokens * D * (D + FF),
    )


def widen_grad_kernel(start, rows, me_ref, mixed_ref, dhid_ref, *refs):
    send_out, keep_out, send_ref, keep_ref, sem, turned = refs[-6:]
    step = pl.program_id(0)
    core = jnp.bitwise_and(me_ref[0], 1)
    chip = lax.shift_right_logical(me_ref[0], 1)

    @pl.when(step == 0)
    def _():
        turned[...] = mixed_ref[...].T

    grad = low(mm(turned[...], dhid_ref[...]))
    mine = lax.div(step, 2) == core
    for part in range(2):

        @pl.when(lax.rem(step, 2) == part)
        def _():
            for wanted, out_ref in ((True, keep_ref), (False, send_ref)):

                @pl.when(mine == wanted)
                def _():
                    for i in range(UNITS):
                        at = position(chip, i)
                        for q in range(2):
                            line = 96 * part + 48 * q
                            out_ref[at, line : line + 48, :] = grad[
                                48 * i : 48 * i + 48, HALF * q : HALF * q + HALF
                            ]

    @pl.when(step == 3)
    def _():
        flush(((send_ref, send_out), (keep_ref, keep_out)), start, rows, sem)


def widen_grad(total_rows, index, mixed_low, dhid, before):
    start = 240 if before else 0
    tokens = mixed_low.shape[0]
    specs = [whole(tokens, D), pl.BlockSpec((tokens, D), lambda r, *_: (0, r))]
    return sum_call(
        widen_grad_kernel, "widen_grad", total_rows, start, 192, (4,), (index,),
        (mixed_low, dhid), specs, [pltpu.VMEM((D, tokens), BF16)], before, 2 * tokens * D * FF,
    )


def entry_grad_kernel(start, rows, len_ref, me_ref, a_ref, b_ref, dq_ref, dk_ref, dv_ref, vec_ref, *refs):
    send_out, keep_out, send_ref, keep_ref, sem, total = refs[-6:]
    row = pl.program_id(0)
    core = jnp.bitwise_and(me_ref[0], 1)
    chip = lax.shift_right_logical(me_ref[0], 1)
    keys = b_ref.shape[1]

    @pl.when(row == 0)
    def _():
        total[...] = jnp.zeros_like(total)

    total[0] += mm(a_ref[0], dq_ref[0], TN)
    for block in range(keys // 256):

        @pl.when(block * 256 < len_ref[row])
        def _():
            lines = pl.ds(block * 256, 256)
            b = b_ref[0, lines, :].T
            total[1] += mm(b, dk_ref[0, lines, :])
            total[2] += mm(b, dv_ref[0, lines, :])

    @pl.when(row == pl.num_programs(0) - 1)
    def _():
        for m in range(3):
            send, keep = halves(core, total[m], HALF)
            for i in range(UNITS):
                at = position(chip, i)
                send_ref[at, 48 * m : 48 * m + 48, :] = low(send[48 * i : 48 * i + 48])
                keep_ref[at, 48 * m : 48 * m + 48, :] = low(keep[48 * i : 48 * i + 48])
        for i in range(UNITS):
            at = position(chip, i)
            send_ref[at, 144:160, :] = vec_ref[i, 1 - core]
            keep_ref[at, 144:160, :] = vec_ref[i, core]
        flush(((send_ref, send_out), (keep_ref, keep_out)), start, rows, sem)


def entry_grad(total_rows, start, index, lengths, a, b, dq, dk, dv, vec, before):
    rows, keys, _ = b.shape
    queries = a.shape[1]
    blk = lambda *shape: pl.BlockSpec((1,) + shape, lambda r, *_: (r,) + (0,) * len(shape))
    specs = [blk(queries, D), blk(keys, D), blk(queries, D), blk(keys, D), blk(keys, D)]
    specs.append(whole(UNITS, 2, 16, HALF))
    return sum_call(
        entry_grad_kernel, "entry_grad", total_rows, start, 160, (rows,), (lengths, index),
        (a, b, dq, dk, dv, vec), specs, [pltpu.VMEM((3, D, D), F32)], before,
        2 * rows * (queries + keys) * D * D,
    )


def retrace_kernel(stride, base, len_ref, me_ref, q_ref, k_ref, v_ref, dctx_ref, probs_ref, *refs):
    dq_ref, dk_ref, dv_ref, dvec_ref, diag_ref, ends_ref, bias_sum, turned = refs[-8:]
    row = pl.program_id(0)
    keys = k_ref.shape[1]
    queries = q_ref.shape[1]
    length = len_ref[row + base]

    @pl.when(row == 0)
    def _():
        bias_sum[...] = jnp.zeros_like(bias_sum)
        dvec_ref[...] = jnp.zeros_like(dvec_ref)

    def group_step(size, pairs, step, carry):
        loaded = []
        for p in range(pairs):
            lanes = pl.ds(pl.multiple_of((step * pairs + p) * 128, 128), 128)
            dctx = lane_masks(dctx_ref[0, :, lanes])
            value = v_ref[0, :size, lanes]
            loaded.append((lanes, dctx, [mm(value, dctx[i], NT) for i in range(2)]))
        made = []
        for p, (lanes, dctx, dprobs) in enumerate(loaded):
            grads, probs = [], []
            for i in range(2):
                h = 2 * (step * pairs + p) + i
                kept = probs_ref[0, h, :size, :]
                prob = wide(kept)
                inner = jnp.sum(prob * dprobs[i], axis=0, keepdims=True)
                inner = inner / jnp.sum(prob, axis=0, keepdims=True)
                grad = low(prob * (dprobs[i] - inner))
                for lane in range(queries // 128):
                    bias_sum[lane, h, :size, :] += wide(grad[:, 128 * lane : 128 * lane + 128])
                grads.append(grad)
                probs.append(kept)
            made.append((lanes, dctx, grads, probs))
        for p, (lanes, dctx, grads, probs) in enumerate(made):
            query = lane_masks(q_ref[0, :, lanes])
            key = k_ref[0, :size, lanes].T
            for i in range(2):
                h = 2 * (step * pairs + p) + i
                turned[pl.ds(pl.multiple_of(HD * h, HD), HD), :] = (
                    mm(key[HD * i : HD * i + HD], grads[i]) * HD**-0.5
                )
            dv_ref[0, :size, lanes] = low(
                mm(jnp.concatenate(probs, axis=1), jnp.concatenate(dctx, axis=0))
            )
            dk_ref[0, :size, lanes] = low(
                mm(jnp.concatenate(grads, axis=1), jnp.concatenate(query, axis=0))
            )
        return carry

    blocks = lax.div(length + 127, 128)
    for w in range(1, keys // 128 + 1):

        @pl.when(blocks == w)
        def _():
            size, pairs = 128 * w, GROUPS[w - 1]
            lax.fori_loop(0, H // 2 // pairs, partial(group_step, size, pairs), 0)
            if size < keys:
                dk_ref[0, size:, :] = jnp.zeros((keys - size, D), BF16)
                dv_ref[0, size:, :] = jnp.zeros((keys - size, D), BF16)
            dvec_ref[1:2, :] += column_sum(wide(dv_ref[0, :size, :]))

    dquery = low(turned[...].T)
    dq_ref[0] = dquery
    dvec_ref[0:1, :] += column_sum(wide(dquery))

    @pl.when(row == pl.num_programs(0) - 1)
    def _():
        ends_ref[...] = jnp.zeros_like(ends_ref)

        def collect(h, carry):
            below = above = jnp.zeros((1, queries), F32)
            for part in range(stride):
                block = jnp.concatenate(
                    [
                        bias_sum[lane, h, pl.ds(part, queries, stride=stride), :]
                        for lane in range(queries // 128)
                    ],
                    axis=1,
                )
                col = lax.broadcasted_iota(jnp.int32, block.shape, 1)
                line = lax.broadcasted_iota(jnp.int32, block.shape, 0)
                place = stride * (line - col) + part
                zero = jnp.zeros_like(block)
                below = below + column_sum(jnp.where(place <= -(NB // 2), block, zero))
                above = above + column_sum(jnp.where(place >= NB // 2 - 1, block, zero))
                inside = jnp.where((place > -(NB // 2)) & (place < NB // 2 - 1), block, zero)
                partial_sum = inside[:8]
                for a in range(1, queries // 8):
                    partial_sum = partial_sum + pltpu.roll(inside[8 * a : 8 * a + 8], queries - 8 * a, 1)
                sub = lax.broadcasted_iota(jnp.int32, partial_sum.shape, 0)
                lined = jnp.where(sub == 0, partial_sum, 0.0)
                for b in range(1, 8):
                    lined = lined + jnp.where(sub == b, pltpu.roll(partial_sum, queries - b, 1), 0.0)
                diag_ref[h, part] = jnp.broadcast_to(column_sum(lined), (8, queries))
            ends_ref[h, 0] = jnp.broadcast_to(below, (8, queries))
            ends_ref[h, 1] = jnp.broadcast_to(above, (8, queries))
            return carry

        lax.fori_loop(0, H, collect, 0)


def retrace(stride, index, lengths, q, k, v, dctx, probs, base, count, before=()):
    rows, keys, _ = k.shape
    queries = q.shape[1]
    blk = lambda *shape: pl.BlockSpec((1,) + shape, lambda r, *_: (r + base,) + (0,) * len(shape))
    full = lambda *shape: pl.BlockSpec(shape, lambda r, *_: (0,) * len(shape))
    sds = jax.ShapeDtypeStruct
    return pl.pallas_call(
        partial(retrace_kernel, stride, base),
        grid_spec=pltpu.PrefetchScalarGridSpec(
            num_scalar_prefetch=2,
            grid=(count,),
            in_specs=[
                blk(queries, D),
                blk(keys, D),
                blk(keys, D),
                blk(queries, D),
                blk(H, keys, queries),
            ]
            + [ANY] * len(before),
            out_specs=[
                blk(queries, D),
                blk(keys, D),
                blk(keys, D),
                full(8, D),
                full(H, stride, 8, queries),
                full(H, 2, 8, queries),
            ],
            scratch_shapes=[
                pltpu.VMEM((queries // 128, H, keys, 128), F32),
                pltpu.VMEM((D, queries), F32),
            ],
        ),
        out_shape=[
            sds((rows, queries, D), BF16),
            sds((rows, keys, D), BF16),
            sds((rows, keys, D), BF16),
            sds((8, D), F32),
            sds((H, stride, 8, queries), F32),
            sds((H, 2, 8, queries), F32),
        ],
        input_output_aliases={7 + i: i for i in range(len(before))},
        compiler_params=pltpu.CompilerParams(vmem_limit_bytes=VMEM_LIMIT),
        cost_estimate=pl.CostEstimate(
            flops=count * keys * queries * D * 10, bytes_accessed=20_000_000, transcendentals=count * H * keys * queries
        ),
        name="retrace",
    )(lengths, index, q, k, v, dctx, probs, *before)


def table_grad(stride, diag, ends):
    queries = diag.shape[-1]
    columns = []
    for bucket in range(NB):
        place = bucket - NB // 2
        if bucket == 0:
            columns.append(jnp.sum(ends[:, 0, 0], axis=-1))
        elif bucket == NB - 1:
            columns.append(jnp.sum(ends[:, 1, 0], axis=-1))
        else:
            part = place % stride
            columns.append(diag[:, part, 0, ((part - place) // stride) % queries])
    return jnp.stack(columns, axis=1).reshape(-1)


def inputs_kernel(stride, base, count, len_ref, me_ref, dq_ref, dk_ref, dv_ref, du_ref, *refs):
    sources = refs[:count]
    out_ref, entry, sem = refs[-3:]
    row = pl.program_id(0)
    keys = dk_ref.shape[1]
    queries = dq_ref.shape[1]

    @pl.when(row == 0)
    def _():
        start_load(me_ref[0], sources, entry, sem.at[0], place_entry)
        wait_load(entry, sem.at[0])

    total = mm(dq_ref[0], entry[0], NT) + du_ref[0]
    if stride == 1:
        out_ref[0] = total + mm(dk_ref[0], entry[1], NT) + mm(dv_ref[0], entry[2], NT)
        return
    total = 0.5 * total
    upper = low(total)
    lower = low(total - wide(upper))
    for block in range(keys // 256):
        rows = pl.ds(block * 256, 256)
        place = lax.broadcasted_iota(jnp.int32, (256, queries), 0) + 256 * block
        mine = lax.broadcasted_iota(jnp.int32, (256, queries), 1)
        pair = jnp.where(lax.shift_right_logical(place, 1) == mine, 1.0, 0.0).astype(BF16)
        spread = mm(pair, upper) + mm(pair, lower)

        @pl.when(block * 256 < len_ref[row + base])
        def _():
            out_ref[0, rows, :] = (
                spread + mm(dk_ref[0, rows, :], entry[1], NT) + mm(dv_ref[0, rows, :], entry[2], NT)
            )

        @pl.when(block * 256 >= len_ref[row + base])
        def _():
            out_ref[0, rows, :] = spread


def input_grads(stride, index, lengths, dq, dk, dv, du, sources, base, count, before=()):
    rows, keys, _ = dk.shape
    queries = dq.shape[1]
    blk = lambda *shape: pl.BlockSpec((1,) + shape, lambda r, *_: (r + base,) + (0,) * len(shape))
    return pl.pallas_call(
        partial(inputs_kernel, stride, base, len(sources)),
        grid_spec=pltpu.PrefetchScalarGridSpec(
            num_scalar_prefetch=2,
            grid=(count,),
            in_specs=[blk(queries, D), blk(keys, D), blk(keys, D), blk(queries, D)] + [ANY] * (len(sources) + len(before)),
            out_specs=blk(keys, D),
            scratch_shapes=[pltpu.VMEM((3, D, D), BF16), pltpu.SemaphoreType.DMA((1,))],
        ),
        out_shape=jax.ShapeDtypeStruct((rows, keys, D), F32),
        input_output_aliases={6 + len(sources) + i: i for i in range(len(before))},
        compiler_params=pltpu.CompilerParams(vmem_limit_bytes=VMEM_LIMIT),
        cost_estimate=pl.CostEstimate(
            flops=2 * count * (queries + keys) * D * D, bytes_accessed=20_000_000, transcendentals=0
        ),
        name="input_grads",
    )(lengths, index, dq, dk, dv, du, *sources, *before)


def vectors_by_unit(dvec, dbias, dtable):
    flat = vector_units(dvec, dbias, dtable, 32)
    return jnp.pad(low(flat), ((0, 0), (0, 16 * HALF - flat.shape[1]))).reshape(UNITS, 2, 16, HALF)


NARROW_CUTS = ((192, 96), (48, 24))
WIDEN_CUTS = ((48, 24),) * 4
FEED_CUTS = NARROW_CUTS + WIDEN_CUTS
ENTRY_CUTS = ((48, 24),) * 3


def join(left, right):
    return jnp.concatenate([left, right], axis=-1)


def feed_shards(left, right):
    widen = jnp.concatenate([left[120:216].reshape(4, 24, HALF), right[120:216].reshape(4, 24, HALF)])
    return (
        join(left[96:120], right[96:120]),
        widen.transpose(1, 0, 2).reshape(24, FF),
        join(left[:96], right[:96]),
    )


def entry_shards(left, right):
    return join(left, right).reshape(3, 24, D)


def absolute_units(pair):
    send, keep = pair
    merged = jnp.stack([keep, send], axis=2)
    rest = merged.shape[1:]
    merged = merged.reshape((4, 4) + rest).transpose(1, 0, 2, 3, 4)
    return wide(merged.reshape((UNITS,) + rest))


def plain_shards(feed, entry):
    feed, entry = absolute_units(feed), absolute_units(entry)
    narrow = feed[:, :192].reshape(FF, D)
    leave = feed[:, 192:240].reshape(D, D)
    widen = feed[:, 240:432].reshape(UNITS, 4, 48, 2, HALF).transpose(0, 2, 3, 1, 4).reshape(D, FF)
    vectors = entry[:, 144:].transpose(0, 2, 1, 3).reshape(32, -1)
    entry = entry[:, :144].reshape(UNITS, 3, 48, D).transpose(1, 0, 2, 3).reshape(3, D, D)
    scatter = lambda value, dim: lax.psum_scatter(value, AX, scatter_dimension=dim, tiled=True)
    rows = vectors.shape[0]
    cut, mid = 8 * D // rows, 8 * D // rows + FF // rows
    last = mid + H * NB // rows
    vec = vectors[:, :cut].reshape(rows, 8, -1).transpose(1, 0, 2).reshape(8, D)
    return (
        scatter(entry, 1),
        scatter(leave, 0),
        scatter(widen, 0),
        scatter(narrow, 0),
        scatter(vec, 1),
        scatter(vectors[:, cut:mid].reshape(-1), 0),
        scatter(vectors[:, mid:last].reshape(-1), 0),
    )


def plain_gather(entry, leave, widen, narrow):
    gather = lambda value, dim: lax.all_gather(value, AX, axis=dim, tiled=True)
    widen = gather(widen, 0).reshape(D, 4, D).transpose(1, 0, 2)
    return (
        (gather(entry, 1),),
        (gather(leave, 0),),
        (widen,),
        (gather(narrow, 0).reshape(64, 48, D),),
    )


def plain_vectors(*small):
    gather = lambda value, dim: lax.all_gather(value, AX, axis=dim, tiled=True)
    parts = []
    for value in small:
        full = gather(value, value.ndim - 1)
        if value.ndim == 2:
            parts.append(full.reshape(8, 32, 24).transpose(1, 0, 2))
        else:
            parts.append(full.reshape(32, -1))
    slabs = vector_slab(*parts).reshape(4, 4, 2, 16, 128).transpose(2, 1, 0, 3, 4)
    return slabs[0].reshape(UNITS, 16, 128), slabs[1].reshape(UNITS, 16, 128)


def on_device(
    devices,
    hidden,
    lengths,
    cotangent,
    inflow,
    outflow,
    widener,
    narrower,
    shifts,
    offsets,
    distance,
    intake,
    outtake,
    expander,
    squeezer,
    adjusts,
    leanings,
    spacing,
):
    rows, seq, width = hidden.shape
    half = seq // 2
    fast = devices == 32
    index = lax.axis_index(AX)
    core = index % 2
    halved = (lengths + 1) // 2
    layer_one = (inflow, outflow, widener, narrower)
    layer_two = (intake, outtake, expander, squeezer)

    small = (shifts, offsets, distance, adjusts, leanings, spacing)
    if fast:
        ticks = Ticks(index.astype(jnp.int32).reshape(1))
        tick = ticks.run
        vec = Job(vector_stages, vector_slab(*small))
        eo1, w1 = gather_jobs(core, True, *layer_one)
        eo2, w2 = gather_jobs(core, False, *layer_two)
        tick([eo1, vec, w1])
        tick([eo1, vec, w1])
        tick([eo1, vec, w1])
        prepared = tick([eo1], lambda me: prepare(me, *vec.result, seq, half))
        tick([eo1, eo2, w2])
    else:
        ticks = Ticks(jnp.zeros((1,), jnp.int32))
        eo1 = w1 = eo2 = w2 = None
        plain_one, plain_two = plain_gather(*layer_one), plain_gather(*layer_two)
        prepared = prepare(ticks.me, *plain_vectors(*small), seq, half)

        def tick(jobs, kernel=None):
            return ticks.run([], kernel)

    def weights(layer, names):
        if fast:
            jobs = {"e": (eo1, eo2), "o": (eo1, eo2), "w": (w1, w2), "n": (w1, w2)}
            return [jobs[name][layer].result for name in names]
        return [(plain_one, plain_two)[layer]["eown".index(name)] for name in names]

    vec1, bias1, tab1, vec2, bias2, tab2 = prepared
    flatten = lambda value: value.reshape(-1, D)
    part = rows // 2

    def begin(stride, me, lens, x, vec_in, layer, tab):
        made = project(stride, me, lens, x, vec_in, *weights(layer, "e"))
        q, k, v = made[-3:]
        return made, attend(stride, me, lens, q, k, v, tab, 0, part)

    def finish(stride, me, lens, made, tab, head):
        return attend(stride, me, lens, *made[-3:], tab, part, rows - part, head)

    made1, head = tick([w1, eo2, w2], lambda me: begin(2, me, lengths, hidden, vec1, 0, tab1))
    ctx1, probs1 = tick([w1, eo2], lambda me: finish(2, me, lengths, made1, tab1, head))
    pooled, pooled_low, q1, k1, v1 = made1
    tick([w1])
    u1, act1, slope1, before1, first_out = tick(
        [eo2, w2],
        lambda me: expand(me, flatten(ctx1), flatten(pooled), vec1, bias1, *weights(0, "own")),
    )
    pooled_layer = first_out.reshape(rows, half, width)

    tick([eo2])
    tick([eo2])
    made2, head = tick([w2], lambda me: begin(1, me, halved, pooled_layer, vec2, 1, tab2))
    ctx2, probs2 = tick([w2], lambda me: finish(1, me, halved, made2, tab2, head))
    q2, k2, v2 = made2
    tick([w2])
    u2, act2, slope2, before2, second_out = tick(
        [], lambda me: expand(me, flatten(ctx2), first_out, vec2, bias2, *weights(1, "own"))
    )

    def reducing(pair, cuts):
        return Job(reduce_stages, core, cuts, *pair) if fast else pair

    dback, mixed_low, dhid, dattn, du, dctx, dvec, dbias = tick(
        [],
        lambda me: contract(me, cotangent.reshape(-1, D), before2, slope2, u2, vec2, *weights(1, "own")),
    )

    narrow2 = tick([], lambda me: narrow_grad(240, me, act2, dback, flatten(ctx2), dattn))
    sumn2 = reducing(narrow2, NARROW_CUTS)
    widen2 = tick([sumn2], lambda me: widen_grad(192, me, mixed_low, dhid, ()))
    sumw2 = reducing(widen2, WIDEN_CUTS)
    back = tick(
        [sumn2, sumw2],
        lambda me: retrace(1, me, halved, q2, k2, v2, dctx.reshape(q2.shape), probs2, 0, rows),
    )
    dq, dk, dv, dvec_top, diag, ends = back
    packed = vectors_by_unit(dvec + dvec_top, dbias, table_grad(1, diag, ends))

    def entry_end(me):
        made = entry_grad(160, 0, me, halved, pooled_layer, pooled_layer, dq, dk, dv, packed, ())
        parts = (dq, dk, dv, du.reshape(q2.shape), *weights(1, "e"))
        return made, input_grads(1, me, halved, *parts, 0, rows)

    entry2, dlayer = tick([sumn2, sumw2], entry_end)
    sume2 = reducing(entry2, ENTRY_CUTS)

    dback, mixed_low, dhid, dattn, du, dctx, dvec, dbias = tick(
        [sumw2, sumn2, sume2],
        lambda me: contract(me, flatten(dlayer), before1, slope1, u1, vec1, *weights(0, "own")),
    )
    narrow1 = tick(
        [sumw2, sumn2, sume2], lambda me: narrow_grad(240, me, act1, dback, flatten(ctx1), dattn)
    )
    sumn1 = reducing(narrow1, NARROW_CUTS)
    widen1 = tick([sumn1, sumw2, sume2], lambda me: widen_grad(192, me, mixed_low, dhid, ()))
    sumw1 = reducing(widen1, WIDEN_CUTS)
    parts = (q1, k1, v1, dctx.reshape(q1.shape), probs1)
    head = tick([sumn1, sumw1, sume2, sumn2], lambda me: retrace(2, me, lengths, *parts, 0, part))
    back = tick(
        [sumn1, sumw1, sume2], lambda me: retrace(2, me, lengths, *parts, part, rows - part, head[:3])
    )
    dq, dk, dv = back[:3]
    dvec_top, diag, ends = [one + two for one, two in zip(head[3:], back[3:])]
    packed = vectors_by_unit(dvec + dvec_top, dbias, table_grad(2, diag, ends))
    entry1 = tick(
        [sumw1, sumn1, sumw2],
        lambda me: entry_grad(160, 0, me, lengths, pooled_low, hidden, dq, dk, dv, packed, ()),
    )
    sume1 = reducing(entry1, ENTRY_CUTS)
    parts = (dq, dk, dv, du.reshape(q1.shape), *weights(0, "e"))
    head = tick(
        [sume1, sumw1, sumn1, sume2], lambda me: input_grads(2, me, lengths, *parts, 0, part)
    )
    hidden_grad = tick(
        [sume1, sumw1, sumn1],
        lambda me: input_grads(2, me, lengths, *parts, part, rows - part, (head,)),
    )
    if fast:
        for job in (sume1, sumw1, sumn1, sumn2, sumw2, sume2):
            while job.result is None:
                tick([job, sumw1] if job is sume1 else [job])
        left, right, rest = sume2.result
        feed = [jnp.concatenate(sides) for sides in zip(sumn2.result[:2], sumw2.result[:2])]
        shards_two = (entry_shards(left, right),) + feed_shards(*feed)
        shards_two = shards_two + split_vectors(rest.reshape(-1), 32)
        left, right, rest = sume1.result
        feed = [jnp.concatenate(sides) for sides in zip(sumn1.result[:2], sumw1.result[:2])]
        shards_one = (entry_shards(left, right),) + feed_shards(*feed)
        shards_one = shards_one + split_vectors(rest.reshape(-1), 32)
    else:
        feed2 = [jnp.concatenate(sides, axis=1) for sides in zip(narrow2, widen2)]
        feed1 = [jnp.concatenate(sides, axis=1) for sides in zip(narrow1, widen1)]
        shards_one, shards_two = plain_shards(feed1, entry1), plain_shards(feed2, entry2)
    return (
        pooled_layer,
        second_out.reshape(rows, half, width),
        hidden_grad,
        *shards_one,
        *shards_two[:4],
        shards_two[4][1:],
        shards_two[5],
        shards_two[6],
        shards_two[4][0],
    )


def solution(mesh):
    both = ("wide", "narrow")
    rows = P(both, None, None)
    weights = (
        P(None, both, None),
        P(both, None),
        P(both, None),
        P(both, None),
        P(None, both),
        P(both),
        P(both),
    )
    return jax.shard_map(
        partial(on_device, mesh.size),
        mesh=mesh,
        in_specs=(rows, P(both), rows) + weights + weights,
        out_specs=(rows, rows, rows) + weights + weights + (P(both),),
        check_vma=False,
    )
```

time: 813 us -> 637 us (0.78)
  waiting for transfers between devices: 232 us -> 120 us
  starting transfers between devices: 146 us -> 86.6 us
  other arithmetic: 49 us -> 85.1 us
  local copies, waits for them, and re-layouts: 61.9 us -> 30.8 us
  Pallas kernels: 313 us -> 304 us
    ppermute x146 -> x104, waiting for transfers between devices: 232 us -> 120 us  [swap(): return lax.ppermute(value, AX, [(i, i ^ mask) for i in range(32)])]
    ppermute x146 -> x104, starting transfers between devices: 146 us -> 86.6 us  [swap(): return lax.ppermute(value, AX, [(i, i ^ mask) for i in range(32)])]
    convert_element_type x12 -> x24, other arithmetic: 0.8 us -> 47.9 us  [low(): return value.astype(BF16)]
    convert_element_type x10 -> x0, local copies, waits for them, and re-layouts: 14.3 us -> none  [wide(): return value.astype(F32)]
    pallas_call x2, Pallas kernels: 59 us -> 47.8 us  [contract(): pl.pallas_call(partial(contract_kernel, (len(leave), len(widen), len(narr...]
    slice x43 -> x30, local copies, waits for them, and re-layouts: 15.8 us -> 6.23 us  [the longest x8 5.96 us: gather_stages(): diag = (swap(across_y[:2], XBIT), swap(across_x[2:], YBIT))]
    pallas_call x12 -> x19, Pallas kernels: 210 us -> 209 us  [the longest x6 71.5 us: sum_call(): pl.pallas_call(partial(kernel, start, rows), grid_spec=pltpu.PrefetchScal...]
  transfers between devices with their start and end apart: 146 -> 104, of which waited for: 57 -> 33; matrix products, arithmetic and copies ran while one was open for 11% -> 13% of each run, Pallas kernels for 19% -> 39%
where the time goes in v2:
time: 637 us; the launch traced here: 630 us
  Pallas kernels  304 us (48%)
  waiting for transfers between devices  120 us (19%)
  starting transfers between devices  86.6 us (14%)
  other arithmetic  85.1 us (13%)
  local copies, waits for them, and re-layouts  30.8 us (5%)
    ppermute x104, waiting for transfers between devices, swap(): return lax.ppermute(value, AX, [(i, i ^ mask) for i in range(32)])  120 us
    ppermute x104, starting transfers between devices, swap(): return lax.ppermute(value, AX, [(i, i ^ mask) for i in range(32)])  86.6 us
    pallas_call x6, Pallas kernels, sum_call(): pl.pallas_call(partial(kernel, start, rows), grid_spec=pltpu.PrefetchScal...  71.5 us
    convert_element_type x24, other arithmetic, low(): return value.astype(BF16)  47.9 us
    pallas_call x2, Pallas kernels, contract(): pl.pallas_call(partial(contract_kernel, (len(leave), len(widen), len(narr...  47.8 us
    pallas_call x2, Pallas kernels, expand(): pl.pallas_call(partial(expand_kernel, (len(leave), len(widen), len(narrow...  47.8 us
    pallas_call x3, Pallas kernels, retrace(): pl.pallas_call(partial(retrace_kernel, stride, base), grid_spec=pltpu.Pre...  45.8 us
    pallas_call x3, Pallas kernels, input_grads(): pl.pallas_call(partial(inputs_kernel, stride, base, len(sources)), grid_s...  31.8 us
  transfers between devices with their start and end apart: 104, of which 33 were waited for; matrix products, arithmetic and copies ran while one was open for 13% of the time, Pallas kernels for 39%

profile of v2, /device:TPU:0, one launch (start us, length us, event | category | flops | bytes accessed | tf_op | source)
XLA Modules:
  0.0 629.6 jit_solution(2357950096179558352)
XLA Ops:
  7.6 5.1 collective-permute-start.3
  14.3 2.9 collective-permute-done.2
  17.9 3.5 collective-permute-start.7
  22.4 2.4 collective-permute-start.10
  24.8 7.7 %collective-permute-done.7 = bf16[4,48,384]{2,1,0:T(8,128)(2,1)S(1)} collective-permute-done((bf16[4,48,384]{2,1,0:T(8,128)(2,1)S(1)}, bf16[4,48,384]{2,1,0:T(8,128)(2,1)S(1)}, u32[]{:S(2)}, u32[]{:S(2)}) %collective-permute-start.7) | collective-permute-done | bytes 147488 | tf_op jit(solution)/shard_map/ppermute | solution.py:51
  41.8 20.0 %collective-permute-done.16 = bf16[2,4,48,768]{3,2,1,0:T(8,128)(2,1)S(1)} collective-permute-done((bf16[2,4,48,768]{3,2,1,0:T(8,128)(2,1)S(1)}, bf16[2,4,48,768]{3,2,1,0:T(8,128)(2,1)S(1)}, u32[]{:S(2)}, u32[]{:S(2)}) %collective-permute-start.16) | collective-permute-done | bytes 589856 | tf_op jit(solution)/shard_map/ppermute | solution.py:51
  73.6 5.4 prepare.1
  85.0 13.1 %project.2 = (f32[4,256,768]{2,1,0:T(8,128)}, bf16[4,256,768]{2,1,0:T(8,128)(2,1)}, bf16[4,256,768]{2,1,0:T(8,128)(2,1)}, bf16[4,512,768]{2,1,0:T(8,128)(2,1)}, bf16[4,512,768]{2,1,0:T(8,128)(2,1)}) custom-call(s32[4]{0:T(128)} %len_ref.15, s32[1]{0:T(128)} %bitcast.me_ref, bf16[4,512,768]{2,1,0:T(8,128)(2,1)} %b_ref.1, ...), custom_call_target="tpu_custom_call" | custom-call | flops 4831838208 | bytes 20000000 | tf_op jit(solution)/shard_map/project/pallas_call | solution.py:430
  98.2 9.9 %attend.4 = (bf16[4,256,768]{2,1,0:T(8,128)(2,1)}, bf16[4,12,512,256]{3,2,1,0:T(8,128)(2,1)}) custom-call(s32[4]{0:T(128)} %len_ref.15, s32[1]{0:T(128)} %bitcast.me_ref, bf16[4,256,768]{2,1,0:T(8,128)(2,1)} %get-tuple-element.483.q_ref, bf16[4,512,768]{2,1,0:T(8,128)(2,1)} %get-tuple-element.484.k_ref, bf16[4,512,768]{2,1,0:T(8,128)(2,1)} %get-tuple-element.485.v_ref, ...), custom_call_target="tpu_custom_call" | custom-call | flops 1610612736 | bytes 20000000 | tf_op jit(solution)/shard_map/attend/pallas_call | solution.py:493
  116.2 8.2 %attend.5 = (bf16[4,256,768]{2,1,0:T(8,128)(2,1)}, bf16[4,12,512,256]{3,2,1,0:T(8,128)(2,1)}) custom-call(s32[4]{0:T(128)} %len_ref.15, s32[1]{0:T(128)} %bitcast.me_ref, bf16[4,256,768]{2,1,0:T(8,128)(2,1)} %get-tuple-element.483.q_ref, bf16[4,512,768]{2,1,0:T(8,128)(2,1)} %get-tuple-element.484.k_ref, ...), custom_call_target="tpu_custom_call", output_to_operand_aliasing={{0}: (6, {}), {1}: (7, {})} | custom-call | flops 1610612736 | bytes 20000000 | tf_op jit(solution)/shard_map/attend/pallas_call | solution.py:493
  124.4 6.6 %collective-permute-done.34 = bf16[2,4,48,384]{3,2,1,0:T(8,128)(2,1)S(1)} collective-permute-done((bf16[2,4,48,384]{3,2,1,0:T(8,128)(2,1)S(1)}, bf16[2,4,48,384]{3,2,1,0:T(8,128)(2,1)S(1)}, u32[]{:S(2)}, u32[]{:S(2)}) %collective-permute-start.34) | collective-permute-done | bytes 294944 | tf_op jit(solution)/shard_map/ppermute | solution.py:51
  137.3 24.1 %expand.2 = (f32[1024,768]{1,0:T(8,128)}, bf16[1024,3072]{1,0:T(8,128)(2,1)}, bf16[1024,3072]{1,0:T(8,128)(2,1)}, f32[1024,768]{1,0:T(8,128)}, bf16[1024,768]{1,0:T(8,128)(2,1)}) custom-call(s32[1]{0:T(128)} %bitcast.me_ref, bf16[1024,768]{1,0:T(8,128)(2,1)} %bitcast.551, f32[1024,768]{1,0:T(8,128)} %bitcast.696, f32[8,768]{1,0:T(8,128)} %get-tuple-element.472.vec_ref, ...), custom_call_target="tpu_custom_call" | custom-call | flops 10871635968 | bytes 30000000 | tf_op jit(solution)/shard_map/expand/pallas_call | solution.py:563
  161.5 4.3 collective-permute-done.40
  169.0 7.7 %collective-permute-done.41.refs_3_ = bf16[2,4,48,384]{3,2,1,0:T(8,128)(2,1)S(1)} collective-permute-done((bf16[2,4,48,384]{3,2,1,0:T(8,128)(2,1)S(1)}, bf16[2,4,48,384]{3,2,1,0:T(8,128)(2,1)S(1)}, u32[]{:S(2)}, u32[]{:S(2)}) %collective-permute-start.41) | collective-permute-done | bytes 294944 | tf_op jit(solution)/shard_map/ppermute | solution.py:51
  182.0 9.9 %project.3 = (bf16[4,256,768]{2,1,0:T(8,128)(2,1)}, bf16[4,256,768]{2,1,0:T(8,128)(2,1)}, bf16[4,256,768]{2,1,0:T(8,128)(2,1)}) custom-call(s32[4]{0:T(128)} %and_select_fusion.len_ref, s32[1]{0:T(128)} %bitcast.me_ref, bf16[4,256,768]{2,1,0:T(8,128)(2,1)} %bitcast.697, f32[8,768]{1,0:T(8,128)} %get-tuple-element.544.vec_ref, ...), custom_call_target="tpu_custom_call" | custom-call | flops 2415919104 | bytes 20000000 | tf_op jit(solution)/shard_map/project/pallas_call | solution.py:430
  191.9 6.8 %attend.6 = (bf16[4,256,768]{2,1,0:T(8,128)(2,1)}, bf16[4,12,256,256]{3,2,1,0:T(8,128)(2,1)}) custom-call(s32[4]{0:T(128)} %and_select_fusion.len_ref, s32[1]{0:T(128)} %bitcast.me_ref, bf16[4,256,768]{2,1,0:T(8,128)(2,1)} %get-tuple-element.555.q_ref, bf16[4,256,768]{2,1,0:T(8,128)(2,1)} %get-tuple-element.556.k_ref, ...), custom_call_target="tpu_custom_call" | custom-call | flops 805306368 | bytes 20000000 | tf_op jit(solution)/shard_map/attend/pallas_call | solution.py:493
  198.8 8.8 %collective-permute-done.48.refs_11_.refs_21_ = bf16[4,4,48,768]{3,2,1,0:T(8,128)(2,1)} collective-permute-done((bf16[4,4,48,768]{3,2,1,0:T(8,128)(2,1)S(1)}, bf16[4,4,48,768]{3,2,1,0:T(8,128)(2,1)}, u32[]{:S(2)}, u32[]{:S(2)}) %collective-permute-start.48) | collective-permute-done | bytes 1179680 | tf_op jit(solution)/shard_map/ppermute | solution.py:51
  212.9 6.0 attend.7
  218.9 7.9 %collective-permute-done.51.refs_14_.refs_24_ = bf16[2,4,48,768]{3,2,1,0:T(8,128)(2,1)S(1)} collective-permute-done((bf16[2,4,48,768]{3,2,1,0:T(8,128)(2,1)S(1)}, bf16[2,4,48,768]{3,2,1,0:T(8,128)(2,1)S(1)}, u32[]{:S(2)}, u32[]{:S(2)}) %collective-permute-start.51) | collective-permute-done | bytes 589856 | tf_op jit(solution)/shard_map/ppermute | solution.py:51
  231.1 23.7 %expand.3 = (f32[1024,768]{1,0:T(8,128)}, bf16[1024,3072]{1,0:T(8,128)(2,1)}, bf16[1024,3072]{1,0:T(8,128)(2,1)}, f32[1024,768]{1,0:T(8,128)}, bf16[1024,768]{1,0:T(8,128)(2,1)}) custom-call(s32[1]{0:T(128)} %bitcast.me_ref, bf16[1024,768]{1,0:T(8,128)(2,1)} %bitcast.553, bf16[1024,768]{1,0:T(8,128)(2,1)} %get-tuple-element.525.resid_ref, ...), custom_call_target="tpu_custom_call" | custom-call | flops 10871635968 | bytes 30000000 | tf_op jit(solution)/shard_map/expand/pallas_call | solution.py:563
  254.8 23.9 %contract.2 = (bf16[1024,768]{1,0:T(8,128)(2,1)}, bf16[1024,768]{1,0:T(8,128)(2,1)}, bf16[1024,3072]{1,0:T(8,128)(2,1)}, bf16[1024,768]{1,0:T(8,128)(2,1)}, f32[...) custom-call(s32[1]{0:T(128)} %bitcast.me_ref, ...), custom_call_target="tpu_custom_call" | custom-call | flops 10871635968 | bytes 50000000 | tf_op jit(solution)/shard_map/contract/pallas_call | solution.py:650
  278.7 12.7 %narrow_grad.2 = (bf16[16,240,384]{2,1,0:T(8,128)(2,1)}, bf16[16,240,384]{2,1,0:T(8,128)(2,1)}) custom-call(s32[1]{0:T(128)} %bitcast.me_ref, bf16[1024,3072]{1,0:T(8,128)(2,1)} %get-tuple-element.596.act_ref, bf16[1024,768]{1,0:T(8,128)(2,1)} %get-tuple-element.597.dback_ref, bf16[1024,768]{1,0:T(8,128)(2,1)} %bitcast.554, ...), custom_call_target="tpu_custom_call" | custom-call | flops 6039797760 | bytes 16000000 | tf_op jit(solution)/shard_map/narrow_grad/pallas_call | solution.py:701
  291.6 11.1 %widen_grad.2 = (bf16[16,192,384]{2,1,0:T(8,128)(2,1)}, bf16[16,192,384]{2,1,0:T(8,128)(2,1)}) custom-call(s32[1]{0:T(128)} %bitcast.me_ref, bf16[1024,768]{1,0:T(8,128)(2,1)} %get-tuple-element.605.mixed_ref, bf16[1024,3072]{1,0:T(8,128)(2,1)} %get-tuple-element.606.dhid_ref), custom_call_target="tpu_custom_call" | custom-call | flops 4831838208 | bytes 16000000 | tf_op jit(solution)/shard_map/widen_grad/pallas_call | solution.py:701
  307.3 14.9 %retrace.3 = (bf16[4,256,768]{2,1,0:T(8,128)(2,1)}, bf16[4,256,768]{2,1,0:T(8,128)(2,1)}, bf16[4,256,768]{2,1,0:T(8,128)(2,1)}, f32[8,768]{1,0:T(8,128)}, f32[12...) custom-call(s32[4]{0:T(128)} %and_select_fusion.len_ref, s32[1]{0:T(128)} %bitcast.me_ref, ...), custom_call_target="tpu_custom_call" | custom-call | flops 2013265920 | bytes 20000000 | tf_op jit(solution)/shard_map/retrace/pallas_call | solution.py:962
  326.6 3.0 fusion.2
  329.6 2.7 collective-permute-start.63
  337.3 10.4 %input_grads.3 = f32[4,256,768]{2,1,0:T(8,128)} custom-call(s32[4]{0:T(128)} %and_select_fusion.len_ref, s32[1]{0:T(128)} %bitcast.me_ref, bf16[4,256,768]{2,1,0:T(8,128)(2,1)} %get-tuple-element.625.dq_ref, bf16[4,256,768]{2,1,0:T(8,128)(2,1)} %get-tuple-element.626.dk_ref, bf16[4,256,768]{2,1,0:T(8,128)(2,1)} %get-tuple-element.627.dv_ref, ...), custom_call_target="tpu_custom_call" | custom-call | flops 2415919104 | bytes 20000000 | tf_op jit(solution)/shard_map/input_grads/pallas_call | solution.py:1061
  347.7 11.3 %entry_grad.2 = (bf16[16,160,384]{2,1,0:T(8,128)(2,1)}, bf16[16,160,384]{2,1,0:T(8,128)(2,1)}) custom-call(s32[4]{0:T(128)} %and_select_fusion.len_ref, s32[1]{0:T(128)} %bitcast.me_ref, bf16[4,256,768]{2,1,0:T(8,128)(2,1)} %bitcast.698, bf16[4,256,768]{2,1,0:T(8,128)(2,1)} %bitcast.699, bf16[4,256,768]{2,1,0:T(8,128)(2,1)} %get-tuple-element.625.dq_ref, ...), custom_call_target="tpu_custom_call" | custom-call | flops 2415919104 | bytes 16000000 | tf_op jit(solution)/shard_map/entry_grad/pallas_call | solution.py:701
  361.6 2.6 fusion.6
  366.2 23.9 %contract.3 = (bf16[1024,768]{1,0:T(8,128)(2,1)}, bf16[1024,768]{1,0:T(8,128)(2,1)}, bf16[1024,3072]{1,0:T(8,128)(2,1)}, bf16[1024,768]{1,0:T(8,128)(2,1)}, f32[...) custom-call(s32[1]{0:T(128)} %bitcast.me_ref, f32[1024,768]{1,0:T(8,128)} %bitcast.519, ...), custom_call_target="tpu_custom_call" | custom-call | flops 10871635968 | bytes 50000000 | tf_op jit(solution)/shard_map/contract/pallas_call | solution.py:650
  401.7 12.6 %narrow_grad.3 = (bf16[16,240,384]{2,1,0:T(8,128)(2,1)}, bf16[16,240,384]{2,1,0:T(8,128)(2,1)}) custom-call(s32[1]{0:T(128)} %bitcast.me_ref, bf16[1024,3072]{1,0:T(8,128)(2,1)} %get-tuple-element.663.act_ref, bf16[1024,768]{1,0:T(8,128)(2,1)} %get-tuple-element.664.dback_ref, bf16[1024,768]{1,0:T(8,128)(2,1)} %bitcast.552, ...), custom_call_target="tpu_custom_call" | custom-call | flops 6039797760 | bytes 16000000 | tf_op jit(solution)/shard_map/narrow_grad/pallas_call | solution.py:701
  415.1 2.7 fusion.10
  423.8 10.9 %widen_grad.3 = (bf16[16,192,384]{2,1,0:T(8,128)(2,1)}, bf16[16,192,384]{2,1,0:T(8,128)(2,1)}) custom-call(s32[1]{0:T(128)} %bitcast.me_ref, bf16[1024,768]{1,0:T(8,128)(2,1)} %get-tuple-element.681.mixed_ref, bf16[1024,3072]{1,0:T(8,128)(2,1)} %get-tuple-element.682.dhid_ref), custom_call_target="tpu_custom_call" | custom-call | flops 4831838208 | bytes 16000000 | tf_op jit(solution)/shard_map/widen_grad/pallas_call | solution.py:701
  443.5 16.3 %retrace.4 = (bf16[4,256,768]{2,1,0:T(8,128)(2,1)}, bf16[4,512,768]{2,1,0:T(8,128)(2,1)}, bf16[4,512,768]{2,1,0:T(8,128)(2,1)}, f32[8,768]{1,0:T(8,128)}, f32[12...) custom-call(s32[4]{0:T(128)} %len_ref.15, s32[1]{0:T(128)} %bitcast.me_ref, ...), custom_call_target="tpu_custom_call" | custom-call | flops 2013265920 | bytes 20000000 | tf_op jit(solution)/shard_map/retrace/pallas_call | solution.py:962
  466.0 3.0 fusion
  469.0 14.7 %retrace.5 = (bf16[4,256,768]{2,1,0:T(8,128)(2,1)}, bf16[4,512,768]{2,1,0:T(8,128)(2,1)}, bf16[4,512,768]{2,1,0:T(8,128)(2,1)}, f32[8,768]{1,0:T(8,128)}, f32[12...) custom-call(s32[4]{0:T(128)} %len_ref.15, ...), custom_call_target="tpu_custom_call", output_to_operand_aliasing={{0}: (7, {}), {1}: (8, {}), {2}: (9, {})} | custom-call | flops 2013265920 | bytes 20000000 | tf_op jit(solution)/shard_map/retrace/pallas_call | solution.py:962
  487.8 3.5 collective-permute-start.83
  494.7 10.1 %collective-permute-done.84 = bf16[4,240,384]{2,1,0:T(8,128)(2,1)} collective-permute-done((bf16[4,240,384]{2,1,0:T(8,128)(2,1)}, bf16[4,240,384]{2,1,0:T(8,128)(2,1)}, u32[]{:S(2)}, u32[]{:S(2)}) %collective-permute-start.84) | collective-permute-done | bytes 737312 | tf_op jit(solution)/shard_map/ppermute | solution.py:51
  509.3 2.8 fusion.4
  516.8 2.6 collective-permute-start.88
  519.3 13.0 %entry_grad.3 = (bf16[16,160,384]{2,1,0:T(8,128)(2,1)}, bf16[16,160,384]{2,1,0:T(8,128)(2,1)}) custom-call(s32[4]{0:T(128)} %len_ref.15, s32[1]{0:T(128)} %bitcast.me_ref, bf16[4,256,768]{2,1,0:T(8,128)(2,1)} %get-tuple-element.748.a_ref, bf16[4,512,768]{2,1,0:T(8,128)(2,1)} %b_ref.1, bf16[4,256,768]{2,1,0:T(8,128)(2,1)} %get-tuple-element.749.dq_ref, ...), custom_call_target="tpu_custom_call" | custom-call | flops 3623878656 | bytes 16000000 | tf_op jit(solution)/shard_map/entry_grad/pallas_call | solution.py:701
  544.9 11.1 %input_grads.4.refs_10_ = f32[4,512,768]{2,1,0:T(8,128)} custom-call(s32[4]{0:T(128)} %len_ref.15, s32[1]{0:T(128)} %bitcast.me_ref, bf16[4,256,768]{2,1,0:T(8,128)(2,1)} %get-tuple-element.749.dq_ref, bf16[4,512,768]{2,1,0:T(8,128)(2,1)} %get-tuple-element.750.dk_ref, bf16[4,512,768]{2,1,0:T(8,128)(2,1)} %get-tuple-element.751.dv_ref, ...), custom_call_target="tpu_custom_call" | custom-call | flops 1811939328 | bytes 20000000 | tf_op jit(solution)/shard_map/input_grads/pallas_call | solution.py:1061
  556.0 3.3 collective-permute-start.92
  560.9 3.2 collective-permute-done.92
  573.3 10.3 %input_grads.5 = f32[4,512,768]{2,1,0:T(8,128)} custom-call(s32[4]{0:T(128)} %len_ref.15, s32[1]{0:T(128)} %bitcast.me_ref, bf16[4,256,768]{2,1,0:T(8,128)(2,1)} %get-tuple-element.749.dq_ref, bf16[4,512,768]{2,1,0:T(8,128)(2,1)} %get-tuple-element.750.dk_ref, bf16[4,512,768]{2,1,0:T(8,128)(2,1)} %get-tuple-element.751.dv_ref, ...), custom_call_target="tpu_custom_call", output_to_operand_aliasing={{}: (16, {})} | custom-call | flops 1811939328 | bytes 20000000 | tf_op jit(solution)/shard_map/input_grads/pallas_call | solution.py:1061
  592.6 9.8 %collective-permute-done.99 = bf16[4,160,384]{2,1,0:T(8,128)(2,1)S(1)} collective-permute-done((bf16[4,160,384]{2,1,0:T(8,128)(2,1)S(1)}, bf16[4,160,384]{2,1,0:T(8,128)(2,1)S(1)}, u32[]{:S(2)}, u32[]{:S(2)}) %collective-permute-start.99) | collective-permute-done | bytes 491552 | tf_op jit(solution)/shard_map/ppermute | solution.py:51
  609.5 8.6 %collective-permute-done.101 = bf16[2,160,384]{2,1,0:T(8,128)(2,1)S(1)} collective-permute-done((bf16[2,160,384]{2,1,0:T(8,128)(2,1)}, bf16[2,160,384]{2,1,0:T(8,128)(2,1)S(1)}, u32[]{:S(2)}, u32[]{:S(2)}) %collective-permute-start.101) | collective-permute-done | bytes 245792 | tf_op jit(solution)/shard_map/ppermute | solution.py:51
  620.6 3.8 collective-permute-done.102
  (510 shorter events, 183.9 us)
Async XLA Ops:
  37.8 24.1 %collective-permute-start.16 = (bf16[2,4,48,768]{3,2,1,0:T(8,128)(2,1)S(1)}, bf16[2,4,48,768]{3,2,1,0:T(8,128)(2,1)S(1)}, u32[]{:S(2)}, u32[]{:S(2)}) collective-permute-start(bf16[2,4,48,768]{3,2,1,0:T(8,128)(2,1)S(1)} %pad_maximum_fusion.3), channel_id=1, source_target_pairs={{0,16},{1,17},{2,18},{3,19},{4,20},{5,21},{6,22},{7,23},{8,24},{9,... | collective-permute-start | bytes 1769480 | tf_op jit(solution)/shard_map/ppermute | solution.py:51
  38.7 24.3 %collective-permute-start.14 = (bf16[4,4,48,384]{3,2,1,0:T(8,128)(2,1)S(1)}, bf16[4,4,48,384]{3,2,1,0:T(8,128)(2,1)S(1)}, u32[]{:S(2)}, u32[]{:S(2)}) collective-permute-start(bf16[4,4,48,384]{3,2,1,0:T(8,128)(2,1)S(1)} %pad_maximum_fusion.2.refs_0_), channel_id=1, source_target_pairs={{0,1},{1,0},{2,3},{3,2},{4,5},{5,4},{6,7},{7,6},{8,9},{9,8},{10,11... | collective-permute-start | bytes 1769480 | tf_op jit(solution)/shard_map/ppermute | solution.py:51
  38.7 24.3 %collective-permute-start.13 = (bf16[4,4,48,384]{3,2,1,0:T(8,128)(2,1)S(1)}, bf16[4,4,48,384]{3,2,1,0:T(8,128)(2,1)S(1)}, u32[]{:S(2)}, u32[]{:S(2)}) collective-permute-start(bf16[4,4,48,384]{3,2,1,0:T(8,128)(2,1)S(1)} %pad_maximum_fusion.2.refs_0_), channel_id=1, source_target_pairs={{0,2},{1,3},{2,0},{3,1},{4,6},{5,7},{6,4},{7,5},{8,10},{9,11},{10,... | collective-permute-start | bytes 1769480 | tf_op jit(solution)/shard_map/ppermute | solution.py:51
  40.2 22.8 %collective-permute-start.12 = (bf16[4,4,48,384]{3,2,1,0:T(8,128)(2,1)S(1)}, bf16[4,4,48,384]{3,2,1,0:T(8,128)(2,1)S(1)}, u32[]{:S(2)}, u32[]{:S(2)}) collective-permute-start(bf16[4,4,48,384]{3,2,1,0:T(8,128)(2,1)S(1)} %pad_maximum_fusion.2.refs_0_), channel_id=1, source_target_pairs={{0,4},{1,5},{2,6},{3,7},{4,0},{5,1},{6,2},{7,3},{8,12},{9,13},{10,... | collective-permute-start | bytes 1769480 | tf_op jit(solution)/shard_map/ppermute | solution.py:51
  41.8 21.2 %collective-permute-start.15 = (bf16[16,16,128]{2,1,0:T(8,128)(2,1)S(1)}, bf16[16,16,128]{2,1,0:T(8,128)(2,1)S(1)}, u32[]{:S(2)}, u32[]{:S(2)}) collective-permute-start(bf16[16,16,128]{2,1,0:T(8,128)(2,1)S(1)} %constant_dynamic-update-slice_fusion.near_ref), channel_id=1, source_target_pairs={{0,1},{1,0},{2,3},{3,2},{4,5},{5,4},{6,7},{7,6},{8,9},{9,8},{10,11... | collective-permute-start | bytes 196616 | tf_op jit(solution)/shard_map/ppermute | solution.py:51
  81.7 26.5 %collective-permute-start.27 = (bf16[4,4,48,768]{3,2,1,0:T(8,128)(2,1)}, bf16[4,4,48,768]{3,2,1,0:T(8,128)(2,1)}, u32[]{:S(2)}, u32[]{:S(2)}) collective-permute-start(bf16[4,4,48,768]{3,2,1,0:T(8,128)(2,1)} %pad_maximum_fusion.refs_10_.refs_20_), channel_id=1, source_target_pairs={{0,1},{1,0},{2,3},{3,2},{4,5},{5,4},{6,7},{7,6},{8,9},{9,8},{10,11... | collective-permute-start | bytes 3538952 | tf_op jit(solution)/shard_map/ppermute | solution.py:51
  81.9 28.5 %collective-permute-start.26 = (bf16[4,4,48,768]{3,2,1,0:T(8,128)(2,1)}, bf16[4,4,48,768]{3,2,1,0:T(8,128)(2,1)}, u32[]{:S(2)}, u32[]{:S(2)}) collective-permute-start(bf16[4,4,48,768]{3,2,1,0:T(8,128)(2,1)} %pad_maximum_fusion.refs_10_.refs_20_), channel_id=1, source_target_pairs={{0,2},{1,3},{2,0},{3,1},{4,6},{5,7},{6,4},{7,5},{8,10},{9,11},{10,... | collective-permute-start | bytes 3538952 | tf_op jit(solution)/shard_map/ppermute | solution.py:51
  82.5 28.2 %collective-permute-start.25 = (bf16[4,4,48,768]{3,2,1,0:T(8,128)(2,1)}, bf16[4,4,48,768]{3,2,1,0:T(8,128)(2,1)}, u32[]{:S(2)}, u32[]{:S(2)}) collective-permute-start(bf16[4,4,48,768]{3,2,1,0:T(8,128)(2,1)} %pad_maximum_fusion.refs_10_.refs_20_), channel_id=1, source_target_pairs={{0,4},{1,5},{2,6},{3,7},{4,0},{5,1},{6,2},{7,3},{8,12},{9,13},{10,... | collective-permute-start | bytes 3538952 | tf_op jit(solution)/shard_map/ppermute | solution.py:51
  83.0 25.1 %collective-permute-start.28 = (bf16[4,48,384]{2,1,0:T(8,128)(2,1)S(1)}, bf16[4,48,384]{2,1,0:T(8,128)(2,1)S(1)}, u32[]{:S(2)}, u32[]{:S(2)}) collective-permute-start(bf16[4,48,384]{2,1,0:T(8,128)(2,1)S(1)} %copy-done.21), channel_id=1, source_target_pairs={{0,8},{1,9},{2,10},{3,11},{4,12},{5,13},{6,14},{7,15},{8,0},{9,1},... | collective-permute-start | bytes 442376 | tf_op jit(solution)/shard_map/ppermute | solution.py:51
  83.7 24.4 %collective-permute-start.29 = (bf16[4,48,768]{2,1,0:T(8,128)(2,1)S(1)}, bf16[4,48,768]{2,1,0:T(8,128)(2,1)S(1)}, u32[]{:S(2)}, u32[]{:S(2)}) collective-permute-start(bf16[4,48,768]{2,1,0:T(8,128)(2,1)S(1)} %maximum_maximum_fusion.1), channel_id=1, source_target_pairs={{0,8},{1,9},{2,10},{3,11},{4,12},{5,13},{6,14},{7,15},{8,0},{9,1},... | collective-permute-start | bytes 884744 | tf_op jit(solution)/shard_map/ppermute | solution.py:51
  110.7 20.5 %collective-permute-start.33 = (bf16[4,4,48,768]{3,2,1,0:T(8,128)(2,1)}, bf16[4,4,48,768]{3,2,1,0:T(8,128)(2,1)S(1)}, u32[]{:S(2)}, u32[]{:S(2)}) collective-permute-start(bf16[4,4,48,768]{3,2,1,0:T(8,128)(2,1)} %collective-permute-done.25.refs_12_.refs_22_), channel_id=1, source_target_pairs={{0,1},{1,0},{2,3},{3,2},{4,5},{5,4},{6,7},{7,6},{8,9},{9,8},{10,11... | collective-permute-start | bytes 3538952 | tf_op jit(solution)/shard_map/ppermute | solution.py:51
  110.7 20.5 %collective-permute-start.32 = (bf16[4,4,48,768]{3,2,1,0:T(8,128)(2,1)}, bf16[4,4,48,768]{3,2,1,0:T(8,128)(2,1)}, u32[]{:S(2)}, u32[]{:S(2)}) collective-permute-start(bf16[4,4,48,768]{3,2,1,0:T(8,128)(2,1)} %collective-permute-done.26.refs_11_.refs_21_), channel_id=1, source_target_pairs={{0,1},{1,0},{2,3},{3,2},{4,5},{5,4},{6,7},{7,6},{8,9},{9,8},{10,11... | collective-permute-start | bytes 3538952 | tf_op jit(solution)/shard_map/ppermute | solution.py:51
  135.1 31.8 %collective-permute-start.39 = (bf16[4,4,48,384]{3,2,1,0:T(8,128)(2,1)S(1)}, bf16[4,4,48,384]{3,2,1,0:T(8,128)(2,1)S(1)}, u32[]{:S(2)}, u32[]{:S(2)}) collective-permute-start(bf16[4,4,48,384]{3,2,1,0:T(8,128)(2,1)S(1)} %pad_maximum_fusion.5.refs_0_), channel_id=1, source_target_pairs={{0,1},{1,0},{2,3},{3,2},{4,5},{5,4},{6,7},{7,6},{8,9},{9,8},{10,11... | collective-permute-start | bytes 1769480 | tf_op jit(solution)/shard_map/ppermute | solution.py:51
  135.3 31.7 %collective-permute-start.38 = (bf16[4,4,48,384]{3,2,1,0:T(8,128)(2,1)S(1)}, bf16[4,4,48,384]{3,2,1,0:T(8,128)(2,1)S(1)}, u32[]{:S(2)}, u32[]{:S(2)}) collective-permute-start(bf16[4,4,48,384]{3,2,1,0:T(8,128)(2,1)S(1)} %pad_maximum_fusion.5.refs_0_), channel_id=1, source_target_pairs={{0,2},{1,3},{2,0},{3,1},{4,6},{5,7},{6,4},{7,5},{8,10},{9,11},{10,... | collective-permute-start | bytes 1769480 | tf_op jit(solution)/shard_map/ppermute | solution.py:51
  135.8 31.1 %collective-permute-start.37 = (bf16[4,4,48,384]{3,2,1,0:T(8,128)(2,1)S(1)}, bf16[4,4,48,384]{3,2,1,0:T(8,128)(2,1)S(1)}, u32[]{:S(2)}, u32[]{:S(2)}) collective-permute-start(bf16[4,4,48,384]{3,2,1,0:T(8,128)(2,1)S(1)} %pad_maximum_fusion.5.refs_0_), channel_id=1, source_target_pairs={{0,4},{1,5},{2,6},{3,7},{4,0},{5,1},{6,2},{7,3},{8,12},{9,13},{10,... | collective-permute-start | bytes 1769480 | tf_op jit(solution)/shard_map/ppermute | solution.py:51
  137.3 28.4 %collective-permute-start.40 = (bf16[2,4,48,768]{3,2,1,0:T(8,128)(2,1)S(1)}, bf16[2,4,48,768]{3,2,1,0:T(8,128)(2,1)}, u32[]{:S(2)}, u32[]{:S(2)}) collective-permute-start(bf16[2,4,48,768]{3,2,1,0:T(8,128)(2,1)S(1)} %pad_maximum_fusion.4), channel_id=1, source_target_pairs={{0,16},{1,17},{2,18},{3,19},{4,20},{5,21},{6,22},{7,23},{8,24},{9,... | collective-permute-start | bytes 1769480 | tf_op jit(solution)/shard_map/ppermute | solution.py:51
  179.0 19.7 %collective-permute-start.49 = (bf16[4,4,48,768]{3,2,1,0:T(8,128)(2,1)S(1)}, bf16[4,4,48,768]{3,2,1,0:T(8,128)(2,1)}, u32[]{:S(2)}, u32[]{:S(2)}) collective-permute-start(bf16[4,4,48,768]{3,2,1,0:T(8,128)(2,1)S(1)} %pad_maximum_fusion.1.refs_10_.refs_20_), channel_id=1, source_target_pairs={{0,1},{1,0},{2,3},{3,2},{4,5},{5,4},{6,7},{7,6},{8,9},{9,8},{10,11... | collective-permute-start | bytes 3538952 | tf_op jit(solution)/shard_map/ppermute | solution.py:51
  179.2 28.4 %collective-permute-start.48 = (bf16[4,4,48,768]{3,2,1,0:T(8,128)(2,1)S(1)}, bf16[4,4,48,768]{3,2,1,0:T(8,128)(2,1)}, u32[]{:S(2)}, u32[]{:S(2)}) collective-permute-start(bf16[4,4,48,768]{3,2,1,0:T(8,128)(2,1)S(1)} %pad_maximum_fusion.1.refs_10_.refs_20_), channel_id=1, source_target_pairs={{0,2},{1,3},{2,0},{3,1},{4,6},{5,7},{6,4},{7,5},{8,10},{9,11},{10,... | collective-permute-start | bytes 3538952 | tf_op jit(solution)/shard_map/ppermute | solution.py:51
  180.7 28.1 %collective-permute-start.47 = (bf16[4,4,48,768]{3,2,1,0:T(8,128)(2,1)S(1)}, bf16[4,4,48,768]{3,2,1,0:T(8,128)(2,1)}, u32[]{:S(2)}, u32[]{:S(2)}) collective-permute-start(bf16[4,4,48,768]{3,2,1,0:T(8,128)(2,1)S(1)} %pad_maximum_fusion.1.refs_10_.refs_20_), channel_id=1, source_target_pairs={{0,4},{1,5},{2,6},{3,7},{4,0},{5,1},{6,2},{7,3},{8,12},{9,13},{10,... | collective-permute-start | bytes 3538952 | tf_op jit(solution)/shard_map/ppermute | solution.py:51
  208.8 18.5 %collective-permute-start.52 = (bf16[4,4,48,768]{3,2,1,0:T(8,128)(2,1)}, bf16[4,4,48,768]{3,2,1,0:T(8,128)(2,1)S(1)}, u32[]{:S(2)}, u32[]{:S(2)}) collective-permute-start(bf16[4,4,48,768]{3,2,1,0:T(8,128)(2,1)} %collective-permute-done.48.refs_11_.refs_21_), channel_id=1, source_target_pairs={{0,1},{1,0},{2,3},{3,2},{4,5},{5,4},{6,7},{7,6},{8,9},{9,8},{10,11... | collective-permute-start | bytes 3538952 | tf_op jit(solution)/shard_map/ppermute | solution.py:51
  302.7 23.9 %collective-permute-start.59 = (bf16[16,192,384]{2,1,0:T(8,128)(2,1)}, bf16[16,192,384]{2,1,0:T(8,128)(2,1)}, u32[]{:S(2)}, u32[]{:S(2)}) collective-permute-start(bf16[16,192,384]{2,1,0:T(8,128)(2,1)} %get-tuple-element.612), channel_id=1, source_target_pairs={{0,1},{1,0},{2,3},{3,2},{4,5},{5,4},{6,7},{7,6},{8,9},{9,8},{10,11... | collective-permute-start | bytes 7077896 | tf_op jit(solution)/shard_map/ppermute | solution.py:51
  305.4 21.2 %collective-permute-start.58 = (bf16[2,240,384]{2,1,0:T(8,128)(2,1)}, bf16[2,240,384]{2,1,0:T(8,128)(2,1)S(1)}, u32[]{:S(2)}, u32[]{:S(2)}) collective-permute-start(bf16[2,240,384]{2,1,0:T(8,128)(2,1)} %get-tuple-element.914), channel_id=1, source_target_pairs={{0,4},{1,5},{2,6},{3,7},{4,0},{5,1},{6,2},{7,3},{8,12},{9,13},{10,... | collective-permute-start | bytes 1105928 | tf_op jit(solution)/shard_map/ppermute | solution.py:51
  306.8 19.8 %collective-permute-start.57 = (bf16[2,240,384]{2,1,0:T(8,128)(2,1)}, bf16[2,240,384]{2,1,0:T(8,128)(2,1)}, u32[]{:S(2)}, u32[]{:S(2)}) collective-permute-start(bf16[2,240,384]{2,1,0:T(8,128)(2,1)} %get-tuple-element.915), channel_id=1, source_target_pairs={{0,2},{1,3},{2,0},{3,1},{4,6},{5,7},{6,4},{7,5},{8,10},{9,11},{10,... | collective-permute-start | bytes 1105928 | tf_op jit(solution)/shard_map/ppermute | solution.py:51
  329.6 29.4 %collective-permute-start.63 = (bf16[4,240,384]{2,1,0:T(8,128)(2,1)}, bf16[4,240,384]{2,1,0:T(8,128)(2,1)}, u32[]{:S(2)}, u32[]{:S(2)}) collective-permute-start(bf16[4,240,384]{2,1,0:T(8,128)(2,1)} %get-tuple-element.912), channel_id=1, source_target_pairs={{0,2},{1,3},{2,0},{3,1},{4,6},{5,7},{6,4},{7,5},{8,10},{9,11},{10,... | collective-permute-start | bytes 2211848 | tf_op jit(solution)/shard_map/ppermute | solution.py:51
  332.3 26.8 %collective-permute-start.62 = (bf16[4,240,384]{2,1,0:T(8,128)(2,1)}, bf16[4,240,384]{2,1,0:T(8,128)(2,1)}, u32[]{:S(2)}, u32[]{:S(2)}) collective-permute-start(bf16[4,240,384]{2,1,0:T(8,128)(2,1)} %get-tuple-element.913), channel_id=1, source_target_pairs={{0,4},{1,5},{2,6},{3,7},{4,0},{5,1},{6,2},{7,3},{8,12},{9,13},{10,... | collective-permute-start | bytes 2211848 | tf_op jit(solution)/shard_map/ppermute | solution.py:51
  335.2 23.8 %collective-permute-start.61 = (bf16[2,192,384]{2,1,0:T(8,128)(2,1)}, bf16[2,192,384]{2,1,0:T(8,128)(2,1)S(1)}, u32[]{:S(2)}, u32[]{:S(2)}) collective-permute-start(bf16[2,192,384]{2,1,0:T(8,128)(2,1)} %get-tuple-element.926), channel_id=1, source_target_pairs={{0,4},{1,5},{2,6},{3,7},{4,0},{5,1},{6,2},{7,3},{8,12},{9,13},{10,... | collective-permute-start | bytes 884744 | tf_op jit(solution)/shard_map/ppermute | solution.py:51
  337.3 21.8 %collective-permute-start.60 = (bf16[2,192,384]{2,1,0:T(8,128)(2,1)S(1)}, bf16[2,192,384]{2,1,0:T(8,128)(2,1)S(1)}, u32[]{:S(2)}, u32[]{:S(2)}) collective-permute-start(bf16[2,192,384]{2,1,0:T(8,128)(2,1)S(1)} %get-tuple-element.927), channel_id=1, source_target_pairs={{0,2},{1,3},{2,0},{3,1},{4,6},{5,7},{6,4},{7,5},{8,10},{9,11},{10,... | collective-permute-start | bytes 884744 | tf_op jit(solution)/shard_map/ppermute | solution.py:51
  359.1 31.1 %collective-permute-start.67 = (bf16[16,160,384]{2,1,0:T(8,128)(2,1)}, bf16[16,160,384]{2,1,0:T(8,128)(2,1)}, u32[]{:S(2)}, u32[]{:S(2)}) collective-permute-start(bf16[16,160,384]{2,1,0:T(8,128)(2,1)} %get-tuple-element.643), channel_id=1, source_target_pairs={{0,1},{1,0},{2,3},{3,2},{4,5},{5,4},{6,7},{7,6},{8,9},{9,8},{10,11... | collective-permute-start | bytes 5898248 | tf_op jit(solution)/shard_map/ppermute | solution.py:51
  361.5 28.6 %collective-permute-start.66 = (bf16[2,240,384]{2,1,0:T(8,128)(2,1)}, bf16[2,240,384]{2,1,0:T(8,128)(2,1)S(1)}, u32[]{:S(2)}, u32[]{:S(2)}) collective-permute-start(bf16[2,240,384]{2,1,0:T(8,128)(2,1)} %pad_maximum_fusion.6), channel_id=1, source_target_pairs={{0,16},{1,17},{2,18},{3,19},{4,20},{5,21},{6,22},{7,23},{8,24},{9,... | collective-permute-start | bytes 1105928 | tf_op jit(solution)/shard_map/ppermute | solution.py:51
  364.2 25.9 %collective-permute-start.65 = (bf16[4,192,384]{2,1,0:T(8,128)(2,1)}, bf16[4,192,384]{2,1,0:T(8,128)(2,1)S(1)}, u32[]{:S(2)}, u32[]{:S(2)}) collective-permute-start(bf16[4,192,384]{2,1,0:T(8,128)(2,1)} %get-tuple-element.924), channel_id=1, source_target_pairs={{0,2},{1,3},{2,0},{3,1},{4,6},{5,7},{6,4},{7,5},{8,10},{9,11},{10,... | collective-permute-start | bytes 1769480 | tf_op jit(solution)/shard_map/ppermute | solution.py:51
  366.2 23.9 %collective-permute-start.64 = (bf16[4,192,384]{2,1,0:T(8,128)(2,1)}, bf16[4,192,384]{2,1,0:T(8,128)(2,1)}, u32[]{:S(2)}, u32[]{:S(2)}) collective-permute-start(bf16[4,192,384]{2,1,0:T(8,128)(2,1)} %get-tuple-element.925), channel_id=1, source_target_pairs={{0,4},{1,5},{2,6},{3,7},{4,0},{5,1},{6,2},{7,3},{8,12},{9,13},{10,... | collective-permute-start | bytes 1769480 | tf_op jit(solution)/shard_map/ppermute | solution.py:51
  392.4 22.0 %collective-permute-start.71 = (bf16[240,384]{1,0:T(8,128)(2,1)}, bf16[240,384]{1,0:T(8,128)(2,1)}, u32[]{:S(2)}, u32[]{:S(2)}) collective-permute-start(bf16[240,384]{1,0:T(8,128)(2,1)} %fusion.29), channel_id=1, source_target_pairs={{0,8},{1,9},{2,10},{3,11},{4,12},{5,13},{6,14},{7,15},{8,0},{9,1},... | collective-permute-start | bytes 552968 | tf_op jit(solution)/shard_map/ppermute | solution.py:51
  415.1 19.6 %collective-permute-start.72 = (bf16[16,240,384]{2,1,0:T(8,128)(2,1)}, bf16[16,240,384]{2,1,0:T(8,128)(2,1)}, u32[]{:S(2)}, u32[]{:S(2)}) collective-permute-start(bf16[16,240,384]{2,1,0:T(8,128)(2,1)} %get-tuple-element.669), channel_id=1, source_target_pairs={{0,1},{1,0},{2,3},{3,2},{4,5},{5,4},{6,7},{7,6},{8,9},{9,8},{10,11... | collective-permute-start | bytes 8847368 | tf_op jit(solution)/shard_map/ppermute | solution.py:51
  434.8 25.1 %collective-permute-start.78 = (bf16[16,192,384]{2,1,0:T(8,128)(2,1)}, bf16[16,192,384]{2,1,0:T(8,128)(2,1)}, u32[]{:S(2)}, u32[]{:S(2)}) collective-permute-start(bf16[16,192,384]{2,1,0:T(8,128)(2,1)} %get-tuple-element.694), channel_id=1, source_target_pairs={{0,1},{1,0},{2,3},{3,2},{4,5},{5,4},{6,7},{7,6},{8,9},{9,8},{10,11... | collective-permute-start | bytes 7077896 | tf_op jit(solution)/shard_map/ppermute | solution.py:51
  436.5 23.3 %collective-permute-start.80 = (f32[120,384]{1,0:T(8,128)S(1)}, f32[120,384]{1,0:T(8,128)S(1)}, u32[]{:S(2)}, u32[]{:S(2)}) collective-permute-start(f32[120,384]{1,0:T(8,128)S(1)} %pad_maximum_fusion.17), channel_id=1, source_target_pairs={{0,1},{1,0},{2,3},{3,2},{4,5},{5,4},{6,7},{7,6},{8,9},{9,8},{10,11... | collective-permute-start | bytes 552968 | tf_op jit(solution)/shard_map/ppermute | solution.py:51
  439.3 20.5 %collective-permute-start.79 = (bf16[2,160,384]{2,1,0:T(8,128)(2,1)}, bf16[2,160,384]{2,1,0:T(8,128)(2,1)}, u32[]{:S(2)}, u32[]{:S(2)}) collective-permute-start(bf16[2,160,384]{2,1,0:T(8,128)(2,1)} %pad_maximum_fusion.13), channel_id=1, source_target_pairs={{0,16},{1,17},{2,18},{3,19},{4,20},{5,21},{6,22},{7,23},{8,24},{9,... | collective-permute-start | bytes 737288 | tf_op jit(solution)/shard_map/ppermute | solution.py:51
  461.8 33.0 %collective-permute-start.85 = (bf16[160,384]{1,0:T(8,128)(2,1)}, bf16[160,384]{1,0:T(8,128)(2,1)}, u32[]{:S(2)}, u32[]{:S(2)}) collective-permute-start(bf16[160,384]{1,0:T(8,128)(2,1)} %fusion.53), channel_id=1, source_target_pairs={{0,8},{1,9},{2,10},{3,11},{4,12},{5,13},{6,14},{7,15},{8,0},{9,1},... | collective-permute-start | bytes 368648 | tf_op jit(solution)/shard_map/ppermute | solution.py:51
  464.0 30.8 %collective-permute-start.82 = (bf16[2,192,384]{2,1,0:T(8,128)(2,1)}, bf16[2,192,384]{2,1,0:T(8,128)(2,1)}, u32[]{:S(2)}, u32[]{:S(2)}) collective-permute-start(bf16[2,192,384]{2,1,0:T(8,128)(2,1)} %get-tuple-element.922), channel_id=1, source_target_pairs={{0,4},{1,5},{2,6},{3,7},{4,0},{5,1},{6,2},{7,3},{8,12},{9,13},{10,... | collective-permute-start | bytes 884744 | tf_op jit(solution)/shard_map/ppermute | solution.py:51
  464.0 30.8 %collective-permute-start.81 = (bf16[2,192,384]{2,1,0:T(8,128)(2,1)}, bf16[2,192,384]{2,1,0:T(8,128)(2,1)}, u32[]{:S(2)}, u32[]{:S(2)}) collective-permute-start(bf16[2,192,384]{2,1,0:T(8,128)(2,1)} %get-tuple-element.923), channel_id=1, source_target_pairs={{0,2},{1,3},{2,0},{3,1},{4,6},{5,7},{6,4},{7,5},{8,10},{9,11},{10,... | collective-permute-start | bytes 884744 | tf_op jit(solution)/shard_map/ppermute | solution.py:51
  485.7 19.2 %collective-permute-start.84 = (bf16[4,240,384]{2,1,0:T(8,128)(2,1)}, bf16[4,240,384]{2,1,0:T(8,128)(2,1)}, u32[]{:S(2)}, u32[]{:S(2)}) collective-permute-start(bf16[4,240,384]{2,1,0:T(8,128)(2,1)} %get-tuple-element.906), channel_id=1, source_target_pairs={{0,2},{1,3},{2,0},{3,1},{4,6},{5,7},{6,4},{7,5},{8,10},{9,11},{10,... | collective-permute-start | bytes 2211848 | tf_op jit(solution)/shard_map/ppermute | solution.py:51
  487.8 19.3 %collective-permute-start.83 = (bf16[4,240,384]{2,1,0:T(8,128)(2,1)}, bf16[4,240,384]{2,1,0:T(8,128)(2,1)}, u32[]{:S(2)}, u32[]{:S(2)}) collective-permute-start(bf16[4,240,384]{2,1,0:T(8,128)(2,1)} %get-tuple-element.907), channel_id=1, source_target_pairs={{0,4},{1,5},{2,6},{3,7},{4,0},{5,1},{6,2},{7,3},{8,12},{9,13},{10,... | collective-permute-start | bytes 2211848 | tf_op jit(solution)/shard_map/ppermute | solution.py:51
  509.2 23.1 %collective-permute-start.89 = (f32[96,384]{1,0:T(8,128)S(1)}, f32[96,384]{1,0:T(8,128)S(1)}, u32[]{:S(2)}, u32[]{:S(2)}) collective-permute-start(f32[96,384]{1,0:T(8,128)S(1)} %pad_maximum_fusion.27), channel_id=1, source_target_pairs={{0,1},{1,0},{2,3},{3,2},{4,5},{5,4},{6,7},{7,6},{8,9},{9,8},{10,11... | collective-permute-start | bytes 442376 | tf_op jit(solution)/shard_map/ppermute | solution.py:51
  512.1 24.1 %collective-permute-start.87 = (bf16[4,192,384]{2,1,0:T(8,128)(2,1)}, bf16[4,192,384]{2,1,0:T(8,128)(2,1)}, u32[]{:S(2)}, u32[]{:S(2)}) collective-permute-start(bf16[4,192,384]{2,1,0:T(8,128)(2,1)} %get-tuple-element.920), channel_id=1, source_target_pairs={{0,2},{1,3},{2,0},{3,1},{4,6},{5,7},{6,4},{7,5},{8,10},{9,11},{10,... | collective-permute-start | bytes 1769480 | tf_op jit(solution)/shard_map/ppermute | solution.py:51
  513.8 22.5 %collective-permute-start.86 = (bf16[4,192,384]{2,1,0:T(8,128)(2,1)}, bf16[4,192,384]{2,1,0:T(8,128)(2,1)}, u32[]{:S(2)}, u32[]{:S(2)}) collective-permute-start(bf16[4,192,384]{2,1,0:T(8,128)(2,1)} %get-tuple-element.921), channel_id=1, source_target_pairs={{0,4},{1,5},{2,6},{3,7},{4,0},{5,1},{6,2},{7,3},{8,12},{9,13},{10,... | collective-permute-start | bytes 1769480 | tf_op jit(solution)/shard_map/ppermute | solution.py:51
  516.8 19.4 %collective-permute-start.88 = (bf16[2,240,384]{2,1,0:T(8,128)(2,1)}, bf16[2,240,384]{2,1,0:T(8,128)(2,1)S(1)}, u32[]{:S(2)}, u32[]{:S(2)}) collective-permute-start(bf16[2,240,384]{2,1,0:T(8,128)(2,1)} %pad_maximum_fusion.7), channel_id=1, source_target_pairs={{0,16},{1,17},{2,18},{3,19},{4,20},{5,21},{6,22},{7,23},{8,24},{9,... | collective-permute-start | bytes 1105928 | tf_op jit(solution)/shard_map/ppermute | solution.py:51
  537.0 27.1 %collective-permute-start.90 = (bf16[16,160,384]{2,1,0:T(8,128)(2,1)}, bf16[16,160,384]{2,1,0:T(8,128)(2,1)}, u32[]{:S(2)}, u32[]{:S(2)}) collective-permute-start(bf16[16,160,384]{2,1,0:T(8,128)(2,1)} %get-tuple-element.766), channel_id=1, source_target_pairs={{0,1},{1,0},{2,3},{3,2},{4,5},{5,4},{6,7},{7,6},{8,9},{9,8},{10,11... | collective-permute-start | bytes 5898248 | tf_op jit(solution)/shard_map/ppermute | solution.py:51
  540.3 19.0 %collective-permute-start.93 = (f32[72,384]{1,0:T(8,128)}, f32[72,384]{1,0:T(8,128)}, u32[]{:S(2)}, u32[]{:S(2)}) collective-permute-start(f32[72,384]{1,0:T(8,128)} %pad_maximum_fusion.31), channel_id=1, source_target_pairs={{0,1},{1,0},{2,3},{3,2},{4,5},{5,4},{6,7},{7,6},{8,9},{9,8},{10,11... | collective-permute-start | bytes 331784 | tf_op jit(solution)/shard_map/ppermute | solution.py:51
  543.0 21.0 %collective-permute-start.91 = (bf16[2,192,384]{2,1,0:T(8,128)(2,1)}, bf16[2,192,384]{2,1,0:T(8,128)(2,1)S(1)}, u32[]{:S(2)}, u32[]{:S(2)}) collective-permute-start(bf16[2,192,384]{2,1,0:T(8,128)(2,1)} %pad_maximum_fusion.10), channel_id=1, source_target_pairs={{0,16},{1,17},{2,18},{3,19},{4,20},{5,21},{6,22},{7,23},{8,24},{9,... | collective-permute-start | bytes 884744 | tf_op jit(solution)/shard_map/ppermute | solution.py:51
  (120 other events, 1188.1 us)

commit v3 on v2

--- a/solution.py
+++ b/solution.py
@@ -155,7 +155,7 @@
     )
 
 
-def reduce_stages(core, cuts, send, keep):
+def reduce_stages(core, cuts, direct, send, keep):
     shape = (4, 4) + keep.shape[1:]
     send, keep = yield send, keep
     keep = keep.reshape(shape)
@@ -175,11 +175,16 @@
     def part(k):
         return (wide(keep[0, k]) + wide(recv[0, k])) + (wide(from_y[k]) + wide(from_x[k]))
 
-    far = swap(jnp.stack([low(part(2)), low(part(3))]), Z1)
-    keep, recv, from_y, from_x, far = yield keep, recv, from_y, from_x, far
-    near = swap(low(part(1) + wide(far[1])), Z0)
-    keep, recv, from_y, from_x, far, near = yield keep, recv, from_y, from_x, far, near
-    total = part(0) + wide(far[0]) + wide(near)
+    if direct:
+        far = tuple(swap(low(part(k)), mask) for k, mask in ((1, Z0), (2, Z1), (3, Z0 | Z1)))
+        keep, recv, from_y, from_x, far = yield keep, recv, from_y, from_x, far
+        total = part(0) + wide(far[0]) + wide(far[1]) + wide(far[2])
+    else:
+        far = swap(jnp.stack([low(part(2)), low(part(3))]), Z1)
+        keep, recv, from_y, from_x, far = yield keep, recv, from_y, from_x, far
+        near = swap(low(part(1) + wide(far[1])), Z0)
+        keep, recv, from_y, from_x, far, near = yield keep, recv, from_y, from_x, far, near
+        total = part(0) + wide(far[0]) + wide(near)
     keeps, sends = [], []
     start = 0
     for rows, group in cuts:
@@ -1248,8 +1253,8 @@
         [], lambda me: expand(me, flatten(ctx2), first_out, vec2, bias2, *weights(1, "own"))
     )
 
-    def reducing(pair, cuts):
-        return Job(reduce_stages, core, cuts, *pair) if fast else pair
+    def reducing(pair, cuts, direct=False):
+        return Job(reduce_stages, core, cuts, direct, *pair) if fast else pair
 
     dback, mixed_low, dhid, dattn, du, dctx, dvec, dbias = tick(
         [],
@@ -1297,15 +1302,19 @@
         [sumw1, sumn1, sumw2],
         lambda me: entry_grad(160, 0, me, lengths, pooled_low, hidden, dq, dk, dv, packed, ()),
     )
-    sume1 = reducing(entry1, ENTRY_CUTS)
+    sume1 = reducing(entry1, ENTRY_CUTS, True)
     parts = (dq, dk, dv, du.reshape(q1.shape), *weights(0, "e"))
-    head = tick(
-        [sume1, sumw1, sumn1, sume2], lambda me: input_grads(2, me, lengths, *parts, 0, part)
-    )
-    hidden_grad = tick(
-        [sume1, sumw1, sumn1],
-        lambda me: input_grads(2, me, lengths, *parts, part, rows - part, (head,)),
-    )
+    ends = (0, 1, 2, rows) if rows > 2 else (0, rows)
+    beside = ([sume1, sumn1, sume2], [sume1, sumn1], [sume1, sumw1])
+    done = ()
+    for first, last, jobs in zip(ends, ends[1:], beside):
+        done = (
+            tick(
+                jobs,
+                lambda me: input_grads(2, me, lengths, *parts, first, last - first, done),
+            ),
+        )
+    (hidden_grad,) = done
     if fast:
         for job in (sume1, sumw1, sumn1, sumn2, sumw2, sume2):
             while job.result is None:

time: 637 us -> 625 us (0.981)
  waiting for transfers between devices: 120 us -> 93.3 us
  Pallas kernels: 304 us -> 318 us
    ppermute x104 -> x105, waiting for transfers between devices: 120 us -> 93.3 us  [swap(): return lax.ppermute(value, AX, [(i, i ^ mask) for i in range(32)])]
    pallas_call x3 -> x4, Pallas kernels: 31.8 us -> 38 us  [input_grads(): pl.pallas_call(partial(inputs_kernel, stride, base, len(sources)), grid_s...]
    ppermute x104 -> x105, starting transfers between devices: 86.6 us -> 88.8 us  [swap(): return lax.ppermute(value, AX, [(i, i ^ mask) for i in range(32)])]
    convert_element_type x24 -> x23, other arithmetic: 47.9 us -> 46.7 us  [low(): return value.astype(BF16)]
  transfers between devices with their start and end apart: 104 -> 105, of which waited for: 33 -> 30; matrix products, arithmetic and copies ran while one was open for 13% -> 13% of each run, Pallas kernels for 39% -> 42%
where the time goes in v3:
time: 625 us; the launch traced here: 616 us
  Pallas kernels  318 us (51%)
  waiting for transfers between devices  93.3 us (15%)
  starting transfers between devices  88.8 us (14%)
  other arithmetic  81.8 us (13%)
  local copies, waits for them, and re-layouts  31.3 us (5%)
    ppermute x105, waiting for transfers between devices, swap(): return lax.ppermute(value, AX, [(i, i ^ mask) for i in range(32)])  93.3 us
    ppermute x105, starting transfers between devices, swap(): return lax.ppermute(value, AX, [(i, i ^ mask) for i in range(32)])  88.8 us
    pallas_call x6, Pallas kernels, sum_call(): pl.pallas_call(partial(kernel, start, rows), grid_spec=pltpu.PrefetchScal...  72.3 us
    pallas_call x3, Pallas kernels, retrace(): pl.pallas_call(partial(retrace_kernel, stride, base), grid_spec=pltpu.Pre...  49.1 us
    pallas_call x2, Pallas kernels, contract(): pl.pallas_call(partial(contract_kernel, (len(leave), len(widen), len(narr...  47.9 us
    pallas_call x2, Pallas kernels, expand(): pl.pallas_call(partial(expand_kernel, (len(leave), len(widen), len(narrow...  47.9 us
    convert_element_type x23, other arithmetic, low(): return value.astype(BF16)  46.7 us
    pallas_call x4, Pallas kernels, input_grads(): pl.pallas_call(partial(inputs_kernel, stride, base, len(sources)), grid_s...  38 us
  transfers between devices with their start and end apart: 105, of which 30 were waited for; matrix products, arithmetic and copies ran while one was open for 13% of the time, Pallas kernels for 42%

profile of v3, /device:TPU:0, one launch (start us, length us, event | category | flops | bytes accessed | tf_op | source)
XLA Modules:
  0.0 616.2 jit_solution(7742000782685990020)
XLA Ops:
  7.6 5.1 collective-permute-start.3
  14.3 2.9 collective-permute-done.2
  17.9 3.5 collective-permute-start.7
  22.4 2.4 collective-permute-start.10
  24.8 7.7 %collective-permute-done.7 = bf16[4,48,384]{2,1,0:T(8,128)(2,1)S(1)} collective-permute-done((bf16[4,48,384]{2,1,0:T(8,128)(2,1)S(1)}, bf16[4,48,384]{2,1,0:T(8,128)(2,1)S(1)}, u32[]{:S(2)}, u32[]{:S(2)}) %collective-permute-start.7) | collective-permute-done | bytes 147488 | tf_op jit(solution)/shard_map/ppermute | solution.py:51
  41.8 20.0 %collective-permute-done.16 = bf16[2,4,48,768]{3,2,1,0:T(8,128)(2,1)S(1)} collective-permute-done((bf16[2,4,48,768]{3,2,1,0:T(8,128)(2,1)S(1)}, bf16[2,4,48,768]{3,2,1,0:T(8,128)(2,1)S(1)}, u32[]{:S(2)}, u32[]{:S(2)}) %collective-permute-start.16) | collective-permute-done | bytes 589856 | tf_op jit(solution)/shard_map/ppermute | solution.py:51
  74.1 5.4 prepare.1
  86.1 13.9 %project.2 = (f32[4,256,768]{2,1,0:T(8,128)}, bf16[4,256,768]{2,1,0:T(8,128)(2,1)}, bf16[4,256,768]{2,1,0:T(8,128)(2,1)}, bf16[4,512,768]{2,1,0:T(8,128)(2,1)}, bf16[4,512,768]{2,1,0:T(8,128)(2,1)}) custom-call(s32[4]{0:T(128)} %len_ref.17, s32[1]{0:T(128)} %bitcast.me_ref, bf16[4,512,768]{2,1,0:T(8,128)(2,1)} %b_ref.1, ...), custom_call_target="tpu_custom_call" | custom-call | flops 4831838208 | bytes 20000000 | tf_op jit(solution)/shard_map/project/pallas_call | solution.py:435
  100.0 7.4 %attend.4 = (bf16[4,256,768]{2,1,0:T(8,128)(2,1)}, bf16[4,12,512,256]{3,2,1,0:T(8,128)(2,1)}) custom-call(s32[4]{0:T(128)} %len_ref.17, s32[1]{0:T(128)} %bitcast.me_ref, bf16[4,256,768]{2,1,0:T(8,128)(2,1)} %get-tuple-element.483.q_ref, bf16[4,512,768]{2,1,0:T(8,128)(2,1)} %get-tuple-element.484.k_ref, bf16[4,512,768]{2,1,0:T(8,128)(2,1)} %get-tuple-element.485.v_ref, ...), custom_call_target="tpu_custom_call" | custom-call | flops 1610612736 | bytes 20000000 | tf_op jit(solution)/shard_map/attend/pallas_call | solution.py:498
  107.6 3.8 collective-permute-done.26.refs_11_.refs_21_
  117.5 12.5 %attend.5 = (bf16[4,256,768]{2,1,0:T(8,128)(2,1)}, bf16[4,12,512,256]{3,2,1,0:T(8,128)(2,1)}) custom-call(s32[4]{0:T(128)} %len_ref.17, s32[1]{0:T(128)} %bitcast.me_ref, bf16[4,256,768]{2,1,0:T(8,128)(2,1)} %get-tuple-element.483.q_ref, bf16[4,512,768]{2,1,0:T(8,128)(2,1)} %get-tuple-element.484.k_ref, ...), custom_call_target="tpu_custom_call", output_to_operand_aliasing={{0}: (6, {}), {1}: (7, {})} | custom-call | flops 1610612736 | bytes 20000000 | tf_op jit(solution)/shard_map/attend/pallas_call | solution.py:498
  130.0 3.0 collective-permute-done.34
  139.0 24.2 %expand.2 = (f32[1024,768]{1,0:T(8,128)}, bf16[1024,3072]{1,0:T(8,128)(2,1)}, bf16[1024,3072]{1,0:T(8,128)(2,1)}, f32[1024,768]{1,0:T(8,128)}, bf16[1024,768]{1,0:T(8,128)(2,1)}) custom-call(s32[1]{0:T(128)} %bitcast.me_ref, bf16[1024,768]{1,0:T(8,128)(2,1)} %bitcast.553, f32[1024,768]{1,0:T(8,128)} %bitcast.698, f32[8,768]{1,0:T(8,128)} %get-tuple-element.472.vec_ref, ...), custom_call_target="tpu_custom_call" | custom-call | flops 10871635968 | bytes 30000000 | tf_op jit(solution)/shard_map/expand/pallas_call | solution.py:568
  163.2 4.3 collective-permute-done.40
  169.2 8.1 %collective-permute-done.41.refs_3_ = bf16[2,4,48,384]{3,2,1,0:T(8,128)(2,1)S(1)} collective-permute-done((bf16[2,4,48,384]{3,2,1,0:T(8,128)(2,1)S(1)}, bf16[2,4,48,384]{3,2,1,0:T(8,128)(2,1)S(1)}, u32[]{:S(2)}, u32[]{:S(2)}) %collective-permute-start.41) | collective-permute-done | bytes 294944 | tf_op jit(solution)/shard_map/ppermute | solution.py:51
  182.4 9.9 %project.3 = (bf16[4,256,768]{2,1,0:T(8,128)(2,1)}, bf16[4,256,768]{2,1,0:T(8,128)(2,1)}, bf16[4,256,768]{2,1,0:T(8,128)(2,1)}) custom-call(s32[4]{0:T(128)} %and_select_fusion.len_ref, s32[1]{0:T(128)} %bitcast.me_ref, bf16[4,256,768]{2,1,0:T(8,128)(2,1)} %bitcast.699, f32[8,768]{1,0:T(8,128)} %get-tuple-element.544.vec_ref, ...), custom_call_target="tpu_custom_call" | custom-call | flops 2415919104 | bytes 20000000 | tf_op jit(solution)/shard_map/project/pallas_call | solution.py:435
  192.3 6.0 attend.6
  198.3 9.9 %collective-permute-done.48.refs_11_.refs_21_ = bf16[4,4,48,768]{3,2,1,0:T(8,128)(2,1)} collective-permute-done((bf16[4,4,48,768]{3,2,1,0:T(8,128)(2,1)S(1)}, bf16[4,4,48,768]{3,2,1,0:T(8,128)(2,1)}, u32[]{:S(2)}, u32[]{:S(2)}) %collective-permute-start.48) | collective-permute-done | bytes 1179680 | tf_op jit(solution)/shard_map/ppermute | solution.py:51
  213.2 7.7 %attend.7 = (bf16[4,256,768]{2,1,0:T(8,128)(2,1)}, bf16[4,12,256,256]{3,2,1,0:T(8,128)(2,1)}) custom-call(s32[4]{0:T(128)} %and_select_fusion.len_ref, s32[1]{0:T(128)} %bitcast.me_ref, bf16[4,256,768]{2,1,0:T(8,128)(2,1)} %get-tuple-element.555.q_ref, bf16[4,256,768]{2,1,0:T(8,128)(2,1)} %get-tuple-element.556.k_ref, ...), custom_call_target="tpu_custom_call", output_to_operand_aliasing={{0}: (6, {}), {1}: (7, {})} | custom-call | flops 805306368 | bytes 20000000 | tf_op jit(solution)/shard_map/attend/pallas_call | solution.py:498
  220.9 6.5 %collective-permute-done.51.refs_14_.refs_24_ = bf16[2,4,48,768]{3,2,1,0:T(8,128)(2,1)S(1)} collective-permute-done((bf16[2,4,48,768]{3,2,1,0:T(8,128)(2,1)S(1)}, bf16[2,4,48,768]{3,2,1,0:T(8,128)(2,1)S(1)}, u32[]{:S(2)}, u32[]{:S(2)}) %collective-permute-start.51) | collective-permute-done | bytes 589856 | tf_op jit(solution)/shard_map/ppermute | solution.py:51
  231.4 23.7 %expand.3 = (f32[1024,768]{1,0:T(8,128)}, bf16[1024,3072]{1,0:T(8,128)(2,1)}, bf16[1024,3072]{1,0:T(8,128)(2,1)}, f32[1024,768]{1,0:T(8,128)}, bf16[1024,768]{1,0:T(8,128)(2,1)}) custom-call(s32[1]{0:T(128)} %bitcast.me_ref, bf16[1024,768]{1,0:T(8,128)(2,1)} %bitcast.555, bf16[1024,768]{1,0:T(8,128)(2,1)} %get-tuple-element.525.resid_ref, ...), custom_call_target="tpu_custom_call" | custom-call | flops 10871635968 | bytes 30000000 | tf_op jit(solution)/shard_map/expand/pallas_call | solution.py:568
  255.1 24.0 %contract.2 = (bf16[1024,768]{1,0:T(8,128)(2,1)}, bf16[1024,768]{1,0:T(8,128)(2,1)}, bf16[1024,3072]{1,0:T(8,128)(2,1)}, bf16[1024,768]{1,0:T(8,128)(2,1)}, f32[...) custom-call(s32[1]{0:T(128)} %bitcast.me_ref, ...), custom_call_target="tpu_custom_call" | custom-call | flops 10871635968 | bytes 50000000 | tf_op jit(solution)/shard_map/contract/pallas_call | solution.py:655
  279.1 12.7 %narrow_grad.2 = (bf16[16,240,384]{2,1,0:T(8,128)(2,1)}, bf16[16,240,384]{2,1,0:T(8,128)(2,1)}) custom-call(s32[1]{0:T(128)} %bitcast.me_ref, bf16[1024,3072]{1,0:T(8,128)(2,1)} %get-tuple-element.596.act_ref, bf16[1024,768]{1,0:T(8,128)(2,1)} %get-tuple-element.597.dback_ref, bf16[1024,768]{1,0:T(8,128)(2,1)} %bitcast.556, ...), custom_call_target="tpu_custom_call" | custom-call | flops 6039797760 | bytes 16000000 | tf_op jit(solution)/shard_map/narrow_grad/pallas_call | solution.py:706
  292.0 11.0 %widen_grad.2 = (bf16[16,192,384]{2,1,0:T(8,128)(2,1)}, bf16[16,192,384]{2,1,0:T(8,128)(2,1)}) custom-call(s32[1]{0:T(128)} %bitcast.me_ref, bf16[1024,768]{1,0:T(8,128)(2,1)} %get-tuple-element.605.mixed_ref, bf16[1024,3072]{1,0:T(8,128)(2,1)} %get-tuple-element.606.dhid_ref), custom_call_target="tpu_custom_call" | custom-call | flops 4831838208 | bytes 16000000 | tf_op jit(solution)/shard_map/widen_grad/pallas_call | solution.py:706
  308.1 16.1 %retrace.3 = (bf16[4,256,768]{2,1,0:T(8,128)(2,1)}, bf16[4,256,768]{2,1,0:T(8,128)(2,1)}, bf16[4,256,768]{2,1,0:T(8,128)(2,1)}, f32[8,768]{1,0:T(8,128)}, f32[12...) custom-call(s32[4]{0:T(128)} %and_select_fusion.len_ref, s32[1]{0:T(128)} %bitcast.me_ref, ...), custom_call_target="tpu_custom_call" | custom-call | flops 2013265920 | bytes 20000000 | tf_op jit(solution)/shard_map/retrace/pallas_call | solution.py:967
  328.6 2.7 fusion.2
  338.4 10.4 %input_grads.4 = f32[4,256,768]{2,1,0:T(8,128)} custom-call(s32[4]{0:T(128)} %and_select_fusion.len_ref, s32[1]{0:T(128)} %bitcast.me_ref, bf16[4,256,768]{2,1,0:T(8,128)(2,1)} %get-tuple-element.625.dq_ref, bf16[4,256,768]{2,1,0:T(8,128)(2,1)} %get-tuple-element.626.dk_ref, bf16[4,256,768]{2,1,0:T(8,128)(2,1)} %get-tuple-element.627.dv_ref, ...), custom_call_target="tpu_custom_call" | custom-call | flops 2415919104 | bytes 20000000 | tf_op jit(solution)/shard_map/input_grads/pallas_call | solution.py:1066
  348.9 11.2 %entry_grad.2 = (bf16[16,160,384]{2,1,0:T(8,128)(2,1)}, bf16[16,160,384]{2,1,0:T(8,128)(2,1)}) custom-call(s32[4]{0:T(128)} %and_select_fusion.len_ref, s32[1]{0:T(128)} %bitcast.me_ref, bf16[4,256,768]{2,1,0:T(8,128)(2,1)} %bitcast.700, bf16[4,256,768]{2,1,0:T(8,128)(2,1)} %bitcast.701, bf16[4,256,768]{2,1,0:T(8,128)(2,1)} %get-tuple-element.625.dq_ref, ...), custom_call_target="tpu_custom_call" | custom-call | flops 2415919104 | bytes 16000000 | tf_op jit(solution)/shard_map/entry_grad/pallas_call | solution.py:706
  362.7 2.7 fusion.6
  366.9 23.9 %contract.3 = (bf16[1024,768]{1,0:T(8,128)(2,1)}, bf16[1024,768]{1,0:T(8,128)(2,1)}, bf16[1024,3072]{1,0:T(8,128)(2,1)}, bf16[1024,768]{1,0:T(8,128)(2,1)}, f32[...) custom-call(s32[1]{0:T(128)} %bitcast.me_ref, f32[1024,768]{1,0:T(8,128)} %bitcast.522, ...), custom_call_target="tpu_custom_call" | custom-call | flops 10871635968 | bytes 50000000 | tf_op jit(solution)/shard_map/contract/pallas_call | solution.py:655
  396.0 2.9 collective-permute-start.68
  403.2 12.7 %narrow_grad.3 = (bf16[16,240,384]{2,1,0:T(8,128)(2,1)}, bf16[16,240,384]{2,1,0:T(8,128)(2,1)}) custom-call(s32[1]{0:T(128)} %bitcast.me_ref, bf16[1024,3072]{1,0:T(8,128)(2,1)} %get-tuple-element.663.act_ref, bf16[1024,768]{1,0:T(8,128)(2,1)} %get-tuple-element.664.dback_ref, bf16[1024,768]{1,0:T(8,128)(2,1)} %bitcast.554, ...), custom_call_target="tpu_custom_call" | custom-call | flops 6039797760 | bytes 16000000 | tf_op jit(solution)/shard_map/narrow_grad/pallas_call | solution.py:706
  416.0 2.9 fusion.10
  424.0 10.9 %widen_grad.3 = (bf16[16,192,384]{2,1,0:T(8,128)(2,1)}, bf16[16,192,384]{2,1,0:T(8,128)(2,1)}) custom-call(s32[1]{0:T(128)} %bitcast.me_ref, bf16[1024,768]{1,0:T(8,128)(2,1)} %get-tuple-element.681.mixed_ref, bf16[1024,3072]{1,0:T(8,128)(2,1)} %get-tuple-element.682.dhid_ref), custom_call_target="tpu_custom_call" | custom-call | flops 4831838208 | bytes 16000000 | tf_op jit(solution)/shard_map/widen_grad/pallas_call | solution.py:706
  444.3 12.8 %retrace.4 = (bf16[4,256,768]{2,1,0:T(8,128)(2,1)}, bf16[4,512,768]{2,1,0:T(8,128)(2,1)}, bf16[4,512,768]{2,1,0:T(8,128)(2,1)}, f32[8,768]{1,0:T(8,128)}, f32[12...) custom-call(s32[4]{0:T(128)} %len_ref.17, s32[1]{0:T(128)} %bitcast.me_ref, ...), custom_call_target="tpu_custom_call" | custom-call | flops 2013265920 | bytes 20000000 | tf_op jit(solution)/shard_map/retrace/pallas_call | solution.py:967
  459.1 3.9 collective-permute-start.85
  465.2 4.5 collective-permute-start.81
  469.7 3.0 fusion
  472.7 20.2 %retrace.5 = (bf16[4,256,768]{2,1,0:T(8,128)(2,1)}, bf16[4,512,768]{2,1,0:T(8,128)(2,1)}, bf16[4,512,768]{2,1,0:T(8,128)(2,1)}, f32[8,768]{1,0:T(8,128)}, f32[12...) custom-call(s32[4]{0:T(128)} %len_ref.17, ...), custom_call_target="tpu_custom_call", output_to_operand_aliasing={{0}: (7, {}), {1}: (8, {}), {2}: (9, {})} | custom-call | flops 2013265920 | bytes 20000000 | tf_op jit(solution)/shard_map/retrace/pallas_call | solution.py:967
  499.2 7.6 %collective-permute-done.84 = bf16[4,240,384]{2,1,0:T(8,128)(2,1)} collective-permute-done((bf16[4,240,384]{2,1,0:T(8,128)(2,1)}, bf16[4,240,384]{2,1,0:T(8,128)(2,1)}, u32[]{:S(2)}, u32[]{:S(2)}) %collective-permute-start.84) | collective-permute-done | bytes 737312 | tf_op jit(solution)/shard_map/ppermute | solution.py:51
  509.0 2.8 fusion.4
  516.1 5.0 collective-permute-start.86
  521.1 13.7 %entry_grad.3 = (bf16[16,160,384]{2,1,0:T(8,128)(2,1)}, bf16[16,160,384]{2,1,0:T(8,128)(2,1)}) custom-call(s32[4]{0:T(128)} %len_ref.17, s32[1]{0:T(128)} %bitcast.me_ref, bf16[4,256,768]{2,1,0:T(8,128)(2,1)} %get-tuple-element.748.a_ref, bf16[4,512,768]{2,1,0:T(8,128)(2,1)} %b_ref.1, bf16[4,256,768]{2,1,0:T(8,128)(2,1)} %get-tuple-element.749.dq_ref, ...), custom_call_target="tpu_custom_call" | custom-call | flops 3623878656 | bytes 16000000 | tf_op jit(solution)/shard_map/entry_grad/pallas_call | solution.py:706
  542.4 7.9 %input_grads.5.refs_10_ = f32[4,512,768]{2,1,0:T(8,128)} custom-call(s32[4]{0:T(128)} %len_ref.17, s32[1]{0:T(128)} %bitcast.me_ref, bf16[4,256,768]{2,1,0:T(8,128)(2,1)} %get-tuple-element.749.dq_ref, bf16[4,512,768]{2,1,0:T(8,128)(2,1)} %get-tuple-element.750.dk_ref, bf16[4,512,768]{2,1,0:T(8,128)(2,1)} %get-tuple-element.751.dv_ref, ...), custom_call_target="tpu_custom_call" | custom-call | flops 905969664 | bytes 20000000 | tf_op jit(solution)/shard_map/input_grads/pallas_call | solution.py:1066
  556.6 7.9 %input_grads.6.refs_10_ = f32[4,512,768]{2,1,0:T(8,128)} custom-call(s32[4]{0:T(128)} %len_ref.17, s32[1]{0:T(128)} %bitcast.me_ref, bf16[4,256,768]{2,1,0:T(8,128)(2,1)} %get-tuple-element.749.dq_ref, bf16[4,512,768]{2,1,0:T(8,128)(2,1)} %get-tuple-element.750.dk_ref, ...), custom_call_target="tpu_custom_call", output_to_operand_aliasing={{}: (16, {})} | custom-call | flops 905969664 | bytes 20000000 | tf_op jit(solution)/shard_map/input_grads/pallas_call | solution.py:1066
  566.9 2.7 fusion.8
  580.6 11.8 %input_grads.7 = f32[4,512,768]{2,1,0:T(8,128)} custom-call(s32[4]{0:T(128)} %len_ref.17, s32[1]{0:T(128)} %bitcast.me_ref, bf16[4,256,768]{2,1,0:T(8,128)(2,1)} %get-tuple-element.749.dq_ref, bf16[4,512,768]{2,1,0:T(8,128)(2,1)} %get-tuple-element.750.dk_ref, bf16[4,512,768]{2,1,0:T(8,128)(2,1)} %get-tuple-element.751.dv_ref, ...), custom_call_target="tpu_custom_call", output_to_operand_aliasing={{}: (16, {})} | custom-call | flops 1811939328 | bytes 20000000 | tf_op jit(solution)/shard_map/input_grads/pallas_call | solution.py:1066
  603.8 5.0 collective-permute-done.100
  (493 shorter events, 172.3 us)
Async XLA Ops:
  37.8 24.1 %collective-permute-start.16 = (bf16[2,4,48,768]{3,2,1,0:T(8,128)(2,1)S(1)}, bf16[2,4,48,768]{3,2,1,0:T(8,128)(2,1)S(1)}, u32[]{:S(2)}, u32[]{:S(2)}) collective-permute-start(bf16[2,4,48,768]{3,2,1,0:T(8,128)(2,1)S(1)} %pad_maximum_fusion.3), channel_id=1, source_target_pairs={{0,16},{1,17},{2,18},{3,19},{4,20},{5,21},{6,22},{7,23},{8,24},{9,... | collective-permute-start | bytes 1769480 | tf_op jit(solution)/shard_map/ppermute | solution.py:51
  38.7 24.3 %collective-permute-start.14 = (bf16[4,4,48,384]{3,2,1,0:T(8,128)(2,1)S(1)}, bf16[4,4,48,384]{3,2,1,0:T(8,128)(2,1)S(1)}, u32[]{:S(2)}, u32[]{:S(2)}) collective-permute-start(bf16[4,4,48,384]{3,2,1,0:T(8,128)(2,1)S(1)} %pad_maximum_fusion.2.refs_0_), channel_id=1, source_target_pairs={{0,1},{1,0},{2,3},{3,2},{4,5},{5,4},{6,7},{7,6},{8,9},{9,8},{10,11... | collective-permute-start | bytes 1769480 | tf_op jit(solution)/shard_map/ppermute | solution.py:51
  38.7 24.3 %collective-permute-start.13 = (bf16[4,4,48,384]{3,2,1,0:T(8,128)(2,1)S(1)}, bf16[4,4,48,384]{3,2,1,0:T(8,128)(2,1)S(1)}, u32[]{:S(2)}, u32[]{:S(2)}) collective-permute-start(bf16[4,4,48,384]{3,2,1,0:T(8,128)(2,1)S(1)} %pad_maximum_fusion.2.refs_0_), channel_id=1, source_target_pairs={{0,2},{1,3},{2,0},{3,1},{4,6},{5,7},{6,4},{7,5},{8,10},{9,11},{10,... | collective-permute-start | bytes 1769480 | tf_op jit(solution)/shard_map/ppermute | solution.py:51
  40.2 22.8 %collective-permute-start.12 = (bf16[4,4,48,384]{3,2,1,0:T(8,128)(2,1)S(1)}, bf16[4,4,48,384]{3,2,1,0:T(8,128)(2,1)S(1)}, u32[]{:S(2)}, u32[]{:S(2)}) collective-permute-start(bf16[4,4,48,384]{3,2,1,0:T(8,128)(2,1)S(1)} %pad_maximum_fusion.2.refs_0_), channel_id=1, source_target_pairs={{0,4},{1,5},{2,6},{3,7},{4,0},{5,1},{6,2},{7,3},{8,12},{9,13},{10,... | collective-permute-start | bytes 1769480 | tf_op jit(solution)/shard_map/ppermute | solution.py:51
  41.8 21.2 %collective-permute-start.15 = (bf16[16,16,128]{2,1,0:T(8,128)(2,1)S(1)}, bf16[16,16,128]{2,1,0:T(8,128)(2,1)S(1)}, u32[]{:S(2)}, u32[]{:S(2)}) collective-permute-start(bf16[16,16,128]{2,1,0:T(8,128)(2,1)S(1)} %constant_dynamic-update-slice_fusion.near_ref), channel_id=1, source_target_pairs={{0,1},{1,0},{2,3},{3,2},{4,5},{5,4},{6,7},{7,6},{8,9},{9,8},{10,11... | collective-permute-start | bytes 196616 | tf_op jit(solution)/shard_map/ppermute | solution.py:51
  82.9 24.7 %collective-permute-start.27 = (bf16[4,4,48,768]{3,2,1,0:T(8,128)(2,1)S(1)}, bf16[4,4,48,768]{3,2,1,0:T(8,128)(2,1)}, u32[]{:S(2)}, u32[]{:S(2)}) collective-permute-start(bf16[4,4,48,768]{3,2,1,0:T(8,128)(2,1)S(1)} %copy-done.16), channel_id=1, source_target_pairs={{0,1},{1,0},{2,3},{3,2},{4,5},{5,4},{6,7},{7,6},{8,9},{9,8},{10,11... | collective-permute-start | bytes 3538952 | tf_op jit(solution)/shard_map/ppermute | solution.py:51
  83.0 28.3 %collective-permute-start.26 = (bf16[4,4,48,768]{3,2,1,0:T(8,128)(2,1)S(1)}, bf16[4,4,48,768]{3,2,1,0:T(8,128)(2,1)}, u32[]{:S(2)}, u32[]{:S(2)}) collective-permute-start(bf16[4,4,48,768]{3,2,1,0:T(8,128)(2,1)S(1)} %copy-done.16), channel_id=1, source_target_pairs={{0,2},{1,3},{2,0},{3,1},{4,6},{5,7},{6,4},{7,5},{8,10},{9,11},{10,... | collective-permute-start | bytes 3538952 | tf_op jit(solution)/shard_map/ppermute | solution.py:51
  83.6 28.1 %collective-permute-start.25 = (bf16[4,4,48,768]{3,2,1,0:T(8,128)(2,1)S(1)}, bf16[4,4,48,768]{3,2,1,0:T(8,128)(2,1)}, u32[]{:S(2)}, u32[]{:S(2)}) collective-permute-start(bf16[4,4,48,768]{3,2,1,0:T(8,128)(2,1)S(1)} %copy-done.16), channel_id=1, source_target_pairs={{0,4},{1,5},{2,6},{3,7},{4,0},{5,1},{6,2},{7,3},{8,12},{9,13},{10,... | collective-permute-start | bytes 3538952 | tf_op jit(solution)/shard_map/ppermute | solution.py:51
  84.1 23.4 %collective-permute-start.28 = (bf16[4,48,384]{2,1,0:T(8,128)(2,1)S(1)}, bf16[4,48,384]{2,1,0:T(8,128)(2,1)S(1)}, u32[]{:S(2)}, u32[]{:S(2)}) collective-permute-start(bf16[4,48,384]{2,1,0:T(8,128)(2,1)S(1)} %copy-done.22), channel_id=1, source_target_pairs={{0,8},{1,9},{2,10},{3,11},{4,12},{5,13},{6,14},{7,15},{8,0},{9,1},... | collective-permute-start | bytes 442376 | tf_op jit(solution)/shard_map/ppermute | solution.py:51
  84.8 22.7 %collective-permute-start.29 = (bf16[4,48,768]{2,1,0:T(8,128)(2,1)S(1)}, bf16[4,48,768]{2,1,0:T(8,128)(2,1)S(1)}, u32[]{:S(2)}, u32[]{:S(2)}) collective-permute-start(bf16[4,48,768]{2,1,0:T(8,128)(2,1)S(1)} %maximum_maximum_fusion.1), channel_id=1, source_target_pairs={{0,8},{1,9},{2,10},{3,11},{4,12},{5,13},{6,14},{7,15},{8,0},{9,1},... | collective-permute-start | bytes 884744 | tf_op jit(solution)/shard_map/ppermute | solution.py:51
  111.6 21.5 %collective-permute-start.33 = (bf16[4,4,48,768]{3,2,1,0:T(8,128)(2,1)}, bf16[4,4,48,768]{3,2,1,0:T(8,128)(2,1)}, u32[]{:S(2)}, u32[]{:S(2)}) collective-permute-start(bf16[4,4,48,768]{3,2,1,0:T(8,128)(2,1)} %collective-permute-done.25.refs_12_.refs_22_), channel_id=1, source_target_pairs={{0,1},{1,0},{2,3},{3,2},{4,5},{5,4},{6,7},{7,6},{8,9},{9,8},{10,11... | collective-permute-start | bytes 3538952 | tf_op jit(solution)/shard_map/ppermute | solution.py:51
  111.6 21.5 %collective-permute-start.32 = (bf16[4,4,48,768]{3,2,1,0:T(8,128)(2,1)}, bf16[4,4,48,768]{3,2,1,0:T(8,128)(2,1)}, u32[]{:S(2)}, u32[]{:S(2)}) collective-permute-start(bf16[4,4,48,768]{3,2,1,0:T(8,128)(2,1)} %collective-permute-done.26.refs_11_.refs_21_), channel_id=1, source_target_pairs={{0,1},{1,0},{2,3},{3,2},{4,5},{5,4},{6,7},{7,6},{8,9},{9,8},{10,11... | collective-permute-start | bytes 3538952 | tf_op jit(solution)/shard_map/ppermute | solution.py:51
  114.4 18.7 %collective-permute-start.31 = (bf16[2,4,48,768]{3,2,1,0:T(8,128)(2,1)S(1)}, bf16[2,4,48,768]{3,2,1,0:T(8,128)(2,1)S(1)}, u32[]{:S(2)}, u32[]{:S(2)}) collective-permute-start(bf16[2,4,48,768]{3,2,1,0:T(8,128)(2,1)S(1)} %slice.1074), channel_id=1, source_target_pairs={{0,4},{1,5},{2,6},{3,7},{4,0},{5,1},{6,2},{7,3},{8,12},{9,13},{10,... | collective-permute-start | bytes 1769480 | tf_op jit(solution)/shard_map/ppermute | solution.py:51
  114.9 18.2 %collective-permute-start.30 = (bf16[2,4,48,768]{3,2,1,0:T(8,128)(2,1)S(1)}, bf16[2,4,48,768]{3,2,1,0:T(8,128)(2,1)S(1)}, u32[]{:S(2)}, u32[]{:S(2)}) collective-permute-start(bf16[2,4,48,768]{3,2,1,0:T(8,128)(2,1)S(1)} %slice.1073), channel_id=1, source_target_pairs={{0,2},{1,3},{2,0},{3,1},{4,6},{5,7},{6,4},{7,5},{8,10},{9,11},{10,... | collective-permute-start | bytes 1769480 | tf_op jit(solution)/shard_map/ppermute | solution.py:51
  136.9 30.7 %collective-permute-start.39 = (bf16[4,4,48,384]{3,2,1,0:T(8,128)(2,1)S(1)}, bf16[4,4,48,384]{3,2,1,0:T(8,128)(2,1)}, u32[]{:S(2)}, u32[]{:S(2)}) collective-permute-start(bf16[4,4,48,384]{3,2,1,0:T(8,128)(2,1)S(1)} %pad_maximum_fusion.5.refs_0_), channel_id=1, source_target_pairs={{0,1},{1,0},{2,3},{3,2},{4,5},{5,4},{6,7},{7,6},{8,9},{9,8},{10,11... | collective-permute-start | bytes 1769480 | tf_op jit(solution)/shard_map/ppermute | solution.py:51
  137.0 30.6 %collective-permute-start.38 = (bf16[4,4,48,384]{3,2,1,0:T(8,128)(2,1)S(1)}, bf16[4,4,48,384]{3,2,1,0:T(8,128)(2,1)S(1)}, u32[]{:S(2)}, u32[]{:S(2)}) collective-permute-start(bf16[4,4,48,384]{3,2,1,0:T(8,128)(2,1)S(1)} %pad_maximum_fusion.5.refs_0_), channel_id=1, source_target_pairs={{0,2},{1,3},{2,0},{3,1},{4,6},{5,7},{6,4},{7,5},{8,10},{9,11},{10,... | collective-permute-start | bytes 1769480 | tf_op jit(solution)/shard_map/ppermute | solution.py:51
  137.4 30.2 %collective-permute-start.37 = (bf16[4,4,48,384]{3,2,1,0:T(8,128)(2,1)S(1)}, bf16[4,4,48,384]{3,2,1,0:T(8,128)(2,1)S(1)}, u32[]{:S(2)}, u32[]{:S(2)}) collective-permute-start(bf16[4,4,48,384]{3,2,1,0:T(8,128)(2,1)S(1)} %pad_maximum_fusion.5.refs_0_), channel_id=1, source_target_pairs={{0,4},{1,5},{2,6},{3,7},{4,0},{5,1},{6,2},{7,3},{8,12},{9,13},{10,... | collective-permute-start | bytes 1769480 | tf_op jit(solution)/shard_map/ppermute | solution.py:51
  139.0 28.5 %collective-permute-start.40 = (bf16[2,4,48,768]{3,2,1,0:T(8,128)(2,1)S(1)}, bf16[2,4,48,768]{3,2,1,0:T(8,128)(2,1)S(1)}, u32[]{:S(2)}, u32[]{:S(2)}) collective-permute-start(bf16[2,4,48,768]{3,2,1,0:T(8,128)(2,1)S(1)} %pad_maximum_fusion.4), channel_id=1, source_target_pairs={{0,16},{1,17},{2,18},{3,19},{4,20},{5,21},{6,22},{7,23},{8,24},{9,... | collective-permute-start | bytes 1769480 | tf_op jit(solution)/shard_map/ppermute | solution.py:51
  179.7 18.6 %collective-permute-start.49 = (bf16[4,4,48,768]{3,2,1,0:T(8,128)(2,1)S(1)}, bf16[4,4,48,768]{3,2,1,0:T(8,128)(2,1)}, u32[]{:S(2)}, u32[]{:S(2)}) collective-permute-start(bf16[4,4,48,768]{3,2,1,0:T(8,128)(2,1)S(1)} %pad_maximum_fusion.1.refs_10_.refs_20_), channel_id=1, source_target_pairs={{0,1},{1,0},{2,3},{3,2},{4,5},{5,4},{6,7},{7,6},{8,9},{9,8},{10,11... | collective-permute-start | bytes 3538952 | tf_op jit(solution)/shard_map/ppermute | solution.py:51
  180.0 28.2 %collective-permute-start.48 = (bf16[4,4,48,768]{3,2,1,0:T(8,128)(2,1)S(1)}, bf16[4,4,48,768]{3,2,1,0:T(8,128)(2,1)}, u32[]{:S(2)}, u32[]{:S(2)}) collective-permute-start(bf16[4,4,48,768]{3,2,1,0:T(8,128)(2,1)S(1)} %pad_maximum_fusion.1.refs_10_.refs_20_), channel_id=1, source_target_pairs={{0,2},{1,3},{2,0},{3,1},{4,6},{5,7},{6,4},{7,5},{8,10},{9,11},{10,... | collective-permute-start | bytes 3538952 | tf_op jit(solution)/shard_map/ppermute | solution.py:51
  181.5 27.9 %collective-permute-start.47 = (bf16[4,4,48,768]{3,2,1,0:T(8,128)(2,1)S(1)}, bf16[4,4,48,768]{3,2,1,0:T(8,128)(2,1)}, u32[]{:S(2)}, u32[]{:S(2)}) collective-permute-start(bf16[4,4,48,768]{3,2,1,0:T(8,128)(2,1)S(1)} %pad_maximum_fusion.1.refs_10_.refs_20_), channel_id=1, source_target_pairs={{0,4},{1,5},{2,6},{3,7},{4,0},{5,1},{6,2},{7,3},{8,12},{9,13},{10,... | collective-permute-start | bytes 3538952 | tf_op jit(solution)/shard_map/ppermute | solution.py:51
  209.4 18.2 %collective-permute-start.53 = (bf16[4,4,48,768]{3,2,1,0:T(8,128)(2,1)}, bf16[4,4,48,768]{3,2,1,0:T(8,128)(2,1)S(1)}, u32[]{:S(2)}, u32[]{:S(2)}) collective-permute-start(bf16[4,4,48,768]{3,2,1,0:T(8,128)(2,1)} %collective-permute-done.47.refs_12_.refs_22_), channel_id=1, source_target_pairs={{0,1},{1,0},{2,3},{3,2},{4,5},{5,4},{6,7},{7,6},{8,9},{9,8},{10,11... | collective-permute-start | bytes 3538952 | tf_op jit(solution)/shard_map/ppermute | solution.py:51
  209.4 18.2 %collective-permute-start.52 = (bf16[4,4,48,768]{3,2,1,0:T(8,128)(2,1)}, bf16[4,4,48,768]{3,2,1,0:T(8,128)(2,1)S(1)}, u32[]{:S(2)}, u32[]{:S(2)}) collective-permute-start(bf16[4,4,48,768]{3,2,1,0:T(8,128)(2,1)} %collective-permute-done.48.refs_11_.refs_21_), channel_id=1, source_target_pairs={{0,1},{1,0},{2,3},{3,2},{4,5},{5,4},{6,7},{7,6},{8,9},{9,8},{10,11... | collective-permute-start | bytes 3538952 | tf_op jit(solution)/shard_map/ppermute | solution.py:51
  303.1 25.5 %collective-permute-start.59 = (bf16[16,192,384]{2,1,0:T(8,128)(2,1)}, bf16[16,192,384]{2,1,0:T(8,128)(2,1)}, u32[]{:S(2)}, u32[]{:S(2)}) collective-permute-start(bf16[16,192,384]{2,1,0:T(8,128)(2,1)} %get-tuple-element.612), channel_id=1, source_target_pairs={{0,1},{1,0},{2,3},{3,2},{4,5},{5,4},{6,7},{7,6},{8,9},{9,8},{10,11... | collective-permute-start | bytes 7077896 | tf_op jit(solution)/shard_map/ppermute | solution.py:51
  305.8 22.8 %collective-permute-start.58 = (bf16[2,240,384]{2,1,0:T(8,128)(2,1)}, bf16[2,240,384]{2,1,0:T(8,128)(2,1)S(1)}, u32[]{:S(2)}, u32[]{:S(2)}) collective-permute-start(bf16[2,240,384]{2,1,0:T(8,128)(2,1)} %get-tuple-element.914), channel_id=1, source_target_pairs={{0,4},{1,5},{2,6},{3,7},{4,0},{5,1},{6,2},{7,3},{8,12},{9,13},{10,... | collective-permute-start | bytes 1105928 | tf_op jit(solution)/shard_map/ppermute | solution.py:51
  307.4 21.1 %collective-permute-start.57 = (bf16[2,240,384]{2,1,0:T(8,128)(2,1)}, bf16[2,240,384]{2,1,0:T(8,128)(2,1)}, u32[]{:S(2)}, u32[]{:S(2)}) collective-permute-start(bf16[2,240,384]{2,1,0:T(8,128)(2,1)} %get-tuple-element.915), channel_id=1, source_target_pairs={{0,2},{1,3},{2,0},{3,1},{4,6},{5,7},{6,4},{7,5},{8,10},{9,11},{10,... | collective-permute-start | bytes 1105928 | tf_op jit(solution)/shard_map/ppermute | solution.py:51
  331.3 28.9 %collective-permute-start.63 = (bf16[4,240,384]{2,1,0:T(8,128)(2,1)}, bf16[4,240,384]{2,1,0:T(8,128)(2,1)}, u32[]{:S(2)}, u32[]{:S(2)}) collective-permute-start(bf16[4,240,384]{2,1,0:T(8,128)(2,1)} %get-tuple-element.912), channel_id=1, source_target_pairs={{0,2},{1,3},{2,0},{3,1},{4,6},{5,7},{6,4},{7,5},{8,10},{9,11},{10,... | collective-permute-start | bytes 2211848 | tf_op jit(solution)/shard_map/ppermute | solution.py:51
  332.7 27.4 %collective-permute-start.62 = (bf16[4,240,384]{2,1,0:T(8,128)(2,1)S(1)}, bf16[4,240,384]{2,1,0:T(8,128)(2,1)}, u32[]{:S(2)}, u32[]{:S(2)}) collective-permute-start(bf16[4,240,384]{2,1,0:T(8,128)(2,1)S(1)} %get-tuple-element.913), channel_id=1, source_target_pairs={{0,4},{1,5},{2,6},{3,7},{4,0},{5,1},{6,2},{7,3},{8,12},{9,13},{10,... | collective-permute-start | bytes 2211848 | tf_op jit(solution)/shard_map/ppermute | solution.py:51
  335.8 24.3 %collective-permute-start.61 = (bf16[2,192,384]{2,1,0:T(8,128)(2,1)}, bf16[2,192,384]{2,1,0:T(8,128)(2,1)S(1)}, u32[]{:S(2)}, u32[]{:S(2)}) collective-permute-start(bf16[2,192,384]{2,1,0:T(8,128)(2,1)} %get-tuple-element.927), channel_id=1, source_target_pairs={{0,4},{1,5},{2,6},{3,7},{4,0},{5,1},{6,2},{7,3},{8,12},{9,13},{10,... | collective-permute-start | bytes 884744 | tf_op jit(solution)/shard_map/ppermute | solution.py:51
  337.8 22.3 %collective-permute-start.60 = (bf16[2,192,384]{2,1,0:T(8,128)(2,1)}, bf16[2,192,384]{2,1,0:T(8,128)(2,1)}, u32[]{:S(2)}, u32[]{:S(2)}) collective-permute-start(bf16[2,192,384]{2,1,0:T(8,128)(2,1)} %get-tuple-element.928), channel_id=1, source_target_pairs={{0,2},{1,3},{2,0},{3,1},{4,6},{5,7},{6,4},{7,5},{8,10},{9,11},{10,... | collective-permute-start | bytes 884744 | tf_op jit(solution)/shard_map/ppermute | solution.py:51
  360.2 30.6 %collective-permute-start.67 = (bf16[16,160,384]{2,1,0:T(8,128)(2,1)}, bf16[16,160,384]{2,1,0:T(8,128)(2,1)}, u32[]{:S(2)}, u32[]{:S(2)}) collective-permute-start(bf16[16,160,384]{2,1,0:T(8,128)(2,1)} %get-tuple-element.643), channel_id=1, source_target_pairs={{0,1},{1,0},{2,3},{3,2},{4,5},{5,4},{6,7},{7,6},{8,9},{9,8},{10,11... | collective-permute-start | bytes 5898248 | tf_op jit(solution)/shard_map/ppermute | solution.py:51
  362.7 28.1 %collective-permute-start.66 = (bf16[2,240,384]{2,1,0:T(8,128)(2,1)}, bf16[2,240,384]{2,1,0:T(8,128)(2,1)}, u32[]{:S(2)}, u32[]{:S(2)}) collective-permute-start(bf16[2,240,384]{2,1,0:T(8,128)(2,1)} %pad_maximum_fusion.6), channel_id=1, source_target_pairs={{0,16},{1,17},{2,18},{3,19},{4,20},{5,21},{6,22},{7,23},{8,24},{9,... | collective-permute-start | bytes 1105928 | tf_op jit(solution)/shard_map/ppermute | solution.py:51
  365.4 25.4 %collective-permute-start.65 = (bf16[4,192,384]{2,1,0:T(8,128)(2,1)}, bf16[4,192,384]{2,1,0:T(8,128)(2,1)S(1)}, u32[]{:S(2)}, u32[]{:S(2)}) collective-permute-start(bf16[4,192,384]{2,1,0:T(8,128)(2,1)} %get-tuple-element.925), channel_id=1, source_target_pairs={{0,2},{1,3},{2,0},{3,1},{4,6},{5,7},{6,4},{7,5},{8,10},{9,11},{10,... | collective-permute-start | bytes 1769480 | tf_op jit(solution)/shard_map/ppermute | solution.py:51
  366.9 24.0 %collective-permute-start.64 = (bf16[4,192,384]{2,1,0:T(8,128)(2,1)}, bf16[4,192,384]{2,1,0:T(8,128)(2,1)S(1)}, u32[]{:S(2)}, u32[]{:S(2)}) collective-permute-start(bf16[4,192,384]{2,1,0:T(8,128)(2,1)} %get-tuple-element.926), channel_id=1, source_target_pairs={{0,4},{1,5},{2,6},{3,7},{4,0},{5,1},{6,2},{7,3},{8,12},{9,13},{10,... | collective-permute-start | bytes 1769480 | tf_op jit(solution)/shard_map/ppermute | solution.py:51
  393.2 22.6 %collective-permute-start.71 = (bf16[240,384]{1,0:T(8,128)(2,1)}, bf16[240,384]{1,0:T(8,128)(2,1)}, u32[]{:S(2)}, u32[]{:S(2)}) collective-permute-start(bf16[240,384]{1,0:T(8,128)(2,1)} %fusion.29), channel_id=1, source_target_pairs={{0,8},{1,9},{2,10},{3,11},{4,12},{5,13},{6,14},{7,15},{8,0},{9,1},... | collective-permute-start | bytes 552968 | tf_op jit(solution)/shard_map/ppermute | solution.py:51
  396.0 19.9 %collective-permute-start.68 = (bf16[2,192,384]{2,1,0:T(8,128)(2,1)}, bf16[2,192,384]{2,1,0:T(8,128)(2,1)}, u32[]{:S(2)}, u32[]{:S(2)}) collective-permute-start(bf16[2,192,384]{2,1,0:T(8,128)(2,1)} %pad_maximum_fusion.9), channel_id=1, source_target_pairs={{0,16},{1,17},{2,18},{3,19},{4,20},{5,21},{6,22},{7,23},{8,24},{9,... | collective-permute-start | bytes 884744 | tf_op jit(solution)/shard_map/ppermute | solution.py:51
  415.9 19.0 %collective-permute-start.72 = (bf16[16,240,384]{2,1,0:T(8,128)(2,1)}, bf16[16,240,384]{2,1,0:T(8,128)(2,1)}, u32[]{:S(2)}, u32[]{:S(2)}) collective-permute-start(bf16[16,240,384]{2,1,0:T(8,128)(2,1)} %get-tuple-element.669), channel_id=1, source_target_pairs={{0,1},{1,0},{2,3},{3,2},{4,5},{5,4},{6,7},{7,6},{8,9},{9,8},{10,11... | collective-permute-start | bytes 8847368 | tf_op jit(solution)/shard_map/ppermute | solution.py:51
  434.9 22.3 %collective-permute-start.78 = (bf16[16,192,384]{2,1,0:T(8,128)(2,1)}, bf16[16,192,384]{2,1,0:T(8,128)(2,1)}, u32[]{:S(2)}, u32[]{:S(2)}) collective-permute-start(bf16[16,192,384]{2,1,0:T(8,128)(2,1)} %get-tuple-element.694), channel_id=1, source_target_pairs={{0,1},{1,0},{2,3},{3,2},{4,5},{5,4},{6,7},{7,6},{8,9},{9,8},{10,11... | collective-permute-start | bytes 7077896 | tf_op jit(solution)/shard_map/ppermute | solution.py:51
  436.7 20.5 %collective-permute-start.80 = (f32[120,384]{1,0:T(8,128)S(1)}, f32[120,384]{1,0:T(8,128)S(1)}, u32[]{:S(2)}, u32[]{:S(2)}) collective-permute-start(f32[120,384]{1,0:T(8,128)S(1)} %pad_maximum_fusion.16), channel_id=1, source_target_pairs={{0,1},{1,0},{2,3},{3,2},{4,5},{5,4},{6,7},{7,6},{8,9},{9,8},{10,11... | collective-permute-start | bytes 552968 | tf_op jit(solution)/shard_map/ppermute | solution.py:51
  459.1 40.1 %collective-permute-start.85 = (bf16[160,384]{1,0:T(8,128)(2,1)}, bf16[160,384]{1,0:T(8,128)(2,1)}, u32[]{:S(2)}, u32[]{:S(2)}) collective-permute-start(bf16[160,384]{1,0:T(8,128)(2,1)} %fusion.51), channel_id=1, source_target_pairs={{0,8},{1,9},{2,10},{3,11},{4,12},{5,13},{6,14},{7,15},{8,0},{9,1},... | collective-permute-start | bytes 368648 | tf_op jit(solution)/shard_map/ppermute | solution.py:51
  465.2 34.0 %collective-permute-start.82 = (bf16[2,192,384]{2,1,0:T(8,128)(2,1)}, bf16[2,192,384]{2,1,0:T(8,128)(2,1)}, u32[]{:S(2)}, u32[]{:S(2)}) collective-permute-start(bf16[2,192,384]{2,1,0:T(8,128)(2,1)} %get-tuple-element.923), channel_id=1, source_target_pairs={{0,4},{1,5},{2,6},{3,7},{4,0},{5,1},{6,2},{7,3},{8,12},{9,13},{10,... | collective-permute-start | bytes 884744 | tf_op jit(solution)/shard_map/ppermute | solution.py:51
  465.2 34.0 %collective-permute-start.81 = (bf16[2,192,384]{2,1,0:T(8,128)(2,1)}, bf16[2,192,384]{2,1,0:T(8,128)(2,1)}, u32[]{:S(2)}, u32[]{:S(2)}) collective-permute-start(bf16[2,192,384]{2,1,0:T(8,128)(2,1)} %get-tuple-element.924), channel_id=1, source_target_pairs={{0,2},{1,3},{2,0},{3,1},{4,6},{5,7},{6,4},{7,5},{8,10},{9,11},{10,... | collective-permute-start | bytes 884744 | tf_op jit(solution)/shard_map/ppermute | solution.py:51
  508.9 25.9 %collective-permute-start.89 = (f32[96,384]{1,0:T(8,128)S(1)}, f32[96,384]{1,0:T(8,128)}, u32[]{:S(2)}, u32[]{:S(2)}) collective-permute-start(f32[96,384]{1,0:T(8,128)S(1)} %pad_maximum_fusion.26), channel_id=1, source_target_pairs={{0,1},{1,0},{2,3},{3,2},{4,5},{5,4},{6,7},{7,6},{8,9},{9,8},{10,11... | collective-permute-start | bytes 442376 | tf_op jit(solution)/shard_map/ppermute | solution.py:51
  511.8 25.4 %collective-permute-start.88 = (bf16[4,192,384]{2,1,0:T(8,128)(2,1)}, bf16[4,192,384]{2,1,0:T(8,128)(2,1)S(1)}, u32[]{:S(2)}, u32[]{:S(2)}) collective-permute-start(bf16[4,192,384]{2,1,0:T(8,128)(2,1)} %get-tuple-element.921), channel_id=1, source_target_pairs={{0,2},{1,3},{2,0},{3,1},{4,6},{5,7},{6,4},{7,5},{8,10},{9,11},{10,... | collective-permute-start | bytes 1769480 | tf_op jit(solution)/shard_map/ppermute | solution.py:51
  513.8 23.5 %collective-permute-start.87 = (bf16[4,192,384]{2,1,0:T(8,128)(2,1)}, bf16[4,192,384]{2,1,0:T(8,128)(2,1)}, u32[]{:S(2)}, u32[]{:S(2)}) collective-permute-start(bf16[4,192,384]{2,1,0:T(8,128)(2,1)} %get-tuple-element.922), channel_id=1, source_target_pairs={{0,4},{1,5},{2,6},{3,7},{4,0},{5,1},{6,2},{7,3},{8,12},{9,13},{10,... | collective-permute-start | bytes 1769480 | tf_op jit(solution)/shard_map/ppermute | solution.py:51
  516.1 21.2 %collective-permute-start.86 = (bf16[2,240,384]{2,1,0:T(8,128)(2,1)}, bf16[2,240,384]{2,1,0:T(8,128)(2,1)}, u32[]{:S(2)}, u32[]{:S(2)}) collective-permute-start(bf16[2,240,384]{2,1,0:T(8,128)(2,1)} %pad_maximum_fusion.7), channel_id=1, source_target_pairs={{0,16},{1,17},{2,18},{3,19},{4,20},{5,21},{6,22},{7,23},{8,24},{9,... | collective-permute-start | bytes 1105928 | tf_op jit(solution)/shard_map/ppermute | solution.py:51
  569.6 22.8 %collective-permute-start.97 = (bf16[4,160,384]{2,1,0:T(8,128)(2,1)}, bf16[4,160,384]{2,1,0:T(8,128)(2,1)}, u32[]{:S(2)}, u32[]{:S(2)}) collective-permute-start(bf16[4,160,384]{2,1,0:T(8,128)(2,1)} %get-tuple-element.929), channel_id=1, source_target_pairs={{0,2},{1,3},{2,0},{3,1},{4,6},{5,7},{6,4},{7,5},{8,10},{9,11},{10,... | collective-permute-start | bytes 1474568 | tf_op jit(solution)/shard_map/ppermute | solution.py:51
  571.6 20.8 %collective-permute-start.96 = (bf16[4,160,384]{2,1,0:T(8,128)(2,1)}, bf16[4,160,384]{2,1,0:T(8,128)(2,1)}, u32[]{:S(2)}, u32[]{:S(2)}) collective-permute-start(bf16[4,160,384]{2,1,0:T(8,128)(2,1)} %get-tuple-element.930), channel_id=1, source_target_pairs={{0,4},{1,5},{2,6},{3,7},{4,0},{5,1},{6,2},{7,3},{8,12},{9,13},{10,... | collective-permute-start | bytes 1474568 | tf_op jit(solution)/shard_map/ppermute | solution.py:51
  (112 other events, 1123.9 us)

commit v4 on v3

--- a/solution.py
+++ b/solution.py
@@ -24,7 +24,7 @@
 NN = (((1,), (0,)), ((), ()))
 NT = (((1,), (1,)), ((), ()))
 TN = (((0,), (0,)), ((), ()))
-GROUPS = (6, 3, 2, 2)
+GROUPS = (6, 6, 3, 3)
 TILE_A = 256
 TILE_B = 256
 VMEM_LIMIT = 60 * 1024 * 1024
@@ -100,15 +100,23 @@
 def gather_stages(pair, direct, keep, send):
     keep, send = yield keep, send
     core = lax.axis_index(AX) % 2
-    recv = swap(send, CORE)
-    slab = pair(pick(core, keep, recv), pick(core, recv, keep))
+    recv = [swap(value, CORE) for value in send]
+    first = [pick(core, mine, other) for mine, other in zip(keep, recv)]
+    second = [pick(core, other, mine) for mine, other in zip(keep, recv)]
+    slab = pair(first, second)
     slab = yield slab
     if direct:
         own = jnp.stack([slab, swap(slab, Z0), swap(slab, Z1), swap(slab, Z0 | Z1)])
     else:
         two = jnp.stack([slab, swap(slab, Z0)])
         two = yield two
-        own = jnp.concatenate([two, swap(two, Z1)])
+        if direct is None:
+            far = swap(two[:, :2], Z1)
+            two, far = yield two, far
+            far = jnp.concatenate([far, swap(two[:, 2:], Z1)], axis=1)
+        else:
+            far = swap(two, Z1)
+        own = jnp.concatenate([two, far])
     own = yield own
     across_y = swap(own, YBIT)
     across_x = swap(own, XBIT)
@@ -131,27 +139,29 @@
 
 
 def pair_entry(first, second):
-    return jnp.concatenate([first.reshape(4, 24, HALF), second.reshape(4, 24, HALF)], axis=1)
+    return jnp.concatenate([first[0], second[0]], axis=1)
 
 
 def pair_wide(first, second):
-    widen = jnp.concatenate([first[:96].reshape(4, 24, HALF), second[:96].reshape(4, 24, HALF)], axis=1)
-    widen = widen.reshape(2, 2, 48, HALF).transpose(0, 2, 1, 3).reshape(2, 48, D)
-    narrow = jnp.concatenate([first[96:].reshape(2, 48, HALF), second[96:].reshape(2, 48, HALF)], axis=2)
+    widen = jnp.concatenate([first[0], second[0]], axis=0).reshape(48, 2, D).transpose(1, 0, 2)
+    narrow = jnp.concatenate([first[1].reshape(2, 48, HALF), second[1].reshape(2, 48, HALF)], axis=2)
     return jnp.concatenate([widen, narrow], axis=0)
 
 
-def gather_jobs(core, direct, entry, leave, widen, narrow):
-    def halved(value):
-        return pick(core, value[0], value[1]), pick(core, value[1], value[0])
-
-    eo = jnp.concatenate([entry, leave[None]]).reshape(96, 2, HALF).transpose(1, 0, 2)
-    widen = widen.reshape(24, 2, 4, HALF).transpose(1, 2, 0, 3).reshape(2, 96, HALF)
-    narrow = narrow.reshape(96, 2, HALF).transpose(1, 0, 2)
-    both = jnp.concatenate([widen, narrow], axis=1)
+def gather_jobs(core, ways, entry, leave, widen, narrow):
+    def halved(*values):
+        sides = []
+        for side in (core, 1 - core):
+            half = lambda value: value.shape[-1] // 2
+            sides.append(
+                [lax.dynamic_slice_in_dim(v, side * half(v), half(v), axis=-1) for v in values]
+            )
+        return sides
+
+    eo = jnp.concatenate([entry, leave[None]])
     return (
-        Job(gather_stages, pair_entry, direct, *halved(eo)),
-        Job(gather_stages, pair_wide, False, *halved(both)),
+        Job(gather_stages, pair_entry, ways[0], *halved(eo)),
+        Job(gather_stages, pair_wide, ways[1], *halved(widen, narrow)),
     )
 
 
@@ -1199,12 +1209,12 @@
         ticks = Ticks(index.astype(jnp.int32).reshape(1))
         tick = ticks.run
         vec = Job(vector_stages, vector_slab(*small))
-        eo1, w1 = gather_jobs(core, True, *layer_one)
-        eo2, w2 = gather_jobs(core, False, *layer_two)
+        eo1, w1 = gather_jobs(core, (True, None), *layer_one)
+        eo2, w2 = gather_jobs(core, (False, False), *layer_two)
         tick([eo1, vec, w1])
         tick([eo1, vec, w1])
         tick([eo1, vec, w1])
-        prepared = tick([eo1], lambda me: prepare(me, *vec.result, seq, half))
+        prepared = tick([eo1, w1], lambda me: prepare(me, *vec.result, seq, half))
         tick([eo1, eo2, w2])
     else:
         ticks = Ticks(jnp.zeros((1,), jnp.int32))

time: 625 us -> 616 us (0.986)
  local copies, waits for them, and re-layouts: 31.3 us -> 25 us
    ppermute x105 -> x108, waiting for transfers between devices: 93.3 us -> 97.2 us  [swap(): return lax.ppermute(value, AX, [(i, i ^ mask) for i in range(32)])]
    ppermute x105 -> x108, starting transfers between devices: 88.8 us -> 85.9 us  [swap(): return lax.ppermute(value, AX, [(i, i ^ mask) for i in range(32)])]
  transfers between devices with their start and end apart: 105 -> 108, of which waited for: 30 -> 35; matrix products, arithmetic and copies ran while one was open for 13% -> 13% of each run, Pallas kernels for 42% -> 42%
where the time goes in v4:
time: 616 us; the launch traced here: 610 us
  Pallas kernels  314 us (51%)
  waiting for transfers between devices  97.2 us (16%)
  starting transfers between devices  85.9 us (14%)
  other arithmetic  85 us (14%)
  local copies, waits for them, and re-layouts  25 us (4%)
    ppermute x108, waiting for transfers between devices, swap(): return lax.ppermute(value, AX, [(i, i ^ mask) for i in range(32)])  97.2 us
    ppermute x108, starting transfers between devices, swap(): return lax.ppermute(value, AX, [(i, i ^ mask) for i in range(32)])  85.9 us
    pallas_call x6, Pallas kernels, sum_call(): pl.pallas_call(partial(kernel, start, rows), grid_spec=pltpu.PrefetchScal...  71.8 us
    pallas_call x2, Pallas kernels, contract(): pl.pallas_call(partial(contract_kernel, (len(leave), len(widen), len(narr...  48.5 us
    convert_element_type x23, other arithmetic, low(): return value.astype(BF16)  47.4 us
    pallas_call x2, Pallas kernels, expand(): pl.pallas_call(partial(expand_kernel, (len(leave), len(widen), len(narrow...  47.3 us
    pallas_call x3, Pallas kernels, retrace(): pl.pallas_call(partial(retrace_kernel, stride, base), grid_spec=pltpu.Pre...  46.5 us
    pallas_call x4, Pallas kernels, input_grads(): pl.pallas_call(partial(inputs_kernel, stride, base, len(sources)), grid_s...  38.4 us
  transfers between devices with their start and end apart: 108, of which 35 were waited for; matrix products, arithmetic and copies ran while one was open for 13% of the time, Pallas kernels for 42%

profile of v4, /device:TPU:0, one launch (start us, length us, event | category | flops | bytes accessed | tf_op | source)
XLA Modules:
  0.0 609.8 jit_solution(563981675478223089)
XLA Ops:
  6.2 5.1 collective-permute-start.3
  12.9 2.9 collective-permute-done.2
  16.2 3.5 collective-permute-start.8
  20.6 2.4 collective-permute-start.11
  23.1 7.7 %collective-permute-done.8 = bf16[4,48,384]{2,1,0:T(8,128)(2,1)S(1)} collective-permute-done((bf16[4,48,384]{2,1,0:T(8,128)(2,1)S(1)}, bf16[4,48,384]{2,1,0:T(8,128)(2,1)S(1)}, u32[]{:S(2)}, u32[]{:S(2)}) %collective-permute-start.8) | collective-permute-done | bytes 147488 | tf_op jit(solution)/shard_map/ppermute | solution.py:51
  41.4 12.8 %collective-permute-done.16 = bf16[2,2,48,768]{3,2,1,0:T(8,128)(2,1)S(1)} collective-permute-done((bf16[2,2,48,768]{3,2,1,0:T(8,128)(2,1)S(1)}, bf16[2,2,48,768]{3,2,1,0:T(8,128)(2,1)S(1)}, u32[]{:S(2)}, u32[]{:S(2)}) %collective-permute-start.16) | collective-permute-done | bytes 294944 | tf_op jit(solution)/shard_map/ppermute | solution.py:51
  61.8 5.4 prepare.1
  67.2 4.0 collective-permute-done.22
  80.8 14.0 %project.2 = (f32[4,256,768]{2,1,0:T(8,128)}, bf16[4,256,768]{2,1,0:T(8,128)(2,1)}, bf16[4,256,768]{2,1,0:T(8,128)(2,1)}, bf16[4,512,768]{2,1,0:T(8,128)(2,1)}, bf16[4,512,768]{2,1,0:T(8,128)(2,1)}) custom-call(s32[4]{0:T(128)} %len_ref.17, s32[1]{0:T(128)} %bitcast.me_ref, bf16[4,512,768]{2,1,0:T(8,128)(2,1)} %b_ref.1, ...), custom_call_target="tpu_custom_call" | custom-call | flops 4831838208 | bytes 20000000 | tf_op jit(solution)/shard_map/project/pallas_call | solution.py:445
  94.8 9.0 %attend.4 = (bf16[4,256,768]{2,1,0:T(8,128)(2,1)}, bf16[4,12,512,256]{3,2,1,0:T(8,128)(2,1)}) custom-call(s32[4]{0:T(128)} %len_ref.17, s32[1]{0:T(128)} %bitcast.me_ref, bf16[4,256,768]{2,1,0:T(8,128)(2,1)} %get-tuple-element.495.q_ref, bf16[4,512,768]{2,1,0:T(8,128)(2,1)} %get-tuple-element.496.k_ref, bf16[4,512,768]{2,1,0:T(8,128)(2,1)} %get-tuple-element.497.v_ref, ...), custom_call_target="tpu_custom_call" | custom-call | flops 1610612736 | bytes 20000000 | tf_op jit(solution)/shard_map/attend/pallas_call | solution.py:508
  110.0 9.3 %attend.5 = (bf16[4,256,768]{2,1,0:T(8,128)(2,1)}, bf16[4,12,512,256]{3,2,1,0:T(8,128)(2,1)}) custom-call(s32[4]{0:T(128)} %len_ref.17, s32[1]{0:T(128)} %bitcast.me_ref, bf16[4,256,768]{2,1,0:T(8,128)(2,1)} %get-tuple-element.495.q_ref, bf16[4,512,768]{2,1,0:T(8,128)(2,1)} %get-tuple-element.496.k_ref, ...), custom_call_target="tpu_custom_call", output_to_operand_aliasing={{0}: (6, {}), {1}: (7, {})} | custom-call | flops 1610612736 | bytes 20000000 | tf_op jit(solution)/shard_map/attend/pallas_call | solution.py:508
  119.3 6.4 %collective-permute-done.37 = bf16[2,4,48,384]{3,2,1,0:T(8,128)(2,1)} collective-permute-done((bf16[2,4,48,384]{3,2,1,0:T(8,128)(2,1)S(1)}, bf16[2,4,48,384]{3,2,1,0:T(8,128)(2,1)}, u32[]{:S(2)}, u32[]{:S(2)}) %collective-permute-start.37) | collective-permute-done | bytes 294944 | tf_op jit(solution)/shard_map/ppermute | solution.py:51
  131.1 23.8 %expand.2 = (f32[1024,768]{1,0:T(8,128)}, bf16[1024,3072]{1,0:T(8,128)(2,1)}, bf16[1024,3072]{1,0:T(8,128)(2,1)}, f32[1024,768]{1,0:T(8,128)}, bf16[1024,768]{1,0:T(8,128)(2,1)}) custom-call(s32[1]{0:T(128)} %bitcast.me_ref, bf16[1024,768]{1,0:T(8,128)(2,1)} %bitcast.515, f32[1024,768]{1,0:T(8,128)} %bitcast.641, f32[8,768]{1,0:T(8,128)} %get-tuple-element.484.vec_ref, ...), custom_call_target="tpu_custom_call" | custom-call | flops 10871635968 | bytes 30000000 | tf_op jit(solution)/shard_map/expand/pallas_call | solution.py:578
  154.9 4.0 collective-permute-done.43
  163.3 6.5 %collective-permute-done.44.refs_3_ = bf16[2,4,48,384]{3,2,1,0:T(8,128)(2,1)S(1)} collective-permute-done((bf16[2,4,48,384]{3,2,1,0:T(8,128)(2,1)S(1)}, bf16[2,4,48,384]{3,2,1,0:T(8,128)(2,1)S(1)}, u32[]{:S(2)}, u32[]{:S(2)}) %collective-permute-start.44) | collective-permute-done | bytes 294944 | tf_op jit(solution)/shard_map/ppermute | solution.py:51
  175.3 9.9 %project.3 = (bf16[4,256,768]{2,1,0:T(8,128)(2,1)}, bf16[4,256,768]{2,1,0:T(8,128)(2,1)}, bf16[4,256,768]{2,1,0:T(8,128)(2,1)}) custom-call(s32[4]{0:T(128)} %and_select_fusion.len_ref, s32[1]{0:T(128)} %bitcast.me_ref, bf16[4,256,768]{2,1,0:T(8,128)(2,1)} %bitcast.642, f32[8,768]{1,0:T(8,128)} %get-tuple-element.556.vec_ref, ...), custom_call_target="tpu_custom_call" | custom-call | flops 2415919104 | bytes 20000000 | tf_op jit(solution)/shard_map/project/pallas_call | solution.py:445
  185.2 7.1 %attend.6 = (bf16[4,256,768]{2,1,0:T(8,128)(2,1)}, bf16[4,12,256,256]{3,2,1,0:T(8,128)(2,1)}) custom-call(s32[4]{0:T(128)} %and_select_fusion.len_ref, s32[1]{0:T(128)} %bitcast.me_ref, bf16[4,256,768]{2,1,0:T(8,128)(2,1)} %get-tuple-element.567.q_ref, bf16[4,256,768]{2,1,0:T(8,128)(2,1)} %get-tuple-element.568.k_ref, ...), custom_call_target="tpu_custom_call" | custom-call | flops 805306368 | bytes 20000000 | tf_op jit(solution)/shard_map/attend/pallas_call | solution.py:508
  192.3 8.7 %collective-permute-done.51.refs_11_.refs_21_ = bf16[4,4,48,768]{3,2,1,0:T(8,128)(2,1)} collective-permute-done((bf16[4,4,48,768]{3,2,1,0:T(8,128)(2,1)S(1)}, bf16[4,4,48,768]{3,2,1,0:T(8,128)(2,1)}, u32[]{:S(2)}, u32[]{:S(2)}) %collective-permute-start.51) | collective-permute-done | bytes 1179680 | tf_op jit(solution)/shard_map/ppermute | solution.py:51
  207.1 6.6 %attend.7 = (bf16[4,256,768]{2,1,0:T(8,128)(2,1)}, bf16[4,12,256,256]{3,2,1,0:T(8,128)(2,1)}) custom-call(s32[4]{0:T(128)} %and_select_fusion.len_ref, s32[1]{0:T(128)} %bitcast.me_ref, bf16[4,256,768]{2,1,0:T(8,128)(2,1)} %get-tuple-element.567.q_ref, bf16[4,256,768]{2,1,0:T(8,128)(2,1)} %get-tuple-element.568.k_ref, ...), custom_call_target="tpu_custom_call", output_to_operand_aliasing={{0}: (6, {}), {1}: (7, {})} | custom-call | flops 805306368 | bytes 20000000 | tf_op jit(solution)/shard_map/attend/pallas_call | solution.py:508
  213.7 6.1 %collective-permute-done.54.refs_14_.refs_24_ = bf16[2,4,48,768]{3,2,1,0:T(8,128)(2,1)S(1)} collective-permute-done((bf16[2,4,48,768]{3,2,1,0:T(8,128)(2,1)S(1)}, bf16[2,4,48,768]{3,2,1,0:T(8,128)(2,1)S(1)}, u32[]{:S(2)}, u32[]{:S(2)}) %collective-permute-start.54) | collective-permute-done | bytes 589856 | tf_op jit(solution)/shard_map/ppermute | solution.py:51
  224.5 23.5 %expand.3 = (f32[1024,768]{1,0:T(8,128)}, bf16[1024,3072]{1,0:T(8,128)(2,1)}, bf16[1024,3072]{1,0:T(8,128)(2,1)}, f32[1024,768]{1,0:T(8,128)}, bf16[1024,768]{1,0:T(8,128)(2,1)}) custom-call(s32[1]{0:T(128)} %bitcast.me_ref, bf16[1024,768]{1,0:T(8,128)(2,1)} %bitcast.517, bf16[1024,768]{1,0:T(8,128)(2,1)} %get-tuple-element.537.resid_ref, ...), custom_call_target="tpu_custom_call" | custom-call | flops 10871635968 | bytes 30000000 | tf_op jit(solution)/shard_map/expand/pallas_call | solution.py:578
  248.0 24.2 %contract.2 = (bf16[1024,768]{1,0:T(8,128)(2,1)}, bf16[1024,768]{1,0:T(8,128)(2,1)}, bf16[1024,3072]{1,0:T(8,128)(2,1)}, bf16[1024,768]{1,0:T(8,128)(2,1)}, f32[...) custom-call(s32[1]{0:T(128)} %bitcast.me_ref, ...), custom_call_target="tpu_custom_call" | custom-call | flops 10871635968 | bytes 50000000 | tf_op jit(solution)/shard_map/contract/pallas_call | solution.py:665
  272.2 12.7 %narrow_grad.2 = (bf16[16,240,384]{2,1,0:T(8,128)(2,1)}, bf16[16,240,384]{2,1,0:T(8,128)(2,1)}) custom-call(s32[1]{0:T(128)} %bitcast.me_ref, bf16[1024,3072]{1,0:T(8,128)(2,1)} %get-tuple-element.608.act_ref, bf16[1024,768]{1,0:T(8,128)(2,1)} %get-tuple-element.609.dback_ref, bf16[1024,768]{1,0:T(8,128)(2,1)} %bitcast.518, ...), custom_call_target="tpu_custom_call" | custom-call | flops 6039797760 | bytes 16000000 | tf_op jit(solution)/shard_map/narrow_grad/pallas_call | solution.py:716
  285.1 10.9 %widen_grad.2 = (bf16[16,192,384]{2,1,0:T(8,128)(2,1)}, bf16[16,192,384]{2,1,0:T(8,128)(2,1)}) custom-call(s32[1]{0:T(128)} %bitcast.me_ref, bf16[1024,768]{1,0:T(8,128)(2,1)} %get-tuple-element.617.mixed_ref, bf16[1024,3072]{1,0:T(8,128)(2,1)} %get-tuple-element.618.dhid_ref), custom_call_target="tpu_custom_call" | custom-call | flops 4831838208 | bytes 16000000 | tf_op jit(solution)/shard_map/widen_grad/pallas_call | solution.py:716
  300.6 15.9 %retrace.3 = (bf16[4,256,768]{2,1,0:T(8,128)(2,1)}, bf16[4,256,768]{2,1,0:T(8,128)(2,1)}, bf16[4,256,768]{2,1,0:T(8,128)(2,1)}, f32[8,768]{1,0:T(8,128)}, f32[12...) custom-call(s32[4]{0:T(128)} %and_select_fusion.len_ref, s32[1]{0:T(128)} %bitcast.me_ref, ...), custom_call_target="tpu_custom_call" | custom-call | flops 2013265920 | bytes 20000000 | tf_op jit(solution)/shard_map/retrace/pallas_call | solution.py:977
  320.9 3.0 fusion.2
  331.0 10.4 %input_grads.4 = f32[4,256,768]{2,1,0:T(8,128)} custom-call(s32[4]{0:T(128)} %and_select_fusion.len_ref, s32[1]{0:T(128)} %bitcast.me_ref, bf16[4,256,768]{2,1,0:T(8,128)(2,1)} %get-tuple-element.637.dq_ref, bf16[4,256,768]{2,1,0:T(8,128)(2,1)} %get-tuple-element.638.dk_ref, bf16[4,256,768]{2,1,0:T(8,128)(2,1)} %get-tuple-element.639.dv_ref, ...), custom_call_target="tpu_custom_call" | custom-call | flops 2415919104 | bytes 20000000 | tf_op jit(solution)/shard_map/input_grads/pallas_call | solution.py:1076
  341.4 11.0 %entry_grad.2 = (bf16[16,160,384]{2,1,0:T(8,128)(2,1)}, bf16[16,160,384]{2,1,0:T(8,128)(2,1)}) custom-call(s32[4]{0:T(128)} %and_select_fusion.len_ref, s32[1]{0:T(128)} %bitcast.me_ref, bf16[4,256,768]{2,1,0:T(8,128)(2,1)} %bitcast.643, bf16[4,256,768]{2,1,0:T(8,128)(2,1)} %bitcast.644, bf16[4,256,768]{2,1,0:T(8,128)(2,1)} %get-tuple-element.637.dq_ref, ...), custom_call_target="tpu_custom_call" | custom-call | flops 2415919104 | bytes 16000000 | tf_op jit(solution)/shard_map/entry_grad/pallas_call | solution.py:716
  355.0 2.7 fusion.6
  359.1 24.3 %contract.3 = (bf16[1024,768]{1,0:T(8,128)(2,1)}, bf16[1024,768]{1,0:T(8,128)(2,1)}, bf16[1024,3072]{1,0:T(8,128)(2,1)}, bf16[1024,768]{1,0:T(8,128)(2,1)}, f32[...) custom-call(s32[1]{0:T(128)} %bitcast.me_ref, f32[1024,768]{1,0:T(8,128)} %bitcast.484, ...), custom_call_target="tpu_custom_call" | custom-call | flops 10871635968 | bytes 50000000 | tf_op jit(solution)/shard_map/contract/pallas_call | solution.py:665
  385.7 3.7 collective-permute-start.74
  395.6 12.6 %narrow_grad.3 = (bf16[16,240,384]{2,1,0:T(8,128)(2,1)}, bf16[16,240,384]{2,1,0:T(8,128)(2,1)}) custom-call(s32[1]{0:T(128)} %bitcast.me_ref, bf16[1024,3072]{1,0:T(8,128)(2,1)} %get-tuple-element.675.act_ref, bf16[1024,768]{1,0:T(8,128)(2,1)} %get-tuple-element.676.dback_ref, bf16[1024,768]{1,0:T(8,128)(2,1)} %bitcast.516, ...), custom_call_target="tpu_custom_call" | custom-call | flops 6039797760 | bytes 16000000 | tf_op jit(solution)/shard_map/narrow_grad/pallas_call | solution.py:716
  409.0 2.7 fusion.10
  416.7 10.7 %widen_grad.3 = (bf16[16,192,384]{2,1,0:T(8,128)(2,1)}, bf16[16,192,384]{2,1,0:T(8,128)(2,1)}) custom-call(s32[1]{0:T(128)} %bitcast.me_ref, bf16[1024,768]{1,0:T(8,128)(2,1)} %get-tuple-element.693.mixed_ref, bf16[1024,3072]{1,0:T(8,128)(2,1)} %get-tuple-element.694.dhid_ref), custom_call_target="tpu_custom_call" | custom-call | flops 4831838208 | bytes 16000000 | tf_op jit(solution)/shard_map/widen_grad/pallas_call | solution.py:716
  438.5 15.2 %retrace.4 = (bf16[4,256,768]{2,1,0:T(8,128)(2,1)}, bf16[4,512,768]{2,1,0:T(8,128)(2,1)}, bf16[4,512,768]{2,1,0:T(8,128)(2,1)}, f32[8,768]{1,0:T(8,128)}, f32[12...) custom-call(s32[4]{0:T(128)} %len_ref.17, s32[1]{0:T(128)} %bitcast.me_ref, ...), custom_call_target="tpu_custom_call" | custom-call | flops 2013265920 | bytes 20000000 | tf_op jit(solution)/shard_map/retrace/pallas_call | solution.py:977
  460.7 3.0 fusion
  463.7 15.4 %retrace.5 = (bf16[4,256,768]{2,1,0:T(8,128)(2,1)}, bf16[4,512,768]{2,1,0:T(8,128)(2,1)}, bf16[4,512,768]{2,1,0:T(8,128)(2,1)}, f32[8,768]{1,0:T(8,128)}, f32[12...) custom-call(s32[4]{0:T(128)} %len_ref.17, ...), custom_call_target="tpu_custom_call", output_to_operand_aliasing={{0}: (7, {}), {1}: (8, {}), {2}: (9, {})} | custom-call | flops 2013265920 | bytes 20000000 | tf_op jit(solution)/shard_map/retrace/pallas_call | solution.py:977
  481.1 2.8 collective-permute-start.87
  488.0 12.0 %collective-permute-done.87 = bf16[4,240,384]{2,1,0:T(8,128)(2,1)} collective-permute-done((bf16[4,240,384]{2,1,0:T(8,128)(2,1)}, bf16[4,240,384]{2,1,0:T(8,128)(2,1)}, u32[]{:S(2)}, u32[]{:S(2)}) %collective-permute-start.87) | collective-permute-done | bytes 737312 | tf_op jit(solution)/shard_map/ppermute | solution.py:51
  506.3 2.8 fusion.4
  514.4 13.9 %entry_grad.3 = (bf16[16,160,384]{2,1,0:T(8,128)(2,1)}, bf16[16,160,384]{2,1,0:T(8,128)(2,1)}) custom-call(s32[4]{0:T(128)} %len_ref.17, s32[1]{0:T(128)} %bitcast.me_ref, bf16[4,256,768]{2,1,0:T(8,128)(2,1)} %get-tuple-element.760.a_ref, bf16[4,512,768]{2,1,0:T(8,128)(2,1)} %b_ref.1, bf16[4,256,768]{2,1,0:T(8,128)(2,1)} %get-tuple-element.761.dq_ref, ...), custom_call_target="tpu_custom_call" | custom-call | flops 3623878656 | bytes 16000000 | tf_op jit(solution)/shard_map/entry_grad/pallas_call | solution.py:716
  529.9 2.3 collective-permute-done.89
  538.1 8.6 %input_grads.5.refs_10_ = f32[4,512,768]{2,1,0:T(8,128)} custom-call(s32[4]{0:T(128)} %len_ref.17, s32[1]{0:T(128)} %bitcast.me_ref, bf16[4,256,768]{2,1,0:T(8,128)(2,1)} %get-tuple-element.761.dq_ref, bf16[4,512,768]{2,1,0:T(8,128)(2,1)} %get-tuple-element.762.dk_ref, bf16[4,512,768]{2,1,0:T(8,128)(2,1)} %get-tuple-element.763.dv_ref, ...), custom_call_target="tpu_custom_call" | custom-call | flops 905969664 | bytes 20000000 | tf_op jit(solution)/shard_map/input_grads/pallas_call | solution.py:1076
  552.5 8.0 %input_grads.6.refs_10_ = f32[4,512,768]{2,1,0:T(8,128)} custom-call(s32[4]{0:T(128)} %len_ref.17, s32[1]{0:T(128)} %bitcast.me_ref, bf16[4,256,768]{2,1,0:T(8,128)(2,1)} %get-tuple-element.761.dq_ref, bf16[4,512,768]{2,1,0:T(8,128)(2,1)} %get-tuple-element.762.dk_ref, ...), custom_call_target="tpu_custom_call", output_to_operand_aliasing={{}: (16, {})} | custom-call | flops 905969664 | bytes 20000000 | tf_op jit(solution)/shard_map/input_grads/pallas_call | solution.py:1076
  562.2 2.7 fusion.8
  569.1 2.6 collective-permute-start.101
  575.5 11.4 %input_grads.7 = f32[4,512,768]{2,1,0:T(8,128)} custom-call(s32[4]{0:T(128)} %len_ref.17, s32[1]{0:T(128)} %bitcast.me_ref, bf16[4,256,768]{2,1,0:T(8,128)(2,1)} %get-tuple-element.761.dq_ref, bf16[4,512,768]{2,1,0:T(8,128)(2,1)} %get-tuple-element.762.dk_ref, bf16[4,512,768]{2,1,0:T(8,128)(2,1)} %get-tuple-element.763.dv_ref, ...), custom_call_target="tpu_custom_call", output_to_operand_aliasing={{}: (16, {})} | custom-call | flops 1811939328 | bytes 20000000 | tf_op jit(solution)/shard_map/input_grads/pallas_call | solution.py:1076
  597.9 4.6 collective-permute-done.103
  (510 shorter events, 178.1 us)
Async XLA Ops:
  36.0 18.2 %collective-permute-start.15 = (bf16[4,4,48,384]{3,2,1,0:T(8,128)(2,1)S(1)}, bf16[4,4,48,384]{3,2,1,0:T(8,128)(2,1)S(1)}, u32[]{:S(2)}, u32[]{:S(2)}) collective-permute-start(bf16[4,4,48,384]{3,2,1,0:T(8,128)(2,1)S(1)} %pad_maximum_fusion.1.refs_0_), channel_id=1, source_target_pairs={{0,1},{1,0},{2,3},{3,2},{4,5},{5,4},{6,7},{7,6},{8,9},{9,8},{10,11... | collective-permute-start | bytes 1769480 | tf_op jit(solution)/shard_map/ppermute | solution.py:51
  36.0 18.2 %collective-permute-start.14 = (bf16[4,4,48,384]{3,2,1,0:T(8,128)(2,1)S(1)}, bf16[4,4,48,384]{3,2,1,0:T(8,128)(2,1)S(1)}, u32[]{:S(2)}, u32[]{:S(2)}) collective-permute-start(bf16[4,4,48,384]{3,2,1,0:T(8,128)(2,1)S(1)} %pad_maximum_fusion.1.refs_0_), channel_id=1, source_target_pairs={{0,2},{1,3},{2,0},{3,1},{4,6},{5,7},{6,4},{7,5},{8,10},{9,11},{10,... | collective-permute-start | bytes 1769480 | tf_op jit(solution)/shard_map/ppermute | solution.py:51
  55.7 17.8 %collective-permute-start.20 = (bf16[4,4,48,384]{3,2,1,0:T(8,128)(2,1)S(1)}, bf16[4,4,48,384]{3,2,1,0:T(8,128)(2,1)S(1)}, u32[]{:S(2)}, u32[]{:S(2)}) collective-permute-start(bf16[4,4,48,384]{3,2,1,0:T(8,128)(2,1)S(1)} %collective-permute-done.14.refs_1_), channel_id=1, source_target_pairs={{0,1},{1,0},{2,3},{3,2},{4,5},{5,4},{6,7},{7,6},{8,9},{9,8},{10,11... | collective-permute-start | bytes 1769480 | tf_op jit(solution)/shard_map/ppermute | solution.py:51
  76.3 28.5 %collective-permute-start.30 = (bf16[4,4,48,768]{3,2,1,0:T(8,128)(2,1)}, bf16[4,4,48,768]{3,2,1,0:T(8,128)(2,1)}, u32[]{:S(2)}, u32[]{:S(2)}) collective-permute-start(bf16[4,4,48,768]{3,2,1,0:T(8,128)(2,1)} %maximum_maximum_fusion.refs_10_.refs_20_), channel_id=1, source_target_pairs={{0,1},{1,0},{2,3},{3,2},{4,5},{5,4},{6,7},{7,6},{8,9},{9,8},{10,11... | collective-permute-start | bytes 3538952 | tf_op jit(solution)/shard_map/ppermute | solution.py:51
  76.7 28.2 %collective-permute-start.29 = (bf16[4,4,48,768]{3,2,1,0:T(8,128)(2,1)}, bf16[4,4,48,768]{3,2,1,0:T(8,128)(2,1)S(1)}, u32[]{:S(2)}, u32[]{:S(2)}) collective-permute-start(bf16[4,4,48,768]{3,2,1,0:T(8,128)(2,1)} %maximum_maximum_fusion.refs_10_.refs_20_), channel_id=1, source_target_pairs={{0,2},{1,3},{2,0},{3,1},{4,6},{5,7},{6,4},{7,5},{8,10},{9,11},{10,... | collective-permute-start | bytes 3538952 | tf_op jit(solution)/shard_map/ppermute | solution.py:51
  77.2 28.0 %collective-permute-start.28 = (bf16[4,4,48,768]{3,2,1,0:T(8,128)(2,1)}, bf16[4,4,48,768]{3,2,1,0:T(8,128)(2,1)}, u32[]{:S(2)}, u32[]{:S(2)}) collective-permute-start(bf16[4,4,48,768]{3,2,1,0:T(8,128)(2,1)} %maximum_maximum_fusion.refs_10_.refs_20_), channel_id=1, source_target_pairs={{0,4},{1,5},{2,6},{3,7},{4,0},{5,1},{6,2},{7,3},{8,12},{9,13},{10,... | collective-permute-start | bytes 3538952 | tf_op jit(solution)/shard_map/ppermute | solution.py:51
  78.7 25.0 %collective-permute-start.31 = (bf16[4,48,384]{2,1,0:T(8,128)(2,1)S(1)}, bf16[4,48,384]{2,1,0:T(8,128)(2,1)S(1)}, u32[]{:S(2)}, u32[]{:S(2)}) collective-permute-start(bf16[4,48,384]{2,1,0:T(8,128)(2,1)S(1)} %pad_maximum_fusion.21), channel_id=1, source_target_pairs={{0,8},{1,9},{2,10},{3,11},{4,12},{5,13},{6,14},{7,15},{8,0},{9,1},... | collective-permute-start | bytes 442376 | tf_op jit(solution)/shard_map/ppermute | solution.py:51
  78.7 25.1 %collective-permute-start.32 = (bf16[4,48,768]{2,1,0:T(8,128)(2,1)S(1)}, bf16[4,48,768]{2,1,0:T(8,128)(2,1)}, u32[]{:S(2)}, u32[]{:S(2)}) collective-permute-start(bf16[4,48,768]{2,1,0:T(8,128)(2,1)S(1)} %maximum_maximum_fusion.2), channel_id=1, source_target_pairs={{0,8},{1,9},{2,10},{3,11},{4,12},{5,13},{6,14},{7,15},{8,0},{9,1},... | collective-permute-start | bytes 884744 | tf_op jit(solution)/shard_map/ppermute | solution.py:51
  105.3 21.5 %collective-permute-start.36 = (bf16[4,4,48,768]{3,2,1,0:T(8,128)(2,1)}, bf16[4,4,48,768]{3,2,1,0:T(8,128)(2,1)}, u32[]{:S(2)}, u32[]{:S(2)}) collective-permute-start(bf16[4,4,48,768]{3,2,1,0:T(8,128)(2,1)} %collective-permute-done.28.refs_12_.refs_22_), channel_id=1, source_target_pairs={{0,1},{1,0},{2,3},{3,2},{4,5},{5,4},{6,7},{7,6},{8,9},{9,8},{10,11... | collective-permute-start | bytes 3538952 | tf_op jit(solution)/shard_map/ppermute | solution.py:51
  105.3 21.5 %collective-permute-start.35 = (bf16[4,4,48,768]{3,2,1,0:T(8,128)(2,1)S(1)}, bf16[4,4,48,768]{3,2,1,0:T(8,128)(2,1)}, u32[]{:S(2)}, u32[]{:S(2)}) collective-permute-start(bf16[4,4,48,768]{3,2,1,0:T(8,128)(2,1)S(1)} %collective-permute-done.29.refs_11_.refs_21_), channel_id=1, source_target_pairs={{0,1},{1,0},{2,3},{3,2},{4,5},{5,4},{6,7},{7,6},{8,9},{9,8},{10,11... | collective-permute-start | bytes 3538952 | tf_op jit(solution)/shard_map/ppermute | solution.py:51
  106.9 19.8 %collective-permute-start.34 = (bf16[2,4,48,768]{3,2,1,0:T(8,128)(2,1)S(1)}, bf16[2,4,48,768]{3,2,1,0:T(8,128)(2,1)}, u32[]{:S(2)}, u32[]{:S(2)}) collective-permute-start(bf16[2,4,48,768]{3,2,1,0:T(8,128)(2,1)S(1)} %slice.1010), channel_id=1, source_target_pairs={{0,4},{1,5},{2,6},{3,7},{4,0},{5,1},{6,2},{7,3},{8,12},{9,13},{10,... | collective-permute-start | bytes 1769480 | tf_op jit(solution)/shard_map/ppermute | solution.py:51
  108.5 18.2 %collective-permute-start.33 = (bf16[2,4,48,768]{3,2,1,0:T(8,128)(2,1)S(1)}, bf16[2,4,48,768]{3,2,1,0:T(8,128)(2,1)}, u32[]{:S(2)}, u32[]{:S(2)}) collective-permute-start(bf16[2,4,48,768]{3,2,1,0:T(8,128)(2,1)S(1)} %slice.1009), channel_id=1, source_target_pairs={{0,2},{1,3},{2,0},{3,1},{4,6},{5,7},{6,4},{7,5},{8,10},{9,11},{10,... | collective-permute-start | bytes 1769480 | tf_op jit(solution)/shard_map/ppermute | solution.py:51
  129.9 30.2 %collective-permute-start.42 = (bf16[4,4,48,384]{3,2,1,0:T(8,128)(2,1)S(1)}, bf16[4,4,48,384]{3,2,1,0:T(8,128)(2,1)}, u32[]{:S(2)}, u32[]{:S(2)}) collective-permute-start(bf16[4,4,48,384]{3,2,1,0:T(8,128)(2,1)S(1)} %pad_maximum_fusion.4.refs_0_), channel_id=1, source_target_pairs={{0,1},{1,0},{2,3},{3,2},{4,5},{5,4},{6,7},{7,6},{8,9},{9,8},{10,11... | collective-permute-start | bytes 1769480 | tf_op jit(solution)/shard_map/ppermute | solution.py:51
  130.0 30.0 %collective-permute-start.41 = (bf16[4,4,48,384]{3,2,1,0:T(8,128)(2,1)S(1)}, bf16[4,4,48,384]{3,2,1,0:T(8,128)(2,1)S(1)}, u32[]{:S(2)}, u32[]{:S(2)}) collective-permute-start(bf16[4,4,48,384]{3,2,1,0:T(8,128)(2,1)S(1)} %pad_maximum_fusion.4.refs_0_), channel_id=1, source_target_pairs={{0,2},{1,3},{2,0},{3,1},{4,6},{5,7},{6,4},{7,5},{8,10},{9,11},{10,... | collective-permute-start | bytes 1769480 | tf_op jit(solution)/shard_map/ppermute | solution.py:51
  130.6 29.5 %collective-permute-start.40 = (bf16[4,4,48,384]{3,2,1,0:T(8,128)(2,1)S(1)}, bf16[4,4,48,384]{3,2,1,0:T(8,128)(2,1)S(1)}, u32[]{:S(2)}, u32[]{:S(2)}) collective-permute-start(bf16[4,4,48,384]{3,2,1,0:T(8,128)(2,1)S(1)} %pad_maximum_fusion.4.refs_0_), channel_id=1, source_target_pairs={{0,4},{1,5},{2,6},{3,7},{4,0},{5,1},{6,2},{7,3},{8,12},{9,13},{10,... | collective-permute-start | bytes 1769480 | tf_op jit(solution)/shard_map/ppermute | solution.py:51
  131.1 27.8 %collective-permute-start.43 = (bf16[2,4,48,768]{3,2,1,0:T(8,128)(2,1)S(1)}, bf16[2,4,48,768]{3,2,1,0:T(8,128)(2,1)}, u32[]{:S(2)}, u32[]{:S(2)}) collective-permute-start(bf16[2,4,48,768]{3,2,1,0:T(8,128)(2,1)S(1)} %pad_maximum_fusion.3), channel_id=1, source_target_pairs={{0,16},{1,17},{2,18},{3,19},{4,20},{5,21},{6,22},{7,23},{8,24},{9,... | collective-permute-start | bytes 1769480 | tf_op jit(solution)/shard_map/ppermute | solution.py:51
  172.5 19.8 %collective-permute-start.52 = (bf16[4,4,48,768]{3,2,1,0:T(8,128)(2,1)S(1)}, bf16[4,4,48,768]{3,2,1,0:T(8,128)(2,1)}, u32[]{:S(2)}, u32[]{:S(2)}) collective-permute-start(bf16[4,4,48,768]{3,2,1,0:T(8,128)(2,1)S(1)} %pad_maximum_fusion.refs_10_.refs_20_), channel_id=1, source_target_pairs={{0,1},{1,0},{2,3},{3,2},{4,5},{5,4},{6,7},{7,6},{8,9},{9,8},{10,11... | collective-permute-start | bytes 3538952 | tf_op jit(solution)/shard_map/ppermute | solution.py:51
  172.7 28.4 %collective-permute-start.51 = (bf16[4,4,48,768]{3,2,1,0:T(8,128)(2,1)S(1)}, bf16[4,4,48,768]{3,2,1,0:T(8,128)(2,1)}, u32[]{:S(2)}, u32[]{:S(2)}) collective-permute-start(bf16[4,4,48,768]{3,2,1,0:T(8,128)(2,1)S(1)} %pad_maximum_fusion.refs_10_.refs_20_), channel_id=1, source_target_pairs={{0,2},{1,3},{2,0},{3,1},{4,6},{5,7},{6,4},{7,5},{8,10},{9,11},{10,... | collective-permute-start | bytes 3538952 | tf_op jit(solution)/shard_map/ppermute | solution.py:51
  173.8 28.1 %collective-permute-start.50 = (bf16[4,4,48,768]{3,2,1,0:T(8,128)(2,1)S(1)}, bf16[4,4,48,768]{3,2,1,0:T(8,128)(2,1)}, u32[]{:S(2)}, u32[]{:S(2)}) collective-permute-start(bf16[4,4,48,768]{3,2,1,0:T(8,128)(2,1)S(1)} %pad_maximum_fusion.refs_10_.refs_20_), channel_id=1, source_target_pairs={{0,4},{1,5},{2,6},{3,7},{4,0},{5,1},{6,2},{7,3},{8,12},{9,13},{10,... | collective-permute-start | bytes 3538952 | tf_op jit(solution)/shard_map/ppermute | solution.py:51
  201.9 18.9 %collective-permute-start.56 = (bf16[4,4,48,768]{3,2,1,0:T(8,128)(2,1)}, bf16[4,4,48,768]{3,2,1,0:T(8,128)(2,1)S(1)}, u32[]{:S(2)}, u32[]{:S(2)}) collective-permute-start(bf16[4,4,48,768]{3,2,1,0:T(8,128)(2,1)} %collective-permute-done.50.refs_12_.refs_22_), channel_id=1, source_target_pairs={{0,1},{1,0},{2,3},{3,2},{4,5},{5,4},{6,7},{7,6},{8,9},{9,8},{10,11... | collective-permute-start | bytes 3538952 | tf_op jit(solution)/shard_map/ppermute | solution.py:51
  201.9 18.9 %collective-permute-start.55 = (bf16[4,4,48,768]{3,2,1,0:T(8,128)(2,1)}, bf16[4,4,48,768]{3,2,1,0:T(8,128)(2,1)S(1)}, u32[]{:S(2)}, u32[]{:S(2)}) collective-permute-start(bf16[4,4,48,768]{3,2,1,0:T(8,128)(2,1)} %collective-permute-done.51.refs_11_.refs_21_), channel_id=1, source_target_pairs={{0,1},{1,0},{2,3},{3,2},{4,5},{5,4},{6,7},{7,6},{8,9},{9,8},{10,11... | collective-permute-start | bytes 3538952 | tf_op jit(solution)/shard_map/ppermute | solution.py:51
  296.0 25.0 %collective-permute-start.62 = (bf16[16,192,384]{2,1,0:T(8,128)(2,1)}, bf16[16,192,384]{2,1,0:T(8,128)(2,1)}, u32[]{:S(2)}, u32[]{:S(2)}) collective-permute-start(bf16[16,192,384]{2,1,0:T(8,128)(2,1)} %get-tuple-element.624), channel_id=1, source_target_pairs={{0,1},{1,0},{2,3},{3,2},{4,5},{5,4},{6,7},{7,6},{8,9},{9,8},{10,11... | collective-permute-start | bytes 7077896 | tf_op jit(solution)/shard_map/ppermute | solution.py:51
  298.7 22.2 %collective-permute-start.61 = (bf16[2,240,384]{2,1,0:T(8,128)(2,1)}, bf16[2,240,384]{2,1,0:T(8,128)(2,1)S(1)}, u32[]{:S(2)}, u32[]{:S(2)}) collective-permute-start(bf16[2,240,384]{2,1,0:T(8,128)(2,1)} %get-tuple-element.926), channel_id=1, source_target_pairs={{0,4},{1,5},{2,6},{3,7},{4,0},{5,1},{6,2},{7,3},{8,12},{9,13},{10,... | collective-permute-start | bytes 1105928 | tf_op jit(solution)/shard_map/ppermute | solution.py:51
  299.7 21.2 %collective-permute-start.60 = (bf16[2,240,384]{2,1,0:T(8,128)(2,1)}, bf16[2,240,384]{2,1,0:T(8,128)(2,1)}, u32[]{:S(2)}, u32[]{:S(2)}) collective-permute-start(bf16[2,240,384]{2,1,0:T(8,128)(2,1)} %get-tuple-element.927), channel_id=1, source_target_pairs={{0,2},{1,3},{2,0},{3,1},{4,6},{5,7},{6,4},{7,5},{8,10},{9,11},{10,... | collective-permute-start | bytes 1105928 | tf_op jit(solution)/shard_map/ppermute | solution.py:51
  323.9 28.5 %collective-permute-start.66 = (bf16[4,240,384]{2,1,0:T(8,128)(2,1)}, bf16[4,240,384]{2,1,0:T(8,128)(2,1)}, u32[]{:S(2)}, u32[]{:S(2)}) collective-permute-start(bf16[4,240,384]{2,1,0:T(8,128)(2,1)} %get-tuple-element.924), channel_id=1, source_target_pairs={{0,2},{1,3},{2,0},{3,1},{4,6},{5,7},{6,4},{7,5},{8,10},{9,11},{10,... | collective-permute-start | bytes 2211848 | tf_op jit(solution)/shard_map/ppermute | solution.py:51
  323.9 28.5 %collective-permute-start.65 = (bf16[4,240,384]{2,1,0:T(8,128)(2,1)}, bf16[4,240,384]{2,1,0:T(8,128)(2,1)}, u32[]{:S(2)}, u32[]{:S(2)}) collective-permute-start(bf16[4,240,384]{2,1,0:T(8,128)(2,1)} %get-tuple-element.925), channel_id=1, source_target_pairs={{0,4},{1,5},{2,6},{3,7},{4,0},{5,1},{6,2},{7,3},{8,12},{9,13},{10,... | collective-permute-start | bytes 2211848 | tf_op jit(solution)/shard_map/ppermute | solution.py:51
  328.0 24.4 %collective-permute-start.64 = (bf16[2,192,384]{2,1,0:T(8,128)(2,1)}, bf16[2,192,384]{2,1,0:T(8,128)(2,1)S(1)}, u32[]{:S(2)}, u32[]{:S(2)}) collective-permute-start(bf16[2,192,384]{2,1,0:T(8,128)(2,1)} %get-tuple-element.939), channel_id=1, source_target_pairs={{0,4},{1,5},{2,6},{3,7},{4,0},{5,1},{6,2},{7,3},{8,12},{9,13},{10,... | collective-permute-start | bytes 884744 | tf_op jit(solution)/shard_map/ppermute | solution.py:51
  328.9 23.5 %collective-permute-start.63 = (bf16[2,192,384]{2,1,0:T(8,128)(2,1)S(1)}, bf16[2,192,384]{2,1,0:T(8,128)(2,1)S(1)}, u32[]{:S(2)}, u32[]{:S(2)}) collective-permute-start(bf16[2,192,384]{2,1,0:T(8,128)(2,1)S(1)} %get-tuple-element.940), channel_id=1, source_target_pairs={{0,2},{1,3},{2,0},{3,1},{4,6},{5,7},{6,4},{7,5},{8,10},{9,11},{10,... | collective-permute-start | bytes 884744 | tf_op jit(solution)/shard_map/ppermute | solution.py:51
  352.4 31.0 %collective-permute-start.70 = (bf16[16,160,384]{2,1,0:T(8,128)(2,1)}, bf16[16,160,384]{2,1,0:T(8,128)(2,1)}, u32[]{:S(2)}, u32[]{:S(2)}) collective-permute-start(bf16[16,160,384]{2,1,0:T(8,128)(2,1)} %get-tuple-element.655), channel_id=1, source_target_pairs={{0,1},{1,0},{2,3},{3,2},{4,5},{5,4},{6,7},{7,6},{8,9},{9,8},{10,11... | collective-permute-start | bytes 5898248 | tf_op jit(solution)/shard_map/ppermute | solution.py:51
  355.0 28.4 %collective-permute-start.69 = (bf16[2,240,384]{2,1,0:T(8,128)(2,1)}, bf16[2,240,384]{2,1,0:T(8,128)(2,1)S(1)}, u32[]{:S(2)}, u32[]{:S(2)}) collective-permute-start(bf16[2,240,384]{2,1,0:T(8,128)(2,1)} %pad_maximum_fusion.5), channel_id=1, source_target_pairs={{0,16},{1,17},{2,18},{3,19},{4,20},{5,21},{6,22},{7,23},{8,24},{9,... | collective-permute-start | bytes 1105928 | tf_op jit(solution)/shard_map/ppermute | solution.py:51
  357.7 25.8 %collective-permute-start.68 = (bf16[4,192,384]{2,1,0:T(8,128)(2,1)}, bf16[4,192,384]{2,1,0:T(8,128)(2,1)S(1)}, u32[]{:S(2)}, u32[]{:S(2)}) collective-permute-start(bf16[4,192,384]{2,1,0:T(8,128)(2,1)} %get-tuple-element.937), channel_id=1, source_target_pairs={{0,2},{1,3},{2,0},{3,1},{4,6},{5,7},{6,4},{7,5},{8,10},{9,11},{10,... | collective-permute-start | bytes 1769480 | tf_op jit(solution)/shard_map/ppermute | solution.py:51
  357.7 25.8 %collective-permute-start.67 = (bf16[4,192,384]{2,1,0:T(8,128)(2,1)}, bf16[4,192,384]{2,1,0:T(8,128)(2,1)}, u32[]{:S(2)}, u32[]{:S(2)}) collective-permute-start(bf16[4,192,384]{2,1,0:T(8,128)(2,1)} %get-tuple-element.938), channel_id=1, source_target_pairs={{0,4},{1,5},{2,6},{3,7},{4,0},{5,1},{6,2},{7,3},{8,12},{9,13},{10,... | collective-permute-start | bytes 1769480 | tf_op jit(solution)/shard_map/ppermute | solution.py:51
  385.7 22.5 %collective-permute-start.74 = (bf16[240,384]{1,0:T(8,128)(2,1)}, bf16[240,384]{1,0:T(8,128)(2,1)}, u32[]{:S(2)}, u32[]{:S(2)}) collective-permute-start(bf16[240,384]{1,0:T(8,128)(2,1)} %fusion.29), channel_id=1, source_target_pairs={{0,8},{1,9},{2,10},{3,11},{4,12},{5,13},{6,14},{7,15},{8,0},{9,1},... | collective-permute-start | bytes 552968 | tf_op jit(solution)/shard_map/ppermute | solution.py:51
  409.0 18.5 %collective-permute-start.75 = (bf16[16,240,384]{2,1,0:T(8,128)(2,1)}, bf16[16,240,384]{2,1,0:T(8,128)(2,1)}, u32[]{:S(2)}, u32[]{:S(2)}) collective-permute-start(bf16[16,240,384]{2,1,0:T(8,128)(2,1)} %get-tuple-element.681), channel_id=1, source_target_pairs={{0,1},{1,0},{2,3},{3,2},{4,5},{5,4},{6,7},{7,6},{8,9},{9,8},{10,11... | collective-permute-start | bytes 8847368 | tf_op jit(solution)/shard_map/ppermute | solution.py:51
  427.5 26.2 %collective-permute-start.81 = (bf16[16,192,384]{2,1,0:T(8,128)(2,1)}, bf16[16,192,384]{2,1,0:T(8,128)(2,1)}, u32[]{:S(2)}, u32[]{:S(2)}) collective-permute-start(bf16[16,192,384]{2,1,0:T(8,128)(2,1)} %get-tuple-element.706), channel_id=1, source_target_pairs={{0,1},{1,0},{2,3},{3,2},{4,5},{5,4},{6,7},{7,6},{8,9},{9,8},{10,11... | collective-permute-start | bytes 7077896 | tf_op jit(solution)/shard_map/ppermute | solution.py:51
  429.2 24.5 %collective-permute-start.83 = (f32[120,384]{1,0:T(8,128)S(1)}, f32[120,384]{1,0:T(8,128)S(1)}, u32[]{:S(2)}, u32[]{:S(2)}) collective-permute-start(f32[120,384]{1,0:T(8,128)S(1)} %pad_maximum_fusion.15), channel_id=1, source_target_pairs={{0,1},{1,0},{2,3},{3,2},{4,5},{5,4},{6,7},{7,6},{8,9},{9,8},{10,11... | collective-permute-start | bytes 552968 | tf_op jit(solution)/shard_map/ppermute | solution.py:51
  432.1 21.6 %collective-permute-start.82 = (bf16[2,160,384]{2,1,0:T(8,128)(2,1)}, bf16[2,160,384]{2,1,0:T(8,128)(2,1)}, u32[]{:S(2)}, u32[]{:S(2)}) collective-permute-start(bf16[2,160,384]{2,1,0:T(8,128)(2,1)} %pad_maximum_fusion.12), channel_id=1, source_target_pairs={{0,16},{1,17},{2,18},{3,19},{4,20},{5,21},{6,22},{7,23},{8,24},{9,... | collective-permute-start | bytes 737288 | tf_op jit(solution)/shard_map/ppermute | solution.py:51
  455.6 32.4 %collective-permute-start.88 = (bf16[160,384]{1,0:T(8,128)(2,1)}, bf16[160,384]{1,0:T(8,128)(2,1)}, u32[]{:S(2)}, u32[]{:S(2)}) collective-permute-start(bf16[160,384]{1,0:T(8,128)(2,1)} %fusion.51), channel_id=1, source_target_pairs={{0,8},{1,9},{2,10},{3,11},{4,12},{5,13},{6,14},{7,15},{8,0},{9,1},... | collective-permute-start | bytes 368648 | tf_op jit(solution)/shard_map/ppermute | solution.py:51
  458.1 29.9 %collective-permute-start.85 = (bf16[2,192,384]{2,1,0:T(8,128)(2,1)}, bf16[2,192,384]{2,1,0:T(8,128)(2,1)}, u32[]{:S(2)}, u32[]{:S(2)}) collective-permute-start(bf16[2,192,384]{2,1,0:T(8,128)(2,1)} %get-tuple-element.935), channel_id=1, source_target_pairs={{0,4},{1,5},{2,6},{3,7},{4,0},{5,1},{6,2},{7,3},{8,12},{9,13},{10,... | collective-permute-start | bytes 884744 | tf_op jit(solution)/shard_map/ppermute | solution.py:51
  460.3 27.8 %collective-permute-start.84 = (bf16[2,192,384]{2,1,0:T(8,128)(2,1)}, bf16[2,192,384]{2,1,0:T(8,128)(2,1)}, u32[]{:S(2)}, u32[]{:S(2)}) collective-permute-start(bf16[2,192,384]{2,1,0:T(8,128)(2,1)} %get-tuple-element.936), channel_id=1, source_target_pairs={{0,2},{1,3},{2,0},{3,1},{4,6},{5,7},{6,4},{7,5},{8,10},{9,11},{10,... | collective-permute-start | bytes 884744 | tf_op jit(solution)/shard_map/ppermute | solution.py:51
  481.1 18.9 %collective-permute-start.87 = (bf16[4,240,384]{2,1,0:T(8,128)(2,1)}, bf16[4,240,384]{2,1,0:T(8,128)(2,1)}, u32[]{:S(2)}, u32[]{:S(2)}) collective-permute-start(bf16[4,240,384]{2,1,0:T(8,128)(2,1)} %get-tuple-element.918), channel_id=1, source_target_pairs={{0,2},{1,3},{2,0},{3,1},{4,6},{5,7},{6,4},{7,5},{8,10},{9,11},{10,... | collective-permute-start | bytes 2211848 | tf_op jit(solution)/shard_map/ppermute | solution.py:51
  483.9 18.4 %collective-permute-start.86 = (bf16[4,240,384]{2,1,0:T(8,128)(2,1)}, bf16[4,240,384]{2,1,0:T(8,128)(2,1)}, u32[]{:S(2)}, u32[]{:S(2)}) collective-permute-start(bf16[4,240,384]{2,1,0:T(8,128)(2,1)} %get-tuple-element.919), channel_id=1, source_target_pairs={{0,4},{1,5},{2,6},{3,7},{4,0},{5,1},{6,2},{7,3},{8,12},{9,13},{10,... | collective-permute-start | bytes 2211848 | tf_op jit(solution)/shard_map/ppermute | solution.py:51
  506.2 22.1 %collective-permute-start.92 = (f32[96,384]{1,0:T(8,128)S(1)}, f32[96,384]{1,0:T(8,128)}, u32[]{:S(2)}, u32[]{:S(2)}) collective-permute-start(f32[96,384]{1,0:T(8,128)S(1)} %pad_maximum_fusion.23), channel_id=1, source_target_pairs={{0,1},{1,0},{2,3},{3,2},{4,5},{5,4},{6,7},{7,6},{8,9},{9,8},{10,11... | collective-permute-start | bytes 442376 | tf_op jit(solution)/shard_map/ppermute | solution.py:51
  509.1 23.2 %collective-permute-start.91 = (bf16[4,192,384]{2,1,0:T(8,128)(2,1)}, bf16[4,192,384]{2,1,0:T(8,128)(2,1)S(1)}, u32[]{:S(2)}, u32[]{:S(2)}) collective-permute-start(bf16[4,192,384]{2,1,0:T(8,128)(2,1)} %get-tuple-element.933), channel_id=1, source_target_pairs={{0,2},{1,3},{2,0},{3,1},{4,6},{5,7},{6,4},{7,5},{8,10},{9,11},{10,... | collective-permute-start | bytes 1769480 | tf_op jit(solution)/shard_map/ppermute | solution.py:51
  510.3 22.0 %collective-permute-start.90 = (bf16[4,192,384]{2,1,0:T(8,128)(2,1)}, bf16[4,192,384]{2,1,0:T(8,128)(2,1)}, u32[]{:S(2)}, u32[]{:S(2)}) collective-permute-start(bf16[4,192,384]{2,1,0:T(8,128)(2,1)} %get-tuple-element.934), channel_id=1, source_target_pairs={{0,4},{1,5},{2,6},{3,7},{4,0},{5,1},{6,2},{7,3},{8,12},{9,13},{10,... | collective-permute-start | bytes 1769480 | tf_op jit(solution)/shard_map/ppermute | solution.py:51
  512.6 19.7 %collective-permute-start.89 = (bf16[2,240,384]{2,1,0:T(8,128)(2,1)}, bf16[2,240,384]{2,1,0:T(8,128)(2,1)}, u32[]{:S(2)}, u32[]{:S(2)}) collective-permute-start(bf16[2,240,384]{2,1,0:T(8,128)(2,1)} %pad_maximum_fusion.6), channel_id=1, source_target_pairs={{0,16},{1,17},{2,18},{3,19},{4,20},{5,21},{6,22},{7,23},{8,24},{9,... | collective-permute-start | bytes 1105928 | tf_op jit(solution)/shard_map/ppermute | solution.py:51
  564.9 22.0 %collective-permute-start.100 = (bf16[4,160,384]{2,1,0:T(8,128)(2,1)}, bf16[4,160,384]{2,1,0:T(8,128)(2,1)}, u32[]{:S(2)}, u32[]{:S(2)}) collective-permute-start(bf16[4,160,384]{2,1,0:T(8,128)(2,1)} %get-tuple-element.941), channel_id=1, source_target_pairs={{0,2},{1,3},{2,0},{3,1},{4,6},{5,7},{6,4},{7,5},{8,10},{9,11},{10,... | collective-permute-start | bytes 1474568 | tf_op jit(solution)/shard_map/ppermute | solution.py:51
  566.6 20.3 %collective-permute-start.99 = (bf16[4,160,384]{2,1,0:T(8,128)(2,1)}, bf16[4,160,384]{2,1,0:T(8,128)(2,1)}, u32[]{:S(2)}, u32[]{:S(2)}) collective-permute-start(bf16[4,160,384]{2,1,0:T(8,128)(2,1)} %get-tuple-element.942), channel_id=1, source_target_pairs={{0,4},{1,5},{2,6},{3,7},{4,0},{5,1},{6,2},{7,3},{8,12},{9,13},{10,... | collective-permute-start | bytes 1474568 | tf_op jit(solution)/shard_map/ppermute | solution.py:51
  (128 other events, 1365.7 us)

commit v5 on v4

--- a/solution.py
+++ b/solution.py
@@ -608,8 +608,8 @@
     c1, c2, c3 = counts
     leave_src, widen_src, narrow_src = refs[:c1], refs[c1 : c1 + c2], refs[c1 + c2 : c1 + c2 + c3]
     refs = refs[c1 + c2 + c3 :]
-    dback_ref, mixed_ref, dhid_ref, dattn_ref, du_ref, dctx_ref, dvec_ref, dbias_ref = refs[:8]
-    leave, widen, narrow, sem = refs[8:]
+    dback_ref, mixed_ref, dhid_ref, dattn_ref, dctx_ref, dvec_ref, dbias_ref = refs[:7]
+    leave, widen, narrow, sem = refs[7:]
     first = pl.program_id(0) == 0
 
     @pl.when(first)
@@ -648,7 +648,6 @@
     dvec_ref[3:4, :] += column_sum(dmixed * unit)
     dvec_ref[4:5, :] += column_sum(dmixed)
     du = norm_pull(dmixed * vec_ref[3:4, :], unit, rstd)
-    du_ref[...] = du
     dattn = low(du)
     dattn_ref[...] = dattn
     dvec_ref[2:3, :] += column_sum(wide(dattn))
@@ -668,7 +667,7 @@
             num_scalar_prefetch=1,
             grid=(tokens // tile,),
             in_specs=[blk(D), blk(D), blk(FF), blk(D), full(8, D)] + [ANY] * len(sources),
-            out_specs=[blk(D), blk(D), blk(FF), blk(D), blk(D), blk(D), full(8, D), full(1, FF)],
+            out_specs=[blk(D), blk(D), blk(FF), blk(D), blk(D), full(8, D), full(1, FF)],
             scratch_shapes=[
                 pltpu.VMEM((D, D), BF16),
                 pltpu.VMEM((4, D, D), BF16),
@@ -681,7 +680,6 @@
             sds((tokens, D), BF16),
             sds((tokens, FF), BF16),
             sds((tokens, D), BF16),
-            sds((tokens, D), F32),
             sds((tokens, D), BF16),
             sds((8, D), F32),
             sds((1, FF), F32),
@@ -1044,7 +1042,7 @@
         start_load(me_ref[0], sources, entry, sem.at[0], place_entry)
         wait_load(entry, sem.at[0])
 
-    total = mm(dq_ref[0], entry[0], NT) + du_ref[0]
+    total = mm(dq_ref[0], entry[0], NT) + wide(du_ref[0])
     if stride == 1:
         out_ref[0] = total + mm(dk_ref[0], entry[1], NT) + mm(dv_ref[0], entry[2], NT)
         return
@@ -1266,7 +1264,7 @@
     def reducing(pair, cuts, direct=False):
         return Job(reduce_stages, core, cuts, direct, *pair) if fast else pair
 
-    dback, mixed_low, dhid, dattn, du, dctx, dvec, dbias = tick(
+    dback, mixed_low, dhid, dattn, dctx, dvec, dbias = tick(
         [],
         lambda me: contract(me, cotangent.reshape(-1, D), before2, slope2, u2, vec2, *weights(1, "own")),
     )
@@ -1284,13 +1282,13 @@
 
     def entry_end(me):
         made = entry_grad(160, 0, me, halved, pooled_layer, pooled_layer, dq, dk, dv, packed, ())
-        parts = (dq, dk, dv, du.reshape(q2.shape), *weights(1, "e"))
+        parts = (dq, dk, dv, dattn.reshape(q2.shape), *weights(1, "e"))
         return made, input_grads(1, me, halved, *parts, 0, rows)
 
     entry2, dlayer = tick([sumn2, sumw2], entry_end)
     sume2 = reducing(entry2, ENTRY_CUTS)
 
-    dback, mixed_low, dhid, dattn, du, dctx, dvec, dbias = tick(
+    dback, mixed_low, dhid, dattn, dctx, dvec, dbias = tick(
         [sumw2, sumn2, sume2],
         lambda me: contract(me, flatten(dlayer), before1, slope1, u1, vec1, *weights(0, "own")),
     )
@@ -1313,7 +1311,7 @@
         lambda me: entry_grad(160, 0, me, lengths, pooled_low, hidden, dq, dk, dv, packed, ()),
     )
     sume1 = reducing(entry1, ENTRY_CUTS, True)
-    parts = (dq, dk, dv, du.reshape(q1.shape), *weights(0, "e"))
+    parts = (dq, dk, dv, dattn.reshape(q1.shape), *weights(0, "e"))
     ends = (0, 1, 2, rows) if rows > 2 else (0, rows)
     beside = ([sume1, sumn1, sume2], [sume1, sumn1], [sume1, sumw1])
     done = ()

time: 616 us -> 615 us (level)
  Pallas kernels: 314 us -> 305 us
  transfers between devices with their start and end apart: 108 -> 108, of which waited for: 35 -> 32; matrix products, arithmetic and copies ran while one was open for 13% -> 13% of each run, Pallas kernels for 42% -> 40%
where the time goes in v5:
time: 615 us; the launch traced here: 607 us
  Pallas kernels  305 us (50%)
  waiting for transfers between devices  103 us (17%)
  starting transfers between devices  88.6 us (14%)
  other arithmetic  83.7 us (14%)
  local copies, waits for them, and re-layouts  24.8 us (4%)
    ppermute x108, waiting for transfers between devices, swap(): return lax.ppermute(value, AX, [(i, i ^ mask) for i in range(32)])  103 us
    ppermute x108, starting transfers between devices, swap(): return lax.ppermute(value, AX, [(i, i ^ mask) for i in range(32)])  88.6 us
    pallas_call x6, Pallas kernels, sum_call(): pl.pallas_call(partial(kernel, start, rows), grid_spec=pltpu.PrefetchScal...  70.6 us
    convert_element_type x23, other arithmetic, low(): return value.astype(BF16)  47.3 us
    pallas_call x2, Pallas kernels, expand(): pl.pallas_call(partial(expand_kernel, (len(leave), len(widen), len(narrow...  47.3 us
    pallas_call x2, Pallas kernels, contract(): pl.pallas_call(partial(contract_kernel, (len(leave), len(widen), len(narr...  46.9 us
    pallas_call x3, Pallas kernels, retrace(): pl.pallas_call(partial(retrace_kernel, stride, base), grid_spec=pltpu.Pre...  44.2 us
    pallas_call x4, Pallas kernels, input_grads(): pl.pallas_call(partial(inputs_kernel, stride, base, len(sources)), grid_s...  37 us
  transfers between devices with their start and end apart: 108, of which 32 were waited for; matrix products, arithmetic and copies ran while one was open for 13% of the time, Pallas kernels for 40%

profile of v5, /device:TPU:0, one launch (start us, length us, event | category | flops | bytes accessed | tf_op | source)
XLA Modules:
  0.0 607.4 jit_solution(17838290059906260036)
XLA Ops:
  6.2 5.1 collective-permute-start.3
  12.9 2.9 collective-permute-done.2
  16.2 3.5 collective-permute-start.8
  20.6 2.4 collective-permute-start.11
  23.1 7.7 %collective-permute-done.8 = bf16[4,48,384]{2,1,0:T(8,128)(2,1)S(1)} collective-permute-done((bf16[4,48,384]{2,1,0:T(8,128)(2,1)S(1)}, bf16[4,48,384]{2,1,0:T(8,128)(2,1)S(1)}, u32[]{:S(2)}, u32[]{:S(2)}) %collective-permute-start.8) | collective-permute-done | bytes 147488 | tf_op jit(solution)/shard_map/ppermute | solution.py:51
  41.4 12.8 %collective-permute-done.16 = bf16[2,2,48,768]{3,2,1,0:T(8,128)(2,1)S(1)} collective-permute-done((bf16[2,2,48,768]{3,2,1,0:T(8,128)(2,1)S(1)}, bf16[2,2,48,768]{3,2,1,0:T(8,128)(2,1)S(1)}, u32[]{:S(2)}, u32[]{:S(2)}) %collective-permute-start.16) | collective-permute-done | bytes 294944 | tf_op jit(solution)/shard_map/ppermute | solution.py:51
  59.9 5.4 prepare.1
  65.3 5.3 collective-permute-done.22
  80.1 13.1 %project.2 = (f32[4,256,768]{2,1,0:T(8,128)}, bf16[4,256,768]{2,1,0:T(8,128)(2,1)}, bf16[4,256,768]{2,1,0:T(8,128)(2,1)}, bf16[4,512,768]{2,1,0:T(8,128)(2,1)}, bf16[4,512,768]{2,1,0:T(8,128)(2,1)}) custom-call(s32[4]{0:T(128)} %len_ref.17, s32[1]{0:T(128)} %bitcast.me_ref, bf16[4,512,768]{2,1,0:T(8,128)(2,1)} %b_ref.1, ...), custom_call_target="tpu_custom_call" | custom-call | flops 4831838208 | bytes 20000000 | tf_op jit(solution)/shard_map/project/pallas_call | solution.py:445
  93.2 7.4 %attend.4 = (bf16[4,256,768]{2,1,0:T(8,128)(2,1)}, bf16[4,12,512,256]{3,2,1,0:T(8,128)(2,1)}) custom-call(s32[4]{0:T(128)} %len_ref.17, s32[1]{0:T(128)} %bitcast.me_ref, bf16[4,256,768]{2,1,0:T(8,128)(2,1)} %get-tuple-element.493.q_ref, bf16[4,512,768]{2,1,0:T(8,128)(2,1)} %get-tuple-element.494.k_ref, bf16[4,512,768]{2,1,0:T(8,128)(2,1)} %get-tuple-element.495.v_ref, ...), custom_call_target="tpu_custom_call" | custom-call | flops 1610612736 | bytes 20000000 | tf_op jit(solution)/shard_map/attend/pallas_call | solution.py:508
  100.7 3.6 collective-permute-done.29.refs_11_.refs_21_
  110.4 9.9 %attend.5 = (bf16[4,256,768]{2,1,0:T(8,128)(2,1)}, bf16[4,12,512,256]{3,2,1,0:T(8,128)(2,1)}) custom-call(s32[4]{0:T(128)} %len_ref.17, s32[1]{0:T(128)} %bitcast.me_ref, bf16[4,256,768]{2,1,0:T(8,128)(2,1)} %get-tuple-element.493.q_ref, bf16[4,512,768]{2,1,0:T(8,128)(2,1)} %get-tuple-element.494.k_ref, ...), custom_call_target="tpu_custom_call", output_to_operand_aliasing={{0}: (6, {}), {1}: (7, {})} | custom-call | flops 1610612736 | bytes 20000000 | tf_op jit(solution)/shard_map/attend/pallas_call | solution.py:508
  120.3 4.2 collective-permute-done.37
  129.2 23.8 %expand.2 = (f32[1024,768]{1,0:T(8,128)}, bf16[1024,3072]{1,0:T(8,128)(2,1)}, bf16[1024,3072]{1,0:T(8,128)(2,1)}, f32[1024,768]{1,0:T(8,128)}, bf16[1024,768]{1,0:T(8,128)(2,1)}) custom-call(s32[1]{0:T(128)} %bitcast.me_ref, bf16[1024,768]{1,0:T(8,128)(2,1)} %bitcast.515, f32[1024,768]{1,0:T(8,128)} %bitcast.642, f32[8,768]{1,0:T(8,128)} %get-tuple-element.482.vec_ref, ...), custom_call_target="tpu_custom_call" | custom-call | flops 10871635968 | bytes 30000000 | tf_op jit(solution)/shard_map/expand/pallas_call | solution.py:578
  153.0 4.6 collective-permute-done.43
  162.6 6.0 collective-permute-done.44.refs_3_
  174.8 9.9 %project.3 = (bf16[4,256,768]{2,1,0:T(8,128)(2,1)}, bf16[4,256,768]{2,1,0:T(8,128)(2,1)}, bf16[4,256,768]{2,1,0:T(8,128)(2,1)}) custom-call(s32[4]{0:T(128)} %and_select_fusion.len_ref, s32[1]{0:T(128)} %bitcast.me_ref, bf16[4,256,768]{2,1,0:T(8,128)(2,1)} %bitcast.643, f32[8,768]{1,0:T(8,128)} %get-tuple-element.554.vec_ref, ...), custom_call_target="tpu_custom_call" | custom-call | flops 2415919104 | bytes 20000000 | tf_op jit(solution)/shard_map/project/pallas_call | solution.py:445
  184.7 6.5 %attend.6 = (bf16[4,256,768]{2,1,0:T(8,128)(2,1)}, bf16[4,12,256,256]{3,2,1,0:T(8,128)(2,1)}) custom-call(s32[4]{0:T(128)} %and_select_fusion.len_ref, s32[1]{0:T(128)} %bitcast.me_ref, bf16[4,256,768]{2,1,0:T(8,128)(2,1)} %get-tuple-element.565.q_ref, bf16[4,256,768]{2,1,0:T(8,128)(2,1)} %get-tuple-element.566.k_ref, ...), custom_call_target="tpu_custom_call" | custom-call | flops 805306368 | bytes 20000000 | tf_op jit(solution)/shard_map/attend/pallas_call | solution.py:508
  191.2 9.2 %collective-permute-done.51.refs_11_.refs_21_ = bf16[4,4,48,768]{3,2,1,0:T(8,128)(2,1)} collective-permute-done((bf16[4,4,48,768]{3,2,1,0:T(8,128)(2,1)S(1)}, bf16[4,4,48,768]{3,2,1,0:T(8,128)(2,1)}, u32[]{:S(2)}, u32[]{:S(2)}) %collective-permute-start.51) | collective-permute-done | bytes 1179680 | tf_op jit(solution)/shard_map/ppermute | solution.py:51
  206.4 6.6 %attend.7 = (bf16[4,256,768]{2,1,0:T(8,128)(2,1)}, bf16[4,12,256,256]{3,2,1,0:T(8,128)(2,1)}) custom-call(s32[4]{0:T(128)} %and_select_fusion.len_ref, s32[1]{0:T(128)} %bitcast.me_ref, bf16[4,256,768]{2,1,0:T(8,128)(2,1)} %get-tuple-element.565.q_ref, bf16[4,256,768]{2,1,0:T(8,128)(2,1)} %get-tuple-element.566.k_ref, ...), custom_call_target="tpu_custom_call", output_to_operand_aliasing={{0}: (6, {}), {1}: (7, {})} | custom-call | flops 805306368 | bytes 20000000 | tf_op jit(solution)/shard_map/attend/pallas_call | solution.py:508
  213.0 5.7 collective-permute-done.54.refs_14_.refs_24_
  223.9 23.5 %expand.3 = (f32[1024,768]{1,0:T(8,128)}, bf16[1024,3072]{1,0:T(8,128)(2,1)}, bf16[1024,3072]{1,0:T(8,128)(2,1)}, f32[1024,768]{1,0:T(8,128)}, bf16[1024,768]{1,0:T(8,128)(2,1)}) custom-call(s32[1]{0:T(128)} %bitcast.me_ref, bf16[1024,768]{1,0:T(8,128)(2,1)} %bitcast.517, bf16[1024,768]{1,0:T(8,128)(2,1)} %get-tuple-element.535.resid_ref, ...), custom_call_target="tpu_custom_call" | custom-call | flops 10871635968 | bytes 30000000 | tf_op jit(solution)/shard_map/expand/pallas_call | solution.py:578
  247.4 23.3 %contract.2 = (bf16[1024,768]{1,0:T(8,128)(2,1)}, bf16[1024,768]{1,0:T(8,128)(2,1)}, bf16[1024,3072]{1,0:T(8,128)(2,1)}, bf16[1024,768]{1,0:T(8,128)(2,1)}, bf16...) custom-call(s32[1]{0:T(128)} %bitcast.me_ref, bf16[1024,768]{1,0:T(8,128)(2,1)} %bitcast.641, ...), custom_call_target="tpu_custom_call" | custom-call | flops 10871635968 | bytes 50000000 | tf_op jit(solution)/shard_map/contract/pallas_call | solution.py:664
  270.7 12.8 %narrow_grad.2 = (bf16[16,240,384]{2,1,0:T(8,128)(2,1)}, bf16[16,240,384]{2,1,0:T(8,128)(2,1)}) custom-call(s32[1]{0:T(128)} %bitcast.me_ref, bf16[1024,3072]{1,0:T(8,128)(2,1)} %get-tuple-element.606.act_ref, bf16[1024,768]{1,0:T(8,128)(2,1)} %get-tuple-element.607.dback_ref, bf16[1024,768]{1,0:T(8,128)(2,1)} %bitcast.518, ...), custom_call_target="tpu_custom_call" | custom-call | flops 6039797760 | bytes 16000000 | tf_op jit(solution)/shard_map/narrow_grad/pallas_call | solution.py:714
  283.7 10.8 %widen_grad.2 = (bf16[16,192,384]{2,1,0:T(8,128)(2,1)}, bf16[16,192,384]{2,1,0:T(8,128)(2,1)}) custom-call(s32[1]{0:T(128)} %bitcast.me_ref, bf16[1024,768]{1,0:T(8,128)(2,1)} %get-tuple-element.615.mixed_ref, bf16[1024,3072]{1,0:T(8,128)(2,1)} %get-tuple-element.616.dhid_ref), custom_call_target="tpu_custom_call" | custom-call | flops 4831838208 | bytes 16000000 | tf_op jit(solution)/shard_map/widen_grad/pallas_call | solution.py:714
  299.2 14.6 %retrace.3 = (bf16[4,256,768]{2,1,0:T(8,128)(2,1)}, bf16[4,256,768]{2,1,0:T(8,128)(2,1)}, bf16[4,256,768]{2,1,0:T(8,128)(2,1)}, f32[8,768]{1,0:T(8,128)}, f32[12...) custom-call(s32[4]{0:T(128)} %and_select_fusion.len_ref, s32[1]{0:T(128)} %bitcast.me_ref, ...), custom_call_target="tpu_custom_call" | custom-call | flops 2013265920 | bytes 20000000 | tf_op jit(solution)/shard_map/retrace/pallas_call | solution.py:975
  318.2 2.8 fusion.2
  328.2 10.1 %input_grads.4 = f32[4,256,768]{2,1,0:T(8,128)} custom-call(s32[4]{0:T(128)} %and_select_fusion.len_ref, s32[1]{0:T(128)} %bitcast.me_ref, bf16[4,256,768]{2,1,0:T(8,128)(2,1)} %get-tuple-element.635.dq_ref, bf16[4,256,768]{2,1,0:T(8,128)(2,1)} %get-tuple-element.636.dk_ref, bf16[4,256,768]{2,1,0:T(8,128)(2,1)} %get-tuple-element.637.dv_ref, ...), custom_call_target="tpu_custom_call" | custom-call | flops 2415919104 | bytes 20000000 | tf_op jit(solution)/shard_map/input_grads/pallas_call | solution.py:1074
  338.3 10.8 %entry_grad.2 = (bf16[16,160,384]{2,1,0:T(8,128)(2,1)}, bf16[16,160,384]{2,1,0:T(8,128)(2,1)}) custom-call(s32[4]{0:T(128)} %and_select_fusion.len_ref, s32[1]{0:T(128)} %bitcast.me_ref, bf16[4,256,768]{2,1,0:T(8,128)(2,1)} %bitcast.644, bf16[4,256,768]{2,1,0:T(8,128)(2,1)} %bitcast.645, bf16[4,256,768]{2,1,0:T(8,128)(2,1)} %get-tuple-element.635.dq_ref, ...), custom_call_target="tpu_custom_call" | custom-call | flops 2415919104 | bytes 16000000 | tf_op jit(solution)/shard_map/entry_grad/pallas_call | solution.py:714
  351.7 2.8 fusion.6
  356.8 23.6 %contract.3 = (bf16[1024,768]{1,0:T(8,128)(2,1)}, bf16[1024,768]{1,0:T(8,128)(2,1)}, bf16[1024,3072]{1,0:T(8,128)(2,1)}, bf16[1024,768]{1,0:T(8,128)(2,1)}, bf16...) custom-call(s32[1]{0:T(128)} %bitcast.me_ref, f32[1024,768]{1,0:T(8,128)} %bitcast.483, ...), custom_call_target="tpu_custom_call" | custom-call | flops 10871635968 | bytes 50000000 | tf_op jit(solution)/shard_map/contract/pallas_call | solution.py:664
  392.7 12.6 %narrow_grad.3 = (bf16[16,240,384]{2,1,0:T(8,128)(2,1)}, bf16[16,240,384]{2,1,0:T(8,128)(2,1)}) custom-call(s32[1]{0:T(128)} %bitcast.me_ref, bf16[1024,3072]{1,0:T(8,128)(2,1)} %get-tuple-element.672.act_ref, bf16[1024,768]{1,0:T(8,128)(2,1)} %get-tuple-element.673.dback_ref, bf16[1024,768]{1,0:T(8,128)(2,1)} %bitcast.516, ...), custom_call_target="tpu_custom_call" | custom-call | flops 6039797760 | bytes 16000000 | tf_op jit(solution)/shard_map/narrow_grad/pallas_call | solution.py:714
  405.5 2.9 fusion.10
  413.6 10.7 %widen_grad.3 = (bf16[16,192,384]{2,1,0:T(8,128)(2,1)}, bf16[16,192,384]{2,1,0:T(8,128)(2,1)}) custom-call(s32[1]{0:T(128)} %bitcast.me_ref, bf16[1024,768]{1,0:T(8,128)(2,1)} %get-tuple-element.690.mixed_ref, bf16[1024,3072]{1,0:T(8,128)(2,1)} %get-tuple-element.691.dhid_ref), custom_call_target="tpu_custom_call" | custom-call | flops 4831838208 | bytes 16000000 | tf_op jit(solution)/shard_map/widen_grad/pallas_call | solution.py:714
  434.7 13.0 %retrace.4 = (bf16[4,256,768]{2,1,0:T(8,128)(2,1)}, bf16[4,512,768]{2,1,0:T(8,128)(2,1)}, bf16[4,512,768]{2,1,0:T(8,128)(2,1)}, f32[8,768]{1,0:T(8,128)}, f32[12...) custom-call(s32[4]{0:T(128)} %len_ref.17, s32[1]{0:T(128)} %bitcast.me_ref, ...), custom_call_target="tpu_custom_call" | custom-call | flops 2013265920 | bytes 20000000 | tf_op jit(solution)/shard_map/retrace/pallas_call | solution.py:975
  453.9 3.9 collective-permute-start.85
  457.8 3.0 fusion
  460.8 16.6 %retrace.5 = (bf16[4,256,768]{2,1,0:T(8,128)(2,1)}, bf16[4,512,768]{2,1,0:T(8,128)(2,1)}, bf16[4,512,768]{2,1,0:T(8,128)(2,1)}, f32[8,768]{1,0:T(8,128)}, f32[12...) custom-call(s32[4]{0:T(128)} %len_ref.17, ...), custom_call_target="tpu_custom_call", output_to_operand_aliasing={{0}: (7, {}), {1}: (8, {}), {2}: (9, {})} | custom-call | flops 2013265920 | bytes 20000000 | tf_op jit(solution)/shard_map/retrace/pallas_call | solution.py:975
  484.8 13.5 %collective-permute-done.87 = bf16[4,240,384]{2,1,0:T(8,128)(2,1)} collective-permute-done((bf16[4,240,384]{2,1,0:T(8,128)(2,1)}, bf16[4,240,384]{2,1,0:T(8,128)(2,1)}, u32[]{:S(2)}, u32[]{:S(2)}) %collective-permute-start.87) | collective-permute-done | bytes 737312 | tf_op jit(solution)/shard_map/ppermute | solution.py:51
  502.3 2.8 fusion.4
  509.7 12.8 %entry_grad.3 = (bf16[16,160,384]{2,1,0:T(8,128)(2,1)}, bf16[16,160,384]{2,1,0:T(8,128)(2,1)}) custom-call(s32[4]{0:T(128)} %len_ref.17, s32[1]{0:T(128)} %bitcast.me_ref, bf16[4,256,768]{2,1,0:T(8,128)(2,1)} %get-tuple-element.757.a_ref, bf16[4,512,768]{2,1,0:T(8,128)(2,1)} %b_ref.1, bf16[4,256,768]{2,1,0:T(8,128)(2,1)} %get-tuple-element.758.dq_ref, ...), custom_call_target="tpu_custom_call" | custom-call | flops 3623878656 | bytes 16000000 | tf_op jit(solution)/shard_map/entry_grad/pallas_call | solution.py:714
  524.1 3.4 collective-permute-done.89
  534.7 7.9 %input_grads.5.refs_10_ = f32[4,512,768]{2,1,0:T(8,128)} custom-call(s32[4]{0:T(128)} %len_ref.17, s32[1]{0:T(128)} %bitcast.me_ref, bf16[4,256,768]{2,1,0:T(8,128)(2,1)} %get-tuple-element.758.dq_ref, bf16[4,512,768]{2,1,0:T(8,128)(2,1)} %get-tuple-element.759.dk_ref, bf16[4,512,768]{2,1,0:T(8,128)(2,1)} %get-tuple-element.760.dv_ref, ...), custom_call_target="tpu_custom_call" | custom-call | flops 905969664 | bytes 20000000 | tf_op jit(solution)/shard_map/input_grads/pallas_call | solution.py:1074
  550.0 7.9 %input_grads.6.refs_10_ = f32[4,512,768]{2,1,0:T(8,128)} custom-call(s32[4]{0:T(128)} %len_ref.17, s32[1]{0:T(128)} %bitcast.me_ref, bf16[4,256,768]{2,1,0:T(8,128)(2,1)} %get-tuple-element.758.dq_ref, bf16[4,512,768]{2,1,0:T(8,128)(2,1)} %get-tuple-element.759.dk_ref, ...), custom_call_target="tpu_custom_call", output_to_operand_aliasing={{}: (16, {})} | custom-call | flops 905969664 | bytes 20000000 | tf_op jit(solution)/shard_map/input_grads/pallas_call | solution.py:1074
  559.6 2.5 fusion.8
  571.9 11.2 %input_grads.7 = f32[4,512,768]{2,1,0:T(8,128)} custom-call(s32[4]{0:T(128)} %len_ref.17, s32[1]{0:T(128)} %bitcast.me_ref, bf16[4,256,768]{2,1,0:T(8,128)(2,1)} %get-tuple-element.758.dq_ref, bf16[4,512,768]{2,1,0:T(8,128)(2,1)} %get-tuple-element.759.dk_ref, bf16[4,512,768]{2,1,0:T(8,128)(2,1)} %get-tuple-element.760.dv_ref, ...), custom_call_target="tpu_custom_call", output_to_operand_aliasing={{}: (16, {})} | custom-call | flops 1811939328 | bytes 20000000 | tf_op jit(solution)/shard_map/input_grads/pallas_call | solution.py:1074
  586.4 2.9 collective-permute-start.104
  594.6 5.3 collective-permute-done.103
  (488 shorter events, 180.7 us)
Async XLA Ops:
  36.0 18.2 %collective-permute-start.15 = (bf16[4,4,48,384]{3,2,1,0:T(8,128)(2,1)S(1)}, bf16[4,4,48,384]{3,2,1,0:T(8,128)(2,1)S(1)}, u32[]{:S(2)}, u32[]{:S(2)}) collective-permute-start(bf16[4,4,48,384]{3,2,1,0:T(8,128)(2,1)S(1)} %pad_maximum_fusion.1.refs_0_), channel_id=1, source_target_pairs={{0,1},{1,0},{2,3},{3,2},{4,5},{5,4},{6,7},{7,6},{8,9},{9,8},{10,11... | collective-permute-start | bytes 1769480 | tf_op jit(solution)/shard_map/ppermute | solution.py:51
  36.0 18.2 %collective-permute-start.14 = (bf16[4,4,48,384]{3,2,1,0:T(8,128)(2,1)S(1)}, bf16[4,4,48,384]{3,2,1,0:T(8,128)(2,1)S(1)}, u32[]{:S(2)}, u32[]{:S(2)}) collective-permute-start(bf16[4,4,48,384]{3,2,1,0:T(8,128)(2,1)S(1)} %pad_maximum_fusion.1.refs_0_), channel_id=1, source_target_pairs={{0,2},{1,3},{2,0},{3,1},{4,6},{5,7},{6,4},{7,5},{8,10},{9,11},{10,... | collective-permute-start | bytes 1769480 | tf_op jit(solution)/shard_map/ppermute | solution.py:51
  55.1 17.8 %collective-permute-start.21 = (bf16[4,4,48,384]{3,2,1,0:T(8,128)(2,1)S(1)}, bf16[4,4,48,384]{3,2,1,0:T(8,128)(2,1)S(1)}, u32[]{:S(2)}, u32[]{:S(2)}) collective-permute-start(bf16[4,4,48,384]{3,2,1,0:T(8,128)(2,1)S(1)} %collective-permute-done.13.refs_2_), channel_id=1, source_target_pairs={{0,1},{1,0},{2,3},{3,2},{4,5},{5,4},{6,7},{7,6},{8,9},{9,8},{10,11... | collective-permute-start | bytes 1769480 | tf_op jit(solution)/shard_map/ppermute | solution.py:51
  55.1 17.8 %collective-permute-start.20 = (bf16[4,4,48,384]{3,2,1,0:T(8,128)(2,1)S(1)}, bf16[4,4,48,384]{3,2,1,0:T(8,128)(2,1)}, u32[]{:S(2)}, u32[]{:S(2)}) collective-permute-start(bf16[4,4,48,384]{3,2,1,0:T(8,128)(2,1)S(1)} %collective-permute-done.14.refs_1_), channel_id=1, source_target_pairs={{0,1},{1,0},{2,3},{3,2},{4,5},{5,4},{6,7},{7,6},{8,9},{9,8},{10,11... | collective-permute-start | bytes 1769480 | tf_op jit(solution)/shard_map/ppermute | solution.py:51
  75.6 25.1 %collective-permute-start.30 = (bf16[4,4,48,768]{3,2,1,0:T(8,128)(2,1)}, bf16[4,4,48,768]{3,2,1,0:T(8,128)(2,1)S(1)}, u32[]{:S(2)}, u32[]{:S(2)}) collective-permute-start(bf16[4,4,48,768]{3,2,1,0:T(8,128)(2,1)} %maximum_maximum_fusion.refs_10_.refs_20_), channel_id=1, source_target_pairs={{0,1},{1,0},{2,3},{3,2},{4,5},{5,4},{6,7},{7,6},{8,9},{9,8},{10,11... | collective-permute-start | bytes 3538952 | tf_op jit(solution)/shard_map/ppermute | solution.py:51
  76.0 28.3 %collective-permute-start.29 = (bf16[4,4,48,768]{3,2,1,0:T(8,128)(2,1)}, bf16[4,4,48,768]{3,2,1,0:T(8,128)(2,1)}, u32[]{:S(2)}, u32[]{:S(2)}) collective-permute-start(bf16[4,4,48,768]{3,2,1,0:T(8,128)(2,1)} %maximum_maximum_fusion.refs_10_.refs_20_), channel_id=1, source_target_pairs={{0,2},{1,3},{2,0},{3,1},{4,6},{5,7},{6,4},{7,5},{8,10},{9,11},{10,... | collective-permute-start | bytes 3538952 | tf_op jit(solution)/shard_map/ppermute | solution.py:51
  76.6 28.1 %collective-permute-start.28 = (bf16[4,4,48,768]{3,2,1,0:T(8,128)(2,1)}, bf16[4,4,48,768]{3,2,1,0:T(8,128)(2,1)}, u32[]{:S(2)}, u32[]{:S(2)}) collective-permute-start(bf16[4,4,48,768]{3,2,1,0:T(8,128)(2,1)} %maximum_maximum_fusion.refs_10_.refs_20_), channel_id=1, source_target_pairs={{0,4},{1,5},{2,6},{3,7},{4,0},{5,1},{6,2},{7,3},{8,12},{9,13},{10,... | collective-permute-start | bytes 3538952 | tf_op jit(solution)/shard_map/ppermute | solution.py:51
  78.1 22.5 %collective-permute-start.31 = (bf16[4,48,384]{2,1,0:T(8,128)(2,1)S(1)}, bf16[4,48,384]{2,1,0:T(8,128)(2,1)S(1)}, u32[]{:S(2)}, u32[]{:S(2)}) collective-permute-start(bf16[4,48,384]{2,1,0:T(8,128)(2,1)S(1)} %pad_maximum_fusion.21), channel_id=1, source_target_pairs={{0,8},{1,9},{2,10},{3,11},{4,12},{5,13},{6,14},{7,15},{8,0},{9,1},... | collective-permute-start | bytes 442376 | tf_op jit(solution)/shard_map/ppermute | solution.py:51
  78.1 22.6 %collective-permute-start.32 = (bf16[4,48,768]{2,1,0:T(8,128)(2,1)S(1)}, bf16[4,48,768]{2,1,0:T(8,128)(2,1)S(1)}, u32[]{:S(2)}, u32[]{:S(2)}) collective-permute-start(bf16[4,48,768]{2,1,0:T(8,128)(2,1)S(1)} %maximum_maximum_fusion.2), channel_id=1, source_target_pairs={{0,8},{1,9},{2,10},{3,11},{4,12},{5,13},{6,14},{7,15},{8,0},{9,1},... | collective-permute-start | bytes 884744 | tf_op jit(solution)/shard_map/ppermute | solution.py:51
  104.6 20.0 %collective-permute-start.36 = (bf16[4,4,48,768]{3,2,1,0:T(8,128)(2,1)}, bf16[4,4,48,768]{3,2,1,0:T(8,128)(2,1)}, u32[]{:S(2)}, u32[]{:S(2)}) collective-permute-start(bf16[4,4,48,768]{3,2,1,0:T(8,128)(2,1)} %collective-permute-done.28.refs_12_.refs_22_), channel_id=1, source_target_pairs={{0,1},{1,0},{2,3},{3,2},{4,5},{5,4},{6,7},{7,6},{8,9},{9,8},{10,11... | collective-permute-start | bytes 3538952 | tf_op jit(solution)/shard_map/ppermute | solution.py:51
  104.6 20.0 %collective-permute-start.35 = (bf16[4,4,48,768]{3,2,1,0:T(8,128)(2,1)}, bf16[4,4,48,768]{3,2,1,0:T(8,128)(2,1)}, u32[]{:S(2)}, u32[]{:S(2)}) collective-permute-start(bf16[4,4,48,768]{3,2,1,0:T(8,128)(2,1)} %collective-permute-done.29.refs_11_.refs_21_), channel_id=1, source_target_pairs={{0,1},{1,0},{2,3},{3,2},{4,5},{5,4},{6,7},{7,6},{8,9},{9,8},{10,11... | collective-permute-start | bytes 3538952 | tf_op jit(solution)/shard_map/ppermute | solution.py:51
  127.8 31.1 %collective-permute-start.42 = (bf16[4,4,48,384]{3,2,1,0:T(8,128)(2,1)S(1)}, bf16[4,4,48,384]{3,2,1,0:T(8,128)(2,1)}, u32[]{:S(2)}, u32[]{:S(2)}) collective-permute-start(bf16[4,4,48,384]{3,2,1,0:T(8,128)(2,1)S(1)} %pad_maximum_fusion.4.refs_0_), channel_id=1, source_target_pairs={{0,1},{1,0},{2,3},{3,2},{4,5},{5,4},{6,7},{7,6},{8,9},{9,8},{10,11... | collective-permute-start | bytes 1769480 | tf_op jit(solution)/shard_map/ppermute | solution.py:51
  127.9 30.9 %collective-permute-start.41 = (bf16[4,4,48,384]{3,2,1,0:T(8,128)(2,1)S(1)}, bf16[4,4,48,384]{3,2,1,0:T(8,128)(2,1)S(1)}, u32[]{:S(2)}, u32[]{:S(2)}) collective-permute-start(bf16[4,4,48,384]{3,2,1,0:T(8,128)(2,1)S(1)} %pad_maximum_fusion.4.refs_0_), channel_id=1, source_target_pairs={{0,2},{1,3},{2,0},{3,1},{4,6},{5,7},{6,4},{7,5},{8,10},{9,11},{10,... | collective-permute-start | bytes 1769480 | tf_op jit(solution)/shard_map/ppermute | solution.py:51
  128.7 30.2 %collective-permute-start.40 = (bf16[4,4,48,384]{3,2,1,0:T(8,128)(2,1)S(1)}, bf16[4,4,48,384]{3,2,1,0:T(8,128)(2,1)S(1)}, u32[]{:S(2)}, u32[]{:S(2)}) collective-permute-start(bf16[4,4,48,384]{3,2,1,0:T(8,128)(2,1)S(1)} %pad_maximum_fusion.4.refs_0_), channel_id=1, source_target_pairs={{0,4},{1,5},{2,6},{3,7},{4,0},{5,1},{6,2},{7,3},{8,12},{9,13},{10,... | collective-permute-start | bytes 1769480 | tf_op jit(solution)/shard_map/ppermute | solution.py:51
  129.2 28.4 %collective-permute-start.43 = (bf16[2,4,48,768]{3,2,1,0:T(8,128)(2,1)S(1)}, bf16[2,4,48,768]{3,2,1,0:T(8,128)(2,1)}, u32[]{:S(2)}, u32[]{:S(2)}) collective-permute-start(bf16[2,4,48,768]{3,2,1,0:T(8,128)(2,1)S(1)} %pad_maximum_fusion.3), channel_id=1, source_target_pairs={{0,16},{1,17},{2,18},{3,19},{4,20},{5,21},{6,22},{7,23},{8,24},{9,... | collective-permute-start | bytes 1769480 | tf_op jit(solution)/shard_map/ppermute | solution.py:51
  171.9 19.3 %collective-permute-start.52 = (bf16[4,4,48,768]{3,2,1,0:T(8,128)(2,1)S(1)}, bf16[4,4,48,768]{3,2,1,0:T(8,128)(2,1)}, u32[]{:S(2)}, u32[]{:S(2)}) collective-permute-start(bf16[4,4,48,768]{3,2,1,0:T(8,128)(2,1)S(1)} %pad_maximum_fusion.refs_10_.refs_20_), channel_id=1, source_target_pairs={{0,1},{1,0},{2,3},{3,2},{4,5},{5,4},{6,7},{7,6},{8,9},{9,8},{10,11... | collective-permute-start | bytes 3538952 | tf_op jit(solution)/shard_map/ppermute | solution.py:51
  172.2 28.2 %collective-permute-start.51 = (bf16[4,4,48,768]{3,2,1,0:T(8,128)(2,1)S(1)}, bf16[4,4,48,768]{3,2,1,0:T(8,128)(2,1)}, u32[]{:S(2)}, u32[]{:S(2)}) collective-permute-start(bf16[4,4,48,768]{3,2,1,0:T(8,128)(2,1)S(1)} %pad_maximum_fusion.refs_10_.refs_20_), channel_id=1, source_target_pairs={{0,2},{1,3},{2,0},{3,1},{4,6},{5,7},{6,4},{7,5},{8,10},{9,11},{10,... | collective-permute-start | bytes 3538952 | tf_op jit(solution)/shard_map/ppermute | solution.py:51
  172.7 28.0 %collective-permute-start.50 = (bf16[4,4,48,768]{3,2,1,0:T(8,128)(2,1)S(1)}, bf16[4,4,48,768]{3,2,1,0:T(8,128)(2,1)}, u32[]{:S(2)}, u32[]{:S(2)}) collective-permute-start(bf16[4,4,48,768]{3,2,1,0:T(8,128)(2,1)S(1)} %pad_maximum_fusion.refs_10_.refs_20_), channel_id=1, source_target_pairs={{0,4},{1,5},{2,6},{3,7},{4,0},{5,1},{6,2},{7,3},{8,12},{9,13},{10,... | collective-permute-start | bytes 3538952 | tf_op jit(solution)/shard_map/ppermute | solution.py:51
  200.7 19.4 %collective-permute-start.56 = (bf16[4,4,48,768]{3,2,1,0:T(8,128)(2,1)}, bf16[4,4,48,768]{3,2,1,0:T(8,128)(2,1)S(1)}, u32[]{:S(2)}, u32[]{:S(2)}) collective-permute-start(bf16[4,4,48,768]{3,2,1,0:T(8,128)(2,1)} %collective-permute-done.50.refs_12_.refs_22_), channel_id=1, source_target_pairs={{0,1},{1,0},{2,3},{3,2},{4,5},{5,4},{6,7},{7,6},{8,9},{9,8},{10,11... | collective-permute-start | bytes 3538952 | tf_op jit(solution)/shard_map/ppermute | solution.py:51
  200.7 19.4 %collective-permute-start.55 = (bf16[4,4,48,768]{3,2,1,0:T(8,128)(2,1)}, bf16[4,4,48,768]{3,2,1,0:T(8,128)(2,1)S(1)}, u32[]{:S(2)}, u32[]{:S(2)}) collective-permute-start(bf16[4,4,48,768]{3,2,1,0:T(8,128)(2,1)} %collective-permute-done.51.refs_11_.refs_21_), channel_id=1, source_target_pairs={{0,1},{1,0},{2,3},{3,2},{4,5},{5,4},{6,7},{7,6},{8,9},{9,8},{10,11... | collective-permute-start | bytes 3538952 | tf_op jit(solution)/shard_map/ppermute | solution.py:51
  294.5 23.7 %collective-permute-start.62 = (bf16[16,192,384]{2,1,0:T(8,128)(2,1)}, bf16[16,192,384]{2,1,0:T(8,128)(2,1)}, u32[]{:S(2)}, u32[]{:S(2)}) collective-permute-start(bf16[16,192,384]{2,1,0:T(8,128)(2,1)} %get-tuple-element.622), channel_id=1, source_target_pairs={{0,1},{1,0},{2,3},{3,2},{4,5},{5,4},{6,7},{7,6},{8,9},{9,8},{10,11... | collective-permute-start | bytes 7077896 | tf_op jit(solution)/shard_map/ppermute | solution.py:51
  297.2 21.0 %collective-permute-start.61 = (bf16[2,240,384]{2,1,0:T(8,128)(2,1)}, bf16[2,240,384]{2,1,0:T(8,128)(2,1)S(1)}, u32[]{:S(2)}, u32[]{:S(2)}) collective-permute-start(bf16[2,240,384]{2,1,0:T(8,128)(2,1)} %get-tuple-element.922), channel_id=1, source_target_pairs={{0,4},{1,5},{2,6},{3,7},{4,0},{5,1},{6,2},{7,3},{8,12},{9,13},{10,... | collective-permute-start | bytes 1105928 | tf_op jit(solution)/shard_map/ppermute | solution.py:51
  297.8 20.5 %collective-permute-start.60 = (bf16[2,240,384]{2,1,0:T(8,128)(2,1)}, bf16[2,240,384]{2,1,0:T(8,128)(2,1)}, u32[]{:S(2)}, u32[]{:S(2)}) collective-permute-start(bf16[2,240,384]{2,1,0:T(8,128)(2,1)} %get-tuple-element.923), channel_id=1, source_target_pairs={{0,2},{1,3},{2,0},{3,1},{4,6},{5,7},{6,4},{7,5},{8,10},{9,11},{10,... | collective-permute-start | bytes 1105928 | tf_op jit(solution)/shard_map/ppermute | solution.py:51
  321.0 28.1 %collective-permute-start.66 = (bf16[4,240,384]{2,1,0:T(8,128)(2,1)}, bf16[4,240,384]{2,1,0:T(8,128)(2,1)}, u32[]{:S(2)}, u32[]{:S(2)}) collective-permute-start(bf16[4,240,384]{2,1,0:T(8,128)(2,1)} %get-tuple-element.920), channel_id=1, source_target_pairs={{0,2},{1,3},{2,0},{3,1},{4,6},{5,7},{6,4},{7,5},{8,10},{9,11},{10,... | collective-permute-start | bytes 2211848 | tf_op jit(solution)/shard_map/ppermute | solution.py:51
  322.9 26.3 %collective-permute-start.65 = (bf16[4,240,384]{2,1,0:T(8,128)(2,1)S(1)}, bf16[4,240,384]{2,1,0:T(8,128)(2,1)}, u32[]{:S(2)}, u32[]{:S(2)}) collective-permute-start(bf16[4,240,384]{2,1,0:T(8,128)(2,1)S(1)} %get-tuple-element.921), channel_id=1, source_target_pairs={{0,4},{1,5},{2,6},{3,7},{4,0},{5,1},{6,2},{7,3},{8,12},{9,13},{10,... | collective-permute-start | bytes 2211848 | tf_op jit(solution)/shard_map/ppermute | solution.py:51
  326.5 22.7 %collective-permute-start.64 = (bf16[2,192,384]{2,1,0:T(8,128)(2,1)}, bf16[2,192,384]{2,1,0:T(8,128)(2,1)S(1)}, u32[]{:S(2)}, u32[]{:S(2)}) collective-permute-start(bf16[2,192,384]{2,1,0:T(8,128)(2,1)} %get-tuple-element.935), channel_id=1, source_target_pairs={{0,4},{1,5},{2,6},{3,7},{4,0},{5,1},{6,2},{7,3},{8,12},{9,13},{10,... | collective-permute-start | bytes 884744 | tf_op jit(solution)/shard_map/ppermute | solution.py:51
  328.0 21.1 %collective-permute-start.63 = (bf16[2,192,384]{2,1,0:T(8,128)(2,1)}, bf16[2,192,384]{2,1,0:T(8,128)(2,1)}, u32[]{:S(2)}, u32[]{:S(2)}) collective-permute-start(bf16[2,192,384]{2,1,0:T(8,128)(2,1)} %get-tuple-element.936), channel_id=1, source_target_pairs={{0,2},{1,3},{2,0},{3,1},{4,6},{5,7},{6,4},{7,5},{8,10},{9,11},{10,... | collective-permute-start | bytes 884744 | tf_op jit(solution)/shard_map/ppermute | solution.py:51
  349.2 31.3 %collective-permute-start.70 = (bf16[16,160,384]{2,1,0:T(8,128)(2,1)}, bf16[16,160,384]{2,1,0:T(8,128)(2,1)}, u32[]{:S(2)}, u32[]{:S(2)}) collective-permute-start(bf16[16,160,384]{2,1,0:T(8,128)(2,1)} %get-tuple-element.652), channel_id=1, source_target_pairs={{0,1},{1,0},{2,3},{3,2},{4,5},{5,4},{6,7},{7,6},{8,9},{9,8},{10,11... | collective-permute-start | bytes 5898248 | tf_op jit(solution)/shard_map/ppermute | solution.py:51
  351.7 28.7 %collective-permute-start.69 = (bf16[2,240,384]{2,1,0:T(8,128)(2,1)}, bf16[2,240,384]{2,1,0:T(8,128)(2,1)}, u32[]{:S(2)}, u32[]{:S(2)}) collective-permute-start(bf16[2,240,384]{2,1,0:T(8,128)(2,1)} %pad_maximum_fusion.5), channel_id=1, source_target_pairs={{0,16},{1,17},{2,18},{3,19},{4,20},{5,21},{6,22},{7,23},{8,24},{9,... | collective-permute-start | bytes 1105928 | tf_op jit(solution)/shard_map/ppermute | solution.py:51
  354.5 25.9 %collective-permute-start.68 = (bf16[4,192,384]{2,1,0:T(8,128)(2,1)}, bf16[4,192,384]{2,1,0:T(8,128)(2,1)S(1)}, u32[]{:S(2)}, u32[]{:S(2)}) collective-permute-start(bf16[4,192,384]{2,1,0:T(8,128)(2,1)} %get-tuple-element.933), channel_id=1, source_target_pairs={{0,2},{1,3},{2,0},{3,1},{4,6},{5,7},{6,4},{7,5},{8,10},{9,11},{10,... | collective-permute-start | bytes 1769480 | tf_op jit(solution)/shard_map/ppermute | solution.py:51
  356.4 24.1 %collective-permute-start.67 = (bf16[4,192,384]{2,1,0:T(8,128)(2,1)}, bf16[4,192,384]{2,1,0:T(8,128)(2,1)S(1)}, u32[]{:S(2)}, u32[]{:S(2)}) collective-permute-start(bf16[4,192,384]{2,1,0:T(8,128)(2,1)} %get-tuple-element.934), channel_id=1, source_target_pairs={{0,4},{1,5},{2,6},{3,7},{4,0},{5,1},{6,2},{7,3},{8,12},{9,13},{10,... | collective-permute-start | bytes 1769480 | tf_op jit(solution)/shard_map/ppermute | solution.py:51
  382.8 22.5 %collective-permute-start.74 = (bf16[240,384]{1,0:T(8,128)(2,1)}, bf16[240,384]{1,0:T(8,128)(2,1)}, u32[]{:S(2)}, u32[]{:S(2)}) collective-permute-start(bf16[240,384]{1,0:T(8,128)(2,1)} %fusion.29), channel_id=1, source_target_pairs={{0,8},{1,9},{2,10},{3,11},{4,12},{5,13},{6,14},{7,15},{8,0},{9,1},... | collective-permute-start | bytes 552968 | tf_op jit(solution)/shard_map/ppermute | solution.py:51
  387.1 18.3 %collective-permute-start.71 = (bf16[2,192,384]{2,1,0:T(8,128)(2,1)}, bf16[2,192,384]{2,1,0:T(8,128)(2,1)}, u32[]{:S(2)}, u32[]{:S(2)}) collective-permute-start(bf16[2,192,384]{2,1,0:T(8,128)(2,1)} %pad_maximum_fusion.8), channel_id=1, source_target_pairs={{0,16},{1,17},{2,18},{3,19},{4,20},{5,21},{6,22},{7,23},{8,24},{9,... | collective-permute-start | bytes 884744 | tf_op jit(solution)/shard_map/ppermute | solution.py:51
  405.4 18.9 %collective-permute-start.75 = (bf16[16,240,384]{2,1,0:T(8,128)(2,1)}, bf16[16,240,384]{2,1,0:T(8,128)(2,1)}, u32[]{:S(2)}, u32[]{:S(2)}) collective-permute-start(bf16[16,240,384]{2,1,0:T(8,128)(2,1)} %get-tuple-element.678), channel_id=1, source_target_pairs={{0,1},{1,0},{2,3},{3,2},{4,5},{5,4},{6,7},{7,6},{8,9},{9,8},{10,11... | collective-permute-start | bytes 8847368 | tf_op jit(solution)/shard_map/ppermute | solution.py:51
  424.3 23.5 %collective-permute-start.81 = (bf16[16,192,384]{2,1,0:T(8,128)(2,1)}, bf16[16,192,384]{2,1,0:T(8,128)(2,1)}, u32[]{:S(2)}, u32[]{:S(2)}) collective-permute-start(bf16[16,192,384]{2,1,0:T(8,128)(2,1)} %get-tuple-element.703), channel_id=1, source_target_pairs={{0,1},{1,0},{2,3},{3,2},{4,5},{5,4},{6,7},{7,6},{8,9},{9,8},{10,11... | collective-permute-start | bytes 7077896 | tf_op jit(solution)/shard_map/ppermute | solution.py:51
  426.1 21.7 %collective-permute-start.83 = (f32[120,384]{1,0:T(8,128)S(1)}, f32[120,384]{1,0:T(8,128)S(1)}, u32[]{:S(2)}, u32[]{:S(2)}) collective-permute-start(f32[120,384]{1,0:T(8,128)S(1)} %pad_maximum_fusion.15), channel_id=1, source_target_pairs={{0,1},{1,0},{2,3},{3,2},{4,5},{5,4},{6,7},{7,6},{8,9},{9,8},{10,11... | collective-permute-start | bytes 552968 | tf_op jit(solution)/shard_map/ppermute | solution.py:51
  429.0 18.8 %collective-permute-start.82 = (bf16[2,160,384]{2,1,0:T(8,128)(2,1)}, bf16[2,160,384]{2,1,0:T(8,128)(2,1)}, u32[]{:S(2)}, u32[]{:S(2)}) collective-permute-start(bf16[2,160,384]{2,1,0:T(8,128)(2,1)} %pad_maximum_fusion.12), channel_id=1, source_target_pairs={{0,16},{1,17},{2,18},{3,19},{4,20},{5,21},{6,22},{7,23},{8,24},{9,... | collective-permute-start | bytes 737288 | tf_op jit(solution)/shard_map/ppermute | solution.py:51
  449.7 35.1 %collective-permute-start.88 = (bf16[160,384]{1,0:T(8,128)(2,1)}, bf16[160,384]{1,0:T(8,128)(2,1)}, u32[]{:S(2)}, u32[]{:S(2)}) collective-permute-start(bf16[160,384]{1,0:T(8,128)(2,1)} %fusion.51), channel_id=1, source_target_pairs={{0,8},{1,9},{2,10},{3,11},{4,12},{5,13},{6,14},{7,15},{8,0},{9,1},... | collective-permute-start | bytes 368648 | tf_op jit(solution)/shard_map/ppermute | solution.py:51
  453.9 30.9 %collective-permute-start.85 = (bf16[2,192,384]{2,1,0:T(8,128)(2,1)}, bf16[2,192,384]{2,1,0:T(8,128)(2,1)}, u32[]{:S(2)}, u32[]{:S(2)}) collective-permute-start(bf16[2,192,384]{2,1,0:T(8,128)(2,1)} %get-tuple-element.931), channel_id=1, source_target_pairs={{0,4},{1,5},{2,6},{3,7},{4,0},{5,1},{6,2},{7,3},{8,12},{9,13},{10,... | collective-permute-start | bytes 884744 | tf_op jit(solution)/shard_map/ppermute | solution.py:51
  457.8 27.0 %collective-permute-start.84 = (bf16[2,192,384]{2,1,0:T(8,128)(2,1)}, bf16[2,192,384]{2,1,0:T(8,128)(2,1)}, u32[]{:S(2)}, u32[]{:S(2)}) collective-permute-start(bf16[2,192,384]{2,1,0:T(8,128)(2,1)} %get-tuple-element.932), channel_id=1, source_target_pairs={{0,2},{1,3},{2,0},{3,1},{4,6},{5,7},{6,4},{7,5},{8,10},{9,11},{10,... | collective-permute-start | bytes 884744 | tf_op jit(solution)/shard_map/ppermute | solution.py:51
  479.4 18.9 %collective-permute-start.87 = (bf16[4,240,384]{2,1,0:T(8,128)(2,1)}, bf16[4,240,384]{2,1,0:T(8,128)(2,1)}, u32[]{:S(2)}, u32[]{:S(2)}) collective-permute-start(bf16[4,240,384]{2,1,0:T(8,128)(2,1)} %get-tuple-element.914), channel_id=1, source_target_pairs={{0,2},{1,3},{2,0},{3,1},{4,6},{5,7},{6,4},{7,5},{8,10},{9,11},{10,... | collective-permute-start | bytes 2211848 | tf_op jit(solution)/shard_map/ppermute | solution.py:51
  480.4 19.7 %collective-permute-start.86 = (bf16[4,240,384]{2,1,0:T(8,128)(2,1)}, bf16[4,240,384]{2,1,0:T(8,128)(2,1)}, u32[]{:S(2)}, u32[]{:S(2)}) collective-permute-start(bf16[4,240,384]{2,1,0:T(8,128)(2,1)} %get-tuple-element.915), channel_id=1, source_target_pairs={{0,4},{1,5},{2,6},{3,7},{4,0},{5,1},{6,2},{7,3},{8,12},{9,13},{10,... | collective-permute-start | bytes 2211848 | tf_op jit(solution)/shard_map/ppermute | solution.py:51
  502.2 20.4 %collective-permute-start.92 = (f32[96,384]{1,0:T(8,128)S(1)}, f32[96,384]{1,0:T(8,128)}, u32[]{:S(2)}, u32[]{:S(2)}) collective-permute-start(f32[96,384]{1,0:T(8,128)S(1)} %pad_maximum_fusion.23), channel_id=1, source_target_pairs={{0,1},{1,0},{2,3},{3,2},{4,5},{5,4},{6,7},{7,6},{8,9},{9,8},{10,11... | collective-permute-start | bytes 442376 | tf_op jit(solution)/shard_map/ppermute | solution.py:51
  505.1 22.4 %collective-permute-start.91 = (bf16[4,192,384]{2,1,0:T(8,128)(2,1)}, bf16[4,192,384]{2,1,0:T(8,128)(2,1)S(1)}, u32[]{:S(2)}, u32[]{:S(2)}) collective-permute-start(bf16[4,192,384]{2,1,0:T(8,128)(2,1)} %get-tuple-element.929), channel_id=1, source_target_pairs={{0,2},{1,3},{2,0},{3,1},{4,6},{5,7},{6,4},{7,5},{8,10},{9,11},{10,... | collective-permute-start | bytes 1769480 | tf_op jit(solution)/shard_map/ppermute | solution.py:51
  506.0 21.6 %collective-permute-start.90 = (bf16[4,192,384]{2,1,0:T(8,128)(2,1)}, bf16[4,192,384]{2,1,0:T(8,128)(2,1)}, u32[]{:S(2)}, u32[]{:S(2)}) collective-permute-start(bf16[4,192,384]{2,1,0:T(8,128)(2,1)} %get-tuple-element.930), channel_id=1, source_target_pairs={{0,4},{1,5},{2,6},{3,7},{4,0},{5,1},{6,2},{7,3},{8,12},{9,13},{10,... | collective-permute-start | bytes 1769480 | tf_op jit(solution)/shard_map/ppermute | solution.py:51
  509.3 18.3 %collective-permute-start.89 = (bf16[2,240,384]{2,1,0:T(8,128)(2,1)}, bf16[2,240,384]{2,1,0:T(8,128)(2,1)}, u32[]{:S(2)}, u32[]{:S(2)}) collective-permute-start(bf16[2,240,384]{2,1,0:T(8,128)(2,1)} %pad_maximum_fusion.6), channel_id=1, source_target_pairs={{0,16},{1,17},{2,18},{3,19},{4,20},{5,21},{6,22},{7,23},{8,24},{9,... | collective-permute-start | bytes 1105928 | tf_op jit(solution)/shard_map/ppermute | solution.py:51
  562.1 21.0 %collective-permute-start.100 = (bf16[4,160,384]{2,1,0:T(8,128)(2,1)}, bf16[4,160,384]{2,1,0:T(8,128)(2,1)}, u32[]{:S(2)}, u32[]{:S(2)}) collective-permute-start(bf16[4,160,384]{2,1,0:T(8,128)(2,1)} %get-tuple-element.937), channel_id=1, source_target_pairs={{0,2},{1,3},{2,0},{3,1},{4,6},{5,7},{6,4},{7,5},{8,10},{9,11},{10,... | collective-permute-start | bytes 1474568 | tf_op jit(solution)/shard_map/ppermute | solution.py:51
  563.7 19.4 %collective-permute-start.99 = (bf16[4,160,384]{2,1,0:T(8,128)(2,1)}, bf16[4,160,384]{2,1,0:T(8,128)(2,1)}, u32[]{:S(2)}, u32[]{:S(2)}) collective-permute-start(bf16[4,160,384]{2,1,0:T(8,128)(2,1)} %get-tuple-element.938), channel_id=1, source_target_pairs={{0,4},{1,5},{2,6},{3,7},{4,0},{5,1},{6,2},{7,3},{8,12},{9,13},{10,... | collective-permute-start | bytes 1474568 | tf_op jit(solution)/shard_map/ppermute | solution.py:51
  (117 other events, 1283.7 us)
